TPU v7x, 32 devices: a whole 2x2x4 slice. The times are simulated.
32 devices in a mesh: parts: 2 (over y), row: 4 (over z), col: 2 (over x), chan: 2 (over core).
Axes of the slice: x: 2, y: 2, z: 4, core: 2. Of those that a mesh axis runs over, the one named last changes fastest.
Arguments:
- pair: bfloat16 [32, 128, 4096], P(('parts', 'row', 'col'), 'chan'), parts along dimension 0, may hold values from -40 to 40
- ln_in_gain: float32 [128], replicated, may hold values from 0.1 to 1.9
- a_weight: bfloat16 [2, 128, 128], P(None, None, 'chan'), may hold values from -0.5 to 0.5
- b_weight: bfloat16 [2, 128, 128], P(None, None, 'chan'), may hold values from -0.5 to 0.5
- ln_out_gain: float32 [128], replicated, may hold values from 0.1 to 1.9
- out_gate_weight: bfloat16 [128, 128], P(None, 'chan'), may hold values from -0.5 to 0.5
- out_weight: bfloat16 [128, 128], P(None, 'chan'), may hold values from -0.5 to 0.5
- a_slots: int32 [32, 4], P('parts'), parts along dimension 0, may hold values from 0 to 15, as said below
- b_slots: int32 [32, 4], P('parts'), parts along dimension 0, may hold values from 0 to 15, as said below
- counts: int32 [32], P('parts'), parts along dimension 0, may hold values from 1 to 4, as said below
Outputs:
- updated: bfloat16 [32, 128, 4096], P(('parts', 'row', 'col'), 'chan'), parts along dimension 0
There are 2 independent parts, one for each index of `parts`. A program takes and returns all parts, laid end to end along the dimension named above; an argument that names none is the same for every part. Nothing has to cross between parts.
Inputs may be any that keep to these rules, and one draw needn't show every extreme that they name: `counts`: block s lies on the tile of index s // 2 = row * 2 + col. Each output block has one to 4 used triplets; tiles with 4 for all their blocks exist in every draw, and loads differ strongly between tiles. `a_slots`: used entries (m < counts[s]) name a block on a tile of the same col whose row is within 1 row of block s's row, counted cyclically over the rows; the used entries of one output block are all different. The other entries may name any block. `b_slots`: used entries (m < counts[s]) name a block on a tile of the same col whose row is within 1 row of block s's row, counted cyclically over the rows; the used entries of one output block are all different. The used entries of a_slots and b_slots of one tile's output blocks together name at most 1 distinct blocks of any one other tile, and in every draw some tile names exactly 1 block of every other tile within reach. The other entries may name any block.
All inputs are finite; a program needn't handle non-finite values.
Results may differ from a plain program's by a relative error of at most 0.0083.
Values may be sent and summed in bfloat16 or wider, within the bound.
No kernel may reach another device: no remote copies, remote signals or barrier semaphores. Data moves between devices by JAX's collectives and lax.ppermute only.
A program may use at most 128 MiB of HBM per device.

v0:
```python
import jax
import jax.numpy as jnp
from jax import lax
from jax.sharding import PartitionSpec as P

BLK = 64


epsilon = 1e-05


def from_behind(value, axis, by):
    devices = lax.axis_size(axis)
    return lax.ppermute(value, axis, [(i, (i + by) % devices) for i in range(devices)])


def layer_norm(values, norm_gain):
    average = jnp.mean(values, axis=-2, keepdims=True)
    centred = values - average
    spread = jnp.mean(centred * centred, axis=-2, keepdims=True)
    return centred * lax.rsqrt(spread + epsilon) * norm_gain[:, None]


def gated_proj(normed, weight):
    gate_part = jnp.einsum("sdp,de->sep", normed, weight[0], preferred_element_type=jnp.float32)
    value_part = jnp.einsum("sdp,de->sep", normed, weight[1], preferred_element_type=jnp.float32)
    return (jax.nn.sigmoid(gate_part) * value_part).astype(jnp.bfloat16)


def per_device(
    pair,
    ln_in_gain,
    a_weight,
    b_weight,
    ln_out_gain,
    out_gate_weight,
    out_weight,
    a_slots,
    b_slots,
    counts,
):
    slot_count = pair.shape[0]
    triplets = a_slots.shape[1]
    grid_rows = lax.axis_size("row")
    grid_cols = lax.axis_size("col")
    grid_row = lax.axis_index("row")
    grid_col = lax.axis_index("col")
    self_index = grid_row * grid_cols + grid_col
    reach_rows = min(1, (grid_rows - 1) // 2)
    gathered = lax.all_gather(pair, "chan", axis=1, tiled=True)
    normed = layer_norm(gathered.astype(jnp.float32), ln_in_gain).astype(jnp.bfloat16)
    left_side = gated_proj(normed, a_weight)
    right_side = gated_proj(normed, b_weight)
    channels = right_side.shape[1]
    both_sides = jnp.stack([left_side, right_side], axis=1)
    left_ids = lax.dynamic_slice_in_dim(a_slots, self_index * slot_count, slot_count, 0)
    right_ids = lax.dynamic_slice_in_dim(b_slots, self_index * slot_count, slot_count, 0)
    own_counts = lax.dynamic_slice_in_dim(counts, self_index * slot_count, slot_count, 0)
    active = jnp.arange(triplets, dtype=jnp.int32)[None, :] < own_counts[:, None]
    pieces = [both_sides]
    left_where = jnp.where(left_ids // slot_count == self_index, left_ids % slot_count, 0)
    right_where = jnp.where(right_ids // slot_count == self_index, right_ids % slot_count, 0)
    next_start = slot_count
    for offset in range(-reach_rows, reach_rows + 1):
        if offset == 0:
            continue
        sender = (grid_row + offset) % grid_rows * grid_cols + grid_col
        pieces.append(from_behind(both_sides, "row", -offset))
        left_position = next_start + left_ids % slot_count
        right_position = next_start + right_ids % slot_count
        left_where = jnp.where(left_ids // slot_count == sender, left_position, left_where)
        right_where = jnp.where(right_ids // slot_count == sender, right_position, right_where)
        next_start = next_start + slot_count
    fetched = jnp.concatenate(pieces, axis=0)
    fetched_blocks = fetched.reshape(fetched.shape[0], 2, channels, BLK, BLK)

    def accumulate(triplet, running):
        left_pick = lax.dynamic_index_in_dim(left_where, triplet, 1, keepdims=False)
        right_pick = lax.dynamic_index_in_dim(right_where, triplet, 1, keepdims=False)
        active_now = lax.dynamic_index_in_dim(active, triplet, 1, keepdims=False)
        left_now = jnp.where(
            active_now[:, None, None, None],
            fetched_blocks[left_pick, 0],
            jnp.zeros((), jnp.bfloat16),
        )
        right_now = fetched_blocks[right_pick, 1]
        return running + jnp.einsum(
            "scik,scjk->scij", left_now, right_now, preferred_element_type=jnp.float32
        )

    update = lax.fori_loop(
        0, triplets, accumulate, jnp.zeros((slot_count, channels, BLK, BLK), jnp.float32)
    )
    update = update.reshape(slot_count, channels, BLK * BLK).astype(jnp.bfloat16)
    full_update = lax.all_gather(update, "chan", axis=1, tiled=True)
    update_normed = layer_norm(full_update.astype(jnp.float32), ln_out_gain).astype(jnp.bfloat16)
    out_gating = jax.nn.sigmoid(
        jnp.einsum("sdp,de->sep", normed, out_gate_weight, preferred_element_type=jnp.float32)
    )
    projected = jnp.einsum(
        "sdp,de->sep", update_normed, out_weight, preferred_element_type=jnp.float32
    )
    return (out_gating * projected).astype(jnp.bfloat16)


def solution(mesh):
    in_specs = (
        P(("parts", "row", "col"), "chan", None),
        P(),
        P(None, None, "chan"),
        P(None, None, "chan"),
        P(),
        P(None, "chan"),
        P(None, "chan"),
        P("parts", None),
        P("parts", None),
        P("parts"),
    )
    out_specs = P(("parts", "row", "col"), "chan", None)
    return jax.shard_map(
        per_device, mesh=mesh, in_specs=in_specs, out_specs=out_specs, check_vma=False
    )
```

profile of v0, /device:TPU:0, one launch (start us, length us, event | category | flops | bytes accessed | tf_op | source)
XLA Modules:
  0.0 262.6 jit_solution(13081661724356689595)
XLA Ops:
  6.5 0.0 copy-start
  6.5 0.0 all-gather.3.cloned.1.call-start
  6.5 0.7 all-gather.3.cloned.1.call-update
  7.3 0.0 all-gather.5.cloned.1.call-start
  7.3 14.9 %all-gather.3.cloned.1.call-done = bf16[2,128,4096]{2,1,0:T(8,128)(2,1)} async-done(((bf16[2,64,4096]{2,1,0:T(8,128)(2,1)}), bf16[2,128,4096]{2,1,0:T(8,128)(2,1)}) %all-gather.3.cloned.1.call-update) | async-done | bytes 2097168 | tf_op jit(solution)/shard_map/all_gather | solution.py:50
  22.2 2.1 convert_reduce_fusion.1
  24.3 0.1 copy-done.1
  24.4 0.6 fusion.26
  25.1 1.2 fusion.10
  26.3 0.0 copy-start.7
  26.4 1.0 fusion.21
  27.4 1.2 fusion.13
  28.6 1.0 fusion.22
  29.7 0.0 copy-start.10
  29.7 1.5 pad_maximum_fusion.1
  31.2 1.7 collective-permute-start
  32.9 2.1 collective-permute-start.1
  35.0 0.0 copy-done.12
  35.0 0.1 dynamic_slice.32
  35.1 0.0 copy-done.9
  35.1 0.1 select_select_fusion
  35.2 46.6 %collective-permute-done = bf16[2,2,64,4096]{3,2,0,1:T(8,128)(2,1)} collective-permute-done((bf16[2,2,64,4096]{3,2,0,1:T(8,128)(2,1)}, bf16[2,2,64,4096]{3,2,0,1:T(8,128)(2,1)}, u32[]{:S(2)}, u32[]{:S(2)}) %collective-permute-start) | collective-permute-done | bytes 2097184 | tf_op jit(solution)/shard_map/ppermute | solution.py:14
  81.8 44.0 %collective-permute-done.1 = bf16[2,2,64,4096]{3,2,0,1:T(8,128)(2,1)} collective-permute-done((bf16[2,2,64,4096]{3,2,0,1:T(8,128)(2,1)}, bf16[2,2,64,4096]{3,2,0,1:T(8,128)(2,1)}, u32[]{:S(2)}, u32[]{:S(2)}) %collective-permute-start.1) | collective-permute-done | bytes 2097184 | tf_op jit(solution)/shard_map/ppermute | solution.py:14
  125.7 5.7 %pad_maximum_fusion = bf16[6,2,64,4096]{3,2,0,1:T(8,128)(2,1)} fusion(bf16[2,2,64,4096]{3,2,0,1:T(8,128)(2,1)} %collective-permute-done.1, bf16[2,2,64,4096]{3,2,0,1:T(8,128)(2,1)} %collective-permute-done, bf16[2,1,64,4096]{3,2,0,1:T(8,128)(2,1)S(1)} %fusion.21, bf16[2,1,64,4096]{3,2,0,1:T(8,128)(2,1)S(1)} %fusion.22), kind=kLoop, calls=%fused_computation.14 | loop fusion | flops 9437184 | bytes 12582912 | tf_op jit(solution)/shard_map/concatenate | solution.py:74
  131.5 18.0 %reshape.34 = bf16[6,2,64,64,64]{4,3,2,0,1:T(8,128)(2,1)} reshape(bf16[6,2,64,4096]{3,2,0,1:T(8,128)(2,1)} %pad_maximum_fusion) | data formatting | bytes 12582912 | tf_op jit(solution)/shard_map/reshape | solution.py:75
  149.4 10.5 %copy.11 = bf16[6,2,64,64,64]{4,3,2,1,0:T(8,128)(2,1)} copy(bf16[6,2,64,64,64]{4,3,2,0,1:T(8,128)(2,1)} %reshape.34) | data formatting | bytes 12582912
  159.9 72.2 %while.14 = (s32[]{:T(128)}, f32[2,64,64,64]{3,2,1,0:T(8,128)}, pred[2,4]{0,1:T(4,128)(4,1)S(1)}, s32[2,4]{0,1:T(4,128)S(1)}, bf16[6,2,64,64,64]{4,3,2,1,0:T(8,1...) while((s32[]{:T(128)}, f32[2,64,64,64]{3,2,1,0:T(8,128)}, pred[2,4]{0,1:T(4,128)(4,1)S(1)}, ...), condition=%wide.region_3.4_spmd.clone, body=%wide.region_2.3_spmd.clone.sunk | while | flops 68681752 | bytes 10485933 | solution.py:91
  159.9 5.5 %gather_fusion = bf16[2,64,64,64]{3,2,1,0:T(8,128)(2,1)S(1)} fusion(bf16[6,2,64,64,64]{4,3,2,1,0:T(8,128)(2,1)} %get-tuple-element.219, s32[2]{0:T(128)S(1)} %get-tuple-element.197), kind=kCustom, calls=%fused_computation.1.clone.clone.1 | custom fusion | bytes 2097168 | tf_op jit(solution)/shard_map/while/body/eval_jaxpr/gather | solution.py:86
  165.4 6.7 %gather_fusion.1 = bf16[2,64,64,64]{3,2,1,0:T(8,128)(2,1)} fusion(bf16[6,2,64,64,64]{4,3,2,1,0:T(8,128)(2,1)} %get-tuple-element.219, s32[2]{0:T(128)S(1)} %get-tuple-element.198), kind=kCustom, calls=%fused_computation.clone.clone.1 | custom fusion | bytes 2097168 | tf_op jit(solution)/shard_map/while/body/eval_jaxpr/gather | solution.py:83
  172.2 4.9 %select_add_fusion.2 = f32[2,64,64,64]{3,2,1,0:T(8,128)} fusion(f32[2,64,64,64]{3,2,1,0:T(8,128)} %get-tuple-element.208, bf16[2,64,64,64]{3,2,1,0:T(8,128)(2,1)S(1)} %gather_fusion, bf16[2,64,64,64]{3,2,1,0:T(8,128)(2,1)} %gather_fusion.1, pred[2]{0:T(512)(128)(4,1)S(1)} %dynamic-slice_bitcast_fusion.2, pred[]{:T(512)S(6)} %compare.13), kind=kOutput, calls=%fused_computation.2.clone.1 | convolution fusion | flops 68681728 | bytes 6291459 | tf_op jit(solution)/shard_map/while/body/eval_jaxpr/scik,scjk->scij/dot_general | solution.py:87
  177.0 5.5 %gather_fusion = bf16[2,64,64,64]{3,2,1,0:T(8,128)(2,1)S(1)} fusion(bf16[6,2,64,64,64]{4,3,2,1,0:T(8,128)(2,1)} %get-tuple-element.219, s32[2]{0:T(128)S(1)} %get-tuple-element.197), kind=kCustom, calls=%fused_computation.1.clone.clone.1 | custom fusion | bytes 2097168 | tf_op jit(solution)/shard_map/while/body/eval_jaxpr/gather | solution.py:86
  182.6 6.7 %gather_fusion.1 = bf16[2,64,64,64]{3,2,1,0:T(8,128)(2,1)} fusion(bf16[6,2,64,64,64]{4,3,2,1,0:T(8,128)(2,1)} %get-tuple-element.219, s32[2]{0:T(128)S(1)} %get-tuple-element.198), kind=kCustom, calls=%fused_computation.clone.clone.1 | custom fusion | bytes 2097168 | tf_op jit(solution)/shard_map/while/body/eval_jaxpr/gather | solution.py:83
  189.3 6.1 %select_add_fusion.2 = f32[2,64,64,64]{3,2,1,0:T(8,128)} fusion(f32[2,64,64,64]{3,2,1,0:T(8,128)} %get-tuple-element.208, bf16[2,64,64,64]{3,2,1,0:T(8,128)(2,1)S(1)} %gather_fusion, bf16[2,64,64,64]{3,2,1,0:T(8,128)(2,1)} %gather_fusion.1, pred[2]{0:T(512)(128)(4,1)S(1)} %dynamic-slice_bitcast_fusion.2, pred[]{:T(512)S(6)} %compare.13), kind=kOutput, calls=%fused_computation.2.clone.1 | convolution fusion | flops 68681728 | bytes 6291459 | tf_op jit(solution)/shard_map/while/body/eval_jaxpr/scik,scjk->scij/dot_general | solution.py:87
  195.4 5.5 %gather_fusion = bf16[2,64,64,64]{3,2,1,0:T(8,128)(2,1)S(1)} fusion(bf16[6,2,64,64,64]{4,3,2,1,0:T(8,128)(2,1)} %get-tuple-element.219, s32[2]{0:T(128)S(1)} %get-tuple-element.197), kind=kCustom, calls=%fused_computation.1.clone.clone.1 | custom fusion | bytes 2097168 | tf_op jit(solution)/shard_map/while/body/eval_jaxpr/gather | solution.py:86
  200.9 6.7 %gather_fusion.1 = bf16[2,64,64,64]{3,2,1,0:T(8,128)(2,1)} fusion(bf16[6,2,64,64,64]{4,3,2,1,0:T(8,128)(2,1)} %get-tuple-element.219, s32[2]{0:T(128)S(1)} %get-tuple-element.198), kind=kCustom, calls=%fused_computation.clone.clone.1 | custom fusion | bytes 2097168 | tf_op jit(solution)/shard_map/while/body/eval_jaxpr/gather | solution.py:83
  207.6 6.1 %select_add_fusion.2 = f32[2,64,64,64]{3,2,1,0:T(8,128)} fusion(f32[2,64,64,64]{3,2,1,0:T(8,128)} %get-tuple-element.208, bf16[2,64,64,64]{3,2,1,0:T(8,128)(2,1)S(1)} %gather_fusion, bf16[2,64,64,64]{3,2,1,0:T(8,128)(2,1)} %gather_fusion.1, pred[2]{0:T(512)(128)(4,1)S(1)} %dynamic-slice_bitcast_fusion.2, pred[]{:T(512)S(6)} %compare.13), kind=kOutput, calls=%fused_computation.2.clone.1 | convolution fusion | flops 68681728 | bytes 6291459 | tf_op jit(solution)/shard_map/while/body/eval_jaxpr/scik,scjk->scij/dot_general | solution.py:87
  213.7 5.5 %gather_fusion = bf16[2,64,64,64]{3,2,1,0:T(8,128)(2,1)S(1)} fusion(bf16[6,2,64,64,64]{4,3,2,1,0:T(8,128)(2,1)} %get-tuple-element.219, s32[2]{0:T(128)S(1)} %get-tuple-element.197), kind=kCustom, calls=%fused_computation.1.clone.clone.1 | custom fusion | bytes 2097168 | tf_op jit(solution)/shard_map/while/body/eval_jaxpr/gather | solution.py:86
  219.3 6.7 %gather_fusion.1 = bf16[2,64,64,64]{3,2,1,0:T(8,128)(2,1)} fusion(bf16[6,2,64,64,64]{4,3,2,1,0:T(8,128)(2,1)} %get-tuple-element.219, s32[2]{0:T(128)S(1)} %get-tuple-element.198), kind=kCustom, calls=%fused_computation.clone.clone.1 | custom fusion | bytes 2097168 | tf_op jit(solution)/shard_map/while/body/eval_jaxpr/gather | solution.py:83
  226.0 6.1 %select_add_fusion.2 = f32[2,64,64,64]{3,2,1,0:T(8,128)} fusion(f32[2,64,64,64]{3,2,1,0:T(8,128)} %get-tuple-element.208, bf16[2,64,64,64]{3,2,1,0:T(8,128)(2,1)S(1)} %gather_fusion, bf16[2,64,64,64]{3,2,1,0:T(8,128)(2,1)} %gather_fusion.1, pred[2]{0:T(512)(128)(4,1)S(1)} %dynamic-slice_bitcast_fusion.2, pred[]{:T(512)S(6)} %compare.13), kind=kOutput, calls=%fused_computation.2.clone.1 | convolution fusion | flops 68681728 | bytes 6291459 | tf_op jit(solution)/shard_map/while/body/eval_jaxpr/scik,scjk->scij/dot_general | solution.py:87
  232.1 4.0 %convert_element_type.31 = bf16[2,64,64,64]{3,2,1,0:T(8,128)(2,1)} convert(f32[2,64,64,64]{3,2,1,0:T(8,128)} %get-tuple-element.114) | non-fusion elementwise | flops 524288 | bytes 3145728 | tf_op jit(solution)/shard_map/convert_element_type | solution.py:94
  236.1 4.3 %convert_element_type.32 = bf16[2,64,4096]{2,1,0:T(8,128)(2,1)} reshape(bf16[2,64,64,64]{3,2,1,0:T(8,128)(2,1)} %convert_element_type.31) | data formatting | bytes 2097152 | tf_op jit(solution)/shard_map/convert_element_type | solution.py:94
  240.4 0.0 all-gather.5.cloned.1.call-update
  240.4 2.5 fusion.16
  243.0 7.9 %all-gather.5.cloned.1.call-done = bf16[2,128,4096]{2,1,0:T(8,128)(2,1)} async-done(((bf16[2,64,4096]{2,1,0:T(8,128)(2,1)}), bf16[2,128,4096]{2,1,0:T(8,128)(2,1)}) %all-gather.5.cloned.1.call-update) | async-done | bytes 2097168 | tf_op jit(solution)/shard_map/all_gather | solution.py:95
  250.9 2.1 convert_reduce_fusion
  253.0 0.1 copy-done.3
  253.1 0.6 fusion.23
  253.7 2.0 fusion.20
  (33 shorter events, 0.2 us)
Async XLA Ops:
  6.5 233.9 %copy-start = (bf16[128,64]{0,1:T(8,128)(2,1)S(1)}, bf16[128,64]{0,1:T(8,128)(2,1)}, u32[]{:S(2)}) copy-start(bf16[128,64]{0,1:T(8,128)(2,1)} %param.17) | copy-start | bytes 49156
  6.5 15.7 %all-gather.3.cloned.1.call-start = ((), (), s32[]{:S(2)}) async-start(), calls=%async_computation | async-start | bytes 3145728 | tf_op jit(solution)/shard_map/all_gather | solution.py:50
  7.3 17.8 %copy-start.6 = (bf16[2,128,64]{1,2,0:T(8,128)(2,1)S(1)}, bf16[2,128,64]{1,2,0:T(8,128)(2,1)}, u32[]{:S(2)}) copy-start(bf16[2,128,64]{1,2,0:T(8,128)(2,1)} %param.15) | copy-start | bytes 98308
  7.3 17.8 %copy-start.8 = (f32[128]{0:T(128)S(1)}, f32[128]{0:T(128)}, u32[]{:S(2)}) copy-start(f32[128]{0:T(128)} %param.13) | copy-start | bytes 1540
  7.3 243.6 %all-gather.5.cloned.1.call-start = ((), (), s32[]{:S(2)}) async-start(), calls=%async_computation.1 | async-start | bytes 3145728 | tf_op jit(solution)/shard_map/all_gather | solution.py:95
  22.2 2.2 copy-start.1
  26.3 1.0 copy-start.7
  29.6 5.4 %copy-start.12 = (s32[16]{0:T(128)S(1)}, s32[16]{0:T(128)}, u32[]{:S(2)}) copy-start(s32[16]{0:T(128)} %param.21) | copy-start | bytes 196
  29.6 5.4 %copy-start.9 = (s32[16,4]{0,1:T(4,128)S(1)}, s32[16,4]{0,1:T(4,128)}, u32[]{:S(2)}) copy-start(s32[16,4]{0,1:T(4,128)} %param.20) | copy-start | bytes 772
  29.7 5.4 %copy-start.10 = (s32[16,4]{0,1:T(4,128)S(1)}, s32[16,4]{0,1:T(4,128)}, u32[]{:S(2)}) copy-start(s32[16,4]{0,1:T(4,128)} %param.19) | copy-start | bytes 772
  31.2 50.6 %collective-permute-start = (bf16[2,2,64,4096]{3,2,0,1:T(8,128)(2,1)}, bf16[2,2,64,4096]{3,2,0,1:T(8,128)(2,1)}, u32[]{:S(2)}, u32[]{:S(2)}) collective-permute-start(bf16[2,2,64,4096]{3,2,0,1:T(8,128)(2,1)} %pad_maximum_fusion.1), channel_id=1, source_target_pairs={{0,4},{4,8},{8,12},{12,0},{1,5},{5,9},{9,13},{13,1},{2,6},{6,10},{... | collective-permute-start | bytes 6291464 | tf_op jit(solution)/shard_map/ppermute | solution.py:14
  32.9 92.8 %collective-permute-start.1 = (bf16[2,2,64,4096]{3,2,0,1:T(8,128)(2,1)}, bf16[2,2,64,4096]{3,2,0,1:T(8,128)(2,1)}, u32[]{:S(2)}, u32[]{:S(2)}) collective-permute-start(bf16[2,2,64,4096]{3,2,0,1:T(8,128)(2,1)} %pad_maximum_fusion.1), channel_id=1, source_target_pairs={{0,12},{4,0},{8,4},{12,8},{1,13},{5,1},{9,5},{13,9},{2,14},{6,2},{... | collective-permute-start | bytes 6291464 | tf_op jit(solution)/shard_map/ppermute | solution.py:14
  236.1 4.3 %copy-start.2 = (bf16[2,128,4096]{2,1,0:T(8,128)(2,1)S(1)}, bf16[2,128,4096]{2,1,0:T(8,128)(2,1)}, u32[]{:S(2)}) copy-start(bf16[2,128,4096]{2,1,0:T(8,128)(2,1)} %all-gather.3.cloned.1.call-done) | copy-start | bytes 6291460
  242.9 10.8 %copy-start.5 = (bf16[128,64]{0,1:T(8,128)(2,1)S(1)}, bf16[128,64]{0,1:T(8,128)(2,1)}, u32[]{:S(2)}) copy-start(bf16[128,64]{0,1:T(8,128)(2,1)} %param.18) | copy-start | bytes 49156
  243.0 10.8 %copy-start.11 = (f32[128]{0:T(128)S(1)}, f32[128]{0:T(128)}, u32[]{:S(2)}) copy-start(f32[128]{0:T(128)} %param.16) | copy-start | bytes 1540
  250.9 2.2 copy-start.3
  250.9 2.9 %copy-start.4 = (f32[2,4096,64]{1,2,0:T(8,128)S(1)}, f32[2,4096,64]{1,2,0:T(8,128)}, u32[]{:S(2)}) copy-start(f32[2,4096,64]{1,2,0:T(8,128)} %fusion.16) | copy-start | bytes 6291460
Sparse Core Ops, SparseCore 0:
  8.9 13.2 all-gather.2
  240.5 10.2 all-gather.4
where the time goes:
time: 264 us; the launch traced here: 263 us
  waiting for transfers between devices  114 us (43%)
  local copies, waits for them, and re-layouts  82 us (31%)
  matrix products  32.1 us (12%)
  other arithmetic  16.9 us (6%)
  between operations  13.6 us (5%)
  starting transfers between devices  3.86 us (1%)
    ppermute x2, waiting for transfers between devices, from_behind(): lax.ppermute(value, axis, [(i, (i + by) % devices) for i in range(devices)])  90.5 us
    gather x4, local copies, waits for them, and re-layouts, accumulate(): fetched_blocks[left_pick, 0]  26.8 us
    dot_general x4, matrix products, accumulate(): jnp.einsum('scik,scjk->scij', left_now, right_now, preferred_element_type...  23.1 us
    gather x4, local copies, waits for them, and re-layouts, accumulate(): right_now = fetched_blocks[right_pick, 1]  22.1 us
    reshape x1, local copies, waits for them, and re-layouts, per_device(): fetched_blocks = fetched.reshape(fetched.shape[0], 2, channels, BLK, BLK)  18 us
    all_gather x1, waiting for transfers between devices, per_device(): gathered = lax.all_gather(pair, 'chan', axis=1, tiled=True)  14.9 us
    unnamed x27, local copies, waits for them, and re-layouts  10.7 us
    all_gather x1, waiting for transfers between devices, per_device(): full_update = lax.all_gather(update, 'chan', axis=1, tiled=True)  7.9 us
  transfers between devices with their start and end apart: 4, of which 4 were waited for; matrix products, arithmetic and copies ran while one was open for 1% of the time, Pallas kernels for 0%

commit v1 on v0

v1 whole, which is shorter than its diff:
```python
import functools

import jax
import jax.numpy as jnp
from jax import lax
from jax.experimental import pallas as pl
from jax.experimental.pallas import tpu as pltpu
from jax.sharding import PartitionSpec as P

BLK = 64
LANES = 128
epsilon = 1e-05
VMEM_LIMIT = 48 * 1024 * 1024
F32 = jnp.float32
BF16 = jnp.bfloat16


def sigmoid(x):
    return 0.5 * jnp.tanh(0.5 * x) + 0.5


def tile_of(row, col):
    return row * lax.axis_size("col") + col


def neighbour_tiles():
    rows = lax.axis_size("row")
    row, col = lax.axis_index("row"), lax.axis_index("col")
    behind = lax.rem(row + rows - 1, rows)
    ahead = lax.rem(row + 1, rows)
    return tile_of(row, col), tile_of(behind, col), tile_of(ahead, col)


def select_kernel(slots, triplets, a_ref, b_ref, n_ref, pair_ref, ahead_ref, behind_ref, sems):
    me, behind, ahead = neighbour_tiles()
    copies = []
    for at, (target, out_ref) in enumerate(((ahead, ahead_ref), (behind, behind_ref))):
        pick = jnp.int32(0)
        for s in range(slots):
            count = n_ref[target * slots + s]
            for m in range(triplets):
                for ids in (a_ref, b_ref):
                    name = ids[target * slots + s, m]
                    mine = jnp.logical_and(m < count, name // slots == me)
                    pick = jnp.where(mine, name % slots, pick)
        copies.append(pltpu.make_async_copy(pair_ref.at[pick], out_ref, sems.at[at]))
        copies[-1].start()
    for copy in copies:
        copy.wait()


def select_blocks(pair, a_slots, b_slots, counts):
    slots, channels, cells = pair.shape
    smem = pl.BlockSpec(memory_space=pltpu.SMEM)
    block = jax.ShapeDtypeStruct((channels, cells), pair.dtype)
    return pl.pallas_call(
        functools.partial(select_kernel, slots, a_slots.shape[1]),
        out_shape=(block, block),
        in_specs=[smem, smem, smem, pl.BlockSpec(memory_space=pl.ANY)],
        out_specs=(pl.BlockSpec(memory_space=pl.ANY), pl.BlockSpec(memory_space=pl.ANY)),
        scratch_shapes=[pltpu.SemaphoreType.DMA((2,))],
        name="select_blocks",
    )(a_slots, b_slots, counts, pair)


def normed_of(mine, theirs, gain):
    half = mine.shape[0]
    total = 2 * half
    mine = mine.astype(F32)
    theirs = theirs.astype(F32)
    mean = (jnp.sum(mine, axis=0, keepdims=True) + jnp.sum(theirs, axis=0, keepdims=True)) / total
    mine = mine - mean
    theirs = theirs - mean
    spread = (
        jnp.sum(mine * mine, axis=0, keepdims=True) + jnp.sum(theirs * theirs, axis=0, keepdims=True)
    ) / total
    scale = lax.rsqrt(spread + epsilon)
    return jnp.concatenate(
        [(mine * scale * gain[:half]).astype(BF16), (theirs * scale * gain[half:]).astype(BF16)],
        axis=0,
    )


def project_kernel(piece, gated, *refs):
    m0, t0, m1, t1, w_ref, g_ref = refs[:6]
    refs = refs[6:] if gated else refs[8:]
    if gated:
        l_ref, p_ref, gate_ref, sl, sp, sq = refs
    else:
        l_ref, p_ref, sl, sp, sq = refs
    chunk = m0.shape[-1]
    half = m0.shape[-2]
    weight = w_ref[...]
    gain = g_ref[...]
    low = lax.broadcasted_iota(jnp.int32, (half, LANES), 1) < BLK
    for start in range(0, chunk, piece):
        sides = []
        for x, (m, t) in enumerate(((m0, t0), (m1, t1))):
            normed = normed_of(m[:, start : start + piece], t[:, start : start + piece], gain)
            y = jnp.dot(weight, normed, preferred_element_type=F32)
            left = sigmoid(y[:half]) * y[half : 2 * half]
            right = sigmoid(y[2 * half : 3 * half]) * y[3 * half : 4 * half]
            sides.append((left, right))
            if gated:
                gate_ref[x, :, start : start + piece] = sigmoid(y[4 * half :]).astype(BF16)
        for sub in range(0, piece, LANES):
            i = (start + sub) // BLK
            even = pl.ds(i * half, half)
            odd = pl.ds((i + 1) * half, half)
            l0, l1 = (side[0][:, sub : sub + LANES] for side in sides)
            r0, r1 = (side[1][:, sub : sub + LANES] for side in sides)
            l0r, l1r, r0r, r1r = (pltpu.roll(v, BLK, 1) for v in (l0, l1, r0, r1))
            sl[even, :] = jnp.where(low, l0, l1r)
            sl[odd, :] = jnp.where(low, l0r, l1)
            sp[even, :] = jnp.where(low, r0, r1r)
            sp[odd, :] = jnp.where(low, r0r, r1)
            sq[even, :] = jnp.where(low, r1, r0r)
            sq[odd, :] = jnp.where(low, r1r, r0)
    rows = chunk // BLK

    @pl.loop(0, half, unroll=8)
    def _(c):
        take = pl.ds(c, rows, stride=half)
        l_ref[0, c] = sl[take, :].astype(BF16)
        p_ref[0, c] = sp[take, :].astype(BF16)
        p_ref[1, c] = sq[take, :].astype(BF16)


def project(blocks, weight, gain, chunk, piece, gated, held=None):
    half, cells = blocks[0].shape[-2:]
    pair_of = 0 if gated else 1
    in_specs = []
    for block, at in blocks_with_index(blocks):
        if block.ndim == 3:
            in_specs.append(
                pl.BlockSpec((None, half, chunk), functools.partial(lambda x, n: (x, 0, n), at))
            )
        else:
            in_specs.append(pl.BlockSpec((half, chunk), lambda n: (0, n)))
    rows = chunk // BLK
    whole = lambda a: pl.BlockSpec(a.shape, lambda n: (0,) * a.ndim)
    in_specs += [whole(weight), whole(gain)]
    operands = [*blocks, weight, gain]
    out_shape = [
        jax.ShapeDtypeStruct((2, half, BLK, LANES), BF16),
        jax.ShapeDtypeStruct((4, half, BLK, LANES), BF16),
    ]
    out_specs = [
        pl.BlockSpec((1, half, rows, LANES), lambda n: (pair_of, 0, n, 0)),
        pl.BlockSpec((2, half, rows, LANES), lambda n: (pair_of, 0, n, 0)),
    ]
    aliases = {}
    if gated:
        out_shape.append(jax.ShapeDtypeStruct((2, half, cells), BF16))
        out_specs.append(pl.BlockSpec((2, half, chunk), lambda n: (0, 0, n)))
    else:
        in_specs += [pl.BlockSpec(memory_space=pl.ANY)] * 2
        aliases = {len(operands): 0, len(operands) + 1: 1}
        operands += held
    return pl.pallas_call(
        functools.partial(project_kernel, piece, gated),
        grid=(cells // chunk,),
        in_specs=in_specs,
        out_specs=out_specs,
        out_shape=out_shape,
        scratch_shapes=[pltpu.VMEM((rows * half, LANES), F32)] * 3,
        input_output_aliases=aliases,
        compiler_params=pltpu.CompilerParams(vmem_limit_bytes=VMEM_LIMIT),
        cost_estimate=pl.CostEstimate(
            flops=2 * 2 * cells * weight.shape[0] * weight.shape[1],
            bytes_accessed=8 * 1024 * 1024,
            transcendentals=4 * half * cells,
        ),
        name="project_own" if gated else "project_fetched",
    )(*operands)


def blocks_with_index(blocks):
    return [(block, at // 2) for at, block in enumerate(blocks)]


def triplet_kernel(slots, triplets, group, a_ref, b_ref, n_ref, l_ref, p_ref, out_ref, acc):
    me, behind, ahead = neighbour_tiles()
    lane = lax.broadcasted_iota(jnp.int32, (1, LANES), 1)
    low = (lane < BLK).astype(F32)
    high = 1.0 - low
    picks = []
    for s in range(slots):
        block = me * slots + s
        count = n_ref[block]
        for pair_at in range(2):
            halves = []
            for part in range(2):
                chosen = jnp.int32(0)
                used = jnp.int32(0)
                for m in range(triplets):
                    left = a_ref[block, m]
                    right = b_ref[block, m]
                    if pair_at == 0:
                        hit = left == me * slots + part
                    else:
                        hit = left // slots == (behind, ahead)[part]
                    hit = jnp.logical_and(hit, m < count)
                    tile = right // slots
                    place = jnp.where(
                        tile == me, right % slots, jnp.where(tile == behind, 2, 3)
                    )
                    chosen = jnp.where(hit, place, chosen)
                    used = jnp.where(hit, 1, used)
                if part == 1:
                    chosen = chosen + 1 - 2 * lax.rem(chosen, 2)
                weight = (low, high)[part] * used.astype(F32)
                halves.append((chosen, weight.astype(BF16)))
            picks.append(halves)

    @pl.loop(0, group, unroll=4)
    def _(c):
        lhs = jnp.concatenate([l_ref[0, c], l_ref[1, c]], axis=1)
        rows = []
        for s in range(slots):
            parts = []
            for pair_at in range(2):
                (low_pick, low_mask), (high_pick, high_mask) = picks[2 * s + pair_at]
                parts.append(p_ref[low_pick, c] * low_mask + p_ref[high_pick, c] * high_mask)
            rows.append(jnp.concatenate(parts, axis=1))
        rhs = jnp.concatenate(rows, axis=0)
        acc[pl.ds(c, BLK, stride=group), :] = lax.dot_general(
            lhs, rhs, (((1,), (1,)), ((), ())), preferred_element_type=F32
        )

    take_low = lax.broadcasted_iota(jnp.int32, (group, LANES), 1) < BLK
    for t in range(BLK // 2):
        even = acc[2 * t * group : (2 * t + 1) * group, :]
        odd = acc[(2 * t + 1) * group : (2 * t + 2) * group, :]
        to = pl.ds(t * LANES, LANES)
        out_ref[0, :, to] = jnp.where(take_low, even, pltpu.roll(odd, BLK, 1)).astype(BF16)
        out_ref[1, :, to] = jnp.where(take_low, pltpu.roll(even, BLK, 1), odd).astype(BF16)


def triplet_sum(lefts, rights, a_slots, b_slots, counts, slots, group):
    half = lefts.shape[1]
    smem = pl.BlockSpec(memory_space=pltpu.SMEM)
    return pl.pallas_call(
        functools.partial(triplet_kernel, slots, a_slots.shape[1], group),
        grid=(half // group,),
        in_specs=[
            smem,
            smem,
            smem,
            pl.BlockSpec((2, group, BLK, LANES), lambda n: (0, n, 0, 0)),
            pl.BlockSpec((4, group, BLK, LANES), lambda n: (0, n, 0, 0)),
        ],
        out_specs=pl.BlockSpec((slots, group, BLK * BLK), lambda n: (0, n, 0)),
        out_shape=jax.ShapeDtypeStruct((slots, half, BLK * BLK), BF16),
        scratch_shapes=[pltpu.VMEM((BLK * group, LANES), F32)],
        compiler_params=pltpu.CompilerParams(vmem_limit_bytes=VMEM_LIMIT),
        name="triplets",
    )(a_slots, b_slots, counts, lefts, rights)


def finish_kernel(piece, mine_ref, theirs_ref, gate_ref, w_ref, g_ref, out_ref):
    weight = w_ref[...]
    gain = g_ref[...]
    for s in range(mine_ref.shape[0]):
        for start in range(0, mine_ref.shape[-1], piece):
            to = slice(start, start + piece)
            normed = normed_of(mine_ref[s, :, to], theirs_ref[s, :, to], gain)
            projected = jnp.dot(weight, normed, preferred_element_type=F32)
            out_ref[s, :, to] = (gate_ref[s, :, to].astype(F32) * projected).astype(BF16)


def finish(mine, theirs, gate, weight, gain, chunk, piece):
    slots, half, cells = mine.shape
    cut = pl.BlockSpec((slots, half, chunk), lambda n: (0, 0, n))
    return pl.pallas_call(
        functools.partial(finish_kernel, piece),
        grid=(cells // chunk,),
        in_specs=[
            cut,
            cut,
            cut,
            pl.BlockSpec(weight.shape, lambda n: (0, 0)),
            pl.BlockSpec(gain.shape, lambda n: (0, 0)),
        ],
        out_specs=cut,
        out_shape=jax.ShapeDtypeStruct(mine.shape, BF16),
        compiler_params=pltpu.CompilerParams(vmem_limit_bytes=VMEM_LIMIT),
        name="finish",
    )(mine, theirs, gate, weight, gain)


def per_device(
    pair,
    ln_in_gain,
    a_weight,
    b_weight,
    ln_out_gain,
    out_gate_weight,
    out_weight,
    a_slots,
    b_slots,
    counts,
):
    slots, half, cells = pair.shape
    rows = lax.axis_size("row")
    up = [(i, (i + 1) % rows) for i in range(rows)]
    down = [(i, (i - 1) % rows) for i in range(rows)]
    swap = [(0, 1), (1, 0)]
    chan = lax.axis_index("chan")

    to_ahead, to_behind = select_blocks(pair, a_slots, b_slots, counts)
    from_behind = lax.ppermute(to_ahead, "row", up)
    from_ahead = lax.ppermute(to_behind, "row", down)
    pair_other = lax.ppermute(pair, "chan", swap)

    def own_first(values, axis):
        return jnp.where(chan == 0, values, jnp.roll(values, half, axis))

    weight = jnp.concatenate(
        [a_weight[0], a_weight[1], b_weight[0], b_weight[1], out_gate_weight], axis=1
    )
    weight = own_first(weight, 0).T
    last_weight = own_first(out_weight, 0).T
    gain = own_first(ln_in_gain, 0)[:, None]
    last_gain = own_first(ln_out_gain, 0)[:, None]

    lefts, rights, gate = project(
        [pair, pair_other, pair, pair_other], weight, gain, 1024, 256, True
    )
    behind_other = lax.ppermute(from_behind, "chan", swap)
    ahead_other = lax.ppermute(from_ahead, "chan", swap)
    lefts, rights = project(
        [from_behind, behind_other, from_ahead, ahead_other],
        weight[: 4 * half],
        gain,
        1024,
        256,
        False,
        [lefts, rights],
    )
    update = triplet_sum(lefts, rights, a_slots, b_slots, counts, slots, 16)
    update_other = lax.ppermute(update, "chan", swap)
    return finish(update, update_other, gate, last_weight, last_gain, 1024, 256)


def solution(mesh):
    in_specs = (
        P(("parts", "row", "col"), "chan", None),
        P(),
        P(None, None, "chan"),
        P(None, None, "chan"),
        P(),
        P(None, "chan"),
        P(None, "chan"),
        P("parts", None),
        P("parts", None),
        P("parts"),
    )
    out_specs = P(("parts", "row", "col"), "chan", None)
    return jax.shard_map(
        per_device, mesh=mesh, in_specs=in_specs, out_specs=out_specs, check_vma=False
    )
```

time: 264 us -> 98 us (0.37)
  waiting for transfers between devices: 114 us -> 20.8 us
  local copies, waits for them, and re-layouts: 82 us -> 8.84 us
  Pallas kernels: 0 us -> 60.8 us
  matrix products: 32.1 us -> 0 us
  other arithmetic: 16.9 us -> 1 us
  between operations: 13.6 us -> 0.1 us
    ppermute x2 -> x6, waiting for transfers between devices: 90.5 us -> 20.8 us  [the longest x1 10.4 us: per_device(): from_ahead = lax.ppermute(to_behind, 'row', down)]
    pallas_call x0 -> x5, Pallas kernels: none -> 60.8 us  [the longest x1 33.9 us: select_blocks(): pl.pallas_call(functools.partial(select_kernel, slots, a_slots.shape[1]),...]
    gather x8 -> x0, local copies, waits for them, and re-layouts: 48.9 us -> none  [the longest x4 26.8 us: accumulate(): fetched_blocks[left_pick, 0]]
    dot_general x10 -> x0, matrix products: 32.1 us -> none  [the longest x4 23.1 us: accumulate(): jnp.einsum('scik,scjk->scij', left_now, right_now, preferred_element_type...]
    all_gather x2 -> x0, waiting for transfers between devices: 22.8 us -> none  [the longest x1 14.9 us: per_device(): gathered = lax.all_gather(pair, 'chan', axis=1, tiled=True)]
    reshape x1 -> x0, local copies, waits for them, and re-layouts: 18 us -> none  [per_device(): fetched_blocks = fetched.reshape(fetched.shape[0], 2, channels, BLK, BLK)]
    concatenate x5 -> x0, other arithmetic: 5.75 us -> none  [the longest x1 5.71 us: per_device(): fetched = jnp.concatenate(pieces, axis=0)]
    reduce_sum x4 -> x0, other arithmetic: 5.4 us -> none  [the longest x2 4.18 us: layer_norm(): average = jnp.mean(values, axis=-2, keepdims=True)]
  transfers between devices with their start and end apart: 4 -> 6, of which waited for: 4 -> 3; matrix products, arithmetic and copies ran while one was open for 1% -> 9% of each run, Pallas kernels for 0% -> 43%
where the time goes in v1:
time: 98 us; the launch traced here: 97.3 us
  Pallas kernels  60.8 us (62%)
  waiting for transfers between devices  20.8 us (21%)
  local copies, waits for them, and re-layouts  8.84 us (9%)
  starting transfers between devices  5.75 us (6%)
  other arithmetic  1 us (1%)
    pallas_call x1, Pallas kernels, select_blocks(): pl.pallas_call(functools.partial(select_kernel, slots, a_slots.shape[1]),...  33.9 us
    pallas_call x2, Pallas kernels, project(): pl.pallas_call(functools.partial(project_kernel, piece, gated), grid=(cel...  17.2 us
    ppermute x1, waiting for transfers between devices, per_device(): from_ahead = lax.ppermute(to_behind, 'row', down)  10.4 us
    ppermute x1, waiting for transfers between devices, per_device(): from_behind = lax.ppermute(to_ahead, 'row', up)  8.54 us
    unnamed x18, local copies, waits for them, and re-layouts  6.83 us
    pallas_call x1, Pallas kernels, triplet_sum(): pl.pallas_call(functools.partial(triplet_kernel, slots, a_slots.shape[1],...  6.45 us
    pallas_call x1, Pallas kernels, finish(): pl.pallas_call(functools.partial(finish_kernel, piece), grid=(cells // ch...  3.24 us
    ppermute x1, starting transfers between devices, per_device(): from_behind = lax.ppermute(to_ahead, 'row', up)  2.63 us
  transfers between devices with their start and end apart: 6, of which 3 were waited for; matrix products, arithmetic and copies ran while one was open for 9% of the time, Pallas kernels for 43%

profile of v1, /device:TPU:0, one launch (start us, length us, event | category | flops | bytes accessed | tf_op | source)
XLA Modules:
  0.0 97.3 jit_solution(7244648198020751111)
XLA Ops:
  0.0 0.5 collective-permute-start.4
  0.5 1.4 %copy.17.a_ref = s32[16,4]{1,0:T(8,128)} copy(s32[16,4]{0,1:T(4,128)} %param.17) | data formatting | bytes 512 | tf_op args[7]
  1.8 1.3 %copy.18.b_ref = s32[16,4]{1,0:T(8,128)} copy(s32[16,4]{0,1:T(4,128)} %param.18) | data formatting | bytes 512 | tf_op args[8]
  3.2 33.9 %select_blocks.1 = (bf16[64,4096]{1,0:T(8,128)(2,1)}, bf16[64,4096]{1,0:T(8,128)(2,1)}) custom-call(s32[16,4]{1,0:T(8,128)} %copy.17.a_ref, s32[16,4]{1,0:T(8,128)} %copy.18.b_ref, s32[16]{0:T(128)} %n_ref.3, bf16[2,64,4096]{2,1,0:T(8,128)(2,1)} %refs_2_.1), custom_call_target="tpu_custom_call" | custom-call | tf_op jit(solution)/shard_map/select_blocks/pallas_call | solution.py:56
  37.1 2.6 %collective-permute-start = (bf16[64,4096]{1,0:T(8,128)(2,1)}, bf16[64,4096]{1,0:T(8,128)(2,1)S(1)}, u32[]{:S(2)}, u32[]{:S(2)}) collective-permute-start(bf16[64,4096]{1,0:T(8,128)(2,1)} %get-tuple-element.12), channel_id=1, source_target_pairs={{0,4},{4,8},{8,12},{12,0},{1,5},{5,9},{9,13},{13,1},{2,6},{6,10},{... | collective-permute-start | bytes 1572872 | tf_op jit(solution)/shard_map/ppermute | solution.py:312
  39.7 2.1 %collective-permute-start.2 = (bf16[64,4096]{1,0:T(8,128)(2,1)}, bf16[64,4096]{1,0:T(8,128)(2,1)S(1)}, u32[]{:S(2)}, u32[]{:S(2)}) collective-permute-start(bf16[64,4096]{1,0:T(8,128)(2,1)} %get-tuple-element.13), channel_id=1, source_target_pairs={{0,12},{4,0},{8,4},{12,8},{1,13},{5,1},{9,5},{13,9},{2,14},{6,2},{... | collective-permute-start | bytes 1572872 | tf_op jit(solution)/shard_map/ppermute | solution.py:313
  41.8 0.7 bitcast_dynamic-update-slice_fusion.3
  42.5 0.7 bitcast_dynamic-update-slice_fusion.2
  43.3 0.8 fusion.7
  44.1 0.7 fusion.2
  44.8 0.7 bitcast_dynamic-update-slice_fusion.1
  45.5 0.7 bitcast_dynamic-update-slice_fusion
  46.2 8.5 %collective-permute-done.refs_0_ = bf16[64,4096]{1,0:T(8,128)(2,1)S(1)} collective-permute-done((bf16[64,4096]{1,0:T(8,128)(2,1)}, bf16[64,4096]{1,0:T(8,128)(2,1)S(1)}, u32[]{:S(2)}, u32[]{:S(2)}) %collective-permute-start) | collective-permute-done | bytes 524320 | tf_op jit(solution)/shard_map/ppermute | solution.py:312
  54.8 0.0 collective-permute-start.1
  54.8 10.4 %collective-permute-done.2.refs_2_ = bf16[64,4096]{1,0:T(8,128)(2,1)S(1)} collective-permute-done((bf16[64,4096]{1,0:T(8,128)(2,1)}, bf16[64,4096]{1,0:T(8,128)(2,1)S(1)}, u32[]{:S(2)}, u32[]{:S(2)}) %collective-permute-start.2) | collective-permute-done | bytes 524320 | tf_op jit(solution)/shard_map/ppermute | solution.py:313
  65.2 0.0 collective-permute-start.3
  65.2 0.7 constant_dynamic-update-slice_fusion
  66.0 0.1 copy.16.refs_5_
  66.1 0.1 fusion.4
  66.2 0.1 fusion.refs_4_
  66.3 0.0 collective-permute-done.4.refs_1_.refs_3_
  66.3 0.0 copy-start
  66.3 1.2 %copy-done = bf16[2,64,4096]{2,1,0:T(8,128)(2,1)S(1)} copy-done((bf16[2,64,4096]{2,1,0:T(8,128)(2,1)S(1)}, bf16[2,64,4096]{2,1,0:T(8,128)(2,1)}, u32[]{:S(2)}) %copy-start) | copy-done | bytes 1048600
  67.5 8.2 %project_own.1 = (bf16[2,64,64,128]{3,2,1,0:T(8,128)(2,1)S(1)}, bf16[4,64,64,128]{3,2,1,0:T(8,128)(2,1)}, bf16[2,64,4096]{2,1,0:T(8,128)(2,1)S(1)}) custom-call(bf16[2,64,4096]{2,1,0:T(8,128)(2,1)S(1)} %copy-done, bf16[2,64,4096]{2,1,0:T(8,128)(2,1)S(1)} %collective-permute-done.4.refs_1_.refs_3_, bf16[2,64,4096]{2,1,0:T(8,128)(2,1)S(1)} %copy-done, ...), custom_call_target="tpu_custom_call" | custom-call | flops 671088640 | bytes 8388608 | tf_op jit(solution)/shard_map/project_own/pallas_call | solution.py:160
  75.8 0.0 collective-permute-done.1.refs_1_
  75.8 0.0 collective-permute-done.3.refs_3_
  75.8 0.0 copy-start.1
  75.8 0.0 copy-start.2
  75.8 0.0 copy-start.3
  75.8 8.9 %project_fetched.1 = (bf16[2,64,64,128]{3,2,1,0:T(8,128)(2,1)S(1)}, bf16[4,64,64,128]{3,2,1,0:T(8,128)(2,1)}) custom-call(bf16[64,4096]{1,0:T(8,128)(2,1)S(1)} %collective-permute-done.refs_0_, bf16[64,4096]{1,0:T(8,128)(2,1)} %collective-permute-done.1.refs_1_, ...), custom_call_target="tpu_custom_call", output_to_operand_aliasing={{0}: (6, {}), {1}: (7, {})} | custom-call | flops 536870912 | bytes 8388608 | tf_op jit(solution)/shard_map/project_fetched/pallas_call | solution.py:160
  84.7 0.0 copy-start.5
  84.7 0.0 copy-start.4
  84.7 0.0 copy-done.1
  84.7 0.0 copy-done.2
  84.7 0.0 copy-done.3
  84.7 6.5 %triplets.1.mine_ref = bf16[2,64,4096]{2,1,0:T(8,128)(2,1)S(1)} custom-call(s32[16,4]{1,0:T(8,128)S(1)} %copy-done.1, s32[16,4]{1,0:T(8,128)S(1)} %copy-done.2, s32[16]{0:T(128)S(1)} %copy-done.3, bf16[2,64,64,128]{3,2,1,0:T(8,128)(2,1)S(1)} %get-tuple-element.16.l_ref, bf16[4,64,64,128]{3,2,1,0:T(8,128)(2,1)} %get-tuple-element.17.p_ref), custom_call_target="tpu_custom_call" | custom-call | tf_op jit(solution)/shard_map/triplets/pallas_call | solution.py:243
  91.2 0.6 collective-permute-start.5
  91.8 0.0 copy-done.5
  91.8 0.1 fusion.6
  91.9 0.1 fusion.3
  91.9 0.1 copy.19.g_ref
  92.0 0.0 copy-done.4
  92.1 0.1 fusion.5
  92.1 0.1 fusion.1.w_ref
  92.2 1.9 %collective-permute-done.5.theirs_ref = bf16[2,64,4096]{2,1,0:T(8,128)(2,1)S(1)} collective-permute-done((bf16[2,64,4096]{2,1,0:T(8,128)(2,1)S(1)}, bf16[2,64,4096]{2,1,0:T(8,128)(2,1)S(1)}, u32[]{:S(2)}, u32[]{:S(2)}) %collective-permute-start.5) | collective-permute-done | bytes 1048608 | tf_op jit(solution)/shard_map/ppermute | solution.py:342
  94.1 3.2 %finish.1 = bf16[2,64,4096]{2,1,0:T(8,128)(2,1)} custom-call(bf16[2,64,4096]{2,1,0:T(8,128)(2,1)S(1)} %triplets.1.mine_ref, bf16[2,64,4096]{2,1,0:T(8,128)(2,1)S(1)} %collective-permute-done.5.theirs_ref, bf16[2,64,4096]{2,1,0:T(8,128)(2,1)S(1)} %get-tuple-element.18.gate_ref, bf16[64,128]{1,0:T(8,128)(2,1)S(1)} %fusion.1.w_ref, f32[128,1]{1,0:T(8,128)S(1)} %copy.19.g_ref), custom_call_target="tpu_custom_call" | custom-call | tf_op jit(solution)/shard_map/finish/pallas_call | solution.py:275
  (1 shorter events, 0.0 us)
Async XLA Ops:
  0.0 66.3 %collective-permute-start.4 = (bf16[2,64,4096]{2,1,0:T(8,128)(2,1)}, bf16[2,64,4096]{2,1,0:T(8,128)(2,1)S(1)}, u32[]{:S(2)}, u32[]{:S(2)}) collective-permute-start(bf16[2,64,4096]{2,1,0:T(8,128)(2,1)} %refs_2_.1), channel_id=1, source_target_pairs={{0,1},{1,0},{2,3},{3,2},{4,5},{5,4},{6,7},{7,6},{8,9},{9,8},{10,11... | collective-permute-start | bytes 3145736 | tf_op jit(solution)/shard_map/ppermute | solution.py:314
  37.1 17.7 %collective-permute-start = (bf16[64,4096]{1,0:T(8,128)(2,1)}, bf16[64,4096]{1,0:T(8,128)(2,1)S(1)}, u32[]{:S(2)}, u32[]{:S(2)}) collective-permute-start(bf16[64,4096]{1,0:T(8,128)(2,1)} %get-tuple-element.12), channel_id=1, source_target_pairs={{0,4},{4,8},{8,12},{12,0},{1,5},{5,9},{9,13},{13,1},{2,6},{6,10},{... | collective-permute-start | bytes 1572872 | tf_op jit(solution)/shard_map/ppermute | solution.py:312
  39.7 25.5 %collective-permute-start.2 = (bf16[64,4096]{1,0:T(8,128)(2,1)}, bf16[64,4096]{1,0:T(8,128)(2,1)S(1)}, u32[]{:S(2)}, u32[]{:S(2)}) collective-permute-start(bf16[64,4096]{1,0:T(8,128)(2,1)} %get-tuple-element.13), channel_id=1, source_target_pairs={{0,12},{4,0},{8,4},{12,8},{1,13},{5,1},{9,5},{13,9},{2,14},{6,2},{... | collective-permute-start | bytes 1572872 | tf_op jit(solution)/shard_map/ppermute | solution.py:313
  54.8 21.0 %collective-permute-start.1 = (bf16[64,4096]{1,0:T(8,128)(2,1)S(1)}, bf16[64,4096]{1,0:T(8,128)(2,1)}, u32[]{:S(2)}, u32[]{:S(2)}) collective-permute-start(bf16[64,4096]{1,0:T(8,128)(2,1)S(1)} %collective-permute-done.refs_0_), channel_id=1, source_target_pairs={{0,1},{1,0},{2,3},{3,2},{4,5},{5,4},{6,7},{7,6},{8,9},{9,8},{10,11... | collective-permute-start | bytes 1572872 | tf_op jit(solution)/shard_map/ppermute | solution.py:330
  65.2 10.5 %collective-permute-start.3 = (bf16[64,4096]{1,0:T(8,128)(2,1)S(1)}, bf16[64,4096]{1,0:T(8,128)(2,1)}, u32[]{:S(2)}, u32[]{:S(2)}) collective-permute-start(bf16[64,4096]{1,0:T(8,128)(2,1)S(1)} %collective-permute-done.2.refs_2_), channel_id=1, source_target_pairs={{0,1},{1,0},{2,3},{3,2},{4,5},{5,4},{6,7},{7,6},{8,9},{9,8},{10,11... | collective-permute-start | bytes 1572872 | tf_op jit(solution)/shard_map/ppermute | solution.py:331
  66.3 1.2 %copy-start = (bf16[2,64,4096]{2,1,0:T(8,128)(2,1)S(1)}, bf16[2,64,4096]{2,1,0:T(8,128)(2,1)}, u32[]{:S(2)}) copy-start(bf16[2,64,4096]{2,1,0:T(8,128)(2,1)} %refs_2_.1) | copy-start | bytes 3145732
  75.8 8.9 %copy-start.1 = (s32[16,4]{1,0:T(8,128)S(1)}, s32[16,4]{1,0:T(8,128)}, u32[]{:S(2)}) copy-start(s32[16,4]{1,0:T(8,128)} %copy.17.a_ref) | copy-start | bytes 772
  75.8 8.9 %copy-start.2 = (s32[16,4]{1,0:T(8,128)S(1)}, s32[16,4]{1,0:T(8,128)}, u32[]{:S(2)}) copy-start(s32[16,4]{1,0:T(8,128)} %copy.18.b_ref) | copy-start | bytes 772
  75.8 8.9 %copy-start.3 = (s32[16]{0:T(128)S(1)}, s32[16]{0:T(128)}, u32[]{:S(2)}) copy-start(s32[16]{0:T(128)} %n_ref.3) | copy-start | bytes 196
  84.7 7.1 %copy-start.5 = (f32[128]{0:T(128)S(1)}, f32[128]{0:T(128)}, u32[]{:S(2)}) copy-start(f32[128]{0:T(128)} %param.14) | copy-start | bytes 1540
  84.7 7.3 %copy-start.4 = (bf16[128,64]{0,1:T(8,128)(2,1)S(1)}, bf16[128,64]{0,1:T(8,128)(2,1)}, u32[]{:S(2)}) copy-start(bf16[128,64]{0,1:T(8,128)(2,1)} %param.16) | copy-start | bytes 49156
  91.2 2.9 %collective-permute-start.5 = (bf16[2,64,4096]{2,1,0:T(8,128)(2,1)S(1)}, bf16[2,64,4096]{2,1,0:T(8,128)(2,1)S(1)}, u32[]{:S(2)}, u32[]{:S(2)}) collective-permute-start(bf16[2,64,4096]{2,1,0:T(8,128)(2,1)S(1)} %triplets.1.mine_ref), channel_id=1, source_target_pairs={{0,1},{1,0},{2,3},{3,2},{4,5},{5,4},{6,7},{7,6},{8,9},{9,8},{10,11... | collective-permute-start | bytes 3145736 | tf_op jit(solution)/shard_map/ppermute | solution.py:342

commit v2 on v1

--- a/solution.py
+++ b/solution.py
@@ -31,18 +31,20 @@
     return tile_of(row, col), tile_of(behind, col), tile_of(ahead, col)
 
 
-def select_kernel(slots, triplets, a_ref, b_ref, n_ref, pair_ref, ahead_ref, behind_ref, sems):
+def select_kernel(slots, triplets, a_ref, b_ref, n_ref, pair_ref, first_ref, second_ref, sems):
     me, behind, ahead = neighbour_tiles()
+    core = lax.axis_index("chan")
+    targets = (jnp.where(core == 0, ahead, behind), jnp.where(core == 0, behind, ahead))
     copies = []
-    for at, (target, out_ref) in enumerate(((ahead, ahead_ref), (behind, behind_ref))):
+    for at, (target, out_ref) in enumerate(zip(targets, (first_ref, second_ref))):
         pick = jnp.int32(0)
         for s in range(slots):
             count = n_ref[target * slots + s]
             for m in range(triplets):
                 for ids in (a_ref, b_ref):
-                    name = ids[target * slots + s, m]
-                    mine = jnp.logical_and(m < count, name // slots == me)
-                    pick = jnp.where(mine, name % slots, pick)
+                    name = ids[m, target * slots + s] - me * slots
+                    mine = jnp.logical_and(name >= 0, name < slots)
+                    pick = jnp.where(jnp.logical_and(m < count, mine), name, pick)
         copies.append(pltpu.make_async_copy(pair_ref.at[pick], out_ref, sems.at[at]))
         copies[-1].start()
     for copy in copies:
@@ -52,15 +54,30 @@
 def select_blocks(pair, a_slots, b_slots, counts):
     slots, channels, cells = pair.shape
     smem = pl.BlockSpec(memory_space=pltpu.SMEM)
+    vmem = pl.BlockSpec(memory_space=pltpu.VMEM)
     block = jax.ShapeDtypeStruct((channels, cells), pair.dtype)
     return pl.pallas_call(
-        functools.partial(select_kernel, slots, a_slots.shape[1]),
+        functools.partial(select_kernel, slots, a_slots.shape[0]),
         out_shape=(block, block),
-        in_specs=[smem, smem, smem, pl.BlockSpec(memory_space=pl.ANY)],
-        out_specs=(pl.BlockSpec(memory_space=pl.ANY), pl.BlockSpec(memory_space=pl.ANY)),
+        in_specs=[smem, smem, smem, pl.BlockSpec(memory_space=pltpu.HBM)],
+        out_specs=(vmem, vmem),
         scratch_shapes=[pltpu.SemaphoreType.DMA((2,))],
         name="select_blocks",
     )(a_slots, b_slots, counts, pair)
+
+
+def own_lanes_first(weight):
+    wide = weight.astype(F32)
+    wide = jnp.where(lax.axis_index("chan") == 0, wide, pltpu.roll(wide, weight.shape[1] // 2, 1))
+    return wide.astype(BF16)
+
+
+def gains_of(g_ref):
+    half = g_ref.shape[0] // 2
+    chan = lax.axis_index("chan")
+    mine = g_ref[pl.ds(pl.multiple_of(chan * half, half), half), :]
+    theirs = g_ref[pl.ds(pl.multiple_of((1 - chan) * half, half), half), :]
+    return mine, theirs
 
 
 def normed_of(mine, theirs, gain):
@@ -76,22 +93,23 @@
     ) / total
     scale = lax.rsqrt(spread + epsilon)
     return jnp.concatenate(
-        [(mine * scale * gain[:half]).astype(BF16), (theirs * scale * gain[half:]).astype(BF16)],
+        [(mine * scale * gain[0]).astype(BF16), (theirs * scale * gain[1]).astype(BF16)],
         axis=0,
     )
 
 
 def project_kernel(piece, gated, *refs):
-    m0, t0, m1, t1, w_ref, g_ref = refs[:6]
-    refs = refs[6:] if gated else refs[8:]
+    m0, t0, m1, t1, a_ref, b_ref, g_ref = refs[:7]
+    weights = [a_ref[0], a_ref[1], b_ref[0], b_ref[1]]
     if gated:
-        l_ref, p_ref, gate_ref, sl, sp, sq = refs
+        weights.append(refs[7][...])
+        l_ref, p_ref, gate_ref, sl, sp, sq = refs[8:]
     else:
-        l_ref, p_ref, sl, sp, sq = refs
+        l_ref, p_ref, sl, sp, sq = refs[9:]
     chunk = m0.shape[-1]
     half = m0.shape[-2]
-    weight = w_ref[...]
-    gain = g_ref[...]
+    weight = own_lanes_first(jnp.concatenate(weights, axis=0))
+    gain = gains_of(g_ref)
     low = lax.broadcasted_iota(jnp.int32, (half, LANES), 1) < BLK
     for start in range(0, chunk, piece):
         sides = []
@@ -126,7 +144,7 @@
         p_ref[1, c] = sq[take, :].astype(BF16)
 
 
-def project(blocks, weight, gain, chunk, piece, gated, held=None):
+def project(blocks, weights, gain, chunk, piece, gated, held=None):
     half, cells = blocks[0].shape[-2:]
     pair_of = 0 if gated else 1
     in_specs = []
@@ -139,8 +157,10 @@
             in_specs.append(pl.BlockSpec((half, chunk), lambda n: (0, n)))
     rows = chunk // BLK
     whole = lambda a: pl.BlockSpec(a.shape, lambda n: (0,) * a.ndim)
-    in_specs += [whole(weight), whole(gain)]
-    operands = [*blocks, weight, gain]
+    operands = [*blocks, weights[0], weights[1], gain]
+    if gated:
+        operands.append(weights[2])
+    in_specs += [whole(value) for value in operands[4:]]
     out_shape = [
         jax.ShapeDtypeStruct((2, half, BLK, LANES), BF16),
         jax.ShapeDtypeStruct((4, half, BLK, LANES), BF16),
@@ -167,7 +187,7 @@
         input_output_aliases=aliases,
         compiler_params=pltpu.CompilerParams(vmem_limit_bytes=VMEM_LIMIT),
         cost_estimate=pl.CostEstimate(
-            flops=2 * 2 * cells * weight.shape[0] * weight.shape[1],
+            flops=2 * 2 * cells * 8 * half * half,
             bytes_accessed=8 * 1024 * 1024,
             transcendentals=4 * half * cells,
         ),
@@ -194,21 +214,22 @@
                 chosen = jnp.int32(0)
                 used = jnp.int32(0)
                 for m in range(triplets):
-                    left = a_ref[block, m]
-                    right = b_ref[block, m]
+                    left = a_ref[m, block]
                     if pair_at == 0:
                         hit = left == me * slots + part
                     else:
-                        hit = left // slots == (behind, ahead)[part]
+                        first = (behind, ahead)[part] * slots
+                        hit = jnp.logical_and(left >= first, left < first + slots)
                     hit = jnp.logical_and(hit, m < count)
-                    tile = right // slots
-                    place = jnp.where(
-                        tile == me, right % slots, jnp.where(tile == behind, 2, 3)
-                    )
+                    place = b_ref[m, block] - me * slots
+                    from_me = jnp.logical_and(place >= 0, place < slots)
+                    right = b_ref[m, block] - behind * slots
+                    from_behind = jnp.logical_and(right >= 0, right < slots)
+                    place = jnp.where(from_me, place, jnp.where(from_behind, 2, 3))
                     chosen = jnp.where(hit, place, chosen)
                     used = jnp.where(hit, 1, used)
                 if part == 1:
-                    chosen = chosen + 1 - 2 * lax.rem(chosen, 2)
+                    chosen = chosen + 1 - 2 * (chosen & 1)
                 weight = (low, high)[part] * used.astype(F32)
                 halves.append((chosen, weight.astype(BF16)))
             picks.append(halves)
@@ -241,7 +262,7 @@
     half = lefts.shape[1]
     smem = pl.BlockSpec(memory_space=pltpu.SMEM)
     return pl.pallas_call(
-        functools.partial(triplet_kernel, slots, a_slots.shape[1], group),
+        functools.partial(triplet_kernel, slots, a_slots.shape[0], group),
         grid=(half // group,),
         in_specs=[
             smem,
@@ -259,8 +280,8 @@
 
 
 def finish_kernel(piece, mine_ref, theirs_ref, gate_ref, w_ref, g_ref, out_ref):
-    weight = w_ref[...]
-    gain = g_ref[...]
+    weight = own_lanes_first(w_ref[...])
+    gain = gains_of(g_ref)
     for s in range(mine_ref.shape[0]):
         for start in range(0, mine_ref.shape[-1], piece):
             to = slice(start, start + piece)
@@ -303,35 +324,33 @@
 ):
     slots, half, cells = pair.shape
     rows = lax.axis_size("row")
-    up = [(i, (i + 1) % rows) for i in range(rows)]
-    down = [(i, (i - 1) % rows) for i in range(rows)]
     swap = [(0, 1), (1, 0)]
     chan = lax.axis_index("chan")
-
-    to_ahead, to_behind = select_blocks(pair, a_slots, b_slots, counts)
-    from_behind = lax.ppermute(to_ahead, "row", up)
-    from_ahead = lax.ppermute(to_behind, "row", down)
+    core0_up = [(2 * i, 2 * ((i + 1) % rows)) for i in range(rows)]
+    core0_down = [(2 * i, 2 * ((i - 1) % rows)) for i in range(rows)]
+    core1_up = [(a + 1, b + 1) for a, b in core0_up]
+    core1_down = [(a + 1, b + 1) for a, b in core0_down]
+
+    a_slots, b_slots = a_slots.T, b_slots.T
+    a_weight, b_weight = jnp.swapaxes(a_weight, 1, 2), jnp.swapaxes(b_weight, 1, 2)
+    gain, last_gain = ln_in_gain[:, None], ln_out_gain[:, None]
+
     pair_other = lax.ppermute(pair, "chan", swap)
-
-    def own_first(values, axis):
-        return jnp.where(chan == 0, values, jnp.roll(values, half, axis))
-
-    weight = jnp.concatenate(
-        [a_weight[0], a_weight[1], b_weight[0], b_weight[1], out_gate_weight], axis=1
-    )
-    weight = own_first(weight, 0).T
-    last_weight = own_first(out_weight, 0).T
-    gain = own_first(ln_in_gain, 0)[:, None]
-    last_gain = own_first(ln_out_gain, 0)[:, None]
-
+    first, second = select_blocks(pair, a_slots, b_slots, counts)
+    first = lax.ppermute(first, ("row", "chan"), core0_up + core1_down)
+    second = lax.ppermute(second, ("row", "chan"), core0_down + core1_up)
+    weights = (a_weight, b_weight, out_gate_weight.T)
     lefts, rights, gate = project(
-        [pair, pair_other, pair, pair_other], weight, gain, 1024, 256, True
-    )
+        [pair, pair_other, pair, pair_other], weights, gain, 1024, 256, True
+    )
+    first, second, lefts = lax.optimization_barrier((first, second, lefts))
+    from_behind = jnp.where(chan == 0, first, second)
+    from_ahead = jnp.where(chan == 0, second, first)
     behind_other = lax.ppermute(from_behind, "chan", swap)
     ahead_other = lax.ppermute(from_ahead, "chan", swap)
     lefts, rights = project(
         [from_behind, behind_other, from_ahead, ahead_other],
-        weight[: 4 * half],
+        weights,
         gain,
         1024,
         256,
@@ -340,7 +359,7 @@
     )
     update = triplet_sum(lefts, rights, a_slots, b_slots, counts, slots, 16)
     update_other = lax.ppermute(update, "chan", swap)
-    return finish(update, update_other, gate, last_weight, last_gain, 1024, 256)
+    return finish(update, update_other, gate, out_weight.T, last_gain, 1024, 256)
 
 
 def solution(mesh):

time: 98 us -> 55.4 us (0.57)
  Pallas kernels: 60.8 us -> 29.1 us
  waiting for transfers between devices: 20.8 us -> 11.8 us
  local copies, waits for them, and re-layouts: 8.84 us -> 4.34 us
  starting transfers between devices: 5.75 us -> 9.51 us
    pallas_call x2, Pallas kernels: 40.4 us -> 9.34 us  [the longest x1 6.24 us: triplet_sum(): pl.pallas_call(functools.partial(triplet_kernel, slots, a_slots.shape[0],...]
    ppermute x2, waiting for transfers between devices: 19 us -> 7.37 us  [the longest x1 6.94 us: per_device(): second = lax.ppermute(second, ('row', 'chan'), core0_down + core1_up)]
    ppermute x1, starting transfers between devices: 0.01 us -> 3.82 us  [per_device(): behind_other = lax.ppermute(from_behind, 'chan', swap)]
    unnamed x18, local copies, waits for them, and re-layouts: 6.83 us -> 3.47 us
    ppermute x1, waiting for transfers between devices: 0.01 us -> 1.46 us  [per_device(): behind_other = lax.ppermute(from_behind, 'chan', swap)]
    slice x5 -> x0, local copies, waits for them, and re-layouts: 1.05 us -> none  [the longest x4 1.04 us: own_first(): return jnp.where(chan == 0, values, jnp.roll(values, half, axis))]
  transfers between devices with their start and end apart: 6 -> 6, of which waited for: 3 -> 5; matrix products, arithmetic and copies ran while one was open for 9% -> 2% of each run, Pallas kernels for 43% -> 21%
where the time goes in v2:
time: 55.4 us; the launch traced here: 54.8 us
  Pallas kernels  29.1 us (53%)
  waiting for transfers between devices  11.8 us (21%)
  starting transfers between devices  9.51 us (17%)
  local copies, waits for them, and re-layouts  4.34 us (8%)
    pallas_call x2, Pallas kernels, project(): pl.pallas_call(functools.partial(project_kernel, piece, gated), grid=(cel...  16.5 us
    ppermute x1, waiting for transfers between devices, per_device(): second = lax.ppermute(second, ('row', 'chan'), core0_down + core1_up)  6.94 us
    pallas_call x1, Pallas kernels, triplet_sum(): pl.pallas_call(functools.partial(triplet_kernel, slots, a_slots.shape[0],...  6.24 us
    ppermute x1, starting transfers between devices, per_device(): behind_other = lax.ppermute(from_behind, 'chan', swap)  3.82 us
    unnamed x18, local copies, waits for them, and re-layouts  3.47 us
    pallas_call x1, Pallas kernels, finish(): pl.pallas_call(functools.partial(finish_kernel, piece), grid=(cells // ch...  3.26 us
    pallas_call x1, Pallas kernels, select_blocks(): pl.pallas_call(functools.partial(select_kernel, slots, a_slots.shape[0]),...  3.1 us
    ppermute x1, starting transfers between devices, per_device(): first = lax.ppermute(first, ('row', 'chan'), core0_up + core1_down)  2.53 us
  transfers between devices with their start and end apart: 6, of which 5 were waited for; matrix products, arithmetic and copies ran while one was open for 2% of the time, Pallas kernels for 21%

profile of v2, /device:TPU:0, one launch (start us, length us, event | category | flops | bytes accessed | tf_op | source)
XLA Modules:
  0.0 54.8 jit_solution(18367765657548321397)
XLA Ops:
  0.0 0.5 collective-permute-start.2
  0.5 3.1 %select_blocks.1 = (bf16[64,4096]{1,0:T(8,128)(2,1)}, bf16[64,4096]{1,0:T(8,128)(2,1)}) custom-call(s32[4,16]{1,0:T(4,128)} %bitcast.14, s32[4,16]{1,0:T(4,128)} %bitcast.16, s32[16]{0:T(128)} %n_ref.3, bf16[2,64,4096]{2,1,0:T(8,128)(2,1)} %refs_2_.1), custom_call_target="tpu_custom_call" | custom-call | tf_op jit(solution)/shard_map/select_blocks/pallas_call | solution.py:59
  3.6 2.5 %collective-permute-start = (bf16[64,4096]{1,0:T(8,128)(2,1)}, bf16[64,4096]{1,0:T(8,128)(2,1)S(1)}, u32[]{:S(2)}, u32[]{:S(2)}) collective-permute-start(bf16[64,4096]{1,0:T(8,128)(2,1)} %get-tuple-element.15), channel_id=1, source_target_pairs={{0,4},{4,8},{8,12},{12,0},{1,13},{5,1},{9,5},{13,9},{2,6},{6,10},{... | collective-permute-start | bytes 1572872 | tf_op jit(solution)/shard_map/ppermute | solution.py:340
  6.1 2.2 %collective-permute-start.1 = (bf16[64,4096]{1,0:T(8,128)(2,1)}, bf16[64,4096]{1,0:T(8,128)(2,1)S(1)}, u32[]{:S(2)}, u32[]{:S(2)}) collective-permute-start(bf16[64,4096]{1,0:T(8,128)(2,1)} %get-tuple-element.16), channel_id=1, source_target_pairs={{0,12},{4,0},{8,4},{12,8},{1,5},{5,9},{9,13},{13,1},{2,14},{6,2},{... | collective-permute-start | bytes 1572872 | tf_op jit(solution)/shard_map/ppermute | solution.py:341
  8.3 0.8 %copy.13.refs_6_ = f32[128,1]{1,0:T(8,128)S(1)} copy(f32[128,1]{0,1:T(1,128)} %bitcast.18) | data formatting | bytes 1024 | tf_op jit(solution)/shard_map/broadcast_in_dim | solution.py:336
  9.0 0.0 collective-permute-done.2.refs_1_.refs_3_
  9.0 0.0 copy-start
  9.1 1.2 %copy-done = bf16[2,64,4096]{2,1,0:T(8,128)(2,1)S(1)} copy-done((bf16[2,64,4096]{2,1,0:T(8,128)(2,1)S(1)}, bf16[2,64,4096]{2,1,0:T(8,128)(2,1)}, u32[]{:S(2)}) %copy-start) | copy-done | bytes 1048600
  10.3 0.0 copy-start.1
  10.3 0.8 %copy-done.1 = bf16[2,128,64]{1,2,0:T(8,128)(2,1)S(1)} copy-done((bf16[2,128,64]{1,2,0:T(8,128)(2,1)S(1)}, bf16[2,128,64]{1,2,0:T(8,128)(2,1)}, u32[]{:S(2)}) %copy-start.1) | copy-done | bytes 32792
  11.0 0.0 copy-start.2
  11.0 0.8 %copy-done.2 = bf16[2,128,64]{1,2,0:T(8,128)(2,1)S(1)} copy-done((bf16[2,128,64]{1,2,0:T(8,128)(2,1)S(1)}, bf16[2,128,64]{1,2,0:T(8,128)(2,1)}, u32[]{:S(2)}) %copy-start.2) | copy-done | bytes 32792
  11.8 0.0 copy-start.3
  11.8 0.7 %copy-done.3 = bf16[128,64]{0,1:T(8,128)(2,1)S(1)} copy-done((bf16[128,64]{0,1:T(8,128)(2,1)S(1)}, bf16[128,64]{0,1:T(8,128)(2,1)}, u32[]{:S(2)}) %copy-start.3) | copy-done | bytes 16408
  12.5 8.4 %project_own.1 = (bf16[2,64,64,128]{3,2,1,0:T(8,128)(2,1)S(1)}, bf16[4,64,64,128]{3,2,1,0:T(8,128)(2,1)}, bf16[2,64,4096]{2,1,0:T(8,128)(2,1)S(1)}) custom-call(bf16[2,64,4096]{2,1,0:T(8,128)(2,1)S(1)} %copy-done, bf16[2,64,4096]{2,1,0:T(8,128)(2,1)S(1)} %collective-permute-done.2.refs_1_.refs_3_, bf16[2,64,4096]{2,1,0:T(8,128)(2,1)S(1)} %copy-done, ...), custom_call_target="tpu_custom_call" | custom-call | flops 536870912 | bytes 8388608 | tf_op jit(solution)/shard_map/project_own/pallas_call | solution.py:180
  20.9 0.4 collective-permute-done
  21.3 6.9 %collective-permute-done.1 = bf16[64,4096]{1,0:T(8,128)(2,1)S(1)} collective-permute-done((bf16[64,4096]{1,0:T(8,128)(2,1)}, bf16[64,4096]{1,0:T(8,128)(2,1)S(1)}, u32[]{:S(2)}, u32[]{:S(2)}) %collective-permute-start.1) | collective-permute-done | bytes 524320 | tf_op jit(solution)/shard_map/ppermute | solution.py:341
  28.3 0.1 broadcast_select_fusion
  28.3 3.8 %collective-permute-start.3 = (bf16[64,4096]{1,0:T(8,128)(2,1)S(1)}, bf16[64,4096]{1,0:T(8,128)(2,1)S(1)}, u32[]{:S(2)}, u32[]{:S(2)}) collective-permute-start(bf16[64,4096]{1,0:T(8,128)(2,1)S(1)} %get-tuple-element.26.refs_0_), channel_id=1, source_target_pairs={{0,1},{1,0},{2,3},{3,2},{4,5},{5,4},{6,7},{7,6},{8,9},{9,8},{10,11... | collective-permute-start | bytes 1572872 | tf_op jit(solution)/shard_map/ppermute | solution.py:349
  32.2 0.1 collective-permute-start.4
  32.2 1.5 %collective-permute-done.3.refs_1_ = bf16[64,4096]{1,0:T(8,128)(2,1)S(1)} collective-permute-done((bf16[64,4096]{1,0:T(8,128)(2,1)S(1)}, bf16[64,4096]{1,0:T(8,128)(2,1)S(1)}, u32[]{:S(2)}, u32[]{:S(2)}) %collective-permute-start.3) | collective-permute-done | bytes 524320 | tf_op jit(solution)/shard_map/ppermute | solution.py:349
  33.7 0.7 %collective-permute-done.4.refs_3_ = bf16[64,4096]{1,0:T(8,128)(2,1)S(1)} collective-permute-done((bf16[64,4096]{1,0:T(8,128)(2,1)S(1)}, bf16[64,4096]{1,0:T(8,128)(2,1)S(1)}, u32[]{:S(2)}, u32[]{:S(2)}) %collective-permute-start.4) | collective-permute-done | bytes 524320 | tf_op jit(solution)/shard_map/ppermute | solution.py:350
  34.4 0.0 copy-start.5
  34.4 0.0 copy-start.6
  34.4 0.0 copy-start.7
  34.5 8.1 %project_fetched.1 = (bf16[2,64,64,128]{3,2,1,0:T(8,128)(2,1)S(1)}, bf16[4,64,64,128]{3,2,1,0:T(8,128)(2,1)}) custom-call(bf16[64,4096]{1,0:T(8,128)(2,1)S(1)} %get-tuple-element.26.refs_0_, bf16[64,4096]{1,0:T(8,128)(2,1)S(1)} %collective-permute-done.3.refs_1_, ...), custom_call_target="tpu_custom_call", output_to_operand_aliasing={{0}: (7, {}), {1}: (8, {})} | custom-call | flops 536870912 | bytes 8388608 | tf_op jit(solution)/shard_map/project_fetched/pallas_call | solution.py:180
  42.6 0.0 copy-start.8
  42.6 0.0 copy-start.4
  42.6 0.0 copy-done.5
  42.6 0.0 copy-done.6
  42.6 0.0 copy-done.7
  42.6 6.2 %triplets.1.mine_ref = bf16[2,64,4096]{2,1,0:T(8,128)(2,1)S(1)} custom-call(s32[4,16]{1,0:T(4,128)S(1)} %bitcast.15, s32[4,16]{1,0:T(4,128)S(1)} %bitcast.17, s32[16]{0:T(128)S(1)} %copy-done.7, bf16[2,64,64,128]{3,2,1,0:T(8,128)(2,1)S(1)} %get-tuple-element.22.l_ref, bf16[4,64,64,128]{3,2,1,0:T(8,128)(2,1)} %get-tuple-element.23.p_ref), custom_call_target="tpu_custom_call" | custom-call | tf_op jit(solution)/shard_map/triplets/pallas_call | solution.py:264
  48.9 0.4 collective-permute-start.5
  49.3 0.0 copy-done.8
  49.3 0.1 copy.15.g_ref
  49.4 2.2 %collective-permute-done.5.theirs_ref = bf16[2,64,4096]{2,1,0:T(8,128)(2,1)S(1)} collective-permute-done((bf16[2,64,4096]{2,1,0:T(8,128)(2,1)S(1)}, bf16[2,64,4096]{2,1,0:T(8,128)(2,1)S(1)}, u32[]{:S(2)}, u32[]{:S(2)}) %collective-permute-start.5) | collective-permute-done | bytes 1048608 | tf_op jit(solution)/shard_map/ppermute | solution.py:361
  51.6 0.0 copy-done.4
  51.6 3.3 %finish.1 = bf16[2,64,4096]{2,1,0:T(8,128)(2,1)} custom-call(bf16[2,64,4096]{2,1,0:T(8,128)(2,1)S(1)} %triplets.1.mine_ref, bf16[2,64,4096]{2,1,0:T(8,128)(2,1)S(1)} %collective-permute-done.5.theirs_ref, bf16[2,64,4096]{2,1,0:T(8,128)(2,1)S(1)} %get-tuple-element.24.gate_ref, bf16[64,128]{1,0:T(8,128)(2,1)S(1)} %bitcast.13, f32[128,1]{1,0:T(8,128)S(1)} %copy.15.g_ref), custom_call_target="tpu_custom_call" | custom-call | tf_op jit(solution)/shard_map/finish/pallas_call | solution.py:296
Async XLA Ops:
  0.0 9.0 %collective-permute-start.2 = (bf16[2,64,4096]{2,1,0:T(8,128)(2,1)}, bf16[2,64,4096]{2,1,0:T(8,128)(2,1)S(1)}, u32[]{:S(2)}, u32[]{:S(2)}) collective-permute-start(bf16[2,64,4096]{2,1,0:T(8,128)(2,1)} %refs_2_.1), channel_id=1, source_target_pairs={{0,1},{1,0},{2,3},{3,2},{4,5},{5,4},{6,7},{7,6},{8,9},{9,8},{10,11... | collective-permute-start | bytes 3145736 | tf_op jit(solution)/shard_map/ppermute | solution.py:338
  3.6 17.8 %collective-permute-start = (bf16[64,4096]{1,0:T(8,128)(2,1)}, bf16[64,4096]{1,0:T(8,128)(2,1)S(1)}, u32[]{:S(2)}, u32[]{:S(2)}) collective-permute-start(bf16[64,4096]{1,0:T(8,128)(2,1)} %get-tuple-element.15), channel_id=1, source_target_pairs={{0,4},{4,8},{8,12},{12,0},{1,13},{5,1},{9,5},{13,9},{2,6},{6,10},{... | collective-permute-start | bytes 1572872 | tf_op jit(solution)/shard_map/ppermute | solution.py:340
  6.1 22.2 %collective-permute-start.1 = (bf16[64,4096]{1,0:T(8,128)(2,1)}, bf16[64,4096]{1,0:T(8,128)(2,1)S(1)}, u32[]{:S(2)}, u32[]{:S(2)}) collective-permute-start(bf16[64,4096]{1,0:T(8,128)(2,1)} %get-tuple-element.16), channel_id=1, source_target_pairs={{0,12},{4,0},{8,4},{12,8},{1,5},{5,9},{9,13},{13,1},{2,14},{6,2},{... | collective-permute-start | bytes 1572872 | tf_op jit(solution)/shard_map/ppermute | solution.py:341
  9.0 1.2 %copy-start = (bf16[2,64,4096]{2,1,0:T(8,128)(2,1)S(1)}, bf16[2,64,4096]{2,1,0:T(8,128)(2,1)}, u32[]{:S(2)}) copy-start(bf16[2,64,4096]{2,1,0:T(8,128)(2,1)} %refs_2_.1) | copy-start | bytes 3145732
  10.3 0.8 %copy-start.1 = (bf16[2,128,64]{1,2,0:T(8,128)(2,1)S(1)}, bf16[2,128,64]{1,2,0:T(8,128)(2,1)}, u32[]{:S(2)}) copy-start(bf16[2,128,64]{1,2,0:T(8,128)(2,1)} %param.12) | copy-start | bytes 98308
  11.0 0.8 %copy-start.2 = (bf16[2,128,64]{1,2,0:T(8,128)(2,1)S(1)}, bf16[2,128,64]{1,2,0:T(8,128)(2,1)}, u32[]{:S(2)}) copy-start(bf16[2,128,64]{1,2,0:T(8,128)(2,1)} %param.13) | copy-start | bytes 98308
  11.8 0.7 %copy-start.3 = (bf16[128,64]{0,1:T(8,128)(2,1)S(1)}, bf16[128,64]{0,1:T(8,128)(2,1)}, u32[]{:S(2)}) copy-start(bf16[128,64]{0,1:T(8,128)(2,1)} %param.15) | copy-start | bytes 49156
  28.3 5.4 %collective-permute-start.3 = (bf16[64,4096]{1,0:T(8,128)(2,1)S(1)}, bf16[64,4096]{1,0:T(8,128)(2,1)S(1)}, u32[]{:S(2)}, u32[]{:S(2)}) collective-permute-start(bf16[64,4096]{1,0:T(8,128)(2,1)S(1)} %get-tuple-element.26.refs_0_), channel_id=1, source_target_pairs={{0,1},{1,0},{2,3},{3,2},{4,5},{5,4},{6,7},{7,6},{8,9},{9,8},{10,11... | collective-permute-start | bytes 1572872 | tf_op jit(solution)/shard_map/ppermute | solution.py:349
  32.2 2.3 %collective-permute-start.4 = (bf16[64,4096]{1,0:T(8,128)(2,1)S(1)}, bf16[64,4096]{1,0:T(8,128)(2,1)S(1)}, u32[]{:S(2)}, u32[]{:S(2)}) collective-permute-start(bf16[64,4096]{1,0:T(8,128)(2,1)S(1)} %get-tuple-element.25.refs_2_), channel_id=1, source_target_pairs={{0,1},{1,0},{2,3},{3,2},{4,5},{5,4},{6,7},{7,6},{8,9},{9,8},{10,11... | collective-permute-start | bytes 1572872 | tf_op jit(solution)/shard_map/ppermute | solution.py:350
  34.4 8.1 %copy-start.5 = (s32[16,4]{0,1:T(4,128)S(1)}, s32[16,4]{0,1:T(4,128)}, u32[]{:S(2)}) copy-start(s32[16,4]{0,1:T(4,128)} %param.17) | copy-start | bytes 772
  34.4 8.1 %copy-start.6 = (s32[16,4]{0,1:T(4,128)S(1)}, s32[16,4]{0,1:T(4,128)}, u32[]{:S(2)}) copy-start(s32[16,4]{0,1:T(4,128)} %param.18) | copy-start | bytes 772
  34.4 8.1 %copy-start.7 = (s32[16]{0:T(128)S(1)}, s32[16]{0:T(128)}, u32[]{:S(2)}) copy-start(s32[16]{0:T(128)} %n_ref.3) | copy-start | bytes 196
  42.6 6.7 %copy-start.8 = (f32[128]{0:T(128)S(1)}, f32[128]{0:T(128)}, u32[]{:S(2)}) copy-start(f32[128]{0:T(128)} %param.14) | copy-start | bytes 1540
  42.6 9.0 %copy-start.4 = (bf16[128,64]{0,1:T(8,128)(2,1)S(1)}, bf16[128,64]{0,1:T(8,128)(2,1)}, u32[]{:S(2)}) copy-start(bf16[128,64]{0,1:T(8,128)(2,1)} %param.16) | copy-start | bytes 49156
  48.9 2.7 %collective-permute-start.5 = (bf16[2,64,4096]{2,1,0:T(8,128)(2,1)S(1)}, bf16[2,64,4096]{2,1,0:T(8,128)(2,1)S(1)}, u32[]{:S(2)}, u32[]{:S(2)}) collective-permute-start(bf16[2,64,4096]{2,1,0:T(8,128)(2,1)S(1)} %triplets.1.mine_ref), channel_id=1, source_target_pairs={{0,1},{1,0},{2,3},{3,2},{4,5},{5,4},{6,7},{7,6},{8,9},{9,8},{10,11... | collective-permute-start | bytes 3145736 | tf_op jit(solution)/shard_map/ppermute | solution.py:361

commit v3 on v2

v3 whole, which is shorter than its diff:
```python
import functools

import jax
import jax.numpy as jnp
from jax import lax
from jax.experimental import pallas as pl
from jax.experimental.pallas import tpu as pltpu
from jax.sharding import PartitionSpec as P

BLK = 64
LANES = 128
epsilon = 1e-05
VMEM_LIMIT = 48 * 1024 * 1024
F32 = jnp.float32
BF16 = jnp.bfloat16


def sigmoid(x):
    return 0.5 * jnp.tanh(0.5 * x) + 0.5


def tile_of(row, col):
    return row * lax.axis_size("col") + col


def neighbour_tiles():
    rows = lax.axis_size("row")
    row, col = lax.axis_index("row"), lax.axis_index("col")
    behind = lax.rem(row + rows - 1, rows)
    ahead = lax.rem(row + 1, rows)
    return tile_of(row, col), tile_of(behind, col), tile_of(ahead, col)


def select_kernel(slots, triplets, cuts, a_ref, b_ref, n_ref, pair_ref, *refs):
    me, behind, ahead = neighbour_tiles()
    out_refs, sems = refs[:-1], refs[-1]
    picks = []
    for target in (ahead, behind):
        pick = jnp.int32(0)
        for s in range(slots):
            count = n_ref[target * slots + s]
            for m in range(triplets):
                for ids in (a_ref, b_ref):
                    name = ids[m, target * slots + s] - me * slots
                    mine = jnp.logical_and(name >= 0, name < slots)
                    pick = jnp.where(jnp.logical_and(m < count, mine), name, pick)
        picks.append(pick)
    copies = []
    for at, (start, size) in enumerate(cuts):
        for which, pick in enumerate(picks):
            out = 2 * at + which
            copies.append(
                pltpu.make_async_copy(
                    pair_ref.at[pick, :, pl.ds(start, size)], out_refs[out], sems.at[out]
                )
            )
            copies[-1].start()
    for copy in copies:
        copy.wait()


def select_blocks(pair, a_slots, b_slots, counts, cuts):
    slots, channels, cells = pair.shape
    smem = pl.BlockSpec(memory_space=pltpu.SMEM)
    vmem = pl.BlockSpec(memory_space=pltpu.VMEM)
    out_shape = [
        jax.ShapeDtypeStruct((channels, size), pair.dtype) for _, size in cuts for _ in range(2)
    ]
    return pl.pallas_call(
        functools.partial(select_kernel, slots, a_slots.shape[0], cuts),
        out_shape=out_shape,
        in_specs=[smem, smem, smem, pl.BlockSpec(memory_space=pltpu.HBM)],
        out_specs=[vmem] * len(out_shape),
        scratch_shapes=[pltpu.SemaphoreType.DMA((len(out_shape),))],
        name="select_blocks",
    )(a_slots, b_slots, counts, pair)


def own_lanes_first(weight):
    wide = weight.astype(F32)
    wide = jnp.where(lax.axis_index("chan") == 0, wide, pltpu.roll(wide, weight.shape[1] // 2, 1))
    return wide.astype(BF16)


def gains_of(g_ref):
    half = g_ref.shape[0] // 2
    chan = lax.axis_index("chan")
    mine = g_ref[pl.ds(pl.multiple_of(chan * half, half), half), :]
    theirs = g_ref[pl.ds(pl.multiple_of((1 - chan) * half, half), half), :]
    return mine, theirs


def normed_of(mine, theirs, gain):
    half = mine.shape[0]
    total = 2 * half
    mine = mine.astype(F32)
    theirs = theirs.astype(F32)
    mean = (jnp.sum(mine, axis=0, keepdims=True) + jnp.sum(theirs, axis=0, keepdims=True)) / total
    mine = mine - mean
    theirs = theirs - mean
    spread = (
        jnp.sum(mine * mine, axis=0, keepdims=True) + jnp.sum(theirs * theirs, axis=0, keepdims=True)
    ) / total
    scale = lax.rsqrt(spread + epsilon)
    return jnp.concatenate(
        [(mine * scale * gain[0]).astype(BF16), (theirs * scale * gain[1]).astype(BF16)],
        axis=0,
    )


def project_kernel(piece, gated, *refs):
    m0, t0, m1, t1, a_ref, b_ref, g_ref = refs[:7]
    weights = [a_ref[0], a_ref[1], b_ref[0], b_ref[1]]
    if gated:
        weights.append(refs[7][...])
        l_ref, p_ref, gate_ref, sl, sp, sq = refs[8:]
    else:
        l_ref, p_ref, sl, sp, sq = refs[9:]
    chunk = m0.shape[-1]
    half = m0.shape[-2]
    weight = own_lanes_first(jnp.concatenate(weights, axis=0))
    gain = gains_of(g_ref)
    low = lax.broadcasted_iota(jnp.int32, (half, LANES), 1) < BLK
    for start in range(0, chunk, piece):
        sides = []
        for x, (m, t) in enumerate(((m0, t0), (m1, t1))):
            normed = normed_of(m[:, start : start + piece], t[:, start : start + piece], gain)
            y = jnp.dot(weight, normed, preferred_element_type=F32)
            left = sigmoid(y[:half]) * y[half : 2 * half]
            right = sigmoid(y[2 * half : 3 * half]) * y[3 * half : 4 * half]
            sides.append((left, right))
            if gated:
                gate_ref[x, :, start : start + piece] = sigmoid(y[4 * half :]).astype(BF16)
        for sub in range(0, piece, LANES):
            i = (start + sub) // BLK
            even = pl.ds(i * half, half)
            odd = pl.ds((i + 1) * half, half)
            l0, l1 = (side[0][:, sub : sub + LANES] for side in sides)
            r0, r1 = (side[1][:, sub : sub + LANES] for side in sides)
            l0r, l1r, r0r, r1r = (pltpu.roll(v, BLK, 1) for v in (l0, l1, r0, r1))
            sl[even, :] = jnp.where(low, l0, l1r)
            sl[odd, :] = jnp.where(low, l0r, l1)
            sp[even, :] = jnp.where(low, r0, r1r)
            sp[odd, :] = jnp.where(low, r0r, r1)
            sq[even, :] = jnp.where(low, r1, r0r)
            sq[odd, :] = jnp.where(low, r1r, r0)
    rows = chunk // BLK

    @pl.loop(0, half, unroll=8)
    def _(c):
        take = pl.ds(c, rows, stride=half)
        l_ref[0, c] = sl[take, :].astype(BF16)
        p_ref[0, c] = sp[take, :].astype(BF16)
        p_ref[1, c] = sq[take, :].astype(BF16)


def project(blocks, weights, gain, chunk, piece, gated, held=None, offset=0):
    half, cells = blocks[0].shape[-2:]
    pair_of = 0 if gated else 1
    in_specs = []
    for block, at in blocks_with_index(blocks):
        if block.ndim == 3:
            in_specs.append(
                pl.BlockSpec((None, half, chunk), functools.partial(lambda x, n: (x, 0, n), at))
            )
        else:
            in_specs.append(pl.BlockSpec((half, chunk), lambda n: (0, n)))
    rows = chunk // BLK
    whole = lambda a: pl.BlockSpec(a.shape, lambda n: (0,) * a.ndim)
    operands = [*blocks, weights[0], weights[1], gain]
    if gated:
        operands.append(weights[2])
    in_specs += [whole(value) for value in operands[4:]]
    out_shape = [
        jax.ShapeDtypeStruct((2, half, BLK, LANES), BF16),
        jax.ShapeDtypeStruct((4, half, BLK, LANES), BF16),
    ]
    out_specs = [
        pl.BlockSpec((1, half, rows, LANES), lambda n: (pair_of, 0, n + offset // chunk, 0)),
        pl.BlockSpec((2, half, rows, LANES), lambda n: (pair_of, 0, n + offset // chunk, 0)),
    ]
    aliases = {}
    if gated:
        out_shape.append(jax.ShapeDtypeStruct((2, half, cells), BF16))
        out_specs.append(pl.BlockSpec((2, half, chunk), lambda n: (0, 0, n)))
    else:
        in_specs += [pl.BlockSpec(memory_space=pl.ANY)] * 2
        aliases = {len(operands): 0, len(operands) + 1: 1}
        operands += held
    return pl.pallas_call(
        functools.partial(project_kernel, piece, gated),
        grid=(cells // chunk,),
        in_specs=in_specs,
        out_specs=out_specs,
        out_shape=out_shape,
        scratch_shapes=[pltpu.VMEM((rows * half, LANES), F32)] * 3,
        input_output_aliases=aliases,
        compiler_params=pltpu.CompilerParams(vmem_limit_bytes=VMEM_LIMIT),
        cost_estimate=pl.CostEstimate(flops=1, bytes_accessed=1, transcendentals=0),
        name="project_own" if gated else "project_fetched",
    )(*operands)


def blocks_with_index(blocks):
    return [(block, at // 2) for at, block in enumerate(blocks)]


def triplet_kernel(s, slots, triplets, group, a_ref, b_ref, n_ref, l_ref, p_ref, out_ref, acc):
    me, behind, ahead = neighbour_tiles()
    lane = lax.broadcasted_iota(jnp.int32, (1, LANES), 1)
    low = (lane < BLK).astype(F32)
    high = 1.0 - low
    block = me * slots + s
    count = n_ref[block]
    picks = []
    for pair_at in range(2):
        for part in range(2):
            chosen = jnp.int32(0)
            used = jnp.int32(0)
            for m in range(triplets):
                left = a_ref[m, block]
                if pair_at == 0:
                    hit = left == me * slots + part
                else:
                    first = (behind, ahead)[part] * slots
                    hit = jnp.logical_and(left >= first, left < first + slots)
                hit = jnp.logical_and(hit, m < count)
                place = b_ref[m, block] - me * slots
                from_me = jnp.logical_and(place >= 0, place < slots)
                right = b_ref[m, block] - behind * slots
                from_behind = jnp.logical_and(right >= 0, right < slots)
                place = jnp.where(from_me, place, jnp.where(from_behind, 2, 3))
                chosen = jnp.where(hit, place, chosen)
                used = jnp.where(hit, 1, used)
            if part == 1:
                chosen = chosen + 1 - 2 * (chosen & 1)
            picks.append((chosen, ((low, high)[part] * used.astype(F32)).astype(BF16)))

    @pl.loop(0, group, unroll=8)
    def _(c):
        lhs = jnp.concatenate([l_ref[0, c], l_ref[1, c]], axis=1)
        parts = [p_ref[pick, c] * mask for pick, mask in picks]
        rhs = jnp.concatenate([parts[0] + parts[1], parts[2] + parts[3]], axis=1)
        acc[pl.ds(c, BLK, stride=group), :] = lax.dot_general(
            lhs,
            jnp.concatenate([rhs, rhs], axis=0),
            (((1,), (1,)), ((), ())),
            preferred_element_type=F32,
        )

    take_low = lax.broadcasted_iota(jnp.int32, (group, LANES), 1) < BLK
    for t in range(BLK // 2):
        even = acc[2 * t * group : (2 * t + 1) * group, :]
        odd = acc[(2 * t + 1) * group : (2 * t + 2) * group, :]
        out_ref[:, t * LANES : (t + 1) * LANES] = jnp.where(take_low, even, odd).astype(BF16)


def triplet_sum(s, lefts, rights, a_slots, b_slots, counts, slots, group):
    half = lefts.shape[1]
    smem = pl.BlockSpec(memory_space=pltpu.SMEM)
    return pl.pallas_call(
        functools.partial(triplet_kernel, s, slots, a_slots.shape[0], group),
        grid=(half // group,),
        in_specs=[
            smem,
            smem,
            smem,
            pl.BlockSpec((2, group, BLK, LANES), lambda n: (0, n, 0, 0)),
            pl.BlockSpec((4, group, BLK, LANES), lambda n: (0, n, 0, 0)),
        ],
        out_specs=pl.BlockSpec((group, BLK * BLK), lambda n: (n, 0)),
        out_shape=jax.ShapeDtypeStruct((half, BLK * BLK), BF16),
        scratch_shapes=[pltpu.VMEM((BLK * group, LANES), F32)],
        compiler_params=pltpu.CompilerParams(vmem_limit_bytes=VMEM_LIMIT),
        cost_estimate=pl.CostEstimate(
            flops=2 * half * BLK * 256 * LANES, bytes_accessed=7 * 1024 * 1024, transcendentals=0
        ),
        name="triplets",
    )(a_slots, b_slots, counts, lefts, rights)


def finish_kernel(piece, mine_ref, theirs_ref, gate_ref, w_ref, g_ref, *refs):
    out_ref = refs[-1]
    weight = own_lanes_first(w_ref[...])
    gain = gains_of(g_ref)
    for start in range(0, mine_ref.shape[-1], piece):
        to = slice(start, start + piece)
        normed = normed_of(mine_ref[:, to], theirs_ref[:, to], gain)
        projected = jnp.dot(weight, normed, preferred_element_type=F32)
        out_ref[:, to] = (gate_ref[:, to].astype(F32) * projected).astype(BF16)


def finish(s, mine, theirs, gate, weight, gain, chunk, piece, held=None):
    half, cells = mine.shape
    cut = pl.BlockSpec((half, chunk), lambda n: (0, n))
    cut_of_s = pl.BlockSpec((None, half, chunk), lambda n: (s, 0, n))
    operands = [mine, theirs, gate, weight, gain]
    in_specs = [
        cut,
        cut,
        cut_of_s,
        pl.BlockSpec(weight.shape, lambda n: (0, 0)),
        pl.BlockSpec(gain.shape, lambda n: (0, 0)),
    ]
    aliases = {}
    if held is not None:
        aliases = {len(operands): 0}
        operands.append(held)
        in_specs.append(pl.BlockSpec(memory_space=pl.ANY))
    return pl.pallas_call(
        functools.partial(finish_kernel, piece),
        grid=(cells // chunk,),
        in_specs=in_specs,
        out_specs=cut_of_s,
        out_shape=jax.ShapeDtypeStruct(gate.shape, BF16),
        input_output_aliases=aliases,
        compiler_params=pltpu.CompilerParams(vmem_limit_bytes=VMEM_LIMIT),
        cost_estimate=pl.CostEstimate(
            flops=2 * cells * 2 * half * half, bytes_accessed=4 * half * cells * 2, transcendentals=0
        ),
        name="finish",
    )(*operands)


def per_device(
    pair,
    ln_in_gain,
    a_weight,
    b_weight,
    ln_out_gain,
    out_gate_weight,
    out_weight,
    a_slots,
    b_slots,
    counts,
):
    slots, half, cells = pair.shape
    rows = lax.axis_size("row")
    swap = [(0, 1), (1, 0)]
    up = [(i, (i + 1) % rows) for i in range(rows)]
    down = [(i, (i - 1) % rows) for i in range(rows)]

    a_slots, b_slots = a_slots.T, b_slots.T
    a_weight, b_weight = jnp.swapaxes(a_weight, 1, 2), jnp.swapaxes(b_weight, 1, 2)
    weights = (a_weight, b_weight, out_gate_weight.T)
    gain, last_gain = ln_in_gain[:, None], ln_out_gain[:, None]

    pair_other = lax.ppermute(pair, "chan", swap)
    cuts = ((0, cells // 4 * 3), (cells // 4 * 3, cells // 4))
    chosen = select_blocks(pair, a_slots, b_slots, counts, cuts)
    arrived = [
        (lax.ppermute(chosen[2 * n], "row", up), lax.ppermute(chosen[2 * n + 1], "row", down))
        for n in range(len(cuts))
    ]
    lefts, rights, gate = project(
        [pair, pair_other, pair, pair_other], weights, gain, 1024, 256, True
    )
    for (start, size), (from_behind, from_ahead) in zip(cuts, arrived):
        from_behind, from_ahead, lefts = lax.optimization_barrier((from_behind, from_ahead, lefts))
        behind_other = lax.ppermute(from_behind, "chan", swap)
        ahead_other = lax.ppermute(from_ahead, "chan", swap)
        lefts, rights = project(
            [from_behind, behind_other, from_ahead, ahead_other],
            weights,
            gain,
            1024,
            256,
            False,
            [lefts, rights],
            start,
        )
    updates = []
    for s in range(slots):
        update = triplet_sum(s, lefts, rights, a_slots, b_slots, counts, slots, 16)
        updates.append((update, lax.ppermute(update, "chan", swap)))
        if s + 1 < slots:
            update, lefts = lax.optimization_barrier((update, lefts))
    out = None
    for s, (mine, theirs) in enumerate(updates):
        out = finish(s, mine, theirs, gate, out_weight.T, last_gain, 1024, 256, out)
    return out


def solution(mesh):
    in_specs = (
        P(("parts", "row", "col"), "chan", None),
        P(),
        P(None, None, "chan"),
        P(None, None, "chan"),
        P(),
        P(None, "chan"),
        P(None, "chan"),
        P("parts", None),
        P("parts", None),
        P("parts"),
    )
    out_specs = P(("parts", "row", "col"), "chan", None)
    return jax.shard_map(
        per_device, mesh=mesh, in_specs=in_specs, out_specs=out_specs, check_vma=False
    )
```

time: 55.4 us -> 56.9 us (1.027)
  Pallas kernels: 29.1 us -> 35 us
  waiting for transfers between devices: 11.8 us -> 6.25 us
  starting transfers between devices: 9.51 us -> 10.7 us
    ppermute x3 -> x6, waiting for transfers between devices: 9.54 us -> 5.21 us  [the longest x2 5.2 us: per_device(): lax.ppermute(chosen[2 * n + 1], 'row', down)]
    ppermute x3 -> x6, starting transfers between devices: 5.16 us -> 9.18 us  [the longest x2 4.79 us: per_device(): lax.ppermute(chosen[2 * n + 1], 'row', down)]
    ppermute x1 -> x2, starting transfers between devices: 3.82 us -> 0.07 us  [per_device(): behind_other = lax.ppermute(from_behind, 'chan', swap)]
    pallas_call x2 -> x3, Pallas kernels: 9.34 us -> 12.8 us  [the longest x2 9.85 us: triplet_sum(): pl.pallas_call(functools.partial(triplet_kernel, s, slots, a_slots.shape[...]
    pallas_call x1 -> x2, Pallas kernels: 3.26 us -> 4.93 us  [finish(): pl.pallas_call(functools.partial(finish_kernel, piece), grid=(cells // ch...]
    ppermute x1 -> x2, starting transfers between devices: 0.08 us -> 1 us  [per_device(): ahead_other = lax.ppermute(from_ahead, 'chan', swap)]
    pallas_call x2 -> x3, Pallas kernels: 16.5 us -> 17.3 us  [project(): pl.pallas_call(functools.partial(project_kernel, piece, gated), grid=(cel...]
    ppermute x1 -> x2, waiting for transfers between devices: 1.46 us -> 0.84 us  [per_device(): behind_other = lax.ppermute(from_behind, 'chan', swap)]
  transfers between devices with their start and end apart: 6 -> 11, of which waited for: 5 -> 3; matrix products, arithmetic and copies ran while one was open for 2% -> 2% of each run, Pallas kernels for 21% -> 44%
where the time goes in v3:
time: 56.9 us; the launch traced here: 56.4 us
  Pallas kernels  35 us (62%)
  starting transfers between devices  10.7 us (19%)
  waiting for transfers between devices  6.25 us (11%)
  local copies, waits for them, and re-layouts  4.36 us (8%)
    pallas_call x3, Pallas kernels, project(): pl.pallas_call(functools.partial(project_kernel, piece, gated), grid=(cel...  17.3 us
    pallas_call x2, Pallas kernels, triplet_sum(): pl.pallas_call(functools.partial(triplet_kernel, s, slots, a_slots.shape[...  9.85 us
    ppermute x2, waiting for transfers between devices, per_device(): lax.ppermute(chosen[2 * n + 1], 'row', down)  5.2 us
    pallas_call x2, Pallas kernels, finish(): pl.pallas_call(functools.partial(finish_kernel, piece), grid=(cells // ch...  4.93 us
    ppermute x2, starting transfers between devices, per_device(): lax.ppermute(chosen[2 * n + 1], 'row', down)  4.79 us
    ppermute x2, starting transfers between devices, per_device(): lax.ppermute(chosen[2 * n], 'row', up)  3.75 us
    unnamed x22, local copies, waits for them, and re-layouts  3.48 us
    pallas_call x1, Pallas kernels, select_blocks(): pl.pallas_call(functools.partial(select_kernel, slots, a_slots.shape[0],...  2.95 us
  transfers between devices with their start and end apart: 11, of which 3 were waited for; matrix products, arithmetic and copies ran while one was open for 2% of the time, Pallas kernels for 44%

profile of v3, /device:TPU:0, one launch (start us, length us, event | category | flops | bytes accessed | tf_op | source)
XLA Modules:
  0.0 56.4 jit_solution(17801967098022577240)
XLA Ops:
  0.0 0.5 collective-permute-start.4
  0.5 3.0 %select_blocks.1 = (bf16[64,3072]{1,0:T(8,128)(2,1)}, bf16[64,3072]{1,0:T(8,128)(2,1)}, bf16[64,1024]{1,0:T(8,128)(2,1)}, bf16[64,1024]{1,0:T(8,128)(2,1)}) custom-call(s32[4,16]{1,0:T(4,128)} %bitcast.16, s32[4,16]{1,0:T(4,128)} %bitcast.19, s32[16]{0:T(128)} %n_ref.5, bf16[2,64,4096]{2,1,0:T(8,128)(2,1)} %refs_2_.1), custom_call_target="tpu_custom_call" | custom-call | tf_op jit(solution)/shard_map/select_blocks/pallas_call | solution.py:69
  3.4 2.6 %collective-permute-start.2 = (bf16[64,3072]{1,0:T(8,128)(2,1)}, bf16[64,3072]{1,0:T(8,128)(2,1)S(1)}, u32[]{:S(2)}, u32[]{:S(2)}) collective-permute-start(bf16[64,3072]{1,0:T(8,128)(2,1)} %get-tuple-element.25), channel_id=1, source_target_pairs={{0,4},{4,8},{8,12},{12,0},{1,5},{5,9},{9,13},{13,1},{2,6},{6,10},{... | collective-permute-start | bytes 1179656 | tf_op jit(solution)/shard_map/ppermute | solution.py:352
  6.1 2.1 %collective-permute-start.3 = (bf16[64,3072]{1,0:T(8,128)(2,1)}, bf16[64,3072]{1,0:T(8,128)(2,1)S(1)}, u32[]{:S(2)}, u32[]{:S(2)}) collective-permute-start(bf16[64,3072]{1,0:T(8,128)(2,1)} %get-tuple-element.26), channel_id=1, source_target_pairs={{0,12},{4,0},{8,4},{12,8},{1,13},{5,1},{9,5},{13,9},{2,14},{6,2},{... | collective-permute-start | bytes 1179656 | tf_op jit(solution)/shard_map/ppermute | solution.py:352
  8.1 0.8 %copy.16.refs_6_ = f32[128,1]{1,0:T(8,128)S(1)} copy(f32[128,1]{0,1:T(1,128)} %bitcast.23) | data formatting | bytes 1024 | tf_op jit(solution)/shard_map/broadcast_in_dim | solution.py:346
  8.9 0.0 collective-permute-done.4.refs_1_.refs_3_
  8.9 0.0 copy-start
  8.9 1.2 %copy-done = bf16[2,64,4096]{2,1,0:T(8,128)(2,1)S(1)} copy-done((bf16[2,64,4096]{2,1,0:T(8,128)(2,1)S(1)}, bf16[2,64,4096]{2,1,0:T(8,128)(2,1)}, u32[]{:S(2)}) %copy-start) | copy-done | bytes 1048600
  10.1 0.8 %copy-done.1 = bf16[2,128,64]{1,2,0:T(8,128)(2,1)S(1)} copy-done((bf16[2,128,64]{1,2,0:T(8,128)(2,1)S(1)}, bf16[2,128,64]{1,2,0:T(8,128)(2,1)}, u32[]{:S(2)}) %copy-start.1) | copy-done | bytes 32792
  10.9 0.0 copy-start.2
  10.9 0.8 %copy-done.2 = bf16[2,128,64]{1,2,0:T(8,128)(2,1)S(1)} copy-done((bf16[2,128,64]{1,2,0:T(8,128)(2,1)S(1)}, bf16[2,128,64]{1,2,0:T(8,128)(2,1)}, u32[]{:S(2)}) %copy-start.2) | copy-done | bytes 32792
  11.6 0.0 copy-start.6
  11.6 0.7 %copy-done.6 = bf16[128,64]{0,1:T(8,128)(2,1)S(1)} copy-done((bf16[128,64]{0,1:T(8,128)(2,1)S(1)}, bf16[128,64]{0,1:T(8,128)(2,1)}, u32[]{:S(2)}) %copy-start.6) | copy-done | bytes 16408
  12.4 8.4 %project_own.1 = (bf16[2,64,64,128]{3,2,1,0:T(8,128)(2,1)S(1)}, bf16[4,64,64,128]{3,2,1,0:T(8,128)(2,1)}, bf16[2,64,4096]{2,1,0:T(8,128)(2,1)S(1)}) custom-call(bf16[2,64,4096]{2,1,0:T(8,128)(2,1)S(1)} %copy-done, bf16[2,64,4096]{2,1,0:T(8,128)(2,1)S(1)} %collective-permute-done.4.refs_1_.refs_3_, bf16[2,64,4096]{2,1,0:T(8,128)(2,1)S(1)} %copy-done, ...), custom_call_target="tpu_custom_call" | custom-call | flops 1 | bytes 1 | tf_op jit(solution)/shard_map/project_own/pallas_call | solution.py:190
  20.7 0.0 collective-permute-done.2.refs_0_
  20.7 5.2 %collective-permute-done.3.refs_2_ = bf16[64,3072]{1,0:T(8,128)(2,1)S(1)} collective-permute-done((bf16[64,3072]{1,0:T(8,128)(2,1)}, bf16[64,3072]{1,0:T(8,128)(2,1)S(1)}, u32[]{:S(2)}, u32[]{:S(2)}) %collective-permute-start.3) | collective-permute-done | bytes 393248 | tf_op jit(solution)/shard_map/ppermute | solution.py:352
  25.9 0.0 collective-permute-start.5
  25.9 0.5 collective-permute-start.6
  26.4 0.0 copy-done.10
  26.5 1.1 %collective-permute-start = (bf16[64,1024]{1,0:T(8,128)(2,1)S(1)}, bf16[64,1024]{1,0:T(8,128)(2,1)S(1)}, u32[]{:S(2)}, u32[]{:S(2)}) collective-permute-start(bf16[64,1024]{1,0:T(8,128)(2,1)S(1)} %copy-done.10), channel_id=1, source_target_pairs={{0,4},{4,8},{8,12},{12,0},{1,5},{5,9},{9,13},{13,1},{2,6},{6,10},{... | collective-permute-start | bytes 393224 | tf_op jit(solution)/shard_map/ppermute | solution.py:352
  27.6 0.0 copy-done.9
  27.6 2.7 %collective-permute-start.1 = (bf16[64,1024]{1,0:T(8,128)(2,1)S(1)}, bf16[64,1024]{1,0:T(8,128)(2,1)S(1)}, u32[]{:S(2)}, u32[]{:S(2)}) collective-permute-start(bf16[64,1024]{1,0:T(8,128)(2,1)S(1)} %copy-done.9), channel_id=1, source_target_pairs={{0,12},{4,0},{8,4},{12,8},{1,13},{5,1},{9,5},{13,9},{2,14},{6,2},{... | collective-permute-start | bytes 393224 | tf_op jit(solution)/shard_map/ppermute | solution.py:352
  30.3 0.0 collective-permute-done.5.refs_1_
  30.3 0.0 collective-permute-done.6.refs_3_
  30.3 6.3 %project_fetched.2 = (bf16[2,64,64,128]{3,2,1,0:T(8,128)(2,1)S(1)}, bf16[4,64,64,128]{3,2,1,0:T(8,128)(2,1)}) custom-call(bf16[64,3072]{1,0:T(8,128)(2,1)S(1)} %collective-permute-done.2.refs_0_, bf16[64,3072]{1,0:T(8,128)(2,1)S(1)} %collective-permute-done.5.refs_1_, ...), custom_call_target="tpu_custom_call", output_to_operand_aliasing={{0}: (7, {}), {1}: (8, {})} | custom-call | flops 1 | bytes 1 | tf_op jit(solution)/shard_map/project_fetched/pallas_call | solution.py:190
  36.6 0.0 collective-permute-done.refs_0_
  36.6 0.0 collective-permute-done.1.refs_2_
  36.6 0.1 collective-permute-start.7
  36.7 0.5 collective-permute-start.8
  37.2 0.8 %collective-permute-done.7.refs_1_ = bf16[64,1024]{1,0:T(8,128)(2,1)S(1)} collective-permute-done((bf16[64,1024]{1,0:T(8,128)(2,1)S(1)}, bf16[64,1024]{1,0:T(8,128)(2,1)S(1)}, u32[]{:S(2)}, u32[]{:S(2)}) %collective-permute-start.7) | collective-permute-done | bytes 131104 | tf_op jit(solution)/shard_map/ppermute | solution.py:360
  38.1 0.2 collective-permute-done.8.refs_3_
  38.2 2.6 %project_fetched.3 = (bf16[2,64,64,128]{3,2,1,0:T(8,128)(2,1)S(1)}, bf16[4,64,64,128]{3,2,1,0:T(8,128)(2,1)}) custom-call(bf16[64,1024]{1,0:T(8,128)(2,1)S(1)} %collective-permute-done.refs_0_, bf16[64,1024]{1,0:T(8,128)(2,1)S(1)} %collective-permute-done.7.refs_1_, ...), custom_call_target="tpu_custom_call", output_to_operand_aliasing={{0}: (7, {}), {1}: (8, {})} | custom-call | flops 1 | bytes 1 | tf_op jit(solution)/shard_map/project_fetched/pallas_call | solution.py:190
  40.8 0.0 copy-done.4
  40.8 0.0 copy-done.5
  40.8 0.0 copy-done.7
  40.8 4.9 %triplets.2.mine_ref = bf16[64,4096]{1,0:T(8,128)(2,1)S(1)} custom-call(s32[4,16]{1,0:T(4,128)S(1)} %bitcast.17, s32[4,16]{1,0:T(4,128)S(1)} %bitcast.20, s32[16]{0:T(128)S(1)} %copy-done.7, bf16[2,64,64,128]{3,2,1,0:T(8,128)(2,1)S(1)} %get-tuple-element.39.l_ref, bf16[4,64,64,128]{3,2,1,0:T(8,128)(2,1)} %get-tuple-element.38.p_ref), custom_call_target="tpu_custom_call" | custom-call | flops 268435456 | bytes 7340032 | tf_op jit(solution)/shard_map/triplets/pallas_call | solution.py:261
  45.8 0.0 copy-start.8
  45.8 0.0 copy-start.3
  45.8 0.4 collective-permute-start.10
  46.2 4.9 %triplets.3.mine_ref = bf16[64,4096]{1,0:T(8,128)(2,1)S(1)} custom-call(s32[4,16]{1,0:T(4,128)S(1)} %bitcast.18, s32[4,16]{1,0:T(4,128)S(1)} %bitcast.21, s32[16]{0:T(128)S(1)} %copy-done.7, bf16[2,64,64,128]{3,2,1,0:T(8,128)(2,1)S(1)} %get-tuple-element.39.l_ref, bf16[4,64,64,128]{3,2,1,0:T(8,128)(2,1)} %get-tuple-element.38.p_ref), custom_call_target="tpu_custom_call" | custom-call | flops 268435456 | bytes 7340032 | tf_op jit(solution)/shard_map/triplets/pallas_call | solution.py:261
  51.1 0.2 collective-permute-start.9
  51.4 0.0 copy-done.8
  51.4 0.1 copy.20.g_ref
  51.5 0.0 collective-permute-done.10.theirs_ref
  51.5 0.0 copy-done.3
  51.5 2.5 %finish.2.refs_0_ = bf16[2,64,4096]{2,1,0:T(8,128)(2,1)} custom-call(bf16[64,4096]{1,0:T(8,128)(2,1)S(1)} %triplets.2.mine_ref, bf16[64,4096]{1,0:T(8,128)(2,1)S(1)} %collective-permute-done.10.theirs_ref, bf16[2,64,4096]{2,1,0:T(8,128)(2,1)S(1)} %get-tuple-element.40.gate_ref, bf16[64,128]{1,0:T(8,128)(2,1)S(1)} %bitcast.14, f32[128,1]{1,0:T(8,128)S(1)} %copy.20.g_ref), custom_call_target="tpu_custom_call" | custom-call | flops 67108864 | bytes 2097152 | tf_op jit(solution)/shard_map/finish/pallas_call | solution.py:310
  54.0 0.0 collective-permute-done.9.theirs_ref
  54.0 2.5 %finish.3 = bf16[2,64,4096]{2,1,0:T(8,128)(2,1)} custom-call(bf16[64,4096]{1,0:T(8,128)(2,1)S(1)} %triplets.3.mine_ref, bf16[64,4096]{1,0:T(8,128)(2,1)S(1)} %collective-permute-done.9.theirs_ref, bf16[2,64,4096]{2,1,0:T(8,128)(2,1)S(1)} %get-tuple-element.40.gate_ref, bf16[64,128]{1,0:T(8,128)(2,1)S(1)} %bitcast.15, ...), custom_call_target="tpu_custom_call", output_to_operand_aliasing={{}: (5, {})} | custom-call | flops 67108864 | bytes 2097152 | tf_op jit(solution)/shard_map/finish/pallas_call | solution.py:310
  (6 shorter events, 0.0 us)
Async XLA Ops:
  0.0 8.9 %collective-permute-start.4 = (bf16[2,64,4096]{2,1,0:T(8,128)(2,1)}, bf16[2,64,4096]{2,1,0:T(8,128)(2,1)S(1)}, u32[]{:S(2)}, u32[]{:S(2)}) collective-permute-start(bf16[2,64,4096]{2,1,0:T(8,128)(2,1)} %refs_2_.1), channel_id=1, source_target_pairs={{0,1},{1,0},{2,3},{3,2},{4,5},{5,4},{6,7},{7,6},{8,9},{9,8},{10,11... | collective-permute-start | bytes 3145736 | tf_op jit(solution)/shard_map/ppermute | solution.py:348
  3.4 17.3 %collective-permute-start.2 = (bf16[64,3072]{1,0:T(8,128)(2,1)}, bf16[64,3072]{1,0:T(8,128)(2,1)S(1)}, u32[]{:S(2)}, u32[]{:S(2)}) collective-permute-start(bf16[64,3072]{1,0:T(8,128)(2,1)} %get-tuple-element.25), channel_id=1, source_target_pairs={{0,4},{4,8},{8,12},{12,0},{1,5},{5,9},{9,13},{13,1},{2,6},{6,10},{... | collective-permute-start | bytes 1179656 | tf_op jit(solution)/shard_map/ppermute | solution.py:352
  6.1 19.9 %collective-permute-start.3 = (bf16[64,3072]{1,0:T(8,128)(2,1)}, bf16[64,3072]{1,0:T(8,128)(2,1)S(1)}, u32[]{:S(2)}, u32[]{:S(2)}) collective-permute-start(bf16[64,3072]{1,0:T(8,128)(2,1)} %get-tuple-element.26), channel_id=1, source_target_pairs={{0,12},{4,0},{8,4},{12,8},{1,13},{5,1},{9,5},{13,9},{2,14},{6,2},{... | collective-permute-start | bytes 1179656 | tf_op jit(solution)/shard_map/ppermute | solution.py:352
  8.9 1.2 %copy-start = (bf16[2,64,4096]{2,1,0:T(8,128)(2,1)S(1)}, bf16[2,64,4096]{2,1,0:T(8,128)(2,1)}, u32[]{:S(2)}) copy-start(bf16[2,64,4096]{2,1,0:T(8,128)(2,1)} %refs_2_.1) | copy-start | bytes 3145732
  10.1 0.8 %copy-start.1 = (bf16[2,128,64]{1,2,0:T(8,128)(2,1)S(1)}, bf16[2,128,64]{1,2,0:T(8,128)(2,1)}, u32[]{:S(2)}) copy-start(bf16[2,128,64]{1,2,0:T(8,128)(2,1)} %param.12) | copy-start | bytes 98308
  10.9 0.8 %copy-start.2 = (bf16[2,128,64]{1,2,0:T(8,128)(2,1)S(1)}, bf16[2,128,64]{1,2,0:T(8,128)(2,1)}, u32[]{:S(2)}) copy-start(bf16[2,128,64]{1,2,0:T(8,128)(2,1)} %param.13) | copy-start | bytes 98308
  11.6 0.7 %copy-start.6 = (bf16[128,64]{0,1:T(8,128)(2,1)S(1)}, bf16[128,64]{0,1:T(8,128)(2,1)}, u32[]{:S(2)}) copy-start(bf16[128,64]{0,1:T(8,128)(2,1)} %param.15) | copy-start | bytes 49156
  12.4 14.1 %copy-start.10 = (bf16[64,1024]{1,0:T(8,128)(2,1)S(1)}, bf16[64,1024]{1,0:T(8,128)(2,1)}, u32[]{:S(2)}) copy-start(bf16[64,1024]{1,0:T(8,128)(2,1)} %get-tuple-element.23) | copy-start | bytes 393220
  12.4 15.2 %copy-start.9 = (bf16[64,1024]{1,0:T(8,128)(2,1)S(1)}, bf16[64,1024]{1,0:T(8,128)(2,1)}, u32[]{:S(2)}) copy-start(bf16[64,1024]{1,0:T(8,128)(2,1)} %get-tuple-element.24) | copy-start | bytes 393220
  25.9 4.3 %collective-permute-start.5 = (bf16[64,3072]{1,0:T(8,128)(2,1)S(1)}, bf16[64,3072]{1,0:T(8,128)(2,1)S(1)}, u32[]{:S(2)}, u32[]{:S(2)}) collective-permute-start(bf16[64,3072]{1,0:T(8,128)(2,1)S(1)} %collective-permute-done.2.refs_0_), channel_id=1, source_target_pairs={{0,1},{1,0},{2,3},{3,2},{4,5},{5,4},{6,7},{7,6},{8,9},{9,8},{10,11... | collective-permute-start | bytes 1179656 | tf_op jit(solution)/shard_map/ppermute | solution.py:360
  25.9 4.3 %collective-permute-start.6 = (bf16[64,3072]{1,0:T(8,128)(2,1)S(1)}, bf16[64,3072]{1,0:T(8,128)(2,1)S(1)}, u32[]{:S(2)}, u32[]{:S(2)}) collective-permute-start(bf16[64,3072]{1,0:T(8,128)(2,1)S(1)} %collective-permute-done.3.refs_2_), channel_id=1, source_target_pairs={{0,1},{1,0},{2,3},{3,2},{4,5},{5,4},{6,7},{7,6},{8,9},{9,8},{10,11... | collective-permute-start | bytes 1179656 | tf_op jit(solution)/shard_map/ppermute | solution.py:361
  26.5 10.2 %collective-permute-start = (bf16[64,1024]{1,0:T(8,128)(2,1)S(1)}, bf16[64,1024]{1,0:T(8,128)(2,1)S(1)}, u32[]{:S(2)}, u32[]{:S(2)}) collective-permute-start(bf16[64,1024]{1,0:T(8,128)(2,1)S(1)} %copy-done.10), channel_id=1, source_target_pairs={{0,4},{4,8},{8,12},{12,0},{1,5},{5,9},{9,13},{13,1},{2,6},{6,10},{... | collective-permute-start | bytes 393224 | tf_op jit(solution)/shard_map/ppermute | solution.py:352
  27.6 9.1 %collective-permute-start.1 = (bf16[64,1024]{1,0:T(8,128)(2,1)S(1)}, bf16[64,1024]{1,0:T(8,128)(2,1)S(1)}, u32[]{:S(2)}, u32[]{:S(2)}) collective-permute-start(bf16[64,1024]{1,0:T(8,128)(2,1)S(1)} %copy-done.9), channel_id=1, source_target_pairs={{0,12},{4,0},{8,4},{12,8},{1,13},{5,1},{9,5},{13,9},{2,14},{6,2},{... | collective-permute-start | bytes 393224 | tf_op jit(solution)/shard_map/ppermute | solution.py:352
  36.6 4.2 %copy-start.4 = (s32[16,4]{0,1:T(4,128)S(1)}, s32[16,4]{0,1:T(4,128)}, u32[]{:S(2)}) copy-start(s32[16,4]{0,1:T(4,128)} %param.17) | copy-start | bytes 772
  36.6 4.2 %copy-start.5 = (s32[16,4]{0,1:T(4,128)S(1)}, s32[16,4]{0,1:T(4,128)}, u32[]{:S(2)}) copy-start(s32[16,4]{0,1:T(4,128)} %param.18) | copy-start | bytes 772
  36.6 4.2 %copy-start.7 = (s32[16]{0:T(128)S(1)}, s32[16]{0:T(128)}, u32[]{:S(2)}) copy-start(s32[16]{0:T(128)} %n_ref.5) | copy-start | bytes 196
  36.6 1.4 %collective-permute-start.7 = (bf16[64,1024]{1,0:T(8,128)(2,1)S(1)}, bf16[64,1024]{1,0:T(8,128)(2,1)S(1)}, u32[]{:S(2)}, u32[]{:S(2)}) collective-permute-start(bf16[64,1024]{1,0:T(8,128)(2,1)S(1)} %collective-permute-done.refs_0_), channel_id=1, source_target_pairs={{0,1},{1,0},{2,3},{3,2},{4,5},{5,4},{6,7},{7,6},{8,9},{9,8},{10,11... | collective-permute-start | bytes 393224 | tf_op jit(solution)/shard_map/ppermute | solution.py:360
  36.7 1.5 %collective-permute-start.8 = (bf16[64,1024]{1,0:T(8,128)(2,1)S(1)}, bf16[64,1024]{1,0:T(8,128)(2,1)S(1)}, u32[]{:S(2)}, u32[]{:S(2)}) collective-permute-start(bf16[64,1024]{1,0:T(8,128)(2,1)S(1)} %collective-permute-done.1.refs_2_), channel_id=1, source_target_pairs={{0,1},{1,0},{2,3},{3,2},{4,5},{5,4},{6,7},{7,6},{8,9},{9,8},{10,11... | collective-permute-start | bytes 393224 | tf_op jit(solution)/shard_map/ppermute | solution.py:361
  45.8 5.6 %copy-start.8 = (f32[128]{0:T(128)S(1)}, f32[128]{0:T(128)}, u32[]{:S(2)}) copy-start(f32[128]{0:T(128)} %param.14) | copy-start | bytes 1540
  45.8 5.7 %copy-start.3 = (bf16[128,64]{0,1:T(8,128)(2,1)S(1)}, bf16[128,64]{0,1:T(8,128)(2,1)}, u32[]{:S(2)}) copy-start(bf16[128,64]{0,1:T(8,128)(2,1)} %param.16) | copy-start | bytes 49156
  45.8 5.7 %collective-permute-start.10 = (bf16[64,4096]{1,0:T(8,128)(2,1)S(1)}, bf16[64,4096]{1,0:T(8,128)(2,1)S(1)}, u32[]{:S(2)}, u32[]{:S(2)}) collective-permute-start(bf16[64,4096]{1,0:T(8,128)(2,1)S(1)} %triplets.2.mine_ref), channel_id=1, source_target_pairs={{0,1},{1,0},{2,3},{3,2},{4,5},{5,4},{6,7},{7,6},{8,9},{9,8},{10,11... | collective-permute-start | bytes 1572872 | tf_op jit(solution)/shard_map/ppermute | solution.py:375
  51.1 2.8 %collective-permute-start.9 = (bf16[64,4096]{1,0:T(8,128)(2,1)S(1)}, bf16[64,4096]{1,0:T(8,128)(2,1)S(1)}, u32[]{:S(2)}, u32[]{:S(2)}) collective-permute-start(bf16[64,4096]{1,0:T(8,128)(2,1)S(1)} %triplets.3.mine_ref), channel_id=1, source_target_pairs={{0,1},{1,0},{2,3},{3,2},{4,5},{5,4},{6,7},{7,6},{8,9},{9,8},{10,11... | collective-permute-start | bytes 1572872 | tf_op jit(solution)/shard_map/ppermute | solution.py:375

commit v4 on v3

v4 whole, which is shorter than its diff:
```python
import functools

import jax
import jax.numpy as jnp
from jax import lax
from jax.experimental import pallas as pl
from jax.experimental.pallas import tpu as pltpu
from jax.sharding import PartitionSpec as P

BLK = 64
LANES = 128
epsilon = 1e-05
VMEM_LIMIT = 24 * 1024 * 1024
F32 = jnp.float32
BF16 = jnp.bfloat16


def sigmoid(x):
    return 0.5 * jnp.tanh(0.5 * x) + 0.5


def tile_of(row, col):
    return row * lax.axis_size("col") + col


def neighbour_tiles():
    rows = lax.axis_size("row")
    row, col = lax.axis_index("row"), lax.axis_index("col")
    behind = lax.rem(row + rows - 1, rows)
    ahead = lax.rem(row + 1, rows)
    return tile_of(row, col), tile_of(behind, col), tile_of(ahead, col)


def select_kernel(slots, triplets, cuts, a_ref, b_ref, n_ref, pair_ref, *refs):
    me, behind, ahead = neighbour_tiles()
    out_refs, sems = refs[:-1], refs[-1]
    picks = []
    for target in (ahead, behind):
        pick = jnp.int32(0)
        for s in range(slots):
            count = n_ref[target * slots + s]
            for m in range(triplets):
                for ids in (a_ref, b_ref):
                    name = ids[m, target * slots + s] - me * slots
                    mine = jnp.logical_and(name >= 0, name < slots)
                    pick = jnp.where(jnp.logical_and(m < count, mine), name, pick)
        picks.append(pick)
    copies = []
    for at, (start, size) in enumerate(cuts):
        for which, pick in enumerate(picks):
            out = 2 * at + which
            copies.append(
                pltpu.make_async_copy(
                    pair_ref.at[pick, :, pl.ds(start, size)], out_refs[out], sems.at[out]
                )
            )
            copies[-1].start()
    for copy in copies:
        copy.wait()


def select_blocks(pair, a_slots, b_slots, counts, cuts):
    slots, channels, cells = pair.shape
    smem = pl.BlockSpec(memory_space=pltpu.SMEM)
    vmem = pl.BlockSpec(memory_space=pltpu.VMEM)
    out_shape = [
        pltpu.VMEM((channels, size), pair.dtype) for _, size in cuts for _ in range(2)
    ]
    return pl.pallas_call(
        functools.partial(select_kernel, slots, a_slots.shape[0], cuts),
        out_shape=out_shape,
        in_specs=[smem, smem, smem, pl.BlockSpec(memory_space=pltpu.HBM)],
        out_specs=[vmem] * len(out_shape),
        scratch_shapes=[pltpu.SemaphoreType.DMA((len(out_shape),))],
        name="select_blocks",
    )(a_slots, b_slots, counts, pair)


def own_lanes_first(weight):
    return jnp.where(
        lax.axis_index("chan") == 0, weight, pltpu.roll(weight, weight.shape[1] // 2, 1)
    )


def gains_of(g_ref):
    half = g_ref.shape[0] // 2
    chan = lax.axis_index("chan")
    mine = g_ref[pl.ds(pl.multiple_of(chan * half, half), half), :]
    theirs = g_ref[pl.ds(pl.multiple_of((1 - chan) * half, half), half), :]
    return mine, theirs


def normed_of(mine, theirs, gain):
    half = mine.shape[0]
    total = 2 * half
    mine = mine.astype(F32)
    theirs = theirs.astype(F32)
    mean = (jnp.sum(mine, axis=0, keepdims=True) + jnp.sum(theirs, axis=0, keepdims=True)) / total
    mine = mine - mean
    theirs = theirs - mean
    spread = (
        jnp.sum(mine * mine, axis=0, keepdims=True) + jnp.sum(theirs * theirs, axis=0, keepdims=True)
    ) / total
    scale = lax.rsqrt(spread + epsilon)
    return jnp.concatenate(
        [(mine * scale * gain[0]).astype(BF16), (theirs * scale * gain[1]).astype(BF16)],
        axis=0,
    )


def gated_rows(w_ref):
    gate, value = w_ref[0].astype(F32), w_ref[1].astype(F32)
    rows = []
    for at in range(0, gate.shape[0], 8):
        rows += [gate[at : at + 8], value[at : at + 8]]
    return [0.5 * row for row in rows]


def project_kernel(piece, chunk, offset, gated, *refs):
    if gated:
        m_ref, t_ref, a_ref, b_ref, g_ref, o_ref, l_ref, p_ref, gate_ref, sl, sp, sq = refs
        blocks = ((m_ref.at[0], t_ref.at[0]), (m_ref.at[1], t_ref.at[1]))
        rows = [0.5 * o_ref[...].astype(F32)]
        pair_of = 0
    else:
        m0, t0, m1, t1, a_ref, b_ref, g_ref, _, _, l_ref, p_ref, sl, sp, sq = refs
        blocks = ((m0, t0), (m1, t1))
        rows = []
        pair_of = 1
    half, cells = blocks[0][0].shape
    weight = jnp.concatenate(gated_rows(a_ref) + gated_rows(b_ref) + rows, axis=0)
    weight = own_lanes_first(weight).astype(BF16)
    gain = gains_of(g_ref)
    low = lax.broadcasted_iota(jnp.int32, (8, LANES), 1) < BLK
    high_rows = chunk // BLK

    @pl.loop(0, cells // chunk)
    def _(n):
        for start in range(0, chunk, piece):
            at = pl.ds(pl.multiple_of(n * chunk + start, piece), piece)
            results = []
            for x, (m, t) in enumerate(blocks):
                normed = normed_of(m[:, at], t[:, at], gain)
                y = jnp.dot(weight, normed, preferred_element_type=F32)
                results.append(y)
                if gated:
                    gate_ref[x, :, at] = (jnp.tanh(y[4 * half :]) + 1.0).astype(BF16)
            for row in range(0, half, 8):
                sides = []
                for side in range(2):
                    for y in results:
                        gate = y[2 * half * side + 2 * row : 2 * half * side + 2 * row + 8]
                        value = y[2 * half * side + 2 * row + 8 : 2 * half * side + 2 * row + 16]
                        sides.append((jnp.tanh(gate) + 1.0) * value)
                for sub in range(0, piece, LANES):
                    i = (start + sub) // BLK
                    even = slice(i * half + row, i * half + row + 8)
                    odd = slice((i + 1) * half + row, (i + 1) * half + row + 8)
                    l0, l1, r0, r1 = (v[:, sub : sub + LANES] for v in sides)
                    l0r, l1r, r0r, r1r = (pltpu.roll(v, BLK, 1) for v in (l0, l1, r0, r1))
                    sl[even, :] = jnp.where(low, l0, l1r)
                    sl[odd, :] = jnp.where(low, l0r, l1)
                    sp[even, :] = jnp.where(low, r0, r1r)
                    sp[odd, :] = jnp.where(low, r0r, r1)
                    sq[even, :] = jnp.where(low, r1, r0r)
                    sq[odd, :] = jnp.where(low, r1r, r0)

        to = pl.ds(pl.multiple_of(n * high_rows + offset // BLK, 16), high_rows)

        @pl.loop(0, half, unroll=8)
        def _(c):
            take = pl.ds(c, high_rows, stride=half)
            l_ref[pair_of, c, to, :] = sl[take, :].astype(BF16)
            p_ref[2 * pair_of, c, to, :] = sp[take, :].astype(BF16)
            p_ref[2 * pair_of + 1, c, to, :] = sq[take, :].astype(BF16)


def project(blocks, weights, gain, chunk, piece, gated, held=None, offset=0):
    half, cells = blocks[0].shape[-2:]
    operands = [*blocks, weights[0], weights[1], gain]
    out_shape = [
        pltpu.VMEM((2, half, BLK, LANES), BF16),
        pltpu.VMEM((4, half, BLK, LANES), BF16),
    ]
    aliases = {}
    if gated:
        operands.append(weights[2])
        out_shape.append(pltpu.VMEM((2, half, cells), BF16))
    else:
        aliases = {len(operands): 0, len(operands) + 1: 1}
        operands += [pltpu.with_memory_space_constraint(value, pltpu.VMEM) for value in held]
    vmem = pl.BlockSpec(memory_space=pltpu.VMEM)
    return pl.pallas_call(
        functools.partial(project_kernel, piece, chunk, offset, gated),
        in_specs=[vmem] * len(operands),
        out_specs=[vmem] * len(out_shape),
        out_shape=out_shape,
        scratch_shapes=[pltpu.VMEM((chunk // BLK * half, LANES), F32)] * 3,
        input_output_aliases=aliases,
        compiler_params=pltpu.CompilerParams(vmem_limit_bytes=VMEM_LIMIT),
        name="project_own" if gated else "project_fetched",
    )(*operands)


def triplet_kernel(s, slots, triplets, group, a_ref, b_ref, n_ref, l_ref, p_ref, out_ref, *accs):
    me, behind, ahead = neighbour_tiles()
    lane = lax.broadcasted_iota(jnp.int32, (1, LANES), 1)
    low = (lane < BLK).astype(F32)
    high = 1.0 - low
    block = me * slots + s
    count = n_ref[block]
    picks = []
    for pair_at in range(2):
        for part in range(2):
            chosen = jnp.int32(0)
            used = jnp.int32(0)
            for m in range(triplets):
                left = a_ref[m, block]
                if pair_at == 0:
                    hit = left == me * slots + part
                else:
                    first = (behind, ahead)[part] * slots
                    hit = jnp.logical_and(left >= first, left < first + slots)
                hit = jnp.logical_and(hit, m < count)
                place = b_ref[m, block] - me * slots
                from_me = jnp.logical_and(place >= 0, place < slots)
                right = b_ref[m, block] - behind * slots
                from_behind = jnp.logical_and(right >= 0, right < slots)
                place = jnp.where(from_me, place, jnp.where(from_behind, 2, 3))
                chosen = jnp.where(hit, place, chosen)
                used = jnp.where(hit, 1, used)
            if part == 1:
                chosen = chosen + 1 - 2 * (chosen & 1)
            picks.append((chosen, ((low, high)[part] * used.astype(F32)).astype(BF16)))

    take_low = lax.broadcasted_iota(jnp.int32, (group, LANES), 1) < BLK
    half = l_ref.shape[1]

    @pl.loop(0, half, step=group * len(accs))
    def _(base):
        for which, acc in enumerate(accs):
            for at in range(group):
                c = base + which * group + at
                lhs = jnp.concatenate([l_ref[0, c], l_ref[1, c]], axis=1)
                parts = [p_ref[pick, c] * mask for pick, mask in picks]
                rhs = jnp.concatenate([parts[0] + parts[1], parts[2] + parts[3]], axis=1)
                acc[pl.ds(at, BLK, stride=group), :] = lax.dot_general(
                    lhs,
                    jnp.concatenate([rhs, rhs], axis=0),
                    (((1,), (1,)), ((), ())),
                    preferred_element_type=F32,
                )
            rows = pl.ds(pl.multiple_of(base + which * group, group), group)
            for t in range(BLK // 2):
                even = acc[2 * t * group : (2 * t + 1) * group, :]
                odd = acc[(2 * t + 1) * group : (2 * t + 2) * group, :]
                out_ref[rows, t * LANES : (t + 1) * LANES] = jnp.where(
                    take_low, even, odd
                ).astype(BF16)


def triplet_sum(s, lefts, rights, a_slots, b_slots, counts, slots, group):
    half = lefts.shape[1]
    smem = pl.BlockSpec(memory_space=pltpu.SMEM)
    vmem = pl.BlockSpec(memory_space=pltpu.VMEM)
    lefts, rights = (
        pltpu.with_memory_space_constraint(value, pltpu.VMEM) for value in (lefts, rights)
    )
    return pl.pallas_call(
        functools.partial(triplet_kernel, s, slots, a_slots.shape[0], group),
        in_specs=[smem, smem, smem, vmem, vmem],
        out_specs=vmem,
        out_shape=pltpu.VMEM((half, BLK * BLK), BF16),
        scratch_shapes=[pltpu.VMEM((BLK * group, LANES), F32)] * 2,
        compiler_params=pltpu.CompilerParams(vmem_limit_bytes=VMEM_LIMIT),
        name="triplets",
    )(a_slots, b_slots, counts, lefts, rights)


def finish_kernel(s, piece, mine_ref, theirs_ref, gate_ref, w_ref, g_ref, *refs):
    out_ref, held, sems = refs[-3:]
    weight = own_lanes_first(0.5 * w_ref[...].astype(F32)).astype(BF16)
    gain = gains_of(g_ref)
    cells = mine_ref.shape[-1]
    steps = sems.shape[0]
    size = cells // steps

    def copy(n):
        to = pl.ds(pl.multiple_of(n * size, size), size)
        return pltpu.make_async_copy(held.at[:, to], out_ref.at[s, :, to], sems.at[n])

    @pl.loop(0, steps)
    def _(n):
        for start in range(0, size, piece):
            to = pl.ds(pl.multiple_of(n * size + start, piece), piece)
            normed = normed_of(mine_ref[:, to], theirs_ref[:, to], gain)
            projected = jnp.dot(weight, normed, preferred_element_type=F32)
            held[:, to] = (gate_ref[s, :, to].astype(F32) * projected).astype(BF16)
        copy(n).start()

    @pl.loop(0, steps)
    def _(n):
        copy(n).wait()


def finish(s, mine, theirs, gate, weight, gain, steps, piece, out=None):
    half, cells = mine.shape
    vmem = pl.BlockSpec(memory_space=pltpu.VMEM)
    operands = [mine, theirs, gate, weight, gain]
    in_specs = [vmem] * 5
    aliases = {}
    if out is not None:
        aliases = {len(operands): 0}
        operands.append(out)
        in_specs.append(pl.BlockSpec(memory_space=pltpu.HBM))
    return pl.pallas_call(
        functools.partial(finish_kernel, s, piece),
        in_specs=in_specs,
        out_specs=pl.BlockSpec(memory_space=pltpu.HBM),
        out_shape=jax.ShapeDtypeStruct(gate.shape, BF16),
        scratch_shapes=[pltpu.VMEM((half, cells), BF16), pltpu.SemaphoreType.DMA((steps,))],
        input_output_aliases=aliases,
        compiler_params=pltpu.CompilerParams(vmem_limit_bytes=VMEM_LIMIT),
        name="finish",
    )(*operands)


def per_device(
    pair,
    ln_in_gain,
    a_weight,
    b_weight,
    ln_out_gain,
    out_gate_weight,
    out_weight,
    a_slots,
    b_slots,
    counts,
):
    slots, half, cells = pair.shape
    rows = lax.axis_size("row")
    swap = [(0, 1), (1, 0)]
    up = [(i, (i + 1) % rows) for i in range(rows)]
    down = [(i, (i - 1) % rows) for i in range(rows)]

    a_slots, b_slots = a_slots.T, b_slots.T
    a_weight, b_weight = jnp.swapaxes(a_weight, 1, 2), jnp.swapaxes(b_weight, 1, 2)
    weights = (a_weight, b_weight, out_gate_weight.T)
    gain, last_gain = ln_in_gain[:, None], ln_out_gain[:, None]

    pair_other = lax.ppermute(pair, "chan", swap)
    cuts = ((0, cells // 4 * 3), (cells // 4 * 3, cells // 4))
    chosen = select_blocks(pair, a_slots, b_slots, counts, cuts)
    arrived = [
        (lax.ppermute(chosen[2 * n], "row", up), lax.ppermute(chosen[2 * n + 1], "row", down))
        for n in range(len(cuts))
    ]
    lefts, rights, gate = project(
        [pair, pair_other], weights, gain, 1024, 256, True
    )
    for (start, size), (from_behind, from_ahead) in zip(cuts, arrived):
        from_behind, from_ahead, lefts = lax.optimization_barrier((from_behind, from_ahead, lefts))
        behind_other = lax.ppermute(from_behind, "chan", swap)
        ahead_other = lax.ppermute(from_ahead, "chan", swap)
        lefts, rights = project(
            [from_behind, behind_other, from_ahead, ahead_other],
            weights,
            gain,
            1024,
            256,
            False,
            [lefts, rights],
            start,
        )
    updates = []
    for s in range(slots):
        update = triplet_sum(s, lefts, rights, a_slots, b_slots, counts, slots, 16)
        updates.append((update, lax.ppermute(update, "chan", swap)))
        if s + 1 < slots:
            update, lefts = lax.optimization_barrier((update, lefts))
    out = None
    for s, (mine, theirs) in enumerate(updates):
        out = finish(s, mine, theirs, gate, out_weight.T, last_gain, 4, 256, out)
    return out


def solution(mesh):
    in_specs = (
        P(("parts", "row", "col"), "chan", None),
        P(),
        P(None, None, "chan"),
        P(None, None, "chan"),
        P(),
        P(None, "chan"),
        P(None, "chan"),
        P("parts", None),
        P("parts", None),
        P("parts"),
    )
    out_specs = P(("parts", "row", "col"), "chan", None)
    return jax.shard_map(
        per_device, mesh=mesh, in_specs=in_specs, out_specs=out_specs, check_vma=False
    )
```

time: 56.9 us -> 49.8 us (0.88)
  Pallas kernels: 35 us -> 26.1 us
  waiting for transfers between devices: 6.25 us -> 7.68 us
  local copies, waits for them, and re-layouts: 4.36 us -> 4.99 us
    pallas_call x2, Pallas kernels: 9.85 us -> 5.03 us  [triplet_sum(): pl.pallas_call(functools.partial(triplet_kernel, s, slots, a_slots.shape[...]
    pallas_call x5, Pallas kernels: 22.2 us -> 18.2 us  [the longest x3 13.9 us: project(): pl.pallas_call(functools.partial(project_kernel, piece, chunk, offset, ga...]
    ppermute x2, waiting for transfers between devices: 5.2 us -> 6.64 us  [per_device(): lax.ppermute(chosen[2 * n + 1], 'row', down)]
    unnamed x22 -> x20, local copies, waits for them, and re-layouts: 3.48 us -> 4.12 us
  transfers between devices with their start and end apart: 11 -> 11, of which waited for: 3 -> 4; matrix products, arithmetic and copies ran while one was open for 2% -> 2% of each run, Pallas kernels for 44% -> 40%
where the time goes in v4:
time: 49.8 us; the launch traced here: 49.4 us
  Pallas kernels  26.1 us (52%)
  starting transfers between devices  10.5 us (21%)
  waiting for transfers between devices  7.68 us (15%)
  local copies, waits for them, and re-layouts  4.99 us (10%)
    pallas_call x3, Pallas kernels, project(): pl.pallas_call(functools.partial(project_kernel, piece, chunk, offset, ga...  13.9 us
    ppermute x2, waiting for transfers between devices, per_device(): lax.ppermute(chosen[2 * n + 1], 'row', down)  6.64 us
    pallas_call x2, Pallas kernels, triplet_sum(): pl.pallas_call(functools.partial(triplet_kernel, s, slots, a_slots.shape[...  5.03 us
    ppermute x2, starting transfers between devices, per_device(): lax.ppermute(chosen[2 * n + 1], 'row', down)  4.52 us
    pallas_call x2, Pallas kernels, finish(): pl.pallas_call(functools.partial(finish_kernel, s, piece), in_specs=in_sp...  4.28 us
    unnamed x20, local copies, waits for them, and re-layouts  4.12 us
    ppermute x2, starting transfers between devices, per_device(): lax.ppermute(chosen[2 * n], 'row', up)  3.84 us
    pallas_call x1, Pallas kernels, select_blocks(): pl.pallas_call(functools.partial(select_kernel, slots, a_slots.shape[0],...  2.82 us
  transfers between devices with their start and end apart: 11, of which 4 were waited for; matrix products, arithmetic and copies ran while one was open for 2% of the time, Pallas kernels for 40%

profile of v4, /device:TPU:0, one launch (start us, length us, event | category | flops | bytes accessed | tf_op | source)
XLA Modules:
  0.0 49.4 jit_solution(10471908191924450141)
XLA Ops:
  0.0 0.5 collective-permute-start.4
  0.5 2.8 %select_blocks.1 = (bf16[64,3072]{1,0:T(8,128)(2,1)}, bf16[64,3072]{1,0:T(8,128)(2,1)S(1)}, bf16[64,1024]{1,0:T(8,128)(2,1)S(1)}, bf16[64,1024]{1,0:T(8,128)(2,1)S(1)}) custom-call(s32[4,16]{1,0:T(4,128)} %bitcast.16, s32[4,16]{1,0:T(4,128)} %bitcast.19, s32[16]{0:T(128)} %n_ref.5, bf16[2,64,4096]{2,1,0:T(8,128)(2,1)} %refs_0_.1), custom_call_target="tpu_custom_call" | custom-call | tf_op jit(solution)/shard_map/select_blocks/pallas_call | solution.py:69
  3.3 0.0 copy-start.8
  3.3 0.6 %copy-done.8 = bf16[64,1024]{1,0:T(8,128)(2,1)} copy-done((bf16[64,1024]{1,0:T(8,128)(2,1)}, bf16[64,1024]{1,0:T(8,128)(2,1)S(1)}, u32[]{:S(2)}) %copy-start.8) | copy-done | bytes 131096
  3.9 2.6 %collective-permute-start.2 = (bf16[64,3072]{1,0:T(8,128)(2,1)}, bf16[64,3072]{1,0:T(8,128)(2,1)S(1)}, u32[]{:S(2)}, u32[]{:S(2)}) collective-permute-start(bf16[64,3072]{1,0:T(8,128)(2,1)} %get-tuple-element.25), channel_id=1, source_target_pairs={{0,4},{4,8},{8,12},{12,0},{1,5},{5,9},{9,13},{13,1},{2,6},{6,10},{... | collective-permute-start | bytes 1179656 | tf_op jit(solution)/shard_map/ppermute | solution.py:355
  6.5 2.0 %collective-permute-start.3 = (bf16[64,3072]{1,0:T(8,128)(2,1)S(1)}, bf16[64,3072]{1,0:T(8,128)(2,1)S(1)}, u32[]{:S(2)}, u32[]{:S(2)}) collective-permute-start(bf16[64,3072]{1,0:T(8,128)(2,1)S(1)} %get-tuple-element.26), channel_id=1, source_target_pairs={{0,12},{4,0},{8,4},{12,8},{1,13},{5,1},{9,5},{13,9},{2,14},{6,2},{... | collective-permute-start | bytes 1179656 | tf_op jit(solution)/shard_map/ppermute | solution.py:355
  8.5 0.8 %copy.16.refs_4_.refs_6_ = f32[128,1]{1,0:T(8,128)S(1)} copy(f32[128,1]{0,1:T(1,128)} %bitcast.23) | data formatting | bytes 1024 | tf_op jit(solution)/shard_map/broadcast_in_dim | solution.py:349
  9.2 0.0 collective-permute-done.4.refs_1_
  9.2 0.0 copy-start
  9.2 1.2 %copy-done = bf16[2,64,4096]{2,1,0:T(8,128)(2,1)S(1)} copy-done((bf16[2,64,4096]{2,1,0:T(8,128)(2,1)S(1)}, bf16[2,64,4096]{2,1,0:T(8,128)(2,1)}, u32[]{:S(2)}) %copy-start) | copy-done | bytes 1048600
  10.5 0.8 %copy-done.1 = bf16[2,128,64]{1,2,0:T(8,128)(2,1)S(1)} copy-done((bf16[2,128,64]{1,2,0:T(8,128)(2,1)S(1)}, bf16[2,128,64]{1,2,0:T(8,128)(2,1)}, u32[]{:S(2)}) %copy-start.1) | copy-done | bytes 32792
  11.2 0.8 %copy-done.2 = bf16[2,128,64]{1,2,0:T(8,128)(2,1)S(1)} copy-done((bf16[2,128,64]{1,2,0:T(8,128)(2,1)S(1)}, bf16[2,128,64]{1,2,0:T(8,128)(2,1)}, u32[]{:S(2)}) %copy-start.2) | copy-done | bytes 32792
  12.0 0.7 %copy-done.6 = bf16[128,64]{0,1:T(8,128)(2,1)S(1)} copy-done((bf16[128,64]{0,1:T(8,128)(2,1)S(1)}, bf16[128,64]{0,1:T(8,128)(2,1)}, u32[]{:S(2)}) %copy-start.6) | copy-done | bytes 16408
  12.7 6.9 %project_own.1 = (bf16[2,64,64,128]{3,2,1,0:T(8,128)(2,1)S(1)}, bf16[4,64,64,128]{3,2,1,0:T(8,128)(2,1)S(1)}, bf16[2,64,4096]{2,1,0:T(8,128)(2,1)S(1)}) custom-call(bf16[2,64,4096]{2,1,0:T(8,128)(2,1)S(1)} %copy-done, bf16[2,64,4096]{2,1,0:T(8,128)(2,1)S(1)} %collective-permute-done.4.refs_1_, bf16[2,64,128]{2,1,0:T(8,128)(2,1)S(1)} %bitcast.8, ...), custom_call_target="tpu_custom_call" | custom-call | tf_op jit(solution)/shard_map/project_own/pallas_call | solution.py:193
  19.6 0.0 collective-permute-done.2.refs_0_
  19.6 6.5 %collective-permute-done.3.refs_2_ = bf16[64,3072]{1,0:T(8,128)(2,1)S(1)} collective-permute-done((bf16[64,3072]{1,0:T(8,128)(2,1)S(1)}, bf16[64,3072]{1,0:T(8,128)(2,1)S(1)}, u32[]{:S(2)}, u32[]{:S(2)}) %collective-permute-start.3) | collective-permute-done | bytes 393248 | tf_op jit(solution)/shard_map/ppermute | solution.py:355
  26.2 0.0 collective-permute-start.5
  26.2 0.5 %collective-permute-start.6 = (bf16[64,3072]{1,0:T(8,128)(2,1)S(1)}, bf16[64,3072]{1,0:T(8,128)(2,1)S(1)}, u32[]{:S(2)}, u32[]{:S(2)}) collective-permute-start(bf16[64,3072]{1,0:T(8,128)(2,1)S(1)} %collective-permute-done.3.refs_2_), channel_id=1, source_target_pairs={{0,1},{1,0},{2,3},{3,2},{4,5},{5,4},{6,7},{7,6},{8,9},{9,8},{10,11... | collective-permute-start | bytes 1179656 | tf_op jit(solution)/shard_map/ppermute | solution.py:364
  26.7 1.3 %collective-permute-start = (bf16[64,1024]{1,0:T(8,128)(2,1)}, bf16[64,1024]{1,0:T(8,128)(2,1)S(1)}, u32[]{:S(2)}, u32[]{:S(2)}) collective-permute-start(bf16[64,1024]{1,0:T(8,128)(2,1)} %copy-done.8), channel_id=1, source_target_pairs={{0,4},{4,8},{8,12},{12,0},{1,5},{5,9},{9,13},{13,1},{2,6},{6,10},{... | collective-permute-start | bytes 393224 | tf_op jit(solution)/shard_map/ppermute | solution.py:355
  28.0 2.6 %collective-permute-start.1 = (bf16[64,1024]{1,0:T(8,128)(2,1)S(1)}, bf16[64,1024]{1,0:T(8,128)(2,1)S(1)}, u32[]{:S(2)}, u32[]{:S(2)}) collective-permute-start(bf16[64,1024]{1,0:T(8,128)(2,1)S(1)} %get-tuple-element.24), channel_id=1, source_target_pairs={{0,12},{4,0},{8,4},{12,8},{1,13},{5,1},{9,5},{13,9},{2,14},{6,2},{... | collective-permute-start | bytes 393224 | tf_op jit(solution)/shard_map/ppermute | solution.py:355
  30.5 0.0 collective-permute-done.5.refs_1_
  30.5 0.0 collective-permute-done.6.refs_3_
  30.5 5.2 %project_fetched.2 = (bf16[2,64,64,128]{3,2,1,0:T(8,128)(2,1)S(1)}, bf16[4,64,64,128]{3,2,1,0:T(8,128)(2,1)S(1)}) custom-call(bf16[64,3072]{1,0:T(8,128)(2,1)S(1)} %collective-permute-done.2.refs_0_, bf16[64,3072]{1,0:T(8,128)(2,1)S(1)} %collective-permute-done.5.refs_1_, ...), custom_call_target="tpu_custom_call", output_to_operand_aliasing={{0}: (7, {}), {1}: (8, {})} | custom-call | tf_op jit(solution)/shard_map/project_fetched/pallas_call | solution.py:193
  35.8 0.0 copy-start.4
  35.8 0.0 copy-start.5
  35.8 0.0 copy-start.7
  35.8 0.0 collective-permute-done.refs_0_
  35.8 0.1 collective-permute-done.1.refs_2_
  35.9 0.0 collective-permute-start.7
  35.9 0.5 %collective-permute-start.8 = (bf16[64,1024]{1,0:T(8,128)(2,1)S(1)}, bf16[64,1024]{1,0:T(8,128)(2,1)S(1)}, u32[]{:S(2)}, u32[]{:S(2)}) collective-permute-start(bf16[64,1024]{1,0:T(8,128)(2,1)S(1)} %collective-permute-done.1.refs_2_), channel_id=1, source_target_pairs={{0,1},{1,0},{2,3},{3,2},{4,5},{5,4},{6,7},{7,6},{8,9},{9,8},{10,11... | collective-permute-start | bytes 393224 | tf_op jit(solution)/shard_map/ppermute | solution.py:364
  36.4 0.8 %collective-permute-done.7.refs_1_ = bf16[64,1024]{1,0:T(8,128)(2,1)S(1)} collective-permute-done((bf16[64,1024]{1,0:T(8,128)(2,1)S(1)}, bf16[64,1024]{1,0:T(8,128)(2,1)S(1)}, u32[]{:S(2)}, u32[]{:S(2)}) %collective-permute-start.7) | collective-permute-done | bytes 131104 | tf_op jit(solution)/shard_map/ppermute | solution.py:363
  37.3 0.2 collective-permute-done.8.refs_3_
  37.5 1.7 %project_fetched.3 = (bf16[2,64,64,128]{3,2,1,0:T(8,128)(2,1)S(1)}, bf16[4,64,64,128]{3,2,1,0:T(8,128)(2,1)S(1)}) custom-call(bf16[64,1024]{1,0:T(8,128)(2,1)S(1)} %collective-permute-done.refs_0_, bf16[64,1024]{1,0:T(8,128)(2,1)S(1)} %collective-permute-done.7.refs_1_, ...), custom_call_target="tpu_custom_call", output_to_operand_aliasing={{0}: (7, {}), {1}: (8, {})} | custom-call | tf_op jit(solution)/shard_map/project_fetched/pallas_call | solution.py:193
  39.2 0.0 copy-done.4
  39.2 0.0 copy-done.5
  39.2 0.0 copy-done.7
  39.3 2.5 %triplets.2.mine_ref = bf16[64,4096]{1,0:T(8,128)(2,1)S(1)} custom-call(s32[4,16]{1,0:T(4,128)S(1)} %bitcast.17, s32[4,16]{1,0:T(4,128)S(1)} %bitcast.20, s32[16]{0:T(128)S(1)} %copy-done.7, bf16[2,64,64,128]{3,2,1,0:T(8,128)(2,1)S(1)} %get-tuple-element.39.l_ref, bf16[4,64,64,128]{3,2,1,0:T(8,128)(2,1)S(1)} %get-tuple-element.38.p_ref), custom_call_target="tpu_custom_call" | custom-call | tf_op jit(solution)/shard_map/triplets/pallas_call | solution.py:269
  41.8 0.0 copy-start.9
  41.8 0.0 copy-start.3
  41.8 0.4 collective-permute-start.10
  42.2 2.5 %triplets.3.mine_ref = bf16[64,4096]{1,0:T(8,128)(2,1)S(1)} custom-call(s32[4,16]{1,0:T(4,128)S(1)} %bitcast.18, s32[4,16]{1,0:T(4,128)S(1)} %bitcast.21, s32[16]{0:T(128)S(1)} %copy-done.7, bf16[2,64,64,128]{3,2,1,0:T(8,128)(2,1)S(1)} %get-tuple-element.39.l_ref, bf16[4,64,64,128]{3,2,1,0:T(8,128)(2,1)S(1)} %get-tuple-element.38.p_ref), custom_call_target="tpu_custom_call" | custom-call | tf_op jit(solution)/shard_map/triplets/pallas_call | solution.py:269
  44.7 0.2 collective-permute-start.9
  45.0 0.0 copy-done.9
  45.0 0.1 copy.20.g_ref
  45.1 0.0 collective-permute-done.10.theirs_ref
  45.1 2.1 %finish.2.refs_0_ = bf16[2,64,4096]{2,1,0:T(8,128)(2,1)} custom-call(bf16[64,4096]{1,0:T(8,128)(2,1)S(1)} %triplets.2.mine_ref, bf16[64,4096]{1,0:T(8,128)(2,1)S(1)} %collective-permute-done.10.theirs_ref, bf16[2,64,4096]{2,1,0:T(8,128)(2,1)S(1)} %get-tuple-element.40.gate_ref, bf16[64,128]{1,0:T(8,128)(2,1)S(1)} %bitcast.14, f32[128,1]{1,0:T(8,128)S(1)} %copy.20.g_ref), custom_call_target="tpu_custom_call" | custom-call | tf_op jit(solution)/shard_map/finish/pallas_call | solution.py:316
  47.2 0.0 collective-permute-done.9.theirs_ref
  47.3 2.1 %finish.3 = bf16[2,64,4096]{2,1,0:T(8,128)(2,1)} custom-call(bf16[64,4096]{1,0:T(8,128)(2,1)S(1)} %triplets.3.mine_ref, bf16[64,4096]{1,0:T(8,128)(2,1)S(1)} %collective-permute-done.9.theirs_ref, bf16[2,64,4096]{2,1,0:T(8,128)(2,1)S(1)} %get-tuple-element.40.gate_ref, bf16[64,128]{1,0:T(8,128)(2,1)S(1)} %bitcast.15, ...), custom_call_target="tpu_custom_call", output_to_operand_aliasing={{}: (5, {})} | custom-call | tf_op jit(solution)/shard_map/finish/pallas_call | solution.py:316
  (4 shorter events, 0.0 us)
Async XLA Ops:
  0.0 9.2 %collective-permute-start.4 = (bf16[2,64,4096]{2,1,0:T(8,128)(2,1)}, bf16[2,64,4096]{2,1,0:T(8,128)(2,1)S(1)}, u32[]{:S(2)}, u32[]{:S(2)}) collective-permute-start(bf16[2,64,4096]{2,1,0:T(8,128)(2,1)} %refs_0_.1), channel_id=1, source_target_pairs={{0,1},{1,0},{2,3},{3,2},{4,5},{5,4},{6,7},{7,6},{8,9},{9,8},{10,11... | collective-permute-start | bytes 3145736 | tf_op jit(solution)/shard_map/ppermute | solution.py:351
  3.3 0.6 %copy-start.8 = (bf16[64,1024]{1,0:T(8,128)(2,1)}, bf16[64,1024]{1,0:T(8,128)(2,1)S(1)}, u32[]{:S(2)}) copy-start(bf16[64,1024]{1,0:T(8,128)(2,1)S(1)} %get-tuple-element.23) | copy-start | bytes 393220
  3.9 15.7 %collective-permute-start.2 = (bf16[64,3072]{1,0:T(8,128)(2,1)}, bf16[64,3072]{1,0:T(8,128)(2,1)S(1)}, u32[]{:S(2)}, u32[]{:S(2)}) collective-permute-start(bf16[64,3072]{1,0:T(8,128)(2,1)} %get-tuple-element.25), channel_id=1, source_target_pairs={{0,4},{4,8},{8,12},{12,0},{1,5},{5,9},{9,13},{13,1},{2,6},{6,10},{... | collective-permute-start | bytes 1179656 | tf_op jit(solution)/shard_map/ppermute | solution.py:355
  6.5 19.7 %collective-permute-start.3 = (bf16[64,3072]{1,0:T(8,128)(2,1)S(1)}, bf16[64,3072]{1,0:T(8,128)(2,1)S(1)}, u32[]{:S(2)}, u32[]{:S(2)}) collective-permute-start(bf16[64,3072]{1,0:T(8,128)(2,1)S(1)} %get-tuple-element.26), channel_id=1, source_target_pairs={{0,12},{4,0},{8,4},{12,8},{1,13},{5,1},{9,5},{13,9},{2,14},{6,2},{... | collective-permute-start | bytes 1179656 | tf_op jit(solution)/shard_map/ppermute | solution.py:355
  9.2 1.2 %copy-start = (bf16[2,64,4096]{2,1,0:T(8,128)(2,1)S(1)}, bf16[2,64,4096]{2,1,0:T(8,128)(2,1)}, u32[]{:S(2)}) copy-start(bf16[2,64,4096]{2,1,0:T(8,128)(2,1)} %refs_0_.1) | copy-start | bytes 3145732
  10.5 0.8 %copy-start.1 = (bf16[2,128,64]{1,2,0:T(8,128)(2,1)S(1)}, bf16[2,128,64]{1,2,0:T(8,128)(2,1)}, u32[]{:S(2)}) copy-start(bf16[2,128,64]{1,2,0:T(8,128)(2,1)} %param.12) | copy-start | bytes 98308
  11.2 0.8 %copy-start.2 = (bf16[2,128,64]{1,2,0:T(8,128)(2,1)S(1)}, bf16[2,128,64]{1,2,0:T(8,128)(2,1)}, u32[]{:S(2)}) copy-start(bf16[2,128,64]{1,2,0:T(8,128)(2,1)} %param.13) | copy-start | bytes 98308
  12.0 0.7 %copy-start.6 = (bf16[128,64]{0,1:T(8,128)(2,1)S(1)}, bf16[128,64]{0,1:T(8,128)(2,1)}, u32[]{:S(2)}) copy-start(bf16[128,64]{0,1:T(8,128)(2,1)} %param.15) | copy-start | bytes 49156
  26.2 4.3 %collective-permute-start.5 = (bf16[64,3072]{1,0:T(8,128)(2,1)S(1)}, bf16[64,3072]{1,0:T(8,128)(2,1)S(1)}, u32[]{:S(2)}, u32[]{:S(2)}) collective-permute-start(bf16[64,3072]{1,0:T(8,128)(2,1)S(1)} %collective-permute-done.2.refs_0_), channel_id=1, source_target_pairs={{0,1},{1,0},{2,3},{3,2},{4,5},{5,4},{6,7},{7,6},{8,9},{9,8},{10,11... | collective-permute-start | bytes 1179656 | tf_op jit(solution)/shard_map/ppermute | solution.py:363
  26.2 4.3 %collective-permute-start.6 = (bf16[64,3072]{1,0:T(8,128)(2,1)S(1)}, bf16[64,3072]{1,0:T(8,128)(2,1)S(1)}, u32[]{:S(2)}, u32[]{:S(2)}) collective-permute-start(bf16[64,3072]{1,0:T(8,128)(2,1)S(1)} %collective-permute-done.3.refs_2_), channel_id=1, source_target_pairs={{0,1},{1,0},{2,3},{3,2},{4,5},{5,4},{6,7},{7,6},{8,9},{9,8},{10,11... | collective-permute-start | bytes 1179656 | tf_op jit(solution)/shard_map/ppermute | solution.py:364
  26.7 9.1 %collective-permute-start = (bf16[64,1024]{1,0:T(8,128)(2,1)}, bf16[64,1024]{1,0:T(8,128)(2,1)S(1)}, u32[]{:S(2)}, u32[]{:S(2)}) collective-permute-start(bf16[64,1024]{1,0:T(8,128)(2,1)} %copy-done.8), channel_id=1, source_target_pairs={{0,4},{4,8},{8,12},{12,0},{1,5},{5,9},{9,13},{13,1},{2,6},{6,10},{... | collective-permute-start | bytes 393224 | tf_op jit(solution)/shard_map/ppermute | solution.py:355
  28.0 8.0 %collective-permute-start.1 = (bf16[64,1024]{1,0:T(8,128)(2,1)S(1)}, bf16[64,1024]{1,0:T(8,128)(2,1)S(1)}, u32[]{:S(2)}, u32[]{:S(2)}) collective-permute-start(bf16[64,1024]{1,0:T(8,128)(2,1)S(1)} %get-tuple-element.24), channel_id=1, source_target_pairs={{0,12},{4,0},{8,4},{12,8},{1,13},{5,1},{9,5},{13,9},{2,14},{6,2},{... | collective-permute-start | bytes 393224 | tf_op jit(solution)/shard_map/ppermute | solution.py:355
  35.8 3.4 %copy-start.4 = (s32[16,4]{0,1:T(4,128)S(1)}, s32[16,4]{0,1:T(4,128)}, u32[]{:S(2)}) copy-start(s32[16,4]{0,1:T(4,128)} %param.17) | copy-start | bytes 772
  35.8 3.4 %copy-start.5 = (s32[16,4]{0,1:T(4,128)S(1)}, s32[16,4]{0,1:T(4,128)}, u32[]{:S(2)}) copy-start(s32[16,4]{0,1:T(4,128)} %param.18) | copy-start | bytes 772
  35.8 3.4 %copy-start.7 = (s32[16]{0:T(128)S(1)}, s32[16]{0:T(128)}, u32[]{:S(2)}) copy-start(s32[16]{0:T(128)} %n_ref.5) | copy-start | bytes 196
  35.9 1.3 %collective-permute-start.7 = (bf16[64,1024]{1,0:T(8,128)(2,1)S(1)}, bf16[64,1024]{1,0:T(8,128)(2,1)S(1)}, u32[]{:S(2)}, u32[]{:S(2)}) collective-permute-start(bf16[64,1024]{1,0:T(8,128)(2,1)S(1)} %collective-permute-done.refs_0_), channel_id=1, source_target_pairs={{0,1},{1,0},{2,3},{3,2},{4,5},{5,4},{6,7},{7,6},{8,9},{9,8},{10,11... | collective-permute-start | bytes 393224 | tf_op jit(solution)/shard_map/ppermute | solution.py:363
  35.9 1.5 %collective-permute-start.8 = (bf16[64,1024]{1,0:T(8,128)(2,1)S(1)}, bf16[64,1024]{1,0:T(8,128)(2,1)S(1)}, u32[]{:S(2)}, u32[]{:S(2)}) collective-permute-start(bf16[64,1024]{1,0:T(8,128)(2,1)S(1)} %collective-permute-done.1.refs_2_), channel_id=1, source_target_pairs={{0,1},{1,0},{2,3},{3,2},{4,5},{5,4},{6,7},{7,6},{8,9},{9,8},{10,11... | collective-permute-start | bytes 393224 | tf_op jit(solution)/shard_map/ppermute | solution.py:364
  41.8 3.2 %copy-start.9 = (f32[128]{0:T(128)S(1)}, f32[128]{0:T(128)}, u32[]{:S(2)}) copy-start(f32[128]{0:T(128)} %param.14) | copy-start | bytes 1540
  41.8 3.3 %copy-start.3 = (bf16[128,64]{0,1:T(8,128)(2,1)S(1)}, bf16[128,64]{0,1:T(8,128)(2,1)}, u32[]{:S(2)}) copy-start(bf16[128,64]{0,1:T(8,128)(2,1)} %param.16) | copy-start | bytes 49156
  41.8 3.3 %collective-permute-start.10 = (bf16[64,4096]{1,0:T(8,128)(2,1)S(1)}, bf16[64,4096]{1,0:T(8,128)(2,1)S(1)}, u32[]{:S(2)}, u32[]{:S(2)}) collective-permute-start(bf16[64,4096]{1,0:T(8,128)(2,1)S(1)} %triplets.2.mine_ref), channel_id=1, source_target_pairs={{0,1},{1,0},{2,3},{3,2},{4,5},{5,4},{6,7},{7,6},{8,9},{9,8},{10,11... | collective-permute-start | bytes 1572872 | tf_op jit(solution)/shard_map/ppermute | solution.py:378
  44.7 2.5 %collective-permute-start.9 = (bf16[64,4096]{1,0:T(8,128)(2,1)S(1)}, bf16[64,4096]{1,0:T(8,128)(2,1)S(1)}, u32[]{:S(2)}, u32[]{:S(2)}) collective-permute-start(bf16[64,4096]{1,0:T(8,128)(2,1)S(1)} %triplets.3.mine_ref), channel_id=1, source_target_pairs={{0,1},{1,0},{2,3},{3,2},{4,5},{5,4},{6,7},{7,6},{8,9},{9,8},{10,11... | collective-permute-start | bytes 1572872 | tf_op jit(solution)/shard_map/ppermute | solution.py:378

commit v5 on v4

--- a/solution.py
+++ b/solution.py
@@ -356,7 +356,7 @@
         for n in range(len(cuts))
     ]
     lefts, rights, gate = project(
-        [pair, pair_other], weights, gain, 1024, 256, True
+        [pair, pair_other], weights, gain, 1024, 1024, True
     )
     for (start, size), (from_behind, from_ahead) in zip(cuts, arrived):
         from_behind, from_ahead, lefts = lax.optimization_barrier((from_behind, from_ahead, lefts))
@@ -367,7 +367,7 @@
             weights,
             gain,
             1024,
-            256,
+            512 if start == 0 else 128,
             False,
             [lefts, rights],
             start,
@@ -380,7 +380,7 @@
             update, lefts = lax.optimization_barrier((update, lefts))
     out = None
     for s, (mine, theirs) in enumerate(updates):
-        out = finish(s, mine, theirs, gate, out_weight.T, last_gain, 4, 256, out)
+        out = finish(s, mine, theirs, gate, out_weight.T, last_gain, 4, (1024, 512)[s % 2], out)
     return out
 
 

time: 49.8 us -> 49.8 us (level)
  waiting for transfers between devices: 7.68 us -> 7.14 us
    ppermute x2, waiting for transfers between devices: 6.64 us -> 6.1 us  [per_device(): lax.ppermute(chosen[2 * n + 1], 'row', down)]
  transfers between devices with their start and end apart: 11 -> 11, of which waited for: 4 -> 3; matrix products, arithmetic and copies ran while one was open for 2% -> 2% of each run, Pallas kernels for 40% -> 41%
where the time goes in v5:
time: 49.8 us; the launch traced here: 49.4 us
  Pallas kernels  26.5 us (53%)
  starting transfers between devices  10.6 us (21%)
  waiting for transfers between devices  7.14 us (14%)
  local copies, waits for them, and re-layouts  4.99 us (10%)
    pallas_call x3, Pallas kernels, project(): pl.pallas_call(functools.partial(project_kernel, piece, chunk, offset, ga...  14.4 us
    ppermute x2, waiting for transfers between devices, per_device(): lax.ppermute(chosen[2 * n + 1], 'row', down)  6.1 us
    pallas_call x2, Pallas kernels, triplet_sum(): pl.pallas_call(functools.partial(triplet_kernel, s, slots, a_slots.shape[...  5.03 us
    ppermute x2, starting transfers between devices, per_device(): lax.ppermute(chosen[2 * n + 1], 'row', down)  4.52 us
    pallas_call x2, Pallas kernels, finish(): pl.pallas_call(functools.partial(finish_kernel, s, piece), in_specs=in_sp...  4.27 us
    unnamed x20, local copies, waits for them, and re-layouts  4.12 us
    ppermute x2, starting transfers between devices, per_device(): lax.ppermute(chosen[2 * n], 'row', up)  3.91 us
    pallas_call x1, Pallas kernels, select_blocks(): pl.pallas_call(functools.partial(select_kernel, slots, a_slots.shape[0],...  2.82 us
  transfers between devices with their start and end apart: 11, of which 3 were waited for; matrix products, arithmetic and copies ran while one was open for 2% of the time, Pallas kernels for 41%

profile of v5, /device:TPU:0, one launch (start us, length us, event | category | flops | bytes accessed | tf_op | source)
XLA Modules:
  0.0 49.4 jit_solution(4256043284962884764)
XLA Ops:
  0.0 0.5 collective-permute-start.4
  0.5 2.8 %select_blocks.1 = (bf16[64,3072]{1,0:T(8,128)(2,1)}, bf16[64,3072]{1,0:T(8,128)(2,1)S(1)}, bf16[64,1024]{1,0:T(8,128)(2,1)S(1)}, bf16[64,1024]{1,0:T(8,128)(2,1)S(1)}) custom-call(s32[4,16]{1,0:T(4,128)} %bitcast.16, s32[4,16]{1,0:T(4,128)} %bitcast.19, s32[16]{0:T(128)} %n_ref.5, bf16[2,64,4096]{2,1,0:T(8,128)(2,1)} %refs_0_.1), custom_call_target="tpu_custom_call" | custom-call | tf_op jit(solution)/shard_map/select_blocks/pallas_call | solution.py:69
  3.3 0.0 copy-start.8
  3.3 0.6 %copy-done.8 = bf16[64,1024]{1,0:T(8,128)(2,1)} copy-done((bf16[64,1024]{1,0:T(8,128)(2,1)}, bf16[64,1024]{1,0:T(8,128)(2,1)S(1)}, u32[]{:S(2)}) %copy-start.8) | copy-done | bytes 131096
  3.9 2.6 %collective-permute-start.2 = (bf16[64,3072]{1,0:T(8,128)(2,1)}, bf16[64,3072]{1,0:T(8,128)(2,1)S(1)}, u32[]{:S(2)}, u32[]{:S(2)}) collective-permute-start(bf16[64,3072]{1,0:T(8,128)(2,1)} %get-tuple-element.25), channel_id=1, source_target_pairs={{0,4},{4,8},{8,12},{12,0},{1,5},{5,9},{9,13},{13,1},{2,6},{6,10},{... | collective-permute-start | bytes 1179656 | tf_op jit(solution)/shard_map/ppermute | solution.py:355
  6.5 2.0 %collective-permute-start.3 = (bf16[64,3072]{1,0:T(8,128)(2,1)S(1)}, bf16[64,3072]{1,0:T(8,128)(2,1)S(1)}, u32[]{:S(2)}, u32[]{:S(2)}) collective-permute-start(bf16[64,3072]{1,0:T(8,128)(2,1)S(1)} %get-tuple-element.26), channel_id=1, source_target_pairs={{0,12},{4,0},{8,4},{12,8},{1,13},{5,1},{9,5},{13,9},{2,14},{6,2},{... | collective-permute-start | bytes 1179656 | tf_op jit(solution)/shard_map/ppermute | solution.py:355
  8.5 0.8 %copy.16.refs_4_.refs_6_ = f32[128,1]{1,0:T(8,128)S(1)} copy(f32[128,1]{0,1:T(1,128)} %bitcast.23) | data formatting | bytes 1024 | tf_op jit(solution)/shard_map/broadcast_in_dim | solution.py:349
  9.3 0.0 collective-permute-done.4.refs_1_
  9.3 0.0 copy-start
  9.3 1.2 %copy-done = bf16[2,64,4096]{2,1,0:T(8,128)(2,1)S(1)} copy-done((bf16[2,64,4096]{2,1,0:T(8,128)(2,1)S(1)}, bf16[2,64,4096]{2,1,0:T(8,128)(2,1)}, u32[]{:S(2)}) %copy-start) | copy-done | bytes 1048600
  10.5 0.8 %copy-done.1 = bf16[2,128,64]{1,2,0:T(8,128)(2,1)S(1)} copy-done((bf16[2,128,64]{1,2,0:T(8,128)(2,1)S(1)}, bf16[2,128,64]{1,2,0:T(8,128)(2,1)}, u32[]{:S(2)}) %copy-start.1) | copy-done | bytes 32792
  11.3 0.8 %copy-done.2 = bf16[2,128,64]{1,2,0:T(8,128)(2,1)S(1)} copy-done((bf16[2,128,64]{1,2,0:T(8,128)(2,1)S(1)}, bf16[2,128,64]{1,2,0:T(8,128)(2,1)}, u32[]{:S(2)}) %copy-start.2) | copy-done | bytes 32792
  12.0 0.7 %copy-done.6 = bf16[128,64]{0,1:T(8,128)(2,1)S(1)} copy-done((bf16[128,64]{0,1:T(8,128)(2,1)S(1)}, bf16[128,64]{0,1:T(8,128)(2,1)}, u32[]{:S(2)}) %copy-start.6) | copy-done | bytes 16408
  12.8 7.3 %project_own.1 = (bf16[2,64,64,128]{3,2,1,0:T(8,128)(2,1)S(1)}, bf16[4,64,64,128]{3,2,1,0:T(8,128)(2,1)S(1)}, bf16[2,64,4096]{2,1,0:T(8,128)(2,1)S(1)}) custom-call(bf16[2,64,4096]{2,1,0:T(8,128)(2,1)S(1)} %copy-done, bf16[2,64,4096]{2,1,0:T(8,128)(2,1)S(1)} %collective-permute-done.4.refs_1_, bf16[2,64,128]{2,1,0:T(8,128)(2,1)S(1)} %bitcast.8, ...), custom_call_target="tpu_custom_call" | custom-call | tf_op jit(solution)/shard_map/project_own/pallas_call | solution.py:193
  20.1 0.0 collective-permute-done.2.refs_0_
  20.1 6.1 %collective-permute-done.3.refs_2_ = bf16[64,3072]{1,0:T(8,128)(2,1)S(1)} collective-permute-done((bf16[64,3072]{1,0:T(8,128)(2,1)S(1)}, bf16[64,3072]{1,0:T(8,128)(2,1)S(1)}, u32[]{:S(2)}, u32[]{:S(2)}) %collective-permute-start.3) | collective-permute-done | bytes 393248 | tf_op jit(solution)/shard_map/ppermute | solution.py:355
  26.2 0.0 collective-permute-start.5
  26.2 0.5 %collective-permute-start.6 = (bf16[64,3072]{1,0:T(8,128)(2,1)S(1)}, bf16[64,3072]{1,0:T(8,128)(2,1)S(1)}, u32[]{:S(2)}, u32[]{:S(2)}) collective-permute-start(bf16[64,3072]{1,0:T(8,128)(2,1)S(1)} %collective-permute-done.3.refs_2_), channel_id=1, source_target_pairs={{0,1},{1,0},{2,3},{3,2},{4,5},{5,4},{6,7},{7,6},{8,9},{9,8},{10,11... | collective-permute-start | bytes 1179656 | tf_op jit(solution)/shard_map/ppermute | solution.py:364
  26.7 1.3 %collective-permute-start = (bf16[64,1024]{1,0:T(8,128)(2,1)}, bf16[64,1024]{1,0:T(8,128)(2,1)S(1)}, u32[]{:S(2)}, u32[]{:S(2)}) collective-permute-start(bf16[64,1024]{1,0:T(8,128)(2,1)} %copy-done.8), channel_id=1, source_target_pairs={{0,4},{4,8},{8,12},{12,0},{1,5},{5,9},{9,13},{13,1},{2,6},{6,10},{... | collective-permute-start | bytes 393224 | tf_op jit(solution)/shard_map/ppermute | solution.py:355
  28.0 2.5 %collective-permute-start.1 = (bf16[64,1024]{1,0:T(8,128)(2,1)S(1)}, bf16[64,1024]{1,0:T(8,128)(2,1)S(1)}, u32[]{:S(2)}, u32[]{:S(2)}) collective-permute-start(bf16[64,1024]{1,0:T(8,128)(2,1)S(1)} %get-tuple-element.24), channel_id=1, source_target_pairs={{0,12},{4,0},{8,4},{12,8},{1,13},{5,1},{9,5},{13,9},{2,14},{6,2},{... | collective-permute-start | bytes 393224 | tf_op jit(solution)/shard_map/ppermute | solution.py:355
  30.5 0.0 collective-permute-done.5.refs_1_
  30.5 0.0 collective-permute-done.6.refs_3_
  30.5 5.4 %project_fetched.2 = (bf16[2,64,64,128]{3,2,1,0:T(8,128)(2,1)S(1)}, bf16[4,64,64,128]{3,2,1,0:T(8,128)(2,1)S(1)}) custom-call(bf16[64,3072]{1,0:T(8,128)(2,1)S(1)} %collective-permute-done.2.refs_0_, bf16[64,3072]{1,0:T(8,128)(2,1)S(1)} %collective-permute-done.5.refs_1_, ...), custom_call_target="tpu_custom_call", output_to_operand_aliasing={{0}: (7, {}), {1}: (8, {})} | custom-call | tf_op jit(solution)/shard_map/project_fetched/pallas_call | solution.py:193
  35.9 0.0 copy-start.4
  35.9 0.0 copy-start.5
  35.9 0.0 copy-start.7
  36.0 0.0 collective-permute-done.refs_0_
  36.0 0.0 collective-permute-done.1.refs_2_
  36.0 0.0 collective-permute-start.7
  36.0 0.5 %collective-permute-start.8 = (bf16[64,1024]{1,0:T(8,128)(2,1)S(1)}, bf16[64,1024]{1,0:T(8,128)(2,1)S(1)}, u32[]{:S(2)}, u32[]{:S(2)}) collective-permute-start(bf16[64,1024]{1,0:T(8,128)(2,1)S(1)} %collective-permute-done.1.refs_2_), channel_id=1, source_target_pairs={{0,1},{1,0},{2,3},{3,2},{4,5},{5,4},{6,7},{7,6},{8,9},{9,8},{10,11... | collective-permute-start | bytes 393224 | tf_op jit(solution)/shard_map/ppermute | solution.py:364
  36.5 0.8 %collective-permute-done.7.refs_1_ = bf16[64,1024]{1,0:T(8,128)(2,1)S(1)} collective-permute-done((bf16[64,1024]{1,0:T(8,128)(2,1)S(1)}, bf16[64,1024]{1,0:T(8,128)(2,1)S(1)}, u32[]{:S(2)}, u32[]{:S(2)}) %collective-permute-start.7) | collective-permute-done | bytes 131104 | tf_op jit(solution)/shard_map/ppermute | solution.py:363
  37.4 0.2 collective-permute-done.8.refs_3_
  37.6 1.7 %project_fetched.3 = (bf16[2,64,64,128]{3,2,1,0:T(8,128)(2,1)S(1)}, bf16[4,64,64,128]{3,2,1,0:T(8,128)(2,1)S(1)}) custom-call(bf16[64,1024]{1,0:T(8,128)(2,1)S(1)} %collective-permute-done.refs_0_, bf16[64,1024]{1,0:T(8,128)(2,1)S(1)} %collective-permute-done.7.refs_1_, ...), custom_call_target="tpu_custom_call", output_to_operand_aliasing={{0}: (7, {}), {1}: (8, {})} | custom-call | tf_op jit(solution)/shard_map/project_fetched/pallas_call | solution.py:193
  39.3 0.0 copy-done.4
  39.3 0.0 copy-done.5
  39.3 0.0 copy-done.7
  39.3 2.5 %triplets.2.mine_ref = bf16[64,4096]{1,0:T(8,128)(2,1)S(1)} custom-call(s32[4,16]{1,0:T(4,128)S(1)} %bitcast.17, s32[4,16]{1,0:T(4,128)S(1)} %bitcast.20, s32[16]{0:T(128)S(1)} %copy-done.7, bf16[2,64,64,128]{3,2,1,0:T(8,128)(2,1)S(1)} %get-tuple-element.39.l_ref, bf16[4,64,64,128]{3,2,1,0:T(8,128)(2,1)S(1)} %get-tuple-element.38.p_ref), custom_call_target="tpu_custom_call" | custom-call | tf_op jit(solution)/shard_map/triplets/pallas_call | solution.py:269
  41.8 0.0 copy-start.9
  41.8 0.0 copy-start.3
  41.9 0.4 collective-permute-start.10
  42.2 2.5 %triplets.3.mine_ref = bf16[64,4096]{1,0:T(8,128)(2,1)S(1)} custom-call(s32[4,16]{1,0:T(4,128)S(1)} %bitcast.18, s32[4,16]{1,0:T(4,128)S(1)} %bitcast.21, s32[16]{0:T(128)S(1)} %copy-done.7, bf16[2,64,64,128]{3,2,1,0:T(8,128)(2,1)S(1)} %get-tuple-element.39.l_ref, bf16[4,64,64,128]{3,2,1,0:T(8,128)(2,1)S(1)} %get-tuple-element.38.p_ref), custom_call_target="tpu_custom_call" | custom-call | tf_op jit(solution)/shard_map/triplets/pallas_call | solution.py:269
  44.8 0.2 collective-permute-start.9
  45.0 0.0 copy-done.9
  45.0 0.1 copy.20.g_ref
  45.1 0.0 collective-permute-done.10.theirs_ref
  45.1 2.1 %finish.2.refs_0_ = bf16[2,64,4096]{2,1,0:T(8,128)(2,1)} custom-call(bf16[64,4096]{1,0:T(8,128)(2,1)S(1)} %triplets.2.mine_ref, bf16[64,4096]{1,0:T(8,128)(2,1)S(1)} %collective-permute-done.10.theirs_ref, bf16[2,64,4096]{2,1,0:T(8,128)(2,1)S(1)} %get-tuple-element.40.gate_ref, bf16[64,128]{1,0:T(8,128)(2,1)S(1)} %bitcast.14, f32[128,1]{1,0:T(8,128)S(1)} %copy.20.g_ref), custom_call_target="tpu_custom_call" | custom-call | tf_op jit(solution)/shard_map/finish/pallas_call | solution.py:316
  47.3 0.0 collective-permute-done.9.theirs_ref
  47.3 2.1 %finish.3 = bf16[2,64,4096]{2,1,0:T(8,128)(2,1)} custom-call(bf16[64,4096]{1,0:T(8,128)(2,1)S(1)} %triplets.3.mine_ref, bf16[64,4096]{1,0:T(8,128)(2,1)S(1)} %collective-permute-done.9.theirs_ref, bf16[2,64,4096]{2,1,0:T(8,128)(2,1)S(1)} %get-tuple-element.40.gate_ref, bf16[64,128]{1,0:T(8,128)(2,1)S(1)} %bitcast.15, ...), custom_call_target="tpu_custom_call", output_to_operand_aliasing={{}: (5, {})} | custom-call | tf_op jit(solution)/shard_map/finish/pallas_call | solution.py:316
  (4 shorter events, 0.0 us)
Async XLA Ops:
  0.0 9.3 %collective-permute-start.4 = (bf16[2,64,4096]{2,1,0:T(8,128)(2,1)}, bf16[2,64,4096]{2,1,0:T(8,128)(2,1)S(1)}, u32[]{:S(2)}, u32[]{:S(2)}) collective-permute-start(bf16[2,64,4096]{2,1,0:T(8,128)(2,1)} %refs_0_.1), channel_id=1, source_target_pairs={{0,1},{1,0},{2,3},{3,2},{4,5},{5,4},{6,7},{7,6},{8,9},{9,8},{10,11... | collective-permute-start | bytes 3145736 | tf_op jit(solution)/shard_map/ppermute | solution.py:351
  3.3 0.6 %copy-start.8 = (bf16[64,1024]{1,0:T(8,128)(2,1)}, bf16[64,1024]{1,0:T(8,128)(2,1)S(1)}, u32[]{:S(2)}) copy-start(bf16[64,1024]{1,0:T(8,128)(2,1)S(1)} %get-tuple-element.23) | copy-start | bytes 393220
  3.9 16.2 %collective-permute-start.2 = (bf16[64,3072]{1,0:T(8,128)(2,1)}, bf16[64,3072]{1,0:T(8,128)(2,1)S(1)}, u32[]{:S(2)}, u32[]{:S(2)}) collective-permute-start(bf16[64,3072]{1,0:T(8,128)(2,1)} %get-tuple-element.25), channel_id=1, source_target_pairs={{0,4},{4,8},{8,12},{12,0},{1,5},{5,9},{9,13},{13,1},{2,6},{6,10},{... | collective-permute-start | bytes 1179656 | tf_op jit(solution)/shard_map/ppermute | solution.py:355
  6.5 19.7 %collective-permute-start.3 = (bf16[64,3072]{1,0:T(8,128)(2,1)S(1)}, bf16[64,3072]{1,0:T(8,128)(2,1)S(1)}, u32[]{:S(2)}, u32[]{:S(2)}) collective-permute-start(bf16[64,3072]{1,0:T(8,128)(2,1)S(1)} %get-tuple-element.26), channel_id=1, source_target_pairs={{0,12},{4,0},{8,4},{12,8},{1,13},{5,1},{9,5},{13,9},{2,14},{6,2},{... | collective-permute-start | bytes 1179656 | tf_op jit(solution)/shard_map/ppermute | solution.py:355
  9.3 1.2 %copy-start = (bf16[2,64,4096]{2,1,0:T(8,128)(2,1)S(1)}, bf16[2,64,4096]{2,1,0:T(8,128)(2,1)}, u32[]{:S(2)}) copy-start(bf16[2,64,4096]{2,1,0:T(8,128)(2,1)} %refs_0_.1) | copy-start | bytes 3145732
  10.5 0.8 %copy-start.1 = (bf16[2,128,64]{1,2,0:T(8,128)(2,1)S(1)}, bf16[2,128,64]{1,2,0:T(8,128)(2,1)}, u32[]{:S(2)}) copy-start(bf16[2,128,64]{1,2,0:T(8,128)(2,1)} %param.12) | copy-start | bytes 98308
  11.3 0.8 %copy-start.2 = (bf16[2,128,64]{1,2,0:T(8,128)(2,1)S(1)}, bf16[2,128,64]{1,2,0:T(8,128)(2,1)}, u32[]{:S(2)}) copy-start(bf16[2,128,64]{1,2,0:T(8,128)(2,1)} %param.13) | copy-start | bytes 98308
  12.0 0.7 %copy-start.6 = (bf16[128,64]{0,1:T(8,128)(2,1)S(1)}, bf16[128,64]{0,1:T(8,128)(2,1)}, u32[]{:S(2)}) copy-start(bf16[128,64]{0,1:T(8,128)(2,1)} %param.15) | copy-start | bytes 49156
  26.2 4.3 %collective-permute-start.5 = (bf16[64,3072]{1,0:T(8,128)(2,1)S(1)}, bf16[64,3072]{1,0:T(8,128)(2,1)S(1)}, u32[]{:S(2)}, u32[]{:S(2)}) collective-permute-start(bf16[64,3072]{1,0:T(8,128)(2,1)S(1)} %collective-permute-done.2.refs_0_), channel_id=1, source_target_pairs={{0,1},{1,0},{2,3},{3,2},{4,5},{5,4},{6,7},{7,6},{8,9},{9,8},{10,11... | collective-permute-start | bytes 1179656 | tf_op jit(solution)/shard_map/ppermute | solution.py:363
  26.2 4.3 %collective-permute-start.6 = (bf16[64,3072]{1,0:T(8,128)(2,1)S(1)}, bf16[64,3072]{1,0:T(8,128)(2,1)S(1)}, u32[]{:S(2)}, u32[]{:S(2)}) collective-permute-start(bf16[64,3072]{1,0:T(8,128)(2,1)S(1)} %collective-permute-done.3.refs_2_), channel_id=1, source_target_pairs={{0,1},{1,0},{2,3},{3,2},{4,5},{5,4},{6,7},{7,6},{8,9},{9,8},{10,11... | collective-permute-start | bytes 1179656 | tf_op jit(solution)/shard_map/ppermute | solution.py:364
  26.7 9.3 %collective-permute-start = (bf16[64,1024]{1,0:T(8,128)(2,1)}, bf16[64,1024]{1,0:T(8,128)(2,1)S(1)}, u32[]{:S(2)}, u32[]{:S(2)}) collective-permute-start(bf16[64,1024]{1,0:T(8,128)(2,1)} %copy-done.8), channel_id=1, source_target_pairs={{0,4},{4,8},{8,12},{12,0},{1,5},{5,9},{9,13},{13,1},{2,6},{6,10},{... | collective-permute-start | bytes 393224 | tf_op jit(solution)/shard_map/ppermute | solution.py:355
  28.0 8.0 %collective-permute-start.1 = (bf16[64,1024]{1,0:T(8,128)(2,1)S(1)}, bf16[64,1024]{1,0:T(8,128)(2,1)S(1)}, u32[]{:S(2)}, u32[]{:S(2)}) collective-permute-start(bf16[64,1024]{1,0:T(8,128)(2,1)S(1)} %get-tuple-element.24), channel_id=1, source_target_pairs={{0,12},{4,0},{8,4},{12,8},{1,13},{5,1},{9,5},{13,9},{2,14},{6,2},{... | collective-permute-start | bytes 393224 | tf_op jit(solution)/shard_map/ppermute | solution.py:355
  35.9 3.4 %copy-start.4 = (s32[16,4]{0,1:T(4,128)S(1)}, s32[16,4]{0,1:T(4,128)}, u32[]{:S(2)}) copy-start(s32[16,4]{0,1:T(4,128)} %param.17) | copy-start | bytes 772
  35.9 3.4 %copy-start.5 = (s32[16,4]{0,1:T(4,128)S(1)}, s32[16,4]{0,1:T(4,128)}, u32[]{:S(2)}) copy-start(s32[16,4]{0,1:T(4,128)} %param.18) | copy-start | bytes 772
  35.9 3.4 %copy-start.7 = (s32[16]{0:T(128)S(1)}, s32[16]{0:T(128)}, u32[]{:S(2)}) copy-start(s32[16]{0:T(128)} %n_ref.5) | copy-start | bytes 196
  36.0 1.4 %collective-permute-start.7 = (bf16[64,1024]{1,0:T(8,128)(2,1)S(1)}, bf16[64,1024]{1,0:T(8,128)(2,1)S(1)}, u32[]{:S(2)}, u32[]{:S(2)}) collective-permute-start(bf16[64,1024]{1,0:T(8,128)(2,1)S(1)} %collective-permute-done.refs_0_), channel_id=1, source_target_pairs={{0,1},{1,0},{2,3},{3,2},{4,5},{5,4},{6,7},{7,6},{8,9},{9,8},{10,11... | collective-permute-start | bytes 393224 | tf_op jit(solution)/shard_map/ppermute | solution.py:363
  36.0 1.5 %collective-permute-start.8 = (bf16[64,1024]{1,0:T(8,128)(2,1)S(1)}, bf16[64,1024]{1,0:T(8,128)(2,1)S(1)}, u32[]{:S(2)}, u32[]{:S(2)}) collective-permute-start(bf16[64,1024]{1,0:T(8,128)(2,1)S(1)} %collective-permute-done.1.refs_2_), channel_id=1, source_target_pairs={{0,1},{1,0},{2,3},{3,2},{4,5},{5,4},{6,7},{7,6},{8,9},{9,8},{10,11... | collective-permute-start | bytes 393224 | tf_op jit(solution)/shard_map/ppermute | solution.py:364
  41.8 3.2 %copy-start.9 = (f32[128]{0:T(128)S(1)}, f32[128]{0:T(128)}, u32[]{:S(2)}) copy-start(f32[128]{0:T(128)} %param.14) | copy-start | bytes 1540
  41.8 3.3 %copy-start.3 = (bf16[128,64]{0,1:T(8,128)(2,1)S(1)}, bf16[128,64]{0,1:T(8,128)(2,1)}, u32[]{:S(2)}) copy-start(bf16[128,64]{0,1:T(8,128)(2,1)} %param.16) | copy-start | bytes 49156
  41.9 3.3 %collective-permute-start.10 = (bf16[64,4096]{1,0:T(8,128)(2,1)S(1)}, bf16[64,4096]{1,0:T(8,128)(2,1)S(1)}, u32[]{:S(2)}, u32[]{:S(2)}) collective-permute-start(bf16[64,4096]{1,0:T(8,128)(2,1)S(1)} %triplets.2.mine_ref), channel_id=1, source_target_pairs={{0,1},{1,0},{2,3},{3,2},{4,5},{5,4},{6,7},{7,6},{8,9},{9,8},{10,11... | collective-permute-start | bytes 1572872 | tf_op jit(solution)/shard_map/ppermute | solution.py:378
  44.8 2.5 %collective-permute-start.9 = (bf16[64,4096]{1,0:T(8,128)(2,1)S(1)}, bf16[64,4096]{1,0:T(8,128)(2,1)S(1)}, u32[]{:S(2)}, u32[]{:S(2)}) collective-permute-start(bf16[64,4096]{1,0:T(8,128)(2,1)S(1)} %triplets.3.mine_ref), channel_id=1, source_target_pairs={{0,1},{1,0},{2,3},{3,2},{4,5},{5,4},{6,7},{7,6},{8,9},{9,8},{10,11... | collective-permute-start | bytes 1572872 | tf_op jit(solution)/shard_map/ppermute | solution.py:378

commit v6 on v4

--- a/solution.py
+++ b/solution.py
@@ -76,36 +76,11 @@
     )(a_slots, b_slots, counts, pair)
 
 
-def own_lanes_first(weight):
-    return jnp.where(
-        lax.axis_index("chan") == 0, weight, pltpu.roll(weight, weight.shape[1] // 2, 1)
-    )
-
-
-def gains_of(g_ref):
-    half = g_ref.shape[0] // 2
-    chan = lax.axis_index("chan")
-    mine = g_ref[pl.ds(pl.multiple_of(chan * half, half), half), :]
-    theirs = g_ref[pl.ds(pl.multiple_of((1 - chan) * half, half), half), :]
-    return mine, theirs
-
-
-def normed_of(mine, theirs, gain):
-    half = mine.shape[0]
-    total = 2 * half
-    mine = mine.astype(F32)
-    theirs = theirs.astype(F32)
-    mean = (jnp.sum(mine, axis=0, keepdims=True) + jnp.sum(theirs, axis=0, keepdims=True)) / total
-    mine = mine - mean
-    theirs = theirs - mean
-    spread = (
-        jnp.sum(mine * mine, axis=0, keepdims=True) + jnp.sum(theirs * theirs, axis=0, keepdims=True)
-    ) / total
-    scale = lax.rsqrt(spread + epsilon)
-    return jnp.concatenate(
-        [(mine * scale * gain[0]).astype(BF16), (theirs * scale * gain[1]).astype(BF16)],
-        axis=0,
-    )
+def prepared(weight, gain):
+    weight = weight * gain
+    weight = weight - jnp.mean(weight, axis=1, keepdims=True)
+    rolled = pltpu.roll(weight, weight.shape[1] // 2, 1)
+    return jnp.where(lax.axis_index("chan") == 0, weight, rolled).astype(BF16)
 
 
 def gated_rows(w_ref):
@@ -116,21 +91,40 @@
     return [0.5 * row for row in rows]
 
 
+def repeated(value, times):
+    return jnp.concatenate([value] * times, axis=0)
+
+
+def centred_of(mine, theirs):
+    values = jnp.concatenate([mine, theirs], axis=0)
+    channels = values.shape[0]
+    ones = jnp.full((16, channels), 1.0 / channels, BF16)
+    mean = jnp.dot(ones, values, preferred_element_type=F32)
+    rounded = mean.astype(BF16)
+    centred = values - repeated(rounded, channels // 16)
+    square = jnp.dot(ones, centred * centred, preferred_element_type=F32)
+    left = mean - rounded.astype(F32)
+    spread = jnp.maximum(square - left * left, 0.0)
+    return centred, lax.rsqrt(spread + epsilon)
+
+
 def project_kernel(piece, chunk, offset, gated, *refs):
     if gated:
-        m_ref, t_ref, a_ref, b_ref, g_ref, o_ref, l_ref, p_ref, gate_ref, sl, sp, sq = refs
+        m_ref, t_ref, a_ref, b_ref, o_ref, u_ref, g_ref, h_ref = refs[:8]
+        l_ref, p_ref, gate_ref, w_ref, v_ref, sl, sp = refs[8:]
         blocks = ((m_ref.at[0], t_ref.at[0]), (m_ref.at[1], t_ref.at[1]))
-        rows = [0.5 * o_ref[...].astype(F32)]
+        rows = gated_rows(a_ref) + gated_rows(b_ref) + [0.5 * o_ref[...].astype(F32)]
+        weight = prepared(jnp.concatenate(rows, axis=0), g_ref[...])
         pair_of = 0
     else:
-        m0, t0, m1, t1, a_ref, b_ref, g_ref, _, _, l_ref, p_ref, sl, sp, sq = refs
+        m0, t0, m1, t1, w_ref, _, _, l_ref, p_ref, sl, sp = refs
         blocks = ((m0, t0), (m1, t1))
-        rows = []
+        weight = w_ref[...]
         pair_of = 1
     half, cells = blocks[0][0].shape
-    weight = jnp.concatenate(gated_rows(a_ref) + gated_rows(b_ref) + rows, axis=0)
-    weight = own_lanes_first(weight).astype(BF16)
-    gain = gains_of(g_ref)
+    if gated:
+        w_ref[...] = weight[: 4 * half]
+        v_ref[...] = prepared(0.5 * u_ref[...].astype(F32), h_ref[...])
     low = lax.broadcasted_iota(jnp.int32, (8, LANES), 1) < BLK
     high_rows = chunk // BLK
 
@@ -140,7 +134,8 @@
             at = pl.ds(pl.multiple_of(n * chunk + start, piece), piece)
             results = []
             for x, (m, t) in enumerate(blocks):
-                normed = normed_of(m[:, at], t[:, at], gain)
+                centred, scale = centred_of(m[:, at], t[:, at])
+                normed = centred * repeated(scale.astype(BF16), 2 * half // 16)
                 y = jnp.dot(weight, normed, preferred_element_type=F32)
                 results.append(y)
                 if gated:
@@ -162,8 +157,6 @@
                     sl[odd, :] = jnp.where(low, l0r, l1)
                     sp[even, :] = jnp.where(low, r0, r1r)
                     sp[odd, :] = jnp.where(low, r0r, r1)
-                    sq[even, :] = jnp.where(low, r1, r0r)
-                    sq[odd, :] = jnp.where(low, r1r, r0)
 
         to = pl.ds(pl.multiple_of(n * high_rows + offset // BLK, 16), high_rows)
 
@@ -171,31 +164,35 @@
         def _(c):
             take = pl.ds(c, high_rows, stride=half)
             l_ref[pair_of, c, to, :] = sl[take, :].astype(BF16)
-            p_ref[2 * pair_of, c, to, :] = sp[take, :].astype(BF16)
-            p_ref[2 * pair_of + 1, c, to, :] = sq[take, :].astype(BF16)
-
-
-def project(blocks, weights, gain, chunk, piece, gated, held=None, offset=0):
-    half, cells = blocks[0].shape[-2:]
-    operands = [*blocks, weights[0], weights[1], gain]
+            right = sp[take, :].astype(BF16)
+            p_ref[2 * pair_of, c, to, :] = right
+            p_ref[2 * pair_of + 1, c, to, :] = pltpu.roll(right, BLK, 1)
+
+
+def project(operands, half, cells, chunk, piece, gated, offset=0):
     out_shape = [
         pltpu.VMEM((2, half, BLK, LANES), BF16),
         pltpu.VMEM((4, half, BLK, LANES), BF16),
     ]
     aliases = {}
     if gated:
-        operands.append(weights[2])
-        out_shape.append(pltpu.VMEM((2, half, cells), BF16))
+        out_shape += [
+            pltpu.VMEM((2, half, cells), BF16),
+            pltpu.VMEM((4 * half, 2 * half), BF16),
+            pltpu.VMEM((half, 2 * half), BF16),
+        ]
     else:
-        aliases = {len(operands): 0, len(operands) + 1: 1}
-        operands += [pltpu.with_memory_space_constraint(value, pltpu.VMEM) for value in held]
+        aliases = {len(operands) - 2: 0, len(operands) - 1: 1}
+        operands = operands[:-2] + [
+            pltpu.with_memory_space_constraint(value, pltpu.VMEM) for value in operands[-2:]
+        ]
     vmem = pl.BlockSpec(memory_space=pltpu.VMEM)
     return pl.pallas_call(
         functools.partial(project_kernel, piece, chunk, offset, gated),
         in_specs=[vmem] * len(operands),
         out_specs=[vmem] * len(out_shape),
         out_shape=out_shape,
-        scratch_shapes=[pltpu.VMEM((chunk // BLK * half, LANES), F32)] * 3,
+        scratch_shapes=[pltpu.VMEM((chunk // BLK * half, LANES), F32)] * 2,
         input_output_aliases=aliases,
         compiler_params=pltpu.CompilerParams(vmem_limit_bytes=VMEM_LIMIT),
         name="project_own" if gated else "project_fetched",
@@ -244,18 +241,15 @@
                 lhs = jnp.concatenate([l_ref[0, c], l_ref[1, c]], axis=1)
                 parts = [p_ref[pick, c] * mask for pick, mask in picks]
                 rhs = jnp.concatenate([parts[0] + parts[1], parts[2] + parts[3]], axis=1)
-                acc[pl.ds(at, BLK, stride=group), :] = lax.dot_general(
-                    lhs,
-                    jnp.concatenate([rhs, rhs], axis=0),
-                    (((1,), (1,)), ((), ())),
-                    preferred_element_type=F32,
+                acc[pl.ds(at, BLK, stride=group), :BLK] = lax.dot_general(
+                    lhs, rhs, (((1,), (1,)), ((), ())), preferred_element_type=F32
                 )
             rows = pl.ds(pl.multiple_of(base + which * group, group), group)
             for t in range(BLK // 2):
                 even = acc[2 * t * group : (2 * t + 1) * group, :]
                 odd = acc[(2 * t + 1) * group : (2 * t + 2) * group, :]
                 out_ref[rows, t * LANES : (t + 1) * LANES] = jnp.where(
-                    take_low, even, odd
+                    take_low, even, pltpu.roll(odd, BLK, 1)
                 ).astype(BF16)
 
 
@@ -277,10 +271,9 @@
     )(a_slots, b_slots, counts, lefts, rights)
 
 
-def finish_kernel(s, piece, mine_ref, theirs_ref, gate_ref, w_ref, g_ref, *refs):
+def finish_kernel(s, piece, mine_ref, theirs_ref, gate_ref, w_ref, *refs):
     out_ref, held, sems = refs[-3:]
-    weight = own_lanes_first(0.5 * w_ref[...].astype(F32)).astype(BF16)
-    gain = gains_of(g_ref)
+    weight = w_ref[...]
     cells = mine_ref.shape[-1]
     steps = sems.shape[0]
     size = cells // steps
@@ -293,9 +286,10 @@
     def _(n):
         for start in range(0, size, piece):
             to = pl.ds(pl.multiple_of(n * size + start, piece), piece)
-            normed = normed_of(mine_ref[:, to], theirs_ref[:, to], gain)
-            projected = jnp.dot(weight, normed, preferred_element_type=F32)
-            held[:, to] = (gate_ref[s, :, to].astype(F32) * projected).astype(BF16)
+            centred, scale = centred_of(mine_ref[:, to], theirs_ref[:, to])
+            projected = jnp.dot(weight, centred, preferred_element_type=F32)
+            scaled = projected * repeated(scale[:8], weight.shape[0] // 8)
+            held[:, to] = (gate_ref[s, :, to].astype(F32) * scaled).astype(BF16)
         copy(n).start()
 
     @pl.loop(0, steps)
@@ -303,11 +297,11 @@
         copy(n).wait()
 
 
-def finish(s, mine, theirs, gate, weight, gain, steps, piece, out=None):
+def finish(s, mine, theirs, gate, weight, steps, piece, out=None):
     half, cells = mine.shape
     vmem = pl.BlockSpec(memory_space=pltpu.VMEM)
-    operands = [mine, theirs, gate, weight, gain]
-    in_specs = [vmem] * 5
+    operands = [mine, theirs, gate, weight]
+    in_specs = [vmem] * 4
     aliases = {}
     if out is not None:
         aliases = {len(operands): 0}
@@ -344,9 +338,14 @@
     down = [(i, (i - 1) % rows) for i in range(rows)]
 
     a_slots, b_slots = a_slots.T, b_slots.T
-    a_weight, b_weight = jnp.swapaxes(a_weight, 1, 2), jnp.swapaxes(b_weight, 1, 2)
-    weights = (a_weight, b_weight, out_gate_weight.T)
-    gain, last_gain = ln_in_gain[:, None], ln_out_gain[:, None]
+    weights = [
+        jnp.swapaxes(a_weight, 1, 2),
+        jnp.swapaxes(b_weight, 1, 2),
+        out_gate_weight.T,
+        out_weight.T,
+        ln_in_gain[None, :],
+        ln_out_gain[None, :],
+    ]
 
     pair_other = lax.ppermute(pair, "chan", swap)
     cuts = ((0, cells // 4 * 3), (cells // 4 * 3, cells // 4))
@@ -355,21 +354,20 @@
         (lax.ppermute(chosen[2 * n], "row", up), lax.ppermute(chosen[2 * n + 1], "row", down))
         for n in range(len(cuts))
     ]
-    lefts, rights, gate = project(
-        [pair, pair_other], weights, gain, 1024, 256, True
+    lefts, rights, gate, weight, last_weight = project(
+        [pair, pair_other, *weights], half, cells, 1024, 256, True
     )
     for (start, size), (from_behind, from_ahead) in zip(cuts, arrived):
         from_behind, from_ahead, lefts = lax.optimization_barrier((from_behind, from_ahead, lefts))
         behind_other = lax.ppermute(from_behind, "chan", swap)
         ahead_other = lax.ppermute(from_ahead, "chan", swap)
         lefts, rights = project(
-            [from_behind, behind_other, from_ahead, ahead_other],
-            weights,
-            gain,
+            [from_behind, behind_other, from_ahead, ahead_other, weight, lefts, rights],
+            half,
+            size,
             1024,
             256,
             False,
-            [lefts, rights],
             start,
         )
     updates = []
@@ -380,7 +378,7 @@
             update, lefts = lax.optimization_barrier((update, lefts))
     out = None
     for s, (mine, theirs) in enumerate(updates):
-        out = finish(s, mine, theirs, gate, out_weight.T, last_gain, 4, 256, out)
+        out = finish(s, mine, theirs, gate, last_weight, 4, 256, out)
     return out
 
 

time: 49.8 us -> 55.2 us (1.11)
  Pallas kernels: 26.1 us -> 37.1 us
  waiting for transfers between devices: 7.68 us -> 1.33 us
    pallas_call x3, Pallas kernels: 13.9 us -> 23.1 us  [project(): pl.pallas_call(functools.partial(project_kernel, piece, chunk, offset, ga...]
    ppermute x2, waiting for transfers between devices: 6.64 us -> 0.29 us  [per_device(): lax.ppermute(chosen[2 * n + 1], 'row', down)]
    pallas_call x2, Pallas kernels: 4.28 us -> 7.47 us  [finish(): pl.pallas_call(functools.partial(finish_kernel, s, piece), in_specs=in_sp...]
    unnamed x20, local copies, waits for them, and re-layouts: 4.12 us -> 5.5 us
    broadcast_in_dim x2 -> x0, local copies, waits for them, and re-layouts: 0.87 us -> none  [per_device(): gain, last_gain = (ln_in_gain[:, None], ln_out_gain[:, None])]
    pallas_call x1, Pallas kernels: 2.82 us -> 2.01 us  [select_blocks(): pl.pallas_call(functools.partial(select_kernel, slots, a_slots.shape[0],...]
    pallas_call x2, Pallas kernels: 5.03 us -> 4.42 us  [triplet_sum(): pl.pallas_call(functools.partial(triplet_kernel, s, slots, a_slots.shape[...]
  transfers between devices with their start and end apart: 11 -> 11, of which waited for: 4 -> 3; matrix products, arithmetic and copies ran while one was open for 2% -> 0% of each run, Pallas kernels for 40% -> 52%
where the time goes in v6:
time: 55.2 us; the launch traced here: 54.7 us
  Pallas kernels  37.1 us (67%)
  starting transfers between devices  10.7 us (19%)
  local copies, waits for them, and re-layouts  5.5 us (10%)
  waiting for transfers between devices  1.33 us (2%)
    pallas_call x3, Pallas kernels, project(): pl.pallas_call(functools.partial(project_kernel, piece, chunk, offset, ga...  23.1 us
    pallas_call x2, Pallas kernels, finish(): pl.pallas_call(functools.partial(finish_kernel, s, piece), in_specs=in_sp...  7.47 us
    unnamed x20, local copies, waits for them, and re-layouts  5.5 us
    ppermute x2, starting transfers between devices, per_device(): lax.ppermute(chosen[2 * n + 1], 'row', down)  4.79 us
    pallas_call x2, Pallas kernels, triplet_sum(): pl.pallas_call(functools.partial(triplet_kernel, s, slots, a_slots.shape[...  4.42 us
    ppermute x2, starting transfers between devices, per_device(): lax.ppermute(chosen[2 * n], 'row', up)  3.76 us
    pallas_call x1, Pallas kernels, select_blocks(): pl.pallas_call(functools.partial(select_kernel, slots, a_slots.shape[0],...  2.01 us
  transfers between devices with their start and end apart: 11, of which 3 were waited for; matrix products, arithmetic and copies ran while one was open for 0% of the time, Pallas kernels for 52%

profile of v6, /device:TPU:0, one launch (start us, length us, event | category | flops | bytes accessed | tf_op | source)
XLA Modules:
  0.0 54.7 jit_solution(15207805862346667453)
XLA Ops:
  0.0 0.5 collective-permute-start.4
  0.5 2.0 %select_blocks.1 = (bf16[64,3072]{1,0:T(8,128)(2,1)S(1)}, bf16[64,3072]{1,0:T(8,128)(2,1)S(1)}, bf16[64,1024]{1,0:T(8,128)(2,1)S(1)}, bf16[64,1024]{1,0:T(8,128)(2,1)S(1)}) custom-call(s32[4,16]{1,0:T(4,128)} %bitcast.10, s32[4,16]{1,0:T(4,128)} %bitcast.13, s32[16]{0:T(128)} %n_ref.5, bf16[2,64,4096]{2,1,0:T(8,128)(2,1)} %refs_0_.1), custom_call_target="tpu_custom_call" | custom-call | tf_op jit(solution)/shard_map/select_blocks/pallas_call | solution.py:69
  2.5 2.6 %collective-permute-start.2 = (bf16[64,3072]{1,0:T(8,128)(2,1)S(1)}, bf16[64,3072]{1,0:T(8,128)(2,1)S(1)}, u32[]{:S(2)}, u32[]{:S(2)}) collective-permute-start(bf16[64,3072]{1,0:T(8,128)(2,1)S(1)} %get-tuple-element.27), channel_id=1, source_target_pairs={{0,4},{4,8},{8,12},{12,0},{1,5},{5,9},{9,13},{13,1},{2,6},{6,10},{... | collective-permute-start | bytes 1179656 | tf_op jit(solution)/shard_map/ppermute | solution.py:354
  5.1 2.1 %collective-permute-start.3 = (bf16[64,3072]{1,0:T(8,128)(2,1)S(1)}, bf16[64,3072]{1,0:T(8,128)(2,1)S(1)}, u32[]{:S(2)}, u32[]{:S(2)}) collective-permute-start(bf16[64,3072]{1,0:T(8,128)(2,1)S(1)} %get-tuple-element.28), channel_id=1, source_target_pairs={{0,12},{4,0},{8,4},{12,8},{1,13},{5,1},{9,5},{13,9},{2,14},{6,2},{... | collective-permute-start | bytes 1179656 | tf_op jit(solution)/shard_map/ppermute | solution.py:354
  7.2 0.0 collective-permute-done.4.refs_1_
  7.2 0.0 copy-start
  7.2 1.2 %copy-done = bf16[2,64,4096]{2,1,0:T(8,128)(2,1)S(1)} copy-done((bf16[2,64,4096]{2,1,0:T(8,128)(2,1)S(1)}, bf16[2,64,4096]{2,1,0:T(8,128)(2,1)}, u32[]{:S(2)}) %copy-start) | copy-done | bytes 1048600
  8.4 0.0 copy-start.1
  8.4 0.8 %copy-done.1 = bf16[2,128,64]{1,2,0:T(8,128)(2,1)S(1)} copy-done((bf16[2,128,64]{1,2,0:T(8,128)(2,1)S(1)}, bf16[2,128,64]{1,2,0:T(8,128)(2,1)}, u32[]{:S(2)}) %copy-start.1) | copy-done | bytes 32792
  9.2 0.0 copy-start.2
  9.2 0.8 %copy-done.2 = bf16[2,128,64]{1,2,0:T(8,128)(2,1)S(1)} copy-done((bf16[2,128,64]{1,2,0:T(8,128)(2,1)S(1)}, bf16[2,128,64]{1,2,0:T(8,128)(2,1)}, u32[]{:S(2)}) %copy-start.2) | copy-done | bytes 32792
  9.9 0.0 copy-start.5
  9.9 0.7 %copy-done.5 = bf16[128,64]{0,1:T(8,128)(2,1)S(1)} copy-done((bf16[128,64]{0,1:T(8,128)(2,1)S(1)}, bf16[128,64]{0,1:T(8,128)(2,1)}, u32[]{:S(2)}) %copy-start.5) | copy-done | bytes 16408
  10.7 0.0 copy-start.6
  10.7 0.7 %copy-done.6 = bf16[128,64]{0,1:T(8,128)(2,1)S(1)} copy-done((bf16[128,64]{0,1:T(8,128)(2,1)S(1)}, bf16[128,64]{0,1:T(8,128)(2,1)}, u32[]{:S(2)}) %copy-start.6) | copy-done | bytes 16408
  11.4 0.0 copy-start.8
  11.4 0.7 %copy-done.8 = f32[128]{0:T(128)S(1)} copy-done((f32[128]{0:T(128)S(1)}, f32[128]{0:T(128)}, u32[]{:S(2)}) %copy-start.8) | copy-done | bytes 536
  12.0 0.7 %copy-done.9 = f32[128]{0:T(128)S(1)} copy-done((f32[128]{0:T(128)S(1)}, f32[128]{0:T(128)}, u32[]{:S(2)}) %copy-start.9) | copy-done | bytes 536
  12.7 11.8 %project_own.1 = (bf16[2,64,64,128]{3,2,1,0:T(8,128)(2,1)S(1)}, bf16[4,64,64,128]{3,2,1,0:T(8,128)(2,1)S(1)}, bf16[2,64,4096]{2,1,0:T(8,128)(2,1)S(1)}, bf16[256,128]{1,0:T(8,128)(2,1)S(1)}, bf16[64,128]{1,0:T(8,128)(2,1)S(1)}) custom-call(bf16[2,64,4096]{2,1,0:T(8,128)(2,1)S(1)} %copy-done, bf16[2,64,4096]{2,1,0:T(8,128)(2,1)S(1)} %collective-permute-done.4.refs_1_, ...), custom_call_target="tpu_custom_call" | custom-call | tf_op jit(solution)/shard_map/project_own/pallas_call | solution.py:190
  24.5 0.0 collective-permute-done.2.refs_0_
  24.5 0.3 collective-permute-done.3.refs_2_
  24.8 0.0 collective-permute-start.5
  24.8 0.5 collective-permute-start.6
  25.3 1.1 %collective-permute-start = (bf16[64,1024]{1,0:T(8,128)(2,1)S(1)}, bf16[64,1024]{1,0:T(8,128)(2,1)S(1)}, u32[]{:S(2)}, u32[]{:S(2)}) collective-permute-start(bf16[64,1024]{1,0:T(8,128)(2,1)S(1)} %get-tuple-element.25), channel_id=1, source_target_pairs={{0,4},{4,8},{8,12},{12,0},{1,5},{5,9},{9,13},{13,1},{2,6},{6,10},{... | collective-permute-start | bytes 393224 | tf_op jit(solution)/shard_map/ppermute | solution.py:354
  26.4 2.7 %collective-permute-start.1 = (bf16[64,1024]{1,0:T(8,128)(2,1)S(1)}, bf16[64,1024]{1,0:T(8,128)(2,1)S(1)}, u32[]{:S(2)}, u32[]{:S(2)}) collective-permute-start(bf16[64,1024]{1,0:T(8,128)(2,1)S(1)} %get-tuple-element.26), channel_id=1, source_target_pairs={{0,12},{4,0},{8,4},{12,8},{1,13},{5,1},{9,5},{13,9},{2,14},{6,2},{... | collective-permute-start | bytes 393224 | tf_op jit(solution)/shard_map/ppermute | solution.py:354
  29.1 0.0 collective-permute-done.5.refs_1_
  29.1 0.0 collective-permute-done.6.refs_3_
  29.1 8.5 %project_fetched.2 = (bf16[2,64,64,128]{3,2,1,0:T(8,128)(2,1)S(1)}, bf16[4,64,64,128]{3,2,1,0:T(8,128)(2,1)S(1)}) custom-call(bf16[64,3072]{1,0:T(8,128)(2,1)S(1)} %collective-permute-done.2.refs_0_, bf16[64,3072]{1,0:T(8,128)(2,1)S(1)} %collective-permute-done.5.refs_1_, ...), custom_call_target="tpu_custom_call", output_to_operand_aliasing={{0}: (5, {}), {1}: (6, {})} | custom-call | tf_op jit(solution)/shard_map/project_fetched/pallas_call | solution.py:190
  37.7 0.0 copy-start.4
  37.7 0.0 copy-start.7
  37.7 0.0 collective-permute-done.refs_0_
  37.7 0.0 collective-permute-done.1.refs_2_
  37.7 0.1 collective-permute-start.7
  37.8 0.5 collective-permute-start.8
  38.3 0.8 %collective-permute-done.7.refs_1_ = bf16[64,1024]{1,0:T(8,128)(2,1)S(1)} collective-permute-done((bf16[64,1024]{1,0:T(8,128)(2,1)S(1)}, bf16[64,1024]{1,0:T(8,128)(2,1)S(1)}, u32[]{:S(2)}, u32[]{:S(2)}) %collective-permute-start.7) | collective-permute-done | bytes 131104 | tf_op jit(solution)/shard_map/ppermute | solution.py:362
  39.1 0.2 collective-permute-done.8.refs_3_
  39.3 2.8 %project_fetched.3 = (bf16[2,64,64,128]{3,2,1,0:T(8,128)(2,1)S(1)}, bf16[4,64,64,128]{3,2,1,0:T(8,128)(2,1)S(1)}) custom-call(bf16[64,1024]{1,0:T(8,128)(2,1)S(1)} %collective-permute-done.refs_0_, bf16[64,1024]{1,0:T(8,128)(2,1)S(1)} %collective-permute-done.7.refs_1_, ...), custom_call_target="tpu_custom_call", output_to_operand_aliasing={{0}: (5, {}), {1}: (6, {})} | custom-call | tf_op jit(solution)/shard_map/project_fetched/pallas_call | solution.py:190
  42.1 0.0 copy-done.3
  42.1 0.0 copy-done.4
  42.1 0.0 copy-done.7
  42.1 2.2 %triplets.2.mine_ref = bf16[64,4096]{1,0:T(8,128)(2,1)S(1)} custom-call(s32[4,16]{1,0:T(4,128)S(1)} %bitcast.11, s32[4,16]{1,0:T(4,128)S(1)} %bitcast.14, s32[16]{0:T(128)S(1)} %copy-done.7, bf16[2,64,64,128]{3,2,1,0:T(8,128)(2,1)S(1)} %get-tuple-element.42.l_ref, bf16[4,64,64,128]{3,2,1,0:T(8,128)(2,1)S(1)} %get-tuple-element.41.p_ref), custom_call_target="tpu_custom_call" | custom-call | tf_op jit(solution)/shard_map/triplets/pallas_call | solution.py:263
  44.4 0.4 collective-permute-start.10
  44.8 2.2 %triplets.3.mine_ref = bf16[64,4096]{1,0:T(8,128)(2,1)S(1)} custom-call(s32[4,16]{1,0:T(4,128)S(1)} %bitcast.12, s32[4,16]{1,0:T(4,128)S(1)} %bitcast.15, s32[16]{0:T(128)S(1)} %copy-done.7, bf16[2,64,64,128]{3,2,1,0:T(8,128)(2,1)S(1)} %get-tuple-element.42.l_ref, bf16[4,64,64,128]{3,2,1,0:T(8,128)(2,1)S(1)} %get-tuple-element.41.p_ref), custom_call_target="tpu_custom_call" | custom-call | tf_op jit(solution)/shard_map/triplets/pallas_call | solution.py:263
  47.0 0.3 collective-permute-start.9
  47.2 0.0 collective-permute-done.10.theirs_ref
  47.2 3.7 %finish.2.refs_0_ = bf16[2,64,4096]{2,1,0:T(8,128)(2,1)} custom-call(bf16[64,4096]{1,0:T(8,128)(2,1)S(1)} %triplets.2.mine_ref, bf16[64,4096]{1,0:T(8,128)(2,1)S(1)} %collective-permute-done.10.theirs_ref, bf16[2,64,4096]{2,1,0:T(8,128)(2,1)S(1)} %get-tuple-element.43.gate_ref, bf16[64,128]{1,0:T(8,128)(2,1)S(1)} %get-tuple-element.44.w_ref), custom_call_target="tpu_custom_call" | custom-call | tf_op jit(solution)/shard_map/finish/pallas_call | solution.py:310
  51.0 0.0 collective-permute-done.9.theirs_ref
  51.0 3.7 %finish.3 = bf16[2,64,4096]{2,1,0:T(8,128)(2,1)} custom-call(bf16[64,4096]{1,0:T(8,128)(2,1)S(1)} %triplets.3.mine_ref, bf16[64,4096]{1,0:T(8,128)(2,1)S(1)} %collective-permute-done.9.theirs_ref, bf16[2,64,4096]{2,1,0:T(8,128)(2,1)S(1)} %get-tuple-element.43.gate_ref, bf16[64,128]{1,0:T(8,128)(2,1)S(1)} %get-tuple-element.44.w_ref, ...), custom_call_target="tpu_custom_call", output_to_operand_aliasing={{}: (4, {})} | custom-call | tf_op jit(solution)/shard_map/finish/pallas_call | solution.py:310
  (2 shorter events, 0.0 us)
Async XLA Ops:
  0.0 7.2 %collective-permute-start.4 = (bf16[2,64,4096]{2,1,0:T(8,128)(2,1)}, bf16[2,64,4096]{2,1,0:T(8,128)(2,1)S(1)}, u32[]{:S(2)}, u32[]{:S(2)}) collective-permute-start(bf16[2,64,4096]{2,1,0:T(8,128)(2,1)} %refs_0_.1), channel_id=1, source_target_pairs={{0,1},{1,0},{2,3},{3,2},{4,5},{5,4},{6,7},{7,6},{8,9},{9,8},{10,11... | collective-permute-start | bytes 3145736 | tf_op jit(solution)/shard_map/ppermute | solution.py:350
  2.5 22.0 %collective-permute-start.2 = (bf16[64,3072]{1,0:T(8,128)(2,1)S(1)}, bf16[64,3072]{1,0:T(8,128)(2,1)S(1)}, u32[]{:S(2)}, u32[]{:S(2)}) collective-permute-start(bf16[64,3072]{1,0:T(8,128)(2,1)S(1)} %get-tuple-element.27), channel_id=1, source_target_pairs={{0,4},{4,8},{8,12},{12,0},{1,5},{5,9},{9,13},{13,1},{2,6},{6,10},{... | collective-permute-start | bytes 1179656 | tf_op jit(solution)/shard_map/ppermute | solution.py:354
  5.1 19.7 %collective-permute-start.3 = (bf16[64,3072]{1,0:T(8,128)(2,1)S(1)}, bf16[64,3072]{1,0:T(8,128)(2,1)S(1)}, u32[]{:S(2)}, u32[]{:S(2)}) collective-permute-start(bf16[64,3072]{1,0:T(8,128)(2,1)S(1)} %get-tuple-element.28), channel_id=1, source_target_pairs={{0,12},{4,0},{8,4},{12,8},{1,13},{5,1},{9,5},{13,9},{2,14},{6,2},{... | collective-permute-start | bytes 1179656 | tf_op jit(solution)/shard_map/ppermute | solution.py:354
  7.2 1.2 %copy-start = (bf16[2,64,4096]{2,1,0:T(8,128)(2,1)S(1)}, bf16[2,64,4096]{2,1,0:T(8,128)(2,1)}, u32[]{:S(2)}) copy-start(bf16[2,64,4096]{2,1,0:T(8,128)(2,1)} %refs_0_.1) | copy-start | bytes 3145732
  8.4 0.8 %copy-start.1 = (bf16[2,128,64]{1,2,0:T(8,128)(2,1)S(1)}, bf16[2,128,64]{1,2,0:T(8,128)(2,1)}, u32[]{:S(2)}) copy-start(bf16[2,128,64]{1,2,0:T(8,128)(2,1)} %param.12) | copy-start | bytes 98308
  9.2 0.8 %copy-start.2 = (bf16[2,128,64]{1,2,0:T(8,128)(2,1)S(1)}, bf16[2,128,64]{1,2,0:T(8,128)(2,1)}, u32[]{:S(2)}) copy-start(bf16[2,128,64]{1,2,0:T(8,128)(2,1)} %param.13) | copy-start | bytes 98308
  9.9 0.7 %copy-start.5 = (bf16[128,64]{0,1:T(8,128)(2,1)S(1)}, bf16[128,64]{0,1:T(8,128)(2,1)}, u32[]{:S(2)}) copy-start(bf16[128,64]{0,1:T(8,128)(2,1)} %param.15) | copy-start | bytes 49156
  10.7 0.7 %copy-start.6 = (bf16[128,64]{0,1:T(8,128)(2,1)S(1)}, bf16[128,64]{0,1:T(8,128)(2,1)}, u32[]{:S(2)}) copy-start(bf16[128,64]{0,1:T(8,128)(2,1)} %param.16) | copy-start | bytes 49156
  11.4 0.7 %copy-start.8 = (f32[128]{0:T(128)S(1)}, f32[128]{0:T(128)}, u32[]{:S(2)}) copy-start(f32[128]{0:T(128)} %param.11) | copy-start | bytes 1540
  12.0 0.7 %copy-start.9 = (f32[128]{0:T(128)S(1)}, f32[128]{0:T(128)}, u32[]{:S(2)}) copy-start(f32[128]{0:T(128)} %param.14) | copy-start | bytes 1540
  24.8 4.3 %collective-permute-start.5 = (bf16[64,3072]{1,0:T(8,128)(2,1)S(1)}, bf16[64,3072]{1,0:T(8,128)(2,1)S(1)}, u32[]{:S(2)}, u32[]{:S(2)}) collective-permute-start(bf16[64,3072]{1,0:T(8,128)(2,1)S(1)} %collective-permute-done.2.refs_0_), channel_id=1, source_target_pairs={{0,1},{1,0},{2,3},{3,2},{4,5},{5,4},{6,7},{7,6},{8,9},{9,8},{10,11... | collective-permute-start | bytes 1179656 | tf_op jit(solution)/shard_map/ppermute | solution.py:362
  24.8 4.3 %collective-permute-start.6 = (bf16[64,3072]{1,0:T(8,128)(2,1)S(1)}, bf16[64,3072]{1,0:T(8,128)(2,1)S(1)}, u32[]{:S(2)}, u32[]{:S(2)}) collective-permute-start(bf16[64,3072]{1,0:T(8,128)(2,1)S(1)} %collective-permute-done.3.refs_2_), channel_id=1, source_target_pairs={{0,1},{1,0},{2,3},{3,2},{4,5},{5,4},{6,7},{7,6},{8,9},{9,8},{10,11... | collective-permute-start | bytes 1179656 | tf_op jit(solution)/shard_map/ppermute | solution.py:363
  25.3 12.4 %collective-permute-start = (bf16[64,1024]{1,0:T(8,128)(2,1)S(1)}, bf16[64,1024]{1,0:T(8,128)(2,1)S(1)}, u32[]{:S(2)}, u32[]{:S(2)}) collective-permute-start(bf16[64,1024]{1,0:T(8,128)(2,1)S(1)} %get-tuple-element.25), channel_id=1, source_target_pairs={{0,4},{4,8},{8,12},{12,0},{1,5},{5,9},{9,13},{13,1},{2,6},{6,10},{... | collective-permute-start | bytes 393224 | tf_op jit(solution)/shard_map/ppermute | solution.py:354
  26.4 11.3 %collective-permute-start.1 = (bf16[64,1024]{1,0:T(8,128)(2,1)S(1)}, bf16[64,1024]{1,0:T(8,128)(2,1)S(1)}, u32[]{:S(2)}, u32[]{:S(2)}) collective-permute-start(bf16[64,1024]{1,0:T(8,128)(2,1)S(1)} %get-tuple-element.26), channel_id=1, source_target_pairs={{0,12},{4,0},{8,4},{12,8},{1,13},{5,1},{9,5},{13,9},{2,14},{6,2},{... | collective-permute-start | bytes 393224 | tf_op jit(solution)/shard_map/ppermute | solution.py:354
  37.6 4.5 %copy-start.3 = (s32[16,4]{0,1:T(4,128)S(1)}, s32[16,4]{0,1:T(4,128)}, u32[]{:S(2)}) copy-start(s32[16,4]{0,1:T(4,128)} %param.17) | copy-start | bytes 772
  37.7 4.5 %copy-start.4 = (s32[16,4]{0,1:T(4,128)S(1)}, s32[16,4]{0,1:T(4,128)}, u32[]{:S(2)}) copy-start(s32[16,4]{0,1:T(4,128)} %param.18) | copy-start | bytes 772
  37.7 4.5 %copy-start.7 = (s32[16]{0:T(128)S(1)}, s32[16]{0:T(128)}, u32[]{:S(2)}) copy-start(s32[16]{0:T(128)} %n_ref.5) | copy-start | bytes 196
  37.7 1.4 %collective-permute-start.7 = (bf16[64,1024]{1,0:T(8,128)(2,1)S(1)}, bf16[64,1024]{1,0:T(8,128)(2,1)S(1)}, u32[]{:S(2)}, u32[]{:S(2)}) collective-permute-start(bf16[64,1024]{1,0:T(8,128)(2,1)S(1)} %collective-permute-done.refs_0_), channel_id=1, source_target_pairs={{0,1},{1,0},{2,3},{3,2},{4,5},{5,4},{6,7},{7,6},{8,9},{9,8},{10,11... | collective-permute-start | bytes 393224 | tf_op jit(solution)/shard_map/ppermute | solution.py:362
  37.8 1.5 %collective-permute-start.8 = (bf16[64,1024]{1,0:T(8,128)(2,1)S(1)}, bf16[64,1024]{1,0:T(8,128)(2,1)S(1)}, u32[]{:S(2)}, u32[]{:S(2)}) collective-permute-start(bf16[64,1024]{1,0:T(8,128)(2,1)S(1)} %collective-permute-done.1.refs_2_), channel_id=1, source_target_pairs={{0,1},{1,0},{2,3},{3,2},{4,5},{5,4},{6,7},{7,6},{8,9},{9,8},{10,11... | collective-permute-start | bytes 393224 | tf_op jit(solution)/shard_map/ppermute | solution.py:363
  44.4 2.9 %collective-permute-start.10 = (bf16[64,4096]{1,0:T(8,128)(2,1)S(1)}, bf16[64,4096]{1,0:T(8,128)(2,1)S(1)}, u32[]{:S(2)}, u32[]{:S(2)}) collective-permute-start(bf16[64,4096]{1,0:T(8,128)(2,1)S(1)} %triplets.2.mine_ref), channel_id=1, source_target_pairs={{0,1},{1,0},{2,3},{3,2},{4,5},{5,4},{6,7},{7,6},{8,9},{9,8},{10,11... | collective-permute-start | bytes 1572872 | tf_op jit(solution)/shard_map/ppermute | solution.py:376
  47.0 4.0 %collective-permute-start.9 = (bf16[64,4096]{1,0:T(8,128)(2,1)S(1)}, bf16[64,4096]{1,0:T(8,128)(2,1)S(1)}, u32[]{:S(2)}, u32[]{:S(2)}) collective-permute-start(bf16[64,4096]{1,0:T(8,128)(2,1)S(1)} %triplets.3.mine_ref), channel_id=1, source_target_pairs={{0,1},{1,0},{2,3},{3,2},{4,5},{5,4},{6,7},{7,6},{8,9},{9,8},{10,11... | collective-permute-start | bytes 1572872 | tf_op jit(solution)/shard_map/ppermute | solution.py:376

commit v7 on v6

--- a/solution.py
+++ b/solution.py
@@ -78,7 +78,6 @@
 
 def prepared(weight, gain):
     weight = weight * gain
-    weight = weight - jnp.mean(weight, axis=1, keepdims=True)
     rolled = pltpu.roll(weight, weight.shape[1] // 2, 1)
     return jnp.where(lax.axis_index("chan") == 0, weight, rolled).astype(BF16)
 
@@ -91,21 +90,16 @@
     return [0.5 * row for row in rows]
 
 
-def repeated(value, times):
-    return jnp.concatenate([value] * times, axis=0)
-
-
-def centred_of(mine, theirs):
-    values = jnp.concatenate([mine, theirs], axis=0)
-    channels = values.shape[0]
-    ones = jnp.full((16, channels), 1.0 / channels, BF16)
-    mean = jnp.dot(ones, values, preferred_element_type=F32)
-    rounded = mean.astype(BF16)
-    centred = values - repeated(rounded, channels // 16)
-    square = jnp.dot(ones, centred * centred, preferred_element_type=F32)
-    left = mean - rounded.astype(F32)
-    spread = jnp.maximum(square - left * left, 0.0)
-    return centred, lax.rsqrt(spread + epsilon)
+def normed_of(mine, theirs):
+    total = 2 * mine.shape[0]
+    mine = mine.astype(F32)
+    theirs = theirs.astype(F32)
+    mean = jnp.sum(mine + theirs, axis=0, keepdims=True) * (1.0 / total)
+    mine = mine - mean
+    theirs = theirs - mean
+    spread = jnp.sum(mine * mine + theirs * theirs, axis=0, keepdims=True) * (1.0 / total)
+    scale = lax.rsqrt(spread + epsilon)
+    return jnp.concatenate([(mine * scale).astype(BF16), (theirs * scale).astype(BF16)], axis=0)
 
 
 def project_kernel(piece, chunk, offset, gated, *refs):
@@ -125,6 +119,11 @@
     if gated:
         w_ref[...] = weight[: 4 * half]
         v_ref[...] = prepared(0.5 * u_ref[...].astype(F32), h_ref[...])
+
+        @pl.loop(0, half)
+        def _(c):
+            p_ref[4, c] = jnp.zeros((BLK, LANES), BF16)
+
     low = lax.broadcasted_iota(jnp.int32, (8, LANES), 1) < BLK
     high_rows = chunk // BLK
 
@@ -132,31 +131,26 @@
     def _(n):
         for start in range(0, chunk, piece):
             at = pl.ds(pl.multiple_of(n * chunk + start, piece), piece)
-            results = []
+            sides = []
             for x, (m, t) in enumerate(blocks):
-                centred, scale = centred_of(m[:, at], t[:, at])
-                normed = centred * repeated(scale.astype(BF16), 2 * half // 16)
-                y = jnp.dot(weight, normed, preferred_element_type=F32)
-                results.append(y)
+                y = jnp.dot(weight, normed_of(m[:, at], t[:, at]), preferred_element_type=F32)
                 if gated:
                     gate_ref[x, :, at] = (jnp.tanh(y[4 * half :]) + 1.0).astype(BF16)
+                for side in range(2):
+                    groups = []
+                    for row in range(2 * half * side, 2 * half * (side + 1), 16):
+                        groups.append((jnp.tanh(y[row : row + 8]) + 1.0) * y[row + 8 : row + 16])
+                    sides.append(groups)
             for row in range(0, half, 8):
-                sides = []
-                for side in range(2):
-                    for y in results:
-                        gate = y[2 * half * side + 2 * row : 2 * half * side + 2 * row + 8]
-                        value = y[2 * half * side + 2 * row + 8 : 2 * half * side + 2 * row + 16]
-                        sides.append((jnp.tanh(gate) + 1.0) * value)
+                l0, r0, l1, r1 = (groups[row // 8] for groups in sides)
                 for sub in range(0, piece, LANES):
                     i = (start + sub) // BLK
                     even = slice(i * half + row, i * half + row + 8)
                     odd = slice((i + 1) * half + row, (i + 1) * half + row + 8)
-                    l0, l1, r0, r1 = (v[:, sub : sub + LANES] for v in sides)
-                    l0r, l1r, r0r, r1r = (pltpu.roll(v, BLK, 1) for v in (l0, l1, r0, r1))
-                    sl[even, :] = jnp.where(low, l0, l1r)
-                    sl[odd, :] = jnp.where(low, l0r, l1)
-                    sp[even, :] = jnp.where(low, r0, r1r)
-                    sp[odd, :] = jnp.where(low, r0r, r1)
+                    cut = slice(sub, sub + LANES)
+                    for held, v0, v1 in ((sl, l0[:, cut], l1[:, cut]), (sp, r0[:, cut], r1[:, cut])):
+                        held[even, :] = jnp.where(low, v0, pltpu.roll(v1, BLK, 1))
+                        held[odd, :] = jnp.where(low, pltpu.roll(v0, BLK, 1), v1)
 
         to = pl.ds(pl.multiple_of(n * high_rows + offset // BLK, 16), high_rows)
 
@@ -172,7 +166,7 @@
 def project(operands, half, cells, chunk, piece, gated, offset=0):
     out_shape = [
         pltpu.VMEM((2, half, BLK, LANES), BF16),
-        pltpu.VMEM((4, half, BLK, LANES), BF16),
+        pltpu.VMEM((5, half, BLK, LANES), BF16),
     ]
     aliases = {}
     if gated:
@@ -201,9 +195,7 @@
 
 def triplet_kernel(s, slots, triplets, group, a_ref, b_ref, n_ref, l_ref, p_ref, out_ref, *accs):
     me, behind, ahead = neighbour_tiles()
-    lane = lax.broadcasted_iota(jnp.int32, (1, LANES), 1)
-    low = (lane < BLK).astype(F32)
-    high = 1.0 - low
+    low = lax.broadcasted_iota(jnp.int32, (BLK, LANES), 1) < BLK
     block = me * slots + s
     count = n_ref[block]
     picks = []
@@ -228,7 +220,7 @@
                 used = jnp.where(hit, 1, used)
             if part == 1:
                 chosen = chosen + 1 - 2 * (chosen & 1)
-            picks.append((chosen, ((low, high)[part] * used.astype(F32)).astype(BF16)))
+            picks.append(jnp.where(used == 1, chosen, 4))
 
     take_low = lax.broadcasted_iota(jnp.int32, (group, LANES), 1) < BLK
     half = l_ref.shape[1]
@@ -239,8 +231,10 @@
             for at in range(group):
                 c = base + which * group + at
                 lhs = jnp.concatenate([l_ref[0, c], l_ref[1, c]], axis=1)
-                parts = [p_ref[pick, c] * mask for pick, mask in picks]
-                rhs = jnp.concatenate([parts[0] + parts[1], parts[2] + parts[3]], axis=1)
+                parts = [p_ref[pick, c] for pick in picks]
+                rhs = jnp.concatenate(
+                    [jnp.where(low, parts[0], parts[1]), jnp.where(low, parts[2], parts[3])], axis=1
+                )
                 acc[pl.ds(at, BLK, stride=group), :BLK] = lax.dot_general(
                     lhs, rhs, (((1,), (1,)), ((), ())), preferred_element_type=F32
                 )
@@ -286,10 +280,9 @@
     def _(n):
         for start in range(0, size, piece):
             to = pl.ds(pl.multiple_of(n * size + start, piece), piece)
-            centred, scale = centred_of(mine_ref[:, to], theirs_ref[:, to])
-            projected = jnp.dot(weight, centred, preferred_element_type=F32)
-            scaled = projected * repeated(scale[:8], weight.shape[0] // 8)
-            held[:, to] = (gate_ref[s, :, to].astype(F32) * scaled).astype(BF16)
+            normed = normed_of(mine_ref[:, to], theirs_ref[:, to])
+            projected = jnp.dot(weight, normed, preferred_element_type=F32)
+            held[:, to] = (gate_ref[s, :, to].astype(F32) * projected).astype(BF16)
         copy(n).start()
 
     @pl.loop(0, steps)
@@ -355,7 +348,7 @@
         for n in range(len(cuts))
     ]
     lefts, rights, gate, weight, last_weight = project(
-        [pair, pair_other, *weights], half, cells, 1024, 256, True
+        [pair, pair_other, *weights], half, cells, 1024, 128, True
     )
     for (start, size), (from_behind, from_ahead) in zip(cuts, arrived):
         from_behind, from_ahead, lefts = lax.optimization_barrier((from_behind, from_ahead, lefts))
@@ -366,7 +359,7 @@
             half,
             size,
             1024,
-            256,
+            128,
             False,
             start,
         )

time: 55.2 us -> 47.6 us (0.86)
  Pallas kernels: 37.1 us -> 25.6 us
  waiting for transfers between devices: 1.33 us -> 5.2 us
    pallas_call x3, Pallas kernels: 23.1 us -> 15.2 us  [project(): pl.pallas_call(functools.partial(project_kernel, piece, chunk, offset, ga...]
    ppermute x2, waiting for transfers between devices: 0.29 us -> 4.16 us  [per_device(): lax.ppermute(chosen[2 * n + 1], 'row', down)]
    pallas_call x2, Pallas kernels: 7.47 us -> 3.93 us  [finish(): pl.pallas_call(functools.partial(finish_kernel, s, piece), in_specs=in_sp...]
  transfers between devices with their start and end apart: 11 -> 11, of which waited for: 3 -> 3; matrix products, arithmetic and copies ran while one was open for 0% -> 0% of each run, Pallas kernels for 52% -> 42%
where the time goes in v7:
time: 47.6 us; the launch traced here: 47.2 us
  Pallas kernels  25.6 us (54%)
  starting transfers between devices  10.7 us (22%)
  local copies, waits for them, and re-layouts  5.5 us (12%)
  waiting for transfers between devices  5.2 us (11%)
    pallas_call x3, Pallas kernels, project(): pl.pallas_call(functools.partial(project_kernel, piece, chunk, offset, ga...  15.2 us
    unnamed x20, local copies, waits for them, and re-layouts  5.5 us
    ppermute x2, starting transfers between devices, per_device(): lax.ppermute(chosen[2 * n + 1], 'row', down)  4.79 us
    pallas_call x2, Pallas kernels, triplet_sum(): pl.pallas_call(functools.partial(triplet_kernel, s, slots, a_slots.shape[...  4.45 us
    ppermute x2, waiting for transfers between devices, per_device(): lax.ppermute(chosen[2 * n + 1], 'row', down)  4.16 us
    pallas_call x2, Pallas kernels, finish(): pl.pallas_call(functools.partial(finish_kernel, s, piece), in_specs=in_sp...  3.93 us
    ppermute x2, starting transfers between devices, per_device(): lax.ppermute(chosen[2 * n], 'row', up)  3.76 us
    pallas_call x1, Pallas kernels, select_blocks(): pl.pallas_call(functools.partial(select_kernel, slots, a_slots.shape[0],...  2.01 us
  transfers between devices with their start and end apart: 11, of which 3 were waited for; matrix products, arithmetic and copies ran while one was open for 0% of the time, Pallas kernels for 42%

profile of v7, /device:TPU:0, one launch (start us, length us, event | category | flops | bytes accessed | tf_op | source)
XLA Modules:
  0.0 47.2 jit_solution(16511334601735206232)
XLA Ops:
  0.0 0.5 collective-permute-start.4
  0.5 2.0 %select_blocks.1 = (bf16[64,3072]{1,0:T(8,128)(2,1)S(1)}, bf16[64,3072]{1,0:T(8,128)(2,1)S(1)}, bf16[64,1024]{1,0:T(8,128)(2,1)S(1)}, bf16[64,1024]{1,0:T(8,128)(2,1)S(1)}) custom-call(s32[4,16]{1,0:T(4,128)} %bitcast.10, s32[4,16]{1,0:T(4,128)} %bitcast.13, s32[16]{0:T(128)} %n_ref.5, bf16[2,64,4096]{2,1,0:T(8,128)(2,1)} %refs_0_.1), custom_call_target="tpu_custom_call" | custom-call | tf_op jit(solution)/shard_map/select_blocks/pallas_call | solution.py:69
  2.5 2.6 %collective-permute-start.2 = (bf16[64,3072]{1,0:T(8,128)(2,1)S(1)}, bf16[64,3072]{1,0:T(8,128)(2,1)S(1)}, u32[]{:S(2)}, u32[]{:S(2)}) collective-permute-start(bf16[64,3072]{1,0:T(8,128)(2,1)S(1)} %get-tuple-element.27), channel_id=1, source_target_pairs={{0,4},{4,8},{8,12},{12,0},{1,5},{5,9},{9,13},{13,1},{2,6},{6,10},{... | collective-permute-start | bytes 1179656 | tf_op jit(solution)/shard_map/ppermute | solution.py:347
  5.1 2.1 %collective-permute-start.3 = (bf16[64,3072]{1,0:T(8,128)(2,1)S(1)}, bf16[64,3072]{1,0:T(8,128)(2,1)S(1)}, u32[]{:S(2)}, u32[]{:S(2)}) collective-permute-start(bf16[64,3072]{1,0:T(8,128)(2,1)S(1)} %get-tuple-element.28), channel_id=1, source_target_pairs={{0,12},{4,0},{8,4},{12,8},{1,13},{5,1},{9,5},{13,9},{2,14},{6,2},{... | collective-permute-start | bytes 1179656 | tf_op jit(solution)/shard_map/ppermute | solution.py:347
  7.2 0.0 collective-permute-done.4.refs_1_
  7.2 1.2 %copy-done = bf16[2,64,4096]{2,1,0:T(8,128)(2,1)S(1)} copy-done((bf16[2,64,4096]{2,1,0:T(8,128)(2,1)S(1)}, bf16[2,64,4096]{2,1,0:T(8,128)(2,1)}, u32[]{:S(2)}) %copy-start) | copy-done | bytes 1048600
  8.4 0.0 copy-start.1
  8.4 0.8 %copy-done.1 = bf16[2,128,64]{1,2,0:T(8,128)(2,1)S(1)} copy-done((bf16[2,128,64]{1,2,0:T(8,128)(2,1)S(1)}, bf16[2,128,64]{1,2,0:T(8,128)(2,1)}, u32[]{:S(2)}) %copy-start.1) | copy-done | bytes 32792
  9.2 0.0 copy-start.2
  9.2 0.8 %copy-done.2 = bf16[2,128,64]{1,2,0:T(8,128)(2,1)S(1)} copy-done((bf16[2,128,64]{1,2,0:T(8,128)(2,1)S(1)}, bf16[2,128,64]{1,2,0:T(8,128)(2,1)}, u32[]{:S(2)}) %copy-start.2) | copy-done | bytes 32792
  9.9 0.0 copy-start.5
  9.9 0.7 %copy-done.5 = bf16[128,64]{0,1:T(8,128)(2,1)S(1)} copy-done((bf16[128,64]{0,1:T(8,128)(2,1)S(1)}, bf16[128,64]{0,1:T(8,128)(2,1)}, u32[]{:S(2)}) %copy-start.5) | copy-done | bytes 16408
  10.7 0.0 copy-start.6
  10.7 0.7 %copy-done.6 = bf16[128,64]{0,1:T(8,128)(2,1)S(1)} copy-done((bf16[128,64]{0,1:T(8,128)(2,1)S(1)}, bf16[128,64]{0,1:T(8,128)(2,1)}, u32[]{:S(2)}) %copy-start.6) | copy-done | bytes 16408
  11.4 0.0 copy-start.8
  11.4 0.7 %copy-done.8 = f32[128]{0:T(128)S(1)} copy-done((f32[128]{0:T(128)S(1)}, f32[128]{0:T(128)}, u32[]{:S(2)}) %copy-start.8) | copy-done | bytes 536
  12.0 0.0 copy-start.9
  12.0 0.7 %copy-done.9 = f32[128]{0:T(128)S(1)} copy-done((f32[128]{0:T(128)S(1)}, f32[128]{0:T(128)}, u32[]{:S(2)}) %copy-start.9) | copy-done | bytes 536
  12.7 7.9 %project_own.1 = (bf16[2,64,64,128]{3,2,1,0:T(8,128)(2,1)S(1)}, bf16[5,64,64,128]{3,2,1,0:T(8,128)(2,1)S(1)}, bf16[2,64,4096]{2,1,0:T(8,128)(2,1)S(1)}, bf16[256,128]{1,0:T(8,128)(2,1)S(1)}, bf16[64,128]{1,0:T(8,128)(2,1)S(1)}) custom-call(bf16[2,64,4096]{2,1,0:T(8,128)(2,1)S(1)} %copy-done, bf16[2,64,4096]{2,1,0:T(8,128)(2,1)S(1)} %collective-permute-done.4.refs_1_, ...), custom_call_target="tpu_custom_call" | custom-call | tf_op jit(solution)/shard_map/project_own/pallas_call | solution.py:184
  20.6 0.0 collective-permute-done.2.refs_0_
  20.6 4.2 %collective-permute-done.3.refs_2_ = bf16[64,3072]{1,0:T(8,128)(2,1)S(1)} collective-permute-done((bf16[64,3072]{1,0:T(8,128)(2,1)S(1)}, bf16[64,3072]{1,0:T(8,128)(2,1)S(1)}, u32[]{:S(2)}, u32[]{:S(2)}) %collective-permute-start.3) | collective-permute-done | bytes 393248 | tf_op jit(solution)/shard_map/ppermute | solution.py:347
  24.8 0.0 collective-permute-start.5
  24.8 0.5 %collective-permute-start.6 = (bf16[64,3072]{1,0:T(8,128)(2,1)S(1)}, bf16[64,3072]{1,0:T(8,128)(2,1)S(1)}, u32[]{:S(2)}, u32[]{:S(2)}) collective-permute-start(bf16[64,3072]{1,0:T(8,128)(2,1)S(1)} %collective-permute-done.3.refs_2_), channel_id=1, source_target_pairs={{0,1},{1,0},{2,3},{3,2},{4,5},{5,4},{6,7},{7,6},{8,9},{9,8},{10,11... | collective-permute-start | bytes 1179656 | tf_op jit(solution)/shard_map/ppermute | solution.py:356
  25.3 1.1 %collective-permute-start = (bf16[64,1024]{1,0:T(8,128)(2,1)S(1)}, bf16[64,1024]{1,0:T(8,128)(2,1)S(1)}, u32[]{:S(2)}, u32[]{:S(2)}) collective-permute-start(bf16[64,1024]{1,0:T(8,128)(2,1)S(1)} %get-tuple-element.25), channel_id=1, source_target_pairs={{0,4},{4,8},{8,12},{12,0},{1,5},{5,9},{9,13},{13,1},{2,6},{6,10},{... | collective-permute-start | bytes 393224 | tf_op jit(solution)/shard_map/ppermute | solution.py:347
  26.4 2.7 %collective-permute-start.1 = (bf16[64,1024]{1,0:T(8,128)(2,1)S(1)}, bf16[64,1024]{1,0:T(8,128)(2,1)S(1)}, u32[]{:S(2)}, u32[]{:S(2)}) collective-permute-start(bf16[64,1024]{1,0:T(8,128)(2,1)S(1)} %get-tuple-element.26), channel_id=1, source_target_pairs={{0,12},{4,0},{8,4},{12,8},{1,13},{5,1},{9,5},{13,9},{2,14},{6,2},{... | collective-permute-start | bytes 393224 | tf_op jit(solution)/shard_map/ppermute | solution.py:347
  29.1 0.0 collective-permute-done.5.refs_1_
  29.1 0.0 collective-permute-done.6.refs_3_
  29.1 5.5 %project_fetched.2 = (bf16[2,64,64,128]{3,2,1,0:T(8,128)(2,1)S(1)}, bf16[5,64,64,128]{3,2,1,0:T(8,128)(2,1)S(1)}) custom-call(bf16[64,3072]{1,0:T(8,128)(2,1)S(1)} %collective-permute-done.2.refs_0_, bf16[64,3072]{1,0:T(8,128)(2,1)S(1)} %collective-permute-done.5.refs_1_, ...), custom_call_target="tpu_custom_call", output_to_operand_aliasing={{0}: (5, {}), {1}: (6, {})} | custom-call | tf_op jit(solution)/shard_map/project_fetched/pallas_call | solution.py:184
  34.6 0.0 copy-start.4
  34.6 0.0 copy-start.7
  34.6 0.0 collective-permute-done.refs_0_
  34.7 0.0 collective-permute-done.1.refs_2_
  34.7 0.1 collective-permute-start.7
  34.7 0.5 %collective-permute-start.8 = (bf16[64,1024]{1,0:T(8,128)(2,1)S(1)}, bf16[64,1024]{1,0:T(8,128)(2,1)S(1)}, u32[]{:S(2)}, u32[]{:S(2)}) collective-permute-start(bf16[64,1024]{1,0:T(8,128)(2,1)S(1)} %collective-permute-done.1.refs_2_), channel_id=1, source_target_pairs={{0,1},{1,0},{2,3},{3,2},{4,5},{5,4},{6,7},{7,6},{8,9},{9,8},{10,11... | collective-permute-start | bytes 393224 | tf_op jit(solution)/shard_map/ppermute | solution.py:356
  35.2 0.8 %collective-permute-done.7.refs_1_ = bf16[64,1024]{1,0:T(8,128)(2,1)S(1)} collective-permute-done((bf16[64,1024]{1,0:T(8,128)(2,1)S(1)}, bf16[64,1024]{1,0:T(8,128)(2,1)S(1)}, u32[]{:S(2)}, u32[]{:S(2)}) %collective-permute-start.7) | collective-permute-done | bytes 131104 | tf_op jit(solution)/shard_map/ppermute | solution.py:355
  36.1 0.2 collective-permute-done.8.refs_3_
  36.3 1.8 %project_fetched.3 = (bf16[2,64,64,128]{3,2,1,0:T(8,128)(2,1)S(1)}, bf16[5,64,64,128]{3,2,1,0:T(8,128)(2,1)S(1)}) custom-call(bf16[64,1024]{1,0:T(8,128)(2,1)S(1)} %collective-permute-done.refs_0_, bf16[64,1024]{1,0:T(8,128)(2,1)S(1)} %collective-permute-done.7.refs_1_, ...), custom_call_target="tpu_custom_call", output_to_operand_aliasing={{0}: (5, {}), {1}: (6, {})} | custom-call | tf_op jit(solution)/shard_map/project_fetched/pallas_call | solution.py:184
  38.1 0.0 copy-done.3
  38.1 0.0 copy-done.4
  38.1 0.0 copy-done.7
  38.1 2.2 %triplets.2.mine_ref = bf16[64,4096]{1,0:T(8,128)(2,1)S(1)} custom-call(s32[4,16]{1,0:T(4,128)S(1)} %bitcast.11, s32[4,16]{1,0:T(4,128)S(1)} %bitcast.14, s32[16]{0:T(128)S(1)} %copy-done.7, bf16[2,64,64,128]{3,2,1,0:T(8,128)(2,1)S(1)} %get-tuple-element.42.l_ref, bf16[5,64,64,128]{3,2,1,0:T(8,128)(2,1)S(1)} %get-tuple-element.41.p_ref), custom_call_target="tpu_custom_call" | custom-call | tf_op jit(solution)/shard_map/triplets/pallas_call | solution.py:257
  40.3 0.4 collective-permute-start.10
  40.7 2.2 %triplets.3.mine_ref = bf16[64,4096]{1,0:T(8,128)(2,1)S(1)} custom-call(s32[4,16]{1,0:T(4,128)S(1)} %bitcast.12, s32[4,16]{1,0:T(4,128)S(1)} %bitcast.15, s32[16]{0:T(128)S(1)} %copy-done.7, bf16[2,64,64,128]{3,2,1,0:T(8,128)(2,1)S(1)} %get-tuple-element.42.l_ref, bf16[5,64,64,128]{3,2,1,0:T(8,128)(2,1)S(1)} %get-tuple-element.41.p_ref), custom_call_target="tpu_custom_call" | custom-call | tf_op jit(solution)/shard_map/triplets/pallas_call | solution.py:257
  42.9 0.3 collective-permute-start.9
  43.2 0.0 collective-permute-done.10.theirs_ref
  43.2 2.0 %finish.2.refs_0_ = bf16[2,64,4096]{2,1,0:T(8,128)(2,1)} custom-call(bf16[64,4096]{1,0:T(8,128)(2,1)S(1)} %triplets.2.mine_ref, bf16[64,4096]{1,0:T(8,128)(2,1)S(1)} %collective-permute-done.10.theirs_ref, bf16[2,64,4096]{2,1,0:T(8,128)(2,1)S(1)} %get-tuple-element.43.gate_ref, bf16[64,128]{1,0:T(8,128)(2,1)S(1)} %get-tuple-element.44.w_ref), custom_call_target="tpu_custom_call" | custom-call | tf_op jit(solution)/shard_map/finish/pallas_call | solution.py:303
  45.2 0.0 collective-permute-done.9.theirs_ref
  45.2 2.0 %finish.3 = bf16[2,64,4096]{2,1,0:T(8,128)(2,1)} custom-call(bf16[64,4096]{1,0:T(8,128)(2,1)S(1)} %triplets.3.mine_ref, bf16[64,4096]{1,0:T(8,128)(2,1)S(1)} %collective-permute-done.9.theirs_ref, bf16[2,64,4096]{2,1,0:T(8,128)(2,1)S(1)} %get-tuple-element.43.gate_ref, bf16[64,128]{1,0:T(8,128)(2,1)S(1)} %get-tuple-element.44.w_ref, ...), custom_call_target="tpu_custom_call", output_to_operand_aliasing={{}: (4, {})} | custom-call | tf_op jit(solution)/shard_map/finish/pallas_call | solution.py:303
  (2 shorter events, 0.0 us)
Async XLA Ops:
  0.0 7.2 %collective-permute-start.4 = (bf16[2,64,4096]{2,1,0:T(8,128)(2,1)}, bf16[2,64,4096]{2,1,0:T(8,128)(2,1)S(1)}, u32[]{:S(2)}, u32[]{:S(2)}) collective-permute-start(bf16[2,64,4096]{2,1,0:T(8,128)(2,1)} %refs_0_.1), channel_id=1, source_target_pairs={{0,1},{1,0},{2,3},{3,2},{4,5},{5,4},{6,7},{7,6},{8,9},{9,8},{10,11... | collective-permute-start | bytes 3145736 | tf_op jit(solution)/shard_map/ppermute | solution.py:343
  2.5 18.1 %collective-permute-start.2 = (bf16[64,3072]{1,0:T(8,128)(2,1)S(1)}, bf16[64,3072]{1,0:T(8,128)(2,1)S(1)}, u32[]{:S(2)}, u32[]{:S(2)}) collective-permute-start(bf16[64,3072]{1,0:T(8,128)(2,1)S(1)} %get-tuple-element.27), channel_id=1, source_target_pairs={{0,4},{4,8},{8,12},{12,0},{1,5},{5,9},{9,13},{13,1},{2,6},{6,10},{... | collective-permute-start | bytes 1179656 | tf_op jit(solution)/shard_map/ppermute | solution.py:347
  5.1 19.7 %collective-permute-start.3 = (bf16[64,3072]{1,0:T(8,128)(2,1)S(1)}, bf16[64,3072]{1,0:T(8,128)(2,1)S(1)}, u32[]{:S(2)}, u32[]{:S(2)}) collective-permute-start(bf16[64,3072]{1,0:T(8,128)(2,1)S(1)} %get-tuple-element.28), channel_id=1, source_target_pairs={{0,12},{4,0},{8,4},{12,8},{1,13},{5,1},{9,5},{13,9},{2,14},{6,2},{... | collective-permute-start | bytes 1179656 | tf_op jit(solution)/shard_map/ppermute | solution.py:347
  7.2 1.2 %copy-start = (bf16[2,64,4096]{2,1,0:T(8,128)(2,1)S(1)}, bf16[2,64,4096]{2,1,0:T(8,128)(2,1)}, u32[]{:S(2)}) copy-start(bf16[2,64,4096]{2,1,0:T(8,128)(2,1)} %refs_0_.1) | copy-start | bytes 3145732
  8.4 0.8 %copy-start.1 = (bf16[2,128,64]{1,2,0:T(8,128)(2,1)S(1)}, bf16[2,128,64]{1,2,0:T(8,128)(2,1)}, u32[]{:S(2)}) copy-start(bf16[2,128,64]{1,2,0:T(8,128)(2,1)} %param.12) | copy-start | bytes 98308
  9.2 0.8 %copy-start.2 = (bf16[2,128,64]{1,2,0:T(8,128)(2,1)S(1)}, bf16[2,128,64]{1,2,0:T(8,128)(2,1)}, u32[]{:S(2)}) copy-start(bf16[2,128,64]{1,2,0:T(8,128)(2,1)} %param.13) | copy-start | bytes 98308
  9.9 0.7 %copy-start.5 = (bf16[128,64]{0,1:T(8,128)(2,1)S(1)}, bf16[128,64]{0,1:T(8,128)(2,1)}, u32[]{:S(2)}) copy-start(bf16[128,64]{0,1:T(8,128)(2,1)} %param.15) | copy-start | bytes 49156
  10.7 0.7 %copy-start.6 = (bf16[128,64]{0,1:T(8,128)(2,1)S(1)}, bf16[128,64]{0,1:T(8,128)(2,1)}, u32[]{:S(2)}) copy-start(bf16[128,64]{0,1:T(8,128)(2,1)} %param.16) | copy-start | bytes 49156
  11.4 0.7 %copy-start.8 = (f32[128]{0:T(128)S(1)}, f32[128]{0:T(128)}, u32[]{:S(2)}) copy-start(f32[128]{0:T(128)} %param.11) | copy-start | bytes 1540
  12.0 0.7 %copy-start.9 = (f32[128]{0:T(128)S(1)}, f32[128]{0:T(128)}, u32[]{:S(2)}) copy-start(f32[128]{0:T(128)} %param.14) | copy-start | bytes 1540
  24.8 4.3 %collective-permute-start.5 = (bf16[64,3072]{1,0:T(8,128)(2,1)S(1)}, bf16[64,3072]{1,0:T(8,128)(2,1)S(1)}, u32[]{:S(2)}, u32[]{:S(2)}) collective-permute-start(bf16[64,3072]{1,0:T(8,128)(2,1)S(1)} %collective-permute-done.2.refs_0_), channel_id=1, source_target_pairs={{0,1},{1,0},{2,3},{3,2},{4,5},{5,4},{6,7},{7,6},{8,9},{9,8},{10,11... | collective-permute-start | bytes 1179656 | tf_op jit(solution)/shard_map/ppermute | solution.py:355
  24.8 4.3 %collective-permute-start.6 = (bf16[64,3072]{1,0:T(8,128)(2,1)S(1)}, bf16[64,3072]{1,0:T(8,128)(2,1)S(1)}, u32[]{:S(2)}, u32[]{:S(2)}) collective-permute-start(bf16[64,3072]{1,0:T(8,128)(2,1)S(1)} %collective-permute-done.3.refs_2_), channel_id=1, source_target_pairs={{0,1},{1,0},{2,3},{3,2},{4,5},{5,4},{6,7},{7,6},{8,9},{9,8},{10,11... | collective-permute-start | bytes 1179656 | tf_op jit(solution)/shard_map/ppermute | solution.py:356
  25.3 9.4 %collective-permute-start = (bf16[64,1024]{1,0:T(8,128)(2,1)S(1)}, bf16[64,1024]{1,0:T(8,128)(2,1)S(1)}, u32[]{:S(2)}, u32[]{:S(2)}) collective-permute-start(bf16[64,1024]{1,0:T(8,128)(2,1)S(1)} %get-tuple-element.25), channel_id=1, source_target_pairs={{0,4},{4,8},{8,12},{12,0},{1,5},{5,9},{9,13},{13,1},{2,6},{6,10},{... | collective-permute-start | bytes 393224 | tf_op jit(solution)/shard_map/ppermute | solution.py:347
  26.4 8.2 %collective-permute-start.1 = (bf16[64,1024]{1,0:T(8,128)(2,1)S(1)}, bf16[64,1024]{1,0:T(8,128)(2,1)S(1)}, u32[]{:S(2)}, u32[]{:S(2)}) collective-permute-start(bf16[64,1024]{1,0:T(8,128)(2,1)S(1)} %get-tuple-element.26), channel_id=1, source_target_pairs={{0,12},{4,0},{8,4},{12,8},{1,13},{5,1},{9,5},{13,9},{2,14},{6,2},{... | collective-permute-start | bytes 393224 | tf_op jit(solution)/shard_map/ppermute | solution.py:347
  34.6 3.5 %copy-start.3 = (s32[16,4]{0,1:T(4,128)S(1)}, s32[16,4]{0,1:T(4,128)}, u32[]{:S(2)}) copy-start(s32[16,4]{0,1:T(4,128)} %param.17) | copy-start | bytes 772
  34.6 3.5 %copy-start.4 = (s32[16,4]{0,1:T(4,128)S(1)}, s32[16,4]{0,1:T(4,128)}, u32[]{:S(2)}) copy-start(s32[16,4]{0,1:T(4,128)} %param.18) | copy-start | bytes 772
  34.6 3.4 %copy-start.7 = (s32[16]{0:T(128)S(1)}, s32[16]{0:T(128)}, u32[]{:S(2)}) copy-start(s32[16]{0:T(128)} %n_ref.5) | copy-start | bytes 196
  34.7 1.4 %collective-permute-start.7 = (bf16[64,1024]{1,0:T(8,128)(2,1)S(1)}, bf16[64,1024]{1,0:T(8,128)(2,1)S(1)}, u32[]{:S(2)}, u32[]{:S(2)}) collective-permute-start(bf16[64,1024]{1,0:T(8,128)(2,1)S(1)} %collective-permute-done.refs_0_), channel_id=1, source_target_pairs={{0,1},{1,0},{2,3},{3,2},{4,5},{5,4},{6,7},{7,6},{8,9},{9,8},{10,11... | collective-permute-start | bytes 393224 | tf_op jit(solution)/shard_map/ppermute | solution.py:355
  34.7 1.5 %collective-permute-start.8 = (bf16[64,1024]{1,0:T(8,128)(2,1)S(1)}, bf16[64,1024]{1,0:T(8,128)(2,1)S(1)}, u32[]{:S(2)}, u32[]{:S(2)}) collective-permute-start(bf16[64,1024]{1,0:T(8,128)(2,1)S(1)} %collective-permute-done.1.refs_2_), channel_id=1, source_target_pairs={{0,1},{1,0},{2,3},{3,2},{4,5},{5,4},{6,7},{7,6},{8,9},{9,8},{10,11... | collective-permute-start | bytes 393224 | tf_op jit(solution)/shard_map/ppermute | solution.py:356
  40.3 2.9 %collective-permute-start.10 = (bf16[64,4096]{1,0:T(8,128)(2,1)S(1)}, bf16[64,4096]{1,0:T(8,128)(2,1)S(1)}, u32[]{:S(2)}, u32[]{:S(2)}) collective-permute-start(bf16[64,4096]{1,0:T(8,128)(2,1)S(1)} %triplets.2.mine_ref), channel_id=1, source_target_pairs={{0,1},{1,0},{2,3},{3,2},{4,5},{5,4},{6,7},{7,6},{8,9},{9,8},{10,11... | collective-permute-start | bytes 1572872 | tf_op jit(solution)/shard_map/ppermute | solution.py:369
  42.9 2.2 %collective-permute-start.9 = (bf16[64,4096]{1,0:T(8,128)(2,1)S(1)}, bf16[64,4096]{1,0:T(8,128)(2,1)S(1)}, u32[]{:S(2)}, u32[]{:S(2)}) collective-permute-start(bf16[64,4096]{1,0:T(8,128)(2,1)S(1)} %triplets.3.mine_ref), channel_id=1, source_target_pairs={{0,1},{1,0},{2,3},{3,2},{4,5},{5,4},{6,7},{7,6},{8,9},{9,8},{10,11... | collective-permute-start | bytes 1572872 | tf_op jit(solution)/shard_map/ppermute | solution.py:369

commit v8 on v7

--- a/solution.py
+++ b/solution.py
@@ -76,8 +76,9 @@
     )(a_slots, b_slots, counts, pair)
 
 
-def prepared(weight, gain):
-    weight = weight * gain
+def prepared(weight, gain=None):
+    if gain is not None:
+        weight = weight * gain
     rolled = pltpu.roll(weight, weight.shape[1] // 2, 1)
     return jnp.where(lax.axis_index("chan") == 0, weight, rolled).astype(BF16)
 
@@ -90,7 +91,7 @@
     return [0.5 * row for row in rows]
 
 
-def normed_of(mine, theirs):
+def normed_of(mine, theirs, gain=None):
     total = 2 * mine.shape[0]
     mine = mine.astype(F32)
     theirs = theirs.astype(F32)
@@ -99,25 +100,40 @@
     theirs = theirs - mean
     spread = jnp.sum(mine * mine + theirs * theirs, axis=0, keepdims=True) * (1.0 / total)
     scale = lax.rsqrt(spread + epsilon)
-    return jnp.concatenate([(mine * scale).astype(BF16), (theirs * scale).astype(BF16)], axis=0)
-
-
-def project_kernel(piece, chunk, offset, gated, *refs):
+    mine = mine * scale
+    theirs = theirs * scale
+    if gain is not None:
+        half = mine.shape[0]
+        mine = mine * gain[:half]
+        theirs = theirs * gain[half:]
+    return jnp.concatenate([mine.astype(BF16), theirs.astype(BF16)], axis=0)
+
+
+def project_kernel(chunk, cuts, offset, gated, *refs):
     if gated:
         m_ref, t_ref, a_ref, b_ref, o_ref, u_ref, g_ref, h_ref = refs[:8]
-        l_ref, p_ref, gate_ref, w_ref, v_ref, sl, sp = refs[8:]
-        blocks = ((m_ref.at[0], t_ref.at[0]), (m_ref.at[1], t_ref.at[1]))
+        l_ref, p_ref, gate_ref, w_ref, v_ref, gain_ref, sl, sp = refs[8:]
+        pieces = [((m_ref.at[0], t_ref.at[0]), (m_ref.at[1], t_ref.at[1]))]
         rows = gated_rows(a_ref) + gated_rows(b_ref) + [0.5 * o_ref[...].astype(F32)]
-        weight = prepared(jnp.concatenate(rows, axis=0), g_ref[...])
+        weight = prepared(jnp.concatenate(rows, axis=0))
         pair_of = 0
     else:
-        m0, t0, m1, t1, w_ref, _, _, l_ref, p_ref, sl, sp = refs
-        blocks = ((m0, t0), (m1, t1))
+        m0, m1 = refs[:2]
+        theirs = refs[2 : 2 + 2 * len(cuts)]
+        w_ref, gain_ref, _, _, l_ref, p_ref, sl, sp = refs[2 + 2 * len(cuts) :]
+        pieces = []
+        for at, (start, size) in enumerate(cuts):
+            cut = pl.ds(start, size)
+            t0, t1 = theirs[2 * at], theirs[2 * at + 1]
+            pieces.append(((m0.at[:, cut], t0), (m1.at[:, cut], t1)))
         weight = w_ref[...]
         pair_of = 1
-    half, cells = blocks[0][0].shape
+    half = l_ref.shape[1]
     if gated:
         w_ref[...] = weight[: 4 * half]
+        mine = g_ref[pl.ds(pl.multiple_of(lax.axis_index("chan") * half, half), half), :]
+        other = g_ref[pl.ds(pl.multiple_of((1 - lax.axis_index("chan")) * half, half), half), :]
+        gain_ref[...] = jnp.broadcast_to(jnp.concatenate([mine, other], axis=0), gain_ref.shape)
         v_ref[...] = prepared(0.5 * u_ref[...].astype(F32), h_ref[...])
 
         @pl.loop(0, half)
@@ -126,14 +142,15 @@
 
     low = lax.broadcasted_iota(jnp.int32, (8, LANES), 1) < BLK
     high_rows = chunk // BLK
-
-    @pl.loop(0, cells // chunk)
-    def _(n):
-        for start in range(0, chunk, piece):
-            at = pl.ds(pl.multiple_of(n * chunk + start, piece), piece)
+    pitch = sl.shape[0] // high_rows
+
+    def step(blocks, n, to):
+        for start in range(0, chunk, LANES):
+            at = pl.ds(pl.multiple_of(n * chunk + start, LANES), LANES)
             sides = []
             for x, (m, t) in enumerate(blocks):
-                y = jnp.dot(weight, normed_of(m[:, at], t[:, at]), preferred_element_type=F32)
+                normed = normed_of(m[:, at], t[:, at], gain_ref[...])
+                y = jnp.dot(weight, normed, preferred_element_type=F32)
                 if gated:
                     gate_ref[x, :, at] = (jnp.tanh(y[4 * half :]) + 1.0).astype(BF16)
                 for side in range(2):
@@ -141,29 +158,32 @@
                     for row in range(2 * half * side, 2 * half * (side + 1), 16):
                         groups.append((jnp.tanh(y[row : row + 8]) + 1.0) * y[row + 8 : row + 16])
                     sides.append(groups)
+            i = start // BLK
             for row in range(0, half, 8):
                 l0, r0, l1, r1 = (groups[row // 8] for groups in sides)
-                for sub in range(0, piece, LANES):
-                    i = (start + sub) // BLK
-                    even = slice(i * half + row, i * half + row + 8)
-                    odd = slice((i + 1) * half + row, (i + 1) * half + row + 8)
-                    cut = slice(sub, sub + LANES)
-                    for held, v0, v1 in ((sl, l0[:, cut], l1[:, cut]), (sp, r0[:, cut], r1[:, cut])):
-                        held[even, :] = jnp.where(low, v0, pltpu.roll(v1, BLK, 1))
-                        held[odd, :] = jnp.where(low, pltpu.roll(v0, BLK, 1), v1)
-
-        to = pl.ds(pl.multiple_of(n * high_rows + offset // BLK, 16), high_rows)
+                even = slice(i * pitch + row, i * pitch + row + 8)
+                odd = slice((i + 1) * pitch + row, (i + 1) * pitch + row + 8)
+                for held, v0, v1 in ((sl, l0, l1), (sp, r0, r1)):
+                    held[even, :] = jnp.where(low, v0, pltpu.roll(v1, BLK, 1))
+                    held[odd, :] = jnp.where(low, pltpu.roll(v0, BLK, 1), v1)
 
         @pl.loop(0, half, unroll=8)
         def _(c):
-            take = pl.ds(c, high_rows, stride=half)
+            take = pl.ds(c, high_rows, stride=pitch)
             l_ref[pair_of, c, to, :] = sl[take, :].astype(BF16)
             right = sp[take, :].astype(BF16)
             p_ref[2 * pair_of, c, to, :] = right
             p_ref[2 * pair_of + 1, c, to, :] = pltpu.roll(right, BLK, 1)
 
-
-def project(operands, half, cells, chunk, piece, gated, offset=0):
+    for (start, size), blocks in zip(cuts, pieces):
+
+        @pl.loop(0, size // chunk)
+        def _(n):
+            first = n * high_rows + (offset + start) // BLK
+            step(blocks, n, pl.ds(pl.multiple_of(first, 16), high_rows))
+
+
+def project(operands, half, cuts, chunk, gated, offset=0):
     out_shape = [
         pltpu.VMEM((2, half, BLK, LANES), BF16),
         pltpu.VMEM((5, half, BLK, LANES), BF16),
@@ -171,9 +191,10 @@
     aliases = {}
     if gated:
         out_shape += [
-            pltpu.VMEM((2, half, cells), BF16),
+            pltpu.VMEM((2, half, BLK * BLK), BF16),
             pltpu.VMEM((4 * half, 2 * half), BF16),
             pltpu.VMEM((half, 2 * half), BF16),
+            pltpu.VMEM((2 * half, LANES), F32),
         ]
     else:
         aliases = {len(operands) - 2: 0, len(operands) - 1: 1}
@@ -182,11 +203,11 @@
         ]
     vmem = pl.BlockSpec(memory_space=pltpu.VMEM)
     return pl.pallas_call(
-        functools.partial(project_kernel, piece, chunk, offset, gated),
+        functools.partial(project_kernel, chunk, cuts, offset, gated),
         in_specs=[vmem] * len(operands),
         out_specs=[vmem] * len(out_shape),
         out_shape=out_shape,
-        scratch_shapes=[pltpu.VMEM((chunk // BLK * half, LANES), F32)] * 2,
+        scratch_shapes=[pltpu.VMEM((chunk // BLK * (half + 8), LANES), F32)] * 2,
         input_output_aliases=aliases,
         compiler_params=pltpu.CompilerParams(vmem_limit_bytes=VMEM_LIMIT),
         name="project_own" if gated else "project_fetched",
@@ -224,6 +245,7 @@
 
     take_low = lax.broadcasted_iota(jnp.int32, (group, LANES), 1) < BLK
     half = l_ref.shape[1]
+    pitch = accs[0].shape[0] // BLK
 
     @pl.loop(0, half, step=group * len(accs))
     def _(base):
@@ -235,13 +257,13 @@
                 rhs = jnp.concatenate(
                     [jnp.where(low, parts[0], parts[1]), jnp.where(low, parts[2], parts[3])], axis=1
                 )
-                acc[pl.ds(at, BLK, stride=group), :BLK] = lax.dot_general(
+                acc[pl.ds(at, BLK, stride=pitch), :BLK] = lax.dot_general(
                     lhs, rhs, (((1,), (1,)), ((), ())), preferred_element_type=F32
                 )
             rows = pl.ds(pl.multiple_of(base + which * group, group), group)
             for t in range(BLK // 2):
-                even = acc[2 * t * group : (2 * t + 1) * group, :]
-                odd = acc[(2 * t + 1) * group : (2 * t + 2) * group, :]
+                even = acc[2 * t * pitch : 2 * t * pitch + group, :]
+                odd = acc[(2 * t + 1) * pitch : (2 * t + 1) * pitch + group, :]
                 out_ref[rows, t * LANES : (t + 1) * LANES] = jnp.where(
                     take_low, even, pltpu.roll(odd, BLK, 1)
                 ).astype(BF16)
@@ -259,54 +281,64 @@
         in_specs=[smem, smem, smem, vmem, vmem],
         out_specs=vmem,
         out_shape=pltpu.VMEM((half, BLK * BLK), BF16),
-        scratch_shapes=[pltpu.VMEM((BLK * group, LANES), F32)] * 2,
+        scratch_shapes=[pltpu.VMEM((BLK * (group + 8), LANES), F32)] * 2,
         compiler_params=pltpu.CompilerParams(vmem_limit_bytes=VMEM_LIMIT),
         name="triplets",
     )(a_slots, b_slots, counts, lefts, rights)
 
 
-def finish_kernel(s, piece, mine_ref, theirs_ref, gate_ref, w_ref, *refs):
-    out_ref, held, sems = refs[-3:]
+def finish_kernel(s, mine_ref, theirs_ref, gate_ref, w_ref, *refs):
     weight = w_ref[...]
     cells = mine_ref.shape[-1]
-    steps = sems.shape[0]
+    if s == 0:
+        held = refs[0]
+        steps = 4
+    else:
+        before_ref, out_ref, held, sems = refs
+        steps = sems.shape[0] - 1
+        before = pltpu.make_async_copy(before_ref, out_ref.at[0], sems.at[steps])
+        before.start()
     size = cells // steps
 
     def copy(n):
         to = pl.ds(pl.multiple_of(n * size, size), size)
-        return pltpu.make_async_copy(held.at[:, to], out_ref.at[s, :, to], sems.at[n])
+        return pltpu.make_async_copy(held.at[:, to], out_ref.at[1, :, to], sems.at[n])
 
     @pl.loop(0, steps)
     def _(n):
-        for start in range(0, size, piece):
-            to = pl.ds(pl.multiple_of(n * size + start, piece), piece)
+        for start in range(0, size, LANES):
+            to = pl.ds(pl.multiple_of(n * size + start, LANES), LANES)
             normed = normed_of(mine_ref[:, to], theirs_ref[:, to])
             projected = jnp.dot(weight, normed, preferred_element_type=F32)
             held[:, to] = (gate_ref[s, :, to].astype(F32) * projected).astype(BF16)
-        copy(n).start()
-
-    @pl.loop(0, steps)
-    def _(n):
-        copy(n).wait()
-
-
-def finish(s, mine, theirs, gate, weight, steps, piece, out=None):
-    half, cells = mine.shape
+        if s > 0:
+            copy(n).start()
+
+    if s > 0:
+
+        @pl.loop(0, steps)
+        def _(n):
+            copy(n).wait()
+
+        before.wait()
+
+
+def finish(s, mine, theirs, gate, weight, before=None):
     vmem = pl.BlockSpec(memory_space=pltpu.VMEM)
     operands = [mine, theirs, gate, weight]
-    in_specs = [vmem] * 4
-    aliases = {}
-    if out is not None:
-        aliases = {len(operands): 0}
-        operands.append(out)
-        in_specs.append(pl.BlockSpec(memory_space=pltpu.HBM))
+    if s == 0:
+        out_shape, out_specs, scratch = pltpu.VMEM(mine.shape, BF16), vmem, []
+    else:
+        operands.append(before)
+        out_shape = jax.ShapeDtypeStruct(gate.shape, BF16)
+        out_specs = pl.BlockSpec(memory_space=pltpu.HBM)
+        scratch = [pltpu.VMEM(mine.shape, BF16), pltpu.SemaphoreType.DMA((5,))]
     return pl.pallas_call(
-        functools.partial(finish_kernel, s, piece),
-        in_specs=in_specs,
-        out_specs=pl.BlockSpec(memory_space=pltpu.HBM),
-        out_shape=jax.ShapeDtypeStruct(gate.shape, BF16),
-        scratch_shapes=[pltpu.VMEM((half, cells), BF16), pltpu.SemaphoreType.DMA((steps,))],
-        input_output_aliases=aliases,
+        functools.partial(finish_kernel, s),
+        in_specs=[vmem] * len(operands),
+        out_specs=out_specs,
+        out_shape=out_shape,
+        scratch_shapes=scratch,
         compiler_params=pltpu.CompilerParams(vmem_limit_bytes=VMEM_LIMIT),
         name="finish",
     )(*operands)
@@ -336,30 +368,33 @@
         jnp.swapaxes(b_weight, 1, 2),
         out_gate_weight.T,
         out_weight.T,
-        ln_in_gain[None, :],
+        ln_in_gain[:, None],
         ln_out_gain[None, :],
     ]
 
     pair_other = lax.ppermute(pair, "chan", swap)
-    cuts = ((0, cells // 4 * 3), (cells // 4 * 3, cells // 4))
+    cuts = ((0, cells // 2), (cells // 2, cells // 2))
     chosen = select_blocks(pair, a_slots, b_slots, counts, cuts)
     arrived = [
         (lax.ppermute(chosen[2 * n], "row", up), lax.ppermute(chosen[2 * n + 1], "row", down))
         for n in range(len(cuts))
     ]
-    lefts, rights, gate, weight, last_weight = project(
-        [pair, pair_other, *weights], half, cells, 1024, 128, True
+    lefts, rights, gate, weight, last_weight, gain = project(
+        [pair, pair_other, *weights], half, ((0, cells),), 1024, True
     )
     for (start, size), (from_behind, from_ahead) in zip(cuts, arrived):
         from_behind, from_ahead, lefts = lax.optimization_barrier((from_behind, from_ahead, lefts))
-        behind_other = lax.ppermute(from_behind, "chan", swap)
-        ahead_other = lax.ppermute(from_ahead, "chan", swap)
+        parts = ((0, size),) if start else ((0, size // 2), (size // 2, size // 2))
+        others = [
+            lax.ppermute(lax.slice_in_dim(value, at, at + wide, axis=1), "chan", swap)
+            for at, wide in parts
+            for value in (from_behind, from_ahead)
+        ]
         lefts, rights = project(
-            [from_behind, behind_other, from_ahead, ahead_other, weight, lefts, rights],
+            [from_behind, from_ahead, *others, weight, gain, lefts, rights],
             half,
-            size,
+            parts,
             1024,
-            128,
             False,
             start,
         )
@@ -371,7 +406,7 @@
             update, lefts = lax.optimization_barrier((update, lefts))
     out = None
     for s, (mine, theirs) in enumerate(updates):
-        out = finish(s, mine, theirs, gate, last_weight, 4, 256, out)
+        out = finish(s, mine, theirs, gate, last_weight, out)
     return out
 
 

time: 47.6 us -> 43.8 us (0.920)
  Pallas kernels: 25.6 us -> 21.4 us
    pallas_call x5, Pallas kernels: 19.2 us -> 15.5 us  [the longest x3 12.2 us: project(): pl.pallas_call(functools.partial(project_kernel, chunk, cuts, offset, gat...]
    ppermute x2, waiting for transfers between devices: 4.16 us -> 1.64 us  [per_device(): lax.ppermute(chosen[2 * n + 1], 'row', down)]
    ppermute x4 -> x6, waiting for transfers between devices: 1.03 us -> 3.27 us  [per_device(): lax.ppermute(lax.slice_in_dim(value, at, at + wide, axis=1), 'chan', swap)]
    ppermute x2, starting transfers between devices: 4.79 us -> 5.91 us  [per_device(): lax.ppermute(chosen[2 * n + 1], 'row', down)]
    ppermute x2, starting transfers between devices: 3.76 us -> 2.63 us  [per_device(): lax.ppermute(chosen[2 * n], 'row', up)]
    broadcast_in_dim x0 -> x1, local copies, waits for them, and re-layouts: none -> 0.76 us  [per_device(): ln_in_gain[:, None]]
    unnamed x20 -> x18, local copies, waits for them, and re-layouts: 5.5 us -> 4.84 us
    pallas_call x2, Pallas kernels: 4.45 us -> 3.84 us  [triplet_sum(): pl.pallas_call(functools.partial(triplet_kernel, s, slots, a_slots.shape[...]
  transfers between devices with their start and end apart: 11 -> 13, of which waited for: 3 -> 7; matrix products, arithmetic and copies ran while one was open for 0% -> 2% of each run, Pallas kernels for 42% -> 33%
where the time goes in v8:
time: 43.8 us; the launch traced here: 43.3 us
  Pallas kernels  21.4 us (49%)
  starting transfers between devices  11 us (25%)
  local copies, waits for them, and re-layouts  5.64 us (13%)
  waiting for transfers between devices  5.16 us (12%)
    pallas_call x3, Pallas kernels, project(): pl.pallas_call(functools.partial(project_kernel, chunk, cuts, offset, gat...  12.2 us
    ppermute x2, starting transfers between devices, per_device(): lax.ppermute(chosen[2 * n + 1], 'row', down)  5.91 us
    unnamed x18, local copies, waits for them, and re-layouts  4.84 us
    pallas_call x2, Pallas kernels, triplet_sum(): pl.pallas_call(functools.partial(triplet_kernel, s, slots, a_slots.shape[...  3.84 us
    ppermute x6, waiting for transfers between devices, per_device(): lax.ppermute(lax.slice_in_dim(value, at, at + wide, axis=1), 'chan', swap)  3.27 us
    pallas_call x2, Pallas kernels, finish(): pl.pallas_call(functools.partial(finish_kernel, s), in_specs=[vmem] * len...  3.27 us
    ppermute x2, starting transfers between devices, per_device(): lax.ppermute(chosen[2 * n], 'row', up)  2.63 us
    pallas_call x1, Pallas kernels, select_blocks(): pl.pallas_call(functools.partial(select_kernel, slots, a_slots.shape[0],...  2.02 us
  transfers between devices with their start and end apart: 13, of which 7 were waited for; matrix products, arithmetic and copies ran while one was open for 2% of the time, Pallas kernels for 33%

profile of v8, /device:TPU:0, one launch (start us, length us, event | category | flops | bytes accessed | tf_op | source)
XLA Modules:
  0.0 43.3 jit_solution(11392938578533305832)
XLA Ops:
  0.0 0.5 %collective-permute-start.4 = (bf16[2,64,4096]{2,1,0:T(8,128)(2,1)}, bf16[2,64,4096]{2,1,0:T(8,128)(2,1)S(1)}, u32[]{:S(2)}, u32[]{:S(2)}) collective-permute-start(bf16[2,64,4096]{2,1,0:T(8,128)(2,1)} %refs_0_.1), channel_id=1, source_target_pairs={{0,1},{1,0},{2,3},{3,2},{4,5},{5,4},{6,7},{7,6},{8,9},{9,8},{10,11... | collective-permute-start | bytes 3145736 | tf_op jit(solution)/shard_map/ppermute | solution.py:375
  0.5 2.0 %select_blocks.1 = (bf16[64,2048]{1,0:T(8,128)(2,1)S(1)}, bf16[64,2048]{1,0:T(8,128)(2,1)S(1)}, bf16[64,2048]{1,0:T(8,128)(2,1)S(1)}, bf16[64,2048]{1,0:T(8,128)(2,1)S(1)}) custom-call(s32[4,16]{1,0:T(4,128)} %bitcast.10, s32[4,16]{1,0:T(4,128)} %bitcast.13, s32[16]{0:T(128)} %n_ref.5, bf16[2,64,4096]{2,1,0:T(8,128)(2,1)} %refs_0_.1), custom_call_target="tpu_custom_call" | custom-call | tf_op jit(solution)/shard_map/select_blocks/pallas_call | solution.py:69
  2.5 2.6 %collective-permute-start.2 = (bf16[64,2048]{1,0:T(8,128)(2,1)S(1)}, bf16[64,2048]{1,0:T(8,128)(2,1)S(1)}, u32[]{:S(2)}, u32[]{:S(2)}) collective-permute-start(bf16[64,2048]{1,0:T(8,128)(2,1)S(1)} %get-tuple-element.28), channel_id=1, source_target_pairs={{0,4},{4,8},{8,12},{12,0},{1,5},{5,9},{9,13},{13,1},{2,6},{6,10},{... | collective-permute-start | bytes 786440 | tf_op jit(solution)/shard_map/ppermute | solution.py:379
  5.1 2.1 %collective-permute-start.3 = (bf16[64,2048]{1,0:T(8,128)(2,1)S(1)}, bf16[64,2048]{1,0:T(8,128)(2,1)S(1)}, u32[]{:S(2)}, u32[]{:S(2)}) collective-permute-start(bf16[64,2048]{1,0:T(8,128)(2,1)S(1)} %get-tuple-element.29), channel_id=1, source_target_pairs={{0,12},{4,0},{8,4},{12,8},{1,13},{5,1},{9,5},{13,9},{2,14},{6,2},{... | collective-permute-start | bytes 786440 | tf_op jit(solution)/shard_map/ppermute | solution.py:379
  7.2 0.0 collective-permute-start
  7.2 3.8 %collective-permute-start.1 = (bf16[64,2048]{1,0:T(8,128)(2,1)S(1)}, bf16[64,2048]{1,0:T(8,128)(2,1)S(1)}, u32[]{:S(2)}, u32[]{:S(2)}) collective-permute-start(bf16[64,2048]{1,0:T(8,128)(2,1)S(1)} %get-tuple-element.27), channel_id=1, source_target_pairs={{0,12},{4,0},{8,4},{12,8},{1,13},{5,1},{9,5},{13,9},{2,14},{6,2},{... | collective-permute-start | bytes 786440 | tf_op jit(solution)/shard_map/ppermute | solution.py:379
  11.0 0.8 %copy.15.refs_6_ = f32[128,1]{1,0:T(8,128)S(1)} copy(f32[128,1]{0,1:T(1,128)} %bitcast.19) | data formatting | bytes 1024 | tf_op jit(solution)/shard_map/broadcast_in_dim | solution.py:371
  11.8 0.0 collective-permute-done.4.refs_1_
  11.8 0.0 copy-start
  11.8 1.2 %copy-done = bf16[2,64,4096]{2,1,0:T(8,128)(2,1)S(1)} copy-done((bf16[2,64,4096]{2,1,0:T(8,128)(2,1)S(1)}, bf16[2,64,4096]{2,1,0:T(8,128)(2,1)}, u32[]{:S(2)}) %copy-start) | copy-done | bytes 1048600
  13.0 0.0 copy-start.1
  13.0 0.8 %copy-done.1 = bf16[2,128,64]{1,2,0:T(8,128)(2,1)S(1)} copy-done((bf16[2,128,64]{1,2,0:T(8,128)(2,1)S(1)}, bf16[2,128,64]{1,2,0:T(8,128)(2,1)}, u32[]{:S(2)}) %copy-start.1) | copy-done | bytes 32792
  13.8 0.8 %copy-done.2 = bf16[2,128,64]{1,2,0:T(8,128)(2,1)S(1)} copy-done((bf16[2,128,64]{1,2,0:T(8,128)(2,1)S(1)}, bf16[2,128,64]{1,2,0:T(8,128)(2,1)}, u32[]{:S(2)}) %copy-start.2) | copy-done | bytes 32792
  14.5 0.7 %copy-done.5 = bf16[128,64]{0,1:T(8,128)(2,1)S(1)} copy-done((bf16[128,64]{0,1:T(8,128)(2,1)S(1)}, bf16[128,64]{0,1:T(8,128)(2,1)}, u32[]{:S(2)}) %copy-start.5) | copy-done | bytes 16408
  15.3 0.7 %copy-done.6 = bf16[128,64]{0,1:T(8,128)(2,1)S(1)} copy-done((bf16[128,64]{0,1:T(8,128)(2,1)S(1)}, bf16[128,64]{0,1:T(8,128)(2,1)}, u32[]{:S(2)}) %copy-start.6) | copy-done | bytes 16408
  16.0 0.7 %copy-done.8 = f32[128]{0:T(128)S(1)} copy-done((f32[128]{0:T(128)S(1)}, f32[128]{0:T(128)}, u32[]{:S(2)}) %copy-start.8) | copy-done | bytes 536
  16.6 6.4 %project_own.1 = (bf16[2,64,64,128]{3,2,1,0:T(8,128)(2,1)S(1)}, bf16[5,64,64,128]{3,2,1,0:T(8,128)(2,1)S(1)}, bf16[2,64,4096]{2,1,0:T(8,128)(2,1)S(1)}, bf16[256...) custom-call(bf16[2,64,4096]{2,1,0:T(8,128)(2,1)S(1)} %copy-done, ...), custom_call_target="tpu_custom_call" | custom-call | tf_op jit(solution)/shard_map/project_own/pallas_call | solution.py:205
  23.1 0.0 collective-permute-done.2.refs_0_
  23.1 0.0 collective-permute-done.3.refs_1_
  23.1 0.1 collective-permute-start.7
  23.2 0.5 %collective-permute-start.5 = (bf16[64,1024]{1,0:T(8,128)(2,1)S(1)}, bf16[64,1024]{1,0:T(8,128)(2,1)S(1)}, u32[]{:S(2)}, u32[]{:S(2)}) collective-permute-start(bf16[64,1024]{1,0:T(8,128)(2,1)S(1)} %get-tuple-element.50), channel_id=1, source_target_pairs={{0,1},{1,0},{2,3},{3,2},{4,5},{5,4},{6,7},{7,6},{8,9},{9,8},{10,11... | collective-permute-start | bytes 393224 | tf_op jit(solution)/shard_map/ppermute | solution.py:389
  23.7 0.1 collective-permute-start.8
  23.9 0.7 %collective-permute-done.7.refs_4_ = bf16[64,1024]{1,0:T(8,128)(2,1)S(1)} collective-permute-done((bf16[64,1024]{1,0:T(8,128)(2,1)S(1)}, bf16[64,1024]{1,0:T(8,128)(2,1)S(1)}, u32[]{:S(2)}, u32[]{:S(2)}) %collective-permute-start.7) | collective-permute-done | bytes 131104 | tf_op jit(solution)/shard_map/ppermute | solution.py:389
  24.5 0.1 collective-permute-start.6
  24.7 0.0 collective-permute-done.5.refs_2_
  24.7 0.4 collective-permute-done.8.refs_5_
  25.1 0.8 %collective-permute-done.6.refs_3_ = bf16[64,1024]{1,0:T(8,128)(2,1)S(1)} collective-permute-done((bf16[64,1024]{1,0:T(8,128)(2,1)S(1)}, bf16[64,1024]{1,0:T(8,128)(2,1)S(1)}, u32[]{:S(2)}, u32[]{:S(2)}) %collective-permute-start.6) | collective-permute-done | bytes 131104 | tf_op jit(solution)/shard_map/ppermute | solution.py:389
  25.9 2.8 %project_fetched.2 = (bf16[2,64,64,128]{3,2,1,0:T(8,128)(2,1)S(1)}, bf16[5,64,64,128]{3,2,1,0:T(8,128)(2,1)S(1)}) custom-call(bf16[64,2048]{1,0:T(8,128)(2,1)S(1)} %collective-permute-done.2.refs_0_, bf16[64,2048]{1,0:T(8,128)(2,1)S(1)} %collective-permute-done.3.refs_1_, ...), custom_call_target="tpu_custom_call", output_to_operand_aliasing={{0}: (8, {}), {1}: (9, {})} | custom-call | tf_op jit(solution)/shard_map/project_fetched/pallas_call | solution.py:205
  28.7 0.0 copy-start.4
  28.7 0.0 copy-start.7
  28.8 0.0 collective-permute-done.refs_0_
  28.8 1.6 %collective-permute-done.1.refs_1_ = bf16[64,2048]{1,0:T(8,128)(2,1)S(1)} collective-permute-done((bf16[64,2048]{1,0:T(8,128)(2,1)S(1)}, bf16[64,2048]{1,0:T(8,128)(2,1)S(1)}, u32[]{:S(2)}, u32[]{:S(2)}) %collective-permute-start.1) | collective-permute-done | bytes 262176 | tf_op jit(solution)/shard_map/ppermute | solution.py:379
  30.4 0.0 collective-permute-start.9
  30.4 0.5 %collective-permute-start.10 = (bf16[64,2048]{1,0:T(8,128)(2,1)S(1)}, bf16[64,2048]{1,0:T(8,128)(2,1)S(1)}, u32[]{:S(2)}, u32[]{:S(2)}) collective-permute-start(bf16[64,2048]{1,0:T(8,128)(2,1)S(1)} %collective-permute-done.1.refs_1_), channel_id=1, source_target_pairs={{0,1},{1,0},{2,3},{3,2},{4,5},{5,4},{6,7},{7,6},{8,9},{9,8},{10,11... | collective-permute-start | bytes 786440 | tf_op jit(solution)/shard_map/ppermute | solution.py:389
  30.9 1.0 %collective-permute-done.9.refs_2_ = bf16[64,2048]{1,0:T(8,128)(2,1)S(1)} collective-permute-done((bf16[64,2048]{1,0:T(8,128)(2,1)S(1)}, bf16[64,2048]{1,0:T(8,128)(2,1)S(1)}, u32[]{:S(2)}, u32[]{:S(2)}) %collective-permute-start.9) | collective-permute-done | bytes 262176 | tf_op jit(solution)/shard_map/ppermute | solution.py:389
  31.9 0.4 collective-permute-done.10.refs_3_
  32.3 2.9 %project_fetched.3 = (bf16[2,64,64,128]{3,2,1,0:T(8,128)(2,1)S(1)}, bf16[5,64,64,128]{3,2,1,0:T(8,128)(2,1)S(1)}) custom-call(bf16[64,2048]{1,0:T(8,128)(2,1)S(1)} %collective-permute-done.refs_0_, bf16[64,2048]{1,0:T(8,128)(2,1)S(1)} %collective-permute-done.1.refs_1_, ...), custom_call_target="tpu_custom_call", output_to_operand_aliasing={{0}: (6, {}), {1}: (7, {})} | custom-call | tf_op jit(solution)/shard_map/project_fetched/pallas_call | solution.py:205
  35.3 0.0 copy-done.3
  35.3 0.0 copy-done.4
  35.3 0.0 copy-done.7
  35.3 1.9 %triplets.2.mine_ref = bf16[64,4096]{1,0:T(8,128)(2,1)S(1)} custom-call(s32[4,16]{1,0:T(4,128)S(1)} %bitcast.11, s32[4,16]{1,0:T(4,128)S(1)} %bitcast.14, s32[16]{0:T(128)S(1)} %copy-done.7, bf16[2,64,64,128]{3,2,1,0:T(8,128)(2,1)S(1)} %get-tuple-element.44.l_ref, bf16[5,64,64,128]{3,2,1,0:T(8,128)(2,1)S(1)} %get-tuple-element.43.p_ref), custom_call_target="tpu_custom_call" | custom-call | tf_op jit(solution)/shard_map/triplets/pallas_call | solution.py:279
  37.2 0.2 collective-permute-start.12
  37.4 1.9 %triplets.3.mine_ref = bf16[64,4096]{1,0:T(8,128)(2,1)S(1)} custom-call(s32[4,16]{1,0:T(4,128)S(1)} %bitcast.12, s32[4,16]{1,0:T(4,128)S(1)} %bitcast.15, s32[16]{0:T(128)S(1)} %copy-done.7, bf16[2,64,64,128]{3,2,1,0:T(8,128)(2,1)S(1)} %get-tuple-element.44.l_ref, bf16[5,64,64,128]{3,2,1,0:T(8,128)(2,1)S(1)} %get-tuple-element.43.p_ref), custom_call_target="tpu_custom_call" | custom-call | tf_op jit(solution)/shard_map/triplets/pallas_call | solution.py:279
  39.3 0.5 %collective-permute-start.11 = (bf16[64,4096]{1,0:T(8,128)(2,1)S(1)}, bf16[64,4096]{1,0:T(8,128)(2,1)S(1)}, u32[]{:S(2)}, u32[]{:S(2)}) collective-permute-start(bf16[64,4096]{1,0:T(8,128)(2,1)S(1)} %triplets.3.mine_ref), channel_id=1, source_target_pairs={{0,1},{1,0},{2,3},{3,2},{4,5},{5,4},{6,7},{7,6},{8,9},{9,8},{10,11... | collective-permute-start | bytes 1572872 | tf_op jit(solution)/shard_map/ppermute | solution.py:404
  39.8 0.0 collective-permute-done.12.theirs_ref
  39.8 1.3 %finish.2.refs_0_ = bf16[64,4096]{1,0:T(8,128)(2,1)S(1)} custom-call(bf16[64,4096]{1,0:T(8,128)(2,1)S(1)} %triplets.2.mine_ref, bf16[64,4096]{1,0:T(8,128)(2,1)S(1)} %collective-permute-done.12.theirs_ref, bf16[2,64,4096]{2,1,0:T(8,128)(2,1)S(1)} %get-tuple-element.45.gate_ref, bf16[64,128]{1,0:T(8,128)(2,1)S(1)} %get-tuple-element.46.w_ref), custom_call_target="tpu_custom_call" | custom-call | tf_op jit(solution)/shard_map/finish/pallas_call | solution.py:336
  41.1 0.2 collective-permute-done.11.theirs_ref
  41.3 2.0 %finish.3 = bf16[2,64,4096]{2,1,0:T(8,128)(2,1)} custom-call(bf16[64,4096]{1,0:T(8,128)(2,1)S(1)} %triplets.3.mine_ref, bf16[64,4096]{1,0:T(8,128)(2,1)S(1)} %collective-permute-done.11.theirs_ref, bf16[2,64,4096]{2,1,0:T(8,128)(2,1)S(1)} %get-tuple-element.45.gate_ref, bf16[64,128]{1,0:T(8,128)(2,1)S(1)} %get-tuple-element.46.w_ref, ...), custom_call_target="tpu_custom_call" | custom-call | tf_op jit(solution)/shard_map/finish/pallas_call | solution.py:336
  (7 shorter events, 0.0 us)
Async XLA Ops:
  0.0 11.8 %collective-permute-start.4 = (bf16[2,64,4096]{2,1,0:T(8,128)(2,1)}, bf16[2,64,4096]{2,1,0:T(8,128)(2,1)S(1)}, u32[]{:S(2)}, u32[]{:S(2)}) collective-permute-start(bf16[2,64,4096]{2,1,0:T(8,128)(2,1)} %refs_0_.1), channel_id=1, source_target_pairs={{0,1},{1,0},{2,3},{3,2},{4,5},{5,4},{6,7},{7,6},{8,9},{9,8},{10,11... | collective-permute-start | bytes 3145736 | tf_op jit(solution)/shard_map/ppermute | solution.py:375
  2.5 20.6 %collective-permute-start.2 = (bf16[64,2048]{1,0:T(8,128)(2,1)S(1)}, bf16[64,2048]{1,0:T(8,128)(2,1)S(1)}, u32[]{:S(2)}, u32[]{:S(2)}) collective-permute-start(bf16[64,2048]{1,0:T(8,128)(2,1)S(1)} %get-tuple-element.28), channel_id=1, source_target_pairs={{0,4},{4,8},{8,12},{12,0},{1,5},{5,9},{9,13},{13,1},{2,6},{6,10},{... | collective-permute-start | bytes 786440 | tf_op jit(solution)/shard_map/ppermute | solution.py:379
  5.1 18.0 %collective-permute-start.3 = (bf16[64,2048]{1,0:T(8,128)(2,1)S(1)}, bf16[64,2048]{1,0:T(8,128)(2,1)S(1)}, u32[]{:S(2)}, u32[]{:S(2)}) collective-permute-start(bf16[64,2048]{1,0:T(8,128)(2,1)S(1)} %get-tuple-element.29), channel_id=1, source_target_pairs={{0,12},{4,0},{8,4},{12,8},{1,13},{5,1},{9,5},{13,9},{2,14},{6,2},{... | collective-permute-start | bytes 786440 | tf_op jit(solution)/shard_map/ppermute | solution.py:379
  7.2 21.6 %collective-permute-start = (bf16[64,2048]{1,0:T(8,128)(2,1)S(1)}, bf16[64,2048]{1,0:T(8,128)(2,1)S(1)}, u32[]{:S(2)}, u32[]{:S(2)}) collective-permute-start(bf16[64,2048]{1,0:T(8,128)(2,1)S(1)} %get-tuple-element.26), channel_id=1, source_target_pairs={{0,4},{4,8},{8,12},{12,0},{1,5},{5,9},{9,13},{13,1},{2,6},{6,10},{... | collective-permute-start | bytes 786440 | tf_op jit(solution)/shard_map/ppermute | solution.py:379
  7.2 23.2 %collective-permute-start.1 = (bf16[64,2048]{1,0:T(8,128)(2,1)S(1)}, bf16[64,2048]{1,0:T(8,128)(2,1)S(1)}, u32[]{:S(2)}, u32[]{:S(2)}) collective-permute-start(bf16[64,2048]{1,0:T(8,128)(2,1)S(1)} %get-tuple-element.27), channel_id=1, source_target_pairs={{0,12},{4,0},{8,4},{12,8},{1,13},{5,1},{9,5},{13,9},{2,14},{6,2},{... | collective-permute-start | bytes 786440 | tf_op jit(solution)/shard_map/ppermute | solution.py:379
  11.8 1.2 %copy-start = (bf16[2,64,4096]{2,1,0:T(8,128)(2,1)S(1)}, bf16[2,64,4096]{2,1,0:T(8,128)(2,1)}, u32[]{:S(2)}) copy-start(bf16[2,64,4096]{2,1,0:T(8,128)(2,1)} %refs_0_.1) | copy-start | bytes 3145732
  13.0 0.8 %copy-start.1 = (bf16[2,128,64]{1,2,0:T(8,128)(2,1)S(1)}, bf16[2,128,64]{1,2,0:T(8,128)(2,1)}, u32[]{:S(2)}) copy-start(bf16[2,128,64]{1,2,0:T(8,128)(2,1)} %param.12) | copy-start | bytes 98308
  13.8 0.8 %copy-start.2 = (bf16[2,128,64]{1,2,0:T(8,128)(2,1)S(1)}, bf16[2,128,64]{1,2,0:T(8,128)(2,1)}, u32[]{:S(2)}) copy-start(bf16[2,128,64]{1,2,0:T(8,128)(2,1)} %param.13) | copy-start | bytes 98308
  14.5 0.7 %copy-start.5 = (bf16[128,64]{0,1:T(8,128)(2,1)S(1)}, bf16[128,64]{0,1:T(8,128)(2,1)}, u32[]{:S(2)}) copy-start(bf16[128,64]{0,1:T(8,128)(2,1)} %param.15) | copy-start | bytes 49156
  15.3 0.7 %copy-start.6 = (bf16[128,64]{0,1:T(8,128)(2,1)S(1)}, bf16[128,64]{0,1:T(8,128)(2,1)}, u32[]{:S(2)}) copy-start(bf16[128,64]{0,1:T(8,128)(2,1)} %param.16) | copy-start | bytes 49156
  16.0 0.7 %copy-start.8 = (f32[128]{0:T(128)S(1)}, f32[128]{0:T(128)}, u32[]{:S(2)}) copy-start(f32[128]{0:T(128)} %param.14) | copy-start | bytes 1540
  23.1 1.4 %collective-permute-start.7 = (bf16[64,1024]{1,0:T(8,128)(2,1)S(1)}, bf16[64,1024]{1,0:T(8,128)(2,1)S(1)}, u32[]{:S(2)}, u32[]{:S(2)}) collective-permute-start(bf16[64,1024]{1,0:T(8,128)(2,1)S(1)} %get-tuple-element.49), channel_id=1, source_target_pairs={{0,1},{1,0},{2,3},{3,2},{4,5},{5,4},{6,7},{7,6},{8,9},{9,8},{10,11... | collective-permute-start | bytes 393224 | tf_op jit(solution)/shard_map/ppermute | solution.py:389
  23.2 1.5 %collective-permute-start.5 = (bf16[64,1024]{1,0:T(8,128)(2,1)S(1)}, bf16[64,1024]{1,0:T(8,128)(2,1)S(1)}, u32[]{:S(2)}, u32[]{:S(2)}) collective-permute-start(bf16[64,1024]{1,0:T(8,128)(2,1)S(1)} %get-tuple-element.50), channel_id=1, source_target_pairs={{0,1},{1,0},{2,3},{3,2},{4,5},{5,4},{6,7},{7,6},{8,9},{9,8},{10,11... | collective-permute-start | bytes 393224 | tf_op jit(solution)/shard_map/ppermute | solution.py:389
  23.7 1.4 %collective-permute-start.8 = (bf16[64,1024]{1,0:T(8,128)(2,1)S(1)}, bf16[64,1024]{1,0:T(8,128)(2,1)S(1)}, u32[]{:S(2)}, u32[]{:S(2)}) collective-permute-start(bf16[64,1024]{1,0:T(8,128)(2,1)S(1)} %get-tuple-element.47), channel_id=1, source_target_pairs={{0,1},{1,0},{2,3},{3,2},{4,5},{5,4},{6,7},{7,6},{8,9},{9,8},{10,11... | collective-permute-start | bytes 393224 | tf_op jit(solution)/shard_map/ppermute | solution.py:389
  24.5 1.3 %collective-permute-start.6 = (bf16[64,1024]{1,0:T(8,128)(2,1)S(1)}, bf16[64,1024]{1,0:T(8,128)(2,1)S(1)}, u32[]{:S(2)}, u32[]{:S(2)}) collective-permute-start(bf16[64,1024]{1,0:T(8,128)(2,1)S(1)} %get-tuple-element.48), channel_id=1, source_target_pairs={{0,1},{1,0},{2,3},{3,2},{4,5},{5,4},{6,7},{7,6},{8,9},{9,8},{10,11... | collective-permute-start | bytes 393224 | tf_op jit(solution)/shard_map/ppermute | solution.py:389
  28.7 6.5 %copy-start.3 = (s32[16,4]{0,1:T(4,128)S(1)}, s32[16,4]{0,1:T(4,128)}, u32[]{:S(2)}) copy-start(s32[16,4]{0,1:T(4,128)} %param.17) | copy-start | bytes 772
  28.7 6.5 %copy-start.4 = (s32[16,4]{0,1:T(4,128)S(1)}, s32[16,4]{0,1:T(4,128)}, u32[]{:S(2)}) copy-start(s32[16,4]{0,1:T(4,128)} %param.18) | copy-start | bytes 772
  28.7 6.5 %copy-start.7 = (s32[16]{0:T(128)S(1)}, s32[16]{0:T(128)}, u32[]{:S(2)}) copy-start(s32[16]{0:T(128)} %n_ref.5) | copy-start | bytes 196
  30.4 1.5 %collective-permute-start.9 = (bf16[64,2048]{1,0:T(8,128)(2,1)S(1)}, bf16[64,2048]{1,0:T(8,128)(2,1)S(1)}, u32[]{:S(2)}, u32[]{:S(2)}) collective-permute-start(bf16[64,2048]{1,0:T(8,128)(2,1)S(1)} %collective-permute-done.refs_0_), channel_id=1, source_target_pairs={{0,1},{1,0},{2,3},{3,2},{4,5},{5,4},{6,7},{7,6},{8,9},{9,8},{10,11... | collective-permute-start | bytes 786440 | tf_op jit(solution)/shard_map/ppermute | solution.py:389
  30.4 1.9 %collective-permute-start.10 = (bf16[64,2048]{1,0:T(8,128)(2,1)S(1)}, bf16[64,2048]{1,0:T(8,128)(2,1)S(1)}, u32[]{:S(2)}, u32[]{:S(2)}) collective-permute-start(bf16[64,2048]{1,0:T(8,128)(2,1)S(1)} %collective-permute-done.1.refs_1_), channel_id=1, source_target_pairs={{0,1},{1,0},{2,3},{3,2},{4,5},{5,4},{6,7},{7,6},{8,9},{9,8},{10,11... | collective-permute-start | bytes 786440 | tf_op jit(solution)/shard_map/ppermute | solution.py:389
  37.2 2.6 %collective-permute-start.12 = (bf16[64,4096]{1,0:T(8,128)(2,1)S(1)}, bf16[64,4096]{1,0:T(8,128)(2,1)S(1)}, u32[]{:S(2)}, u32[]{:S(2)}) collective-permute-start(bf16[64,4096]{1,0:T(8,128)(2,1)S(1)} %triplets.2.mine_ref), channel_id=1, source_target_pairs={{0,1},{1,0},{2,3},{3,2},{4,5},{5,4},{6,7},{7,6},{8,9},{9,8},{10,11... | collective-permute-start | bytes 1572872 | tf_op jit(solution)/shard_map/ppermute | solution.py:404
  39.3 2.0 %collective-permute-start.11 = (bf16[64,4096]{1,0:T(8,128)(2,1)S(1)}, bf16[64,4096]{1,0:T(8,128)(2,1)S(1)}, u32[]{:S(2)}, u32[]{:S(2)}) collective-permute-start(bf16[64,4096]{1,0:T(8,128)(2,1)S(1)} %triplets.3.mine_ref), channel_id=1, source_target_pairs={{0,1},{1,0},{2,3},{3,2},{4,5},{5,4},{6,7},{7,6},{8,9},{9,8},{10,11... | collective-permute-start | bytes 1572872 | tf_op jit(solution)/shard_map/ppermute | solution.py:404

commit v9 on v8

--- a/solution.py
+++ b/solution.py
@@ -109,112 +109,196 @@
     return jnp.concatenate([mine.astype(BF16), theirs.astype(BF16)], axis=0)
 
 
-def project_kernel(chunk, cuts, offset, gated, *refs):
-    if gated:
-        m_ref, t_ref, a_ref, b_ref, o_ref, u_ref, g_ref, h_ref = refs[:8]
-        l_ref, p_ref, gate_ref, w_ref, v_ref, gain_ref, sl, sp = refs[8:]
-        pieces = [((m_ref.at[0], t_ref.at[0]), (m_ref.at[1], t_ref.at[1]))]
-        rows = gated_rows(a_ref) + gated_rows(b_ref) + [0.5 * o_ref[...].astype(F32)]
-        weight = prepared(jnp.concatenate(rows, axis=0))
-        pair_of = 0
-    else:
-        m0, m1 = refs[:2]
-        theirs = refs[2 : 2 + 2 * len(cuts)]
-        w_ref, gain_ref, _, _, l_ref, p_ref, sl, sp = refs[2 + 2 * len(cuts) :]
-        pieces = []
-        for at, (start, size) in enumerate(cuts):
-            cut = pl.ds(start, size)
-            t0, t1 = theirs[2 * at], theirs[2 * at + 1]
-            pieces.append(((m0.at[:, cut], t0), (m1.at[:, cut], t1)))
-        weight = w_ref[...]
-        pair_of = 1
+def gated_sides(mine, theirs, weight, gain, half):
+    y = jnp.dot(weight, normed_of(mine, theirs, gain), preferred_element_type=F32)
+    sides = []
+    for side in range(2):
+        groups = []
+        for row in range(2 * half * side, 2 * half * (side + 1), 16):
+            groups.append((jnp.tanh(y[row : row + 8]) + 1.0) * y[row + 8 : row + 16])
+        sides.append(groups)
+    return sides, y[4 * half :]
+
+
+def pair_chunk(sides_at, chunk, held, half):
+    low = lax.broadcasted_iota(jnp.int32, (8, LANES), 1) < BLK
+    pitch = held[0].shape[0] // (chunk // BLK)
+    for start in range(0, chunk, LANES):
+        first, second = sides_at(start)
+        i = start // BLK
+        for out, values0, values1 in zip(held, first, second):
+            for at, (v0, v1) in enumerate(zip(values0, values1)):
+                even = slice(i * pitch + 8 * at, i * pitch + 8 * at + 8)
+                odd = slice((i + 1) * pitch + 8 * at, (i + 1) * pitch + 8 * at + 8)
+                out[even, :] = jnp.where(low, v0, pltpu.roll(v1, BLK, 1))
+                out[odd, :] = jnp.where(low, pltpu.roll(v0, BLK, 1), v1)
+        yield
+
+
+def spread_chunk(chunk, held, l_ref, p_ref, pair_of, first_row, half):
+    rows = chunk // BLK
+    pitch = held[0].shape[0] // rows
+    to = pl.ds(pl.multiple_of(first_row, 16), rows)
+    for c in range(half):
+        take = pl.ds(c, rows, stride=pitch)
+        l_ref[pair_of, c, to, :] = held[0][take, :].astype(BF16)
+        right = held[1][take, :].astype(BF16)
+        p_ref[2 * pair_of, c, to, :] = right
+        p_ref[2 * pair_of + 1, c, to, :] = pltpu.roll(right, BLK, 1)
+        if c % 8 == 7:
+            yield
+
+
+def two_chunks(sides_at, n, chunk, held, l_ref, p_ref, pair_of, first_row, half):
+    rows = chunk // BLK
+    steps = [
+        pair_chunk(functools.partial(sides_at, 2 * n + k), chunk, held[2 * k : 2 * k + 2], half)
+        for k in range(2)
+    ]
+    spreads = [
+        spread_chunk(
+            chunk, held[2 * k : 2 * k + 2], l_ref, p_ref, pair_of, first_row + (2 * n + k) * rows, half
+        )
+        for k in range(2)
+    ]
+    for _ in steps[0]:
+        pass
+    for _ in zip(steps[1], spreads[0]):
+        pass
+    for _ in spreads[0]:
+        pass
+    for _ in spreads[1]:
+        pass
+
+
+def cells_at(n, chunk, start):
+    return pl.ds(pl.multiple_of(n * chunk + start, LANES), LANES)
+
+
+def own_kernel(chunk, *refs):
+    t_ref = refs[0]
+    sources = refs[1:8]
+    l_ref, p_ref, gate_ref, w_ref, v_ref, gain_ref = refs[8:14]
+    targets = refs[14:21]
+    held, sems = refs[21:25], refs[25]
+    copies = [
+        pltpu.make_async_copy(source, target, sems.at[at])
+        for at, (source, target) in enumerate(zip(sources, targets))
+    ]
+    for copy in copies:
+        copy.start()
     half = l_ref.shape[1]
-    if gated:
-        w_ref[...] = weight[: 4 * half]
-        mine = g_ref[pl.ds(pl.multiple_of(lax.axis_index("chan") * half, half), half), :]
-        other = g_ref[pl.ds(pl.multiple_of((1 - lax.axis_index("chan")) * half, half), half), :]
-        gain_ref[...] = jnp.broadcast_to(jnp.concatenate([mine, other], axis=0), gain_ref.shape)
-        v_ref[...] = prepared(0.5 * u_ref[...].astype(F32), h_ref[...])
-
-        @pl.loop(0, half)
-        def _(c):
-            p_ref[4, c] = jnp.zeros((BLK, LANES), BF16)
-
-    low = lax.broadcasted_iota(jnp.int32, (8, LANES), 1) < BLK
-    high_rows = chunk // BLK
-    pitch = sl.shape[0] // high_rows
-
-    def step(blocks, n, to):
-        for start in range(0, chunk, LANES):
-            at = pl.ds(pl.multiple_of(n * chunk + start, LANES), LANES)
-            sides = []
-            for x, (m, t) in enumerate(blocks):
-                normed = normed_of(m[:, at], t[:, at], gain_ref[...])
-                y = jnp.dot(weight, normed, preferred_element_type=F32)
-                if gated:
-                    gate_ref[x, :, at] = (jnp.tanh(y[4 * half :]) + 1.0).astype(BF16)
-                for side in range(2):
-                    groups = []
-                    for row in range(2 * half * side, 2 * half * (side + 1), 16):
-                        groups.append((jnp.tanh(y[row : row + 8]) + 1.0) * y[row + 8 : row + 16])
-                    sides.append(groups)
-            i = start // BLK
-            for row in range(0, half, 8):
-                l0, r0, l1, r1 = (groups[row // 8] for groups in sides)
-                even = slice(i * pitch + row, i * pitch + row + 8)
-                odd = slice((i + 1) * pitch + row, (i + 1) * pitch + row + 8)
-                for held, v0, v1 in ((sl, l0, l1), (sp, r0, r1)):
-                    held[even, :] = jnp.where(low, v0, pltpu.roll(v1, BLK, 1))
-                    held[odd, :] = jnp.where(low, pltpu.roll(v0, BLK, 1), v1)
-
-        @pl.loop(0, half, unroll=8)
-        def _(c):
-            take = pl.ds(c, high_rows, stride=pitch)
-            l_ref[pair_of, c, to, :] = sl[take, :].astype(BF16)
-            right = sp[take, :].astype(BF16)
-            p_ref[2 * pair_of, c, to, :] = right
-            p_ref[2 * pair_of + 1, c, to, :] = pltpu.roll(right, BLK, 1)
-
-    for (start, size), blocks in zip(cuts, pieces):
-
-        @pl.loop(0, size // chunk)
-        def _(n):
-            first = n * high_rows + (offset + start) // BLK
-            step(blocks, n, pl.ds(pl.multiple_of(first, 16), high_rows))
-
-
-def project(operands, half, cuts, chunk, gated, offset=0):
-    out_shape = [
-        pltpu.VMEM((2, half, BLK, LANES), BF16),
-        pltpu.VMEM((5, half, BLK, LANES), BF16),
-    ]
-    aliases = {}
-    if gated:
-        out_shape += [
-            pltpu.VMEM((2, half, BLK * BLK), BF16),
-            pltpu.VMEM((4 * half, 2 * half), BF16),
-            pltpu.VMEM((half, 2 * half), BF16),
-            pltpu.VMEM((2 * half, LANES), F32),
+
+    @pl.loop(0, half)
+    def _(c):
+        p_ref[4, c] = jnp.zeros((BLK, LANES), BF16)
+
+    for copy in copies:
+        copy.wait()
+    m_ref, a_ref, b_ref, o_ref, u_ref, g_ref, h_ref = targets
+    rows = gated_rows(a_ref) + gated_rows(b_ref) + [0.5 * o_ref[...].astype(F32)]
+    weight = prepared(jnp.concatenate(rows, axis=0))
+    w_ref[...] = weight[: 4 * half]
+    v_ref[...] = prepared(0.5 * u_ref[...].astype(F32), h_ref[...])
+    across = jnp.transpose(jnp.broadcast_to(g_ref[...], (2 * half, LANES)))
+    in_order = lax.axis_index("chan") == 0
+    gain_ref[:half] = jnp.where(in_order, across[:half], across[half:])
+    gain_ref[half:] = jnp.where(in_order, across[half:], across[:half])
+
+    def sides_at(n, start):
+        at = cells_at(n, chunk, start)
+        both = []
+        for x in range(2):
+            sides, rest = gated_sides(m_ref[x, :, at], t_ref[x, :, at], weight, gain_ref[...], half)
+            gate_ref[x, :, at] = (jnp.tanh(rest) + 1.0).astype(BF16)
+            both.append(sides)
+        return both
+
+    @pl.loop(0, m_ref.shape[-1] // chunk // 2)
+    def _(n):
+        two_chunks(sides_at, n, chunk, held, l_ref, p_ref, 0, 0, half)
+
+
+def both_kernel(chunk, first_row, m0, m1, *refs):
+    theirs = refs[:4]
+    w_ref, gain_ref, _, _, l_ref, p_ref = refs[4:10]
+    held = refs[10:]
+    half = l_ref.shape[1]
+    weight = w_ref[...]
+
+    def sides_at(n, start):
+        at = cells_at(n, chunk, start)
+        within = pl.ds(start, LANES)
+        return [
+            gated_sides(m[:, at], theirs[2 * n + x][:, within], weight, gain_ref[...], half)[0]
+            for x, m in enumerate((m0, m1))
         ]
-    else:
-        aliases = {len(operands) - 2: 0, len(operands) - 1: 1}
-        operands = operands[:-2] + [
-            pltpu.with_memory_space_constraint(value, pltpu.VMEM) for value in operands[-2:]
-        ]
+
+    two_chunks(sides_at, 0, chunk, held, l_ref, p_ref, 1, first_row, half)
+
+
+def early_kernel(chunk, m_ref, t0_ref, t1_ref, w_ref, gain_ref, l_ref, r_ref):
+    weight = w_ref[...]
+    half = m_ref.shape[0]
+    for n, t_ref in enumerate((t0_ref, t1_ref)):
+
+        @pl.loop(0, chunk, step=4 * LANES)
+        def _(base):
+            for start in range(0, 4 * LANES, LANES):
+                within = pl.ds(pl.multiple_of(base + start, LANES), LANES)
+                at = pl.ds(pl.multiple_of(n * chunk + base + start, LANES), LANES)
+                sides, _ = gated_sides(m_ref[:, at], t_ref[:, within], weight, gain_ref[...], half)
+                for out, groups in zip((l_ref, r_ref), sides):
+                    for row, group in enumerate(groups):
+                        out[8 * row : 8 * row + 8, at] = group
+
+
+def late_kernel(chunk, first_row, m_ref, t_ref, l0_ref, r0_ref, w_ref, gain_ref, *refs):
+    l_ref, p_ref = refs[2:4]
+    held = refs[4:]
+    half = l_ref.shape[1]
+    weight = w_ref[...]
+
+    def sides_at(n, start):
+        at = cells_at(n, chunk, start)
+        first = [[ref[row : row + 8, at] for row in range(0, half, 8)] for ref in (l0_ref, r0_ref)]
+        return first, gated_sides(m_ref[:, at], t_ref[:, at], weight, gain_ref[...], half)[0]
+
+    two_chunks(sides_at, 0, chunk, held, l_ref, p_ref, 1, first_row, half)
+
+
+def call(kernel, name, operands, out_shape, scratch, aliased=0, hbm=0):
     vmem = pl.BlockSpec(memory_space=pltpu.VMEM)
+    plain = len(operands) - aliased
+    operands = operands[:plain] + [
+        pltpu.with_memory_space_constraint(value, pltpu.VMEM) for value in operands[plain:]
+    ]
+    operands = operands[: len(operands) - hbm] + [
+        pltpu.with_memory_space_constraint(value, pltpu.HBM)
+        for value in operands[len(operands) - hbm :]
+    ]
+    specs = [vmem] * (len(operands) - hbm) + [pl.BlockSpec(memory_space=pltpu.HBM)] * hbm
     return pl.pallas_call(
-        functools.partial(project_kernel, chunk, cuts, offset, gated),
-        in_specs=[vmem] * len(operands),
+        kernel,
+        in_specs=specs,
         out_specs=[vmem] * len(out_shape),
         out_shape=out_shape,
-        scratch_shapes=[pltpu.VMEM((chunk // BLK * (half + 8), LANES), F32)] * 2,
-        input_output_aliases=aliases,
+        scratch_shapes=scratch,
+        input_output_aliases={plain + at: at for at in range(aliased)},
         compiler_params=pltpu.CompilerParams(vmem_limit_bytes=VMEM_LIMIT),
-        name="project_own" if gated else "project_fetched",
+        name=name,
     )(*operands)
 
 
-def triplet_kernel(s, slots, triplets, group, a_ref, b_ref, n_ref, l_ref, p_ref, out_ref, *accs):
+def operand_shapes(half):
+    return [pltpu.VMEM((2, half, BLK, LANES), BF16), pltpu.VMEM((5, half, BLK, LANES), BF16)]
+
+
+def chunk_scratch(half, chunk):
+    return [pltpu.VMEM((chunk // BLK * (half + 8), LANES), F32)] * 4
+
+
+def triplet_kernel(s, slots, triplets, group, a_ref, b_ref, n_ref, l_ref, p_ref, out_ref, acc):
     me, behind, ahead = neighbour_tiles()
     low = lax.broadcasted_iota(jnp.int32, (BLK, LANES), 1) < BLK
     block = me * slots + s
@@ -245,28 +329,31 @@
 
     take_low = lax.broadcasted_iota(jnp.int32, (group, LANES), 1) < BLK
     half = l_ref.shape[1]
-    pitch = accs[0].shape[0] // BLK
-
-    @pl.loop(0, half, step=group * len(accs))
+    pitch = acc.shape[0] // BLK
+
+    def update_of(c):
+        lhs = jnp.concatenate([l_ref[0, c], l_ref[1, c]], axis=1)
+        parts = [p_ref[pick, c] for pick in picks]
+        rhs = jnp.concatenate(
+            [jnp.where(low, parts[0], parts[1]), jnp.where(low, parts[2], parts[3])], axis=1
+        )
+        return lax.dot_general(lhs, rhs, (((1,), (1,)), ((), ())), preferred_element_type=F32)
+
+    @pl.loop(0, half // 2, step=group)
     def _(base):
-        for which, acc in enumerate(accs):
-            for at in range(group):
-                c = base + which * group + at
-                lhs = jnp.concatenate([l_ref[0, c], l_ref[1, c]], axis=1)
-                parts = [p_ref[pick, c] for pick in picks]
-                rhs = jnp.concatenate(
-                    [jnp.where(low, parts[0], parts[1]), jnp.where(low, parts[2], parts[3])], axis=1
-                )
-                acc[pl.ds(at, BLK, stride=pitch), :BLK] = lax.dot_general(
-                    lhs, rhs, (((1,), (1,)), ((), ())), preferred_element_type=F32
-                )
-            rows = pl.ds(pl.multiple_of(base + which * group, group), group)
-            for t in range(BLK // 2):
-                even = acc[2 * t * pitch : 2 * t * pitch + group, :]
-                odd = acc[(2 * t + 1) * pitch : (2 * t + 1) * pitch + group, :]
-                out_ref[rows, t * LANES : (t + 1) * LANES] = jnp.where(
-                    take_low, even, pltpu.roll(odd, BLK, 1)
-                ).astype(BF16)
+        for at in range(group):
+            c = base + at
+            acc[pl.ds(at, BLK, stride=pitch), :] = jnp.concatenate(
+                [update_of(c), update_of(c + half // 2)], axis=1
+            )
+        rows = pl.ds(pl.multiple_of(base, group), group)
+        upper = pl.ds(pl.multiple_of(base + half // 2, group), group)
+        for t in range(BLK // 2):
+            even = acc[2 * t * pitch : 2 * t * pitch + group, :]
+            odd = acc[(2 * t + 1) * pitch : (2 * t + 1) * pitch + group, :]
+            to = slice(t * LANES, (t + 1) * LANES)
+            out_ref[rows, to] = jnp.where(take_low, even, pltpu.roll(odd, BLK, 1)).astype(BF16)
+            out_ref[upper, to] = jnp.where(take_low, pltpu.roll(even, BLK, 1), odd).astype(BF16)
 
 
 def triplet_sum(s, lefts, rights, a_slots, b_slots, counts, slots, group):
@@ -281,7 +368,7 @@
         in_specs=[smem, smem, smem, vmem, vmem],
         out_specs=vmem,
         out_shape=pltpu.VMEM((half, BLK * BLK), BF16),
-        scratch_shapes=[pltpu.VMEM((BLK * (group + 8), LANES), F32)] * 2,
+        scratch_shapes=[pltpu.VMEM((BLK * (group + 8), LANES), F32)],
         compiler_params=pltpu.CompilerParams(vmem_limit_bytes=VMEM_LIMIT),
         name="triplets",
     )(a_slots, b_slots, counts, lefts, rights)
@@ -332,7 +419,7 @@
         operands.append(before)
         out_shape = jax.ShapeDtypeStruct(gate.shape, BF16)
         out_specs = pl.BlockSpec(memory_space=pltpu.HBM)
-        scratch = [pltpu.VMEM(mine.shape, BF16), pltpu.SemaphoreType.DMA((5,))]
+        scratch = [pltpu.VMEM(mine.shape, BF16), pltpu.SemaphoreType.DMA((9,))]
     return pl.pallas_call(
         functools.partial(finish_kernel, s),
         in_specs=[vmem] * len(operands),
@@ -368,7 +455,7 @@
         jnp.swapaxes(b_weight, 1, 2),
         out_gate_weight.T,
         out_weight.T,
-        ln_in_gain[:, None],
+        ln_in_gain[None, :],
         ln_out_gain[None, :],
     ]
 
@@ -379,25 +466,60 @@
         (lax.ppermute(chosen[2 * n], "row", up), lax.ppermute(chosen[2 * n + 1], "row", down))
         for n in range(len(cuts))
     ]
-    lefts, rights, gate, weight, last_weight, gain = project(
-        [pair, pair_other, *weights], half, ((0, cells),), 1024, True
-    )
-    for (start, size), (from_behind, from_ahead) in zip(cuts, arrived):
-        from_behind, from_ahead, lefts = lax.optimization_barrier((from_behind, from_ahead, lefts))
-        parts = ((0, size),) if start else ((0, size // 2), (size // 2, size // 2))
-        others = [
-            lax.ppermute(lax.slice_in_dim(value, at, at + wide, axis=1), "chan", swap)
-            for at, wide in parts
-            for value in (from_behind, from_ahead)
-        ]
-        lefts, rights = project(
-            [from_behind, from_ahead, *others, weight, gain, lefts, rights],
-            half,
-            parts,
-            1024,
-            False,
-            start,
-        )
+    chunk = cells // 4
+    sources = [pair, *weights]
+    lefts, rights, gate, weight, last_weight, gain = call(
+        functools.partial(own_kernel, chunk),
+        "project_own",
+        [pair_other, *sources],
+        operand_shapes(half)
+        + [
+            pltpu.VMEM((slots, half, cells), BF16),
+            pltpu.VMEM((4 * half, 2 * half), BF16),
+            pltpu.VMEM((half, 2 * half), BF16),
+            pltpu.VMEM((2 * half, LANES), F32),
+        ],
+        [pltpu.VMEM(value.shape, value.dtype) for value in sources]
+        + chunk_scratch(half, chunk)
+        + [pltpu.SemaphoreType.DMA((len(sources),))],
+        hbm=len(sources),
+    )
+    from_behind, from_ahead, lefts = lax.optimization_barrier((*arrived[0], lefts))
+    others = [
+        lax.ppermute(lax.slice_in_dim(value, at, at + chunk, axis=1), "chan", swap)
+        for at in (0, chunk)
+        for value in (from_behind, from_ahead)
+    ]
+    lefts, rights = call(
+        functools.partial(both_kernel, chunk, 0),
+        "project_first",
+        [from_behind, from_ahead, *others, weight, gain, lefts, rights],
+        operand_shapes(half),
+        chunk_scratch(half, chunk),
+        aliased=2,
+    )
+    from_behind, lefts = lax.optimization_barrier((arrived[1][0], lefts))
+    others = [
+        lax.ppermute(lax.slice_in_dim(from_behind, at, at + chunk, axis=1), "chan", swap)
+        for at in (0, chunk)
+    ]
+    early = call(
+        functools.partial(early_kernel, chunk),
+        "project_early",
+        [from_behind, *others, weight, gain],
+        [pltpu.VMEM((half, 2 * chunk), F32)] * 2,
+        [],
+    )
+    from_ahead, early = lax.optimization_barrier((arrived[1][1], early))
+    ahead_other = lax.ppermute(from_ahead, "chan", swap)
+    lefts, rights = call(
+        functools.partial(late_kernel, chunk, BLK // 2),
+        "project_late",
+        [from_ahead, ahead_other, *early, weight, gain, lefts, rights],
+        operand_shapes(half),
+        chunk_scratch(half, chunk),
+        aliased=2,
+    )
     updates = []
     for s in range(slots):
         update = triplet_sum(s, lefts, rights, a_slots, b_slots, counts, slots, 16)

time: 43.8 us -> 42.9 us (0.979)
  waiting for transfers between devices: 5.16 us -> 12.7 us
  local copies, waits for them, and re-layouts: 5.64 us -> 0.07 us
  Pallas kernels: 21.4 us -> 19.6 us
  starting transfers between devices: 11 us -> 10.3 us
    ppermute x2, waiting for transfers between devices: 1.64 us -> 7.46 us  [per_device(): lax.ppermute(chosen[2 * n + 1], 'row', down)]
    unnamed x18 -> x6, local copies, waits for them, and re-layouts: 4.84 us -> 0.02 us
    pallas_call x3 -> x4, Pallas kernels: 12.2 us -> 9.68 us  [call(): pl.pallas_call(kernel, in_specs=specs, out_specs=[vmem] * len(out_shape),...]
    ppermute x2, waiting for transfers between devices: 0.01 us -> 2.19 us  [per_device(): lax.ppermute(chosen[2 * n], 'row', up)]
    ppermute x2, starting transfers between devices: 5.91 us -> 4.78 us  [per_device(): lax.ppermute(chosen[2 * n + 1], 'row', down)]
    broadcast_in_dim x1 -> x0, local copies, waits for them, and re-layouts: 0.76 us -> none  [per_device(): ln_in_gain[:, None]]
    pallas_call x2, Pallas kernels: 3.27 us -> 3.92 us  [finish(): pl.pallas_call(functools.partial(finish_kernel, s), in_specs=[vmem] * len...]
    ppermute x6 -> x7, waiting for transfers between devices: 3.27 us -> 2.77 us  [the longest x1 1.5 us: per_device(): ahead_other = lax.ppermute(from_ahead, 'chan', swap)]
  transfers between devices with their start and end apart: 13 -> 14, of which waited for: 7 -> 9; matrix products, arithmetic and copies ran while one was open for 2% -> 0% of each run, Pallas kernels for 33% -> 32%
where the time goes in v9:
time: 42.9 us; the launch traced here: 42.7 us
  Pallas kernels  19.6 us (46%)
  waiting for transfers between devices  12.7 us (30%)
  starting transfers between devices  10.3 us (24%)
    pallas_call x4, Pallas kernels, call(): pl.pallas_call(kernel, in_specs=specs, out_specs=[vmem] * len(out_shape),...  9.68 us
    ppermute x2, waiting for transfers between devices, per_device(): lax.ppermute(chosen[2 * n + 1], 'row', down)  7.46 us
    ppermute x2, starting transfers between devices, per_device(): lax.ppermute(chosen[2 * n + 1], 'row', down)  4.78 us
    pallas_call x2, Pallas kernels, triplet_sum(): pl.pallas_call(functools.partial(triplet_kernel, s, slots, a_slots.shape[...  3.94 us
    pallas_call x2, Pallas kernels, finish(): pl.pallas_call(functools.partial(finish_kernel, s), in_specs=[vmem] * len...  3.92 us
    ppermute x2, starting transfers between devices, per_device(): lax.ppermute(chosen[2 * n], 'row', up)  2.63 us
    ppermute x2, waiting for transfers between devices, per_device(): lax.ppermute(chosen[2 * n], 'row', up)  2.19 us
    pallas_call x1, Pallas kernels, select_blocks(): pl.pallas_call(functools.partial(select_kernel, slots, a_slots.shape[0],...  2.02 us
  transfers between devices with their start and end apart: 14, of which 9 were waited for; matrix products, arithmetic and copies ran while one was open for 0% of the time, Pallas kernels for 32%

profile of v9, /device:TPU:0, one launch (start us, length us, event | category | flops | bytes accessed | tf_op | source)
XLA Modules:
  0.0 42.7 jit_solution(5417859998982996074)
XLA Ops:
  0.0 0.5 %collective-permute-start.4 = (bf16[2,64,4096]{2,1,0:T(8,128)(2,1)}, bf16[2,64,4096]{2,1,0:T(8,128)(2,1)S(1)}, u32[]{:S(2)}, u32[]{:S(2)}) collective-permute-start(bf16[2,64,4096]{2,1,0:T(8,128)(2,1)} %refs_1_.1), channel_id=1, source_target_pairs={{0,1},{1,0},{2,3},{3,2},{4,5},{5,4},{6,7},{7,6},{8,9},{9,8},{10,11... | collective-permute-start | bytes 3145736 | tf_op jit(solution)/shard_map/ppermute | solution.py:462
  0.5 2.0 %select_blocks.1 = (bf16[64,2048]{1,0:T(8,128)(2,1)S(1)}, bf16[64,2048]{1,0:T(8,128)(2,1)S(1)}, bf16[64,2048]{1,0:T(8,128)(2,1)S(1)}, bf16[64,2048]{1,0:T(8,128)(2,1)S(1)}) custom-call(s32[4,16]{1,0:T(4,128)} %bitcast.8, s32[4,16]{1,0:T(4,128)} %bitcast.11, s32[16]{0:T(128)} %n_ref.5, bf16[2,64,4096]{2,1,0:T(8,128)(2,1)} %refs_1_.1), custom_call_target="tpu_custom_call" | custom-call | tf_op jit(solution)/shard_map/select_blocks/pallas_call | solution.py:69
  2.5 2.6 %collective-permute-start.2 = (bf16[64,2048]{1,0:T(8,128)(2,1)S(1)}, bf16[64,2048]{1,0:T(8,128)(2,1)S(1)}, u32[]{:S(2)}, u32[]{:S(2)}) collective-permute-start(bf16[64,2048]{1,0:T(8,128)(2,1)S(1)} %get-tuple-element.32), channel_id=1, source_target_pairs={{0,4},{4,8},{8,12},{12,0},{1,5},{5,9},{9,13},{13,1},{2,6},{6,10},{... | collective-permute-start | bytes 786440 | tf_op jit(solution)/shard_map/ppermute | solution.py:466
  5.1 2.1 %collective-permute-start.3 = (bf16[64,2048]{1,0:T(8,128)(2,1)S(1)}, bf16[64,2048]{1,0:T(8,128)(2,1)S(1)}, u32[]{:S(2)}, u32[]{:S(2)}) collective-permute-start(bf16[64,2048]{1,0:T(8,128)(2,1)S(1)} %get-tuple-element.33), channel_id=1, source_target_pairs={{0,12},{4,0},{8,4},{12,8},{1,13},{5,1},{9,5},{13,9},{2,14},{6,2},{... | collective-permute-start | bytes 786440 | tf_op jit(solution)/shard_map/ppermute | solution.py:466
  7.2 0.0 collective-permute-start.1
  7.2 0.0 collective-permute-done.4.refs_0_
  7.2 5.4 %project_own.1 = (bf16[2,64,64,128]{3,2,1,0:T(8,128)(2,1)S(1)}, bf16[5,64,64,128]{3,2,1,0:T(8,128)(2,1)S(1)}, bf16[2,64,4096]{2,1,0:T(8,128)(2,1)S(1)}, bf16[256...) custom-call(bf16[2,64,4096]{2,1,0:T(8,128)(2,1)S(1)} %collective-permute-done.4.refs_0_, ...), custom_call_target="tpu_custom_call" | custom-call | tf_op jit(solution)/shard_map/project_own/pallas_call | solution.py:281
  12.6 1.7 %collective-permute-done.2.m0 = bf16[64,2048]{1,0:T(8,128)(2,1)S(1)} collective-permute-done((bf16[64,2048]{1,0:T(8,128)(2,1)S(1)}, bf16[64,2048]{1,0:T(8,128)(2,1)S(1)}, u32[]{:S(2)}, u32[]{:S(2)}) %collective-permute-start.2) | collective-permute-done | bytes 262176 | tf_op jit(solution)/shard_map/ppermute | solution.py:466
  14.3 4.8 %collective-permute-done.3.m1 = bf16[64,2048]{1,0:T(8,128)(2,1)S(1)} collective-permute-done((bf16[64,2048]{1,0:T(8,128)(2,1)S(1)}, bf16[64,2048]{1,0:T(8,128)(2,1)S(1)}, u32[]{:S(2)}, u32[]{:S(2)}) %collective-permute-start.3) | collective-permute-done | bytes 262176 | tf_op jit(solution)/shard_map/ppermute | solution.py:466
  19.2 0.1 collective-permute-start.7
  19.3 0.5 %collective-permute-start.5 = (bf16[64,1024]{1,0:T(8,128)(2,1)S(1)}, bf16[64,1024]{1,0:T(8,128)(2,1)S(1)}, u32[]{:S(2)}, u32[]{:S(2)}) collective-permute-start(bf16[64,1024]{1,0:T(8,128)(2,1)S(1)} %get-tuple-element.60), channel_id=1, source_target_pairs={{0,1},{1,0},{2,3},{3,2},{4,5},{5,4},{6,7},{7,6},{8,9},{9,8},{10,11... | collective-permute-start | bytes 393224 | tf_op jit(solution)/shard_map/ppermute | solution.py:489
  19.8 0.1 collective-permute-start.8
  19.9 0.4 %collective-permute-start.6 = (bf16[64,1024]{1,0:T(8,128)(2,1)S(1)}, bf16[64,1024]{1,0:T(8,128)(2,1)S(1)}, u32[]{:S(2)}, u32[]{:S(2)}) collective-permute-start(bf16[64,1024]{1,0:T(8,128)(2,1)S(1)} %get-tuple-element.58), channel_id=1, source_target_pairs={{0,1},{1,0},{2,3},{3,2},{4,5},{5,4},{6,7},{7,6},{8,9},{9,8},{10,11... | collective-permute-start | bytes 393224 | tf_op jit(solution)/shard_map/ppermute | solution.py:489
  20.4 0.2 collective-permute-done.7.refs_2_
  20.6 2.7 %collective-permute-start = (bf16[64,2048]{1,0:T(8,128)(2,1)S(1)}, bf16[64,2048]{1,0:T(8,128)(2,1)S(1)}, u32[]{:S(2)}, u32[]{:S(2)}) collective-permute-start(bf16[64,2048]{1,0:T(8,128)(2,1)S(1)} %get-tuple-element.30), channel_id=1, source_target_pairs={{0,12},{4,0},{8,4},{12,8},{1,13},{5,1},{9,5},{13,9},{2,14},{6,2},{... | collective-permute-start | bytes 786440 | tf_op jit(solution)/shard_map/ppermute | solution.py:466
  23.3 0.0 collective-permute-done.5.refs_0_
  23.3 0.0 collective-permute-done.8.refs_3_
  23.3 0.0 collective-permute-done.6.refs_1_
  23.3 1.8 %project_first.1 = (bf16[2,64,64,128]{3,2,1,0:T(8,128)(2,1)S(1)}, bf16[5,64,64,128]{3,2,1,0:T(8,128)(2,1)S(1)}) custom-call(bf16[64,2048]{1,0:T(8,128)(2,1)S(1)} %collective-permute-done.2.m0, bf16[64,2048]{1,0:T(8,128)(2,1)S(1)} %collective-permute-done.3.m1, ...), custom_call_target="tpu_custom_call", output_to_operand_aliasing={{0}: (8, {}), {1}: (9, {})} | custom-call | tf_op jit(solution)/shard_map/project_first/pallas_call | solution.py:281
  25.1 0.0 copy-start
  25.1 0.0 copy-start.1
  25.1 0.0 copy-start.2
  25.1 0.5 %collective-permute-done.1.m_ref = bf16[64,2048]{1,0:T(8,128)(2,1)S(1)} collective-permute-done((bf16[64,2048]{1,0:T(8,128)(2,1)S(1)}, bf16[64,2048]{1,0:T(8,128)(2,1)S(1)}, u32[]{:S(2)}, u32[]{:S(2)}) %collective-permute-start.1) | collective-permute-done | bytes 262176 | tf_op jit(solution)/shard_map/ppermute | solution.py:466
  25.6 0.1 collective-permute-start.10
  25.7 0.5 %collective-permute-start.9 = (bf16[64,1024]{1,0:T(8,128)(2,1)S(1)}, bf16[64,1024]{1,0:T(8,128)(2,1)S(1)}, u32[]{:S(2)}, u32[]{:S(2)}) collective-permute-start(bf16[64,1024]{1,0:T(8,128)(2,1)S(1)} %get-tuple-element.56), channel_id=1, source_target_pairs={{0,1},{1,0},{2,3},{3,2},{4,5},{5,4},{6,7},{7,6},{8,9},{9,8},{10,11... | collective-permute-start | bytes 393224 | tf_op jit(solution)/shard_map/ppermute | solution.py:503
  26.2 0.8 %collective-permute-done.10.t1_ref = bf16[64,1024]{1,0:T(8,128)(2,1)S(1)} collective-permute-done((bf16[64,1024]{1,0:T(8,128)(2,1)S(1)}, bf16[64,1024]{1,0:T(8,128)(2,1)S(1)}, u32[]{:S(2)}, u32[]{:S(2)}) %collective-permute-start.10) | collective-permute-done | bytes 131104 | tf_op jit(solution)/shard_map/ppermute | solution.py:503
  27.0 0.2 collective-permute-done.9.t0_ref
  27.2 1.2 %project_early.1 = (f32[64,2048]{1,0:T(8,128)S(1)}, f32[64,2048]{1,0:T(8,128)S(1)}) custom-call(bf16[64,2048]{1,0:T(8,128)(2,1)S(1)} %collective-permute-done.1.m_ref, bf16[64,1024]{1,0:T(8,128)(2,1)S(1)} %collective-permute-done.9.t0_ref, bf16[64,1024]{1,0:T(8,128)(2,1)S(1)} %collective-permute-done.10.t1_ref, ...), custom_call_target="tpu_custom_call" | custom-call | tf_op jit(solution)/shard_map/project_early/pallas_call | solution.py:281
  28.4 2.6 %collective-permute-done.m_ref = bf16[64,2048]{1,0:T(8,128)(2,1)S(1)} collective-permute-done((bf16[64,2048]{1,0:T(8,128)(2,1)S(1)}, bf16[64,2048]{1,0:T(8,128)(2,1)S(1)}, u32[]{:S(2)}, u32[]{:S(2)}) %collective-permute-start) | collective-permute-done | bytes 262176 | tf_op jit(solution)/shard_map/ppermute | solution.py:466
  31.0 0.0 collective-permute-start.11
  31.1 1.5 %collective-permute-done.11.t_ref = bf16[64,2048]{1,0:T(8,128)(2,1)S(1)} collective-permute-done((bf16[64,2048]{1,0:T(8,128)(2,1)S(1)}, bf16[64,2048]{1,0:T(8,128)(2,1)S(1)}, u32[]{:S(2)}, u32[]{:S(2)}) %collective-permute-start.11) | collective-permute-done | bytes 262176 | tf_op jit(solution)/shard_map/ppermute | solution.py:514
  32.5 1.4 %project_late.1 = (bf16[2,64,64,128]{3,2,1,0:T(8,128)(2,1)S(1)}, bf16[5,64,64,128]{3,2,1,0:T(8,128)(2,1)S(1)}) custom-call(bf16[64,2048]{1,0:T(8,128)(2,1)S(1)} %collective-permute-done.m_ref, bf16[64,2048]{1,0:T(8,128)(2,1)S(1)} %collective-permute-done.11.t_ref, ...), custom_call_target="tpu_custom_call", output_to_operand_aliasing={{0}: (6, {}), {1}: (7, {})} | custom-call | tf_op jit(solution)/shard_map/project_late/pallas_call | solution.py:281
  33.9 0.0 copy-done
  33.9 0.0 copy-done.1
  33.9 0.0 copy-done.2
  33.9 2.0 %triplets.2.mine_ref = bf16[64,4096]{1,0:T(8,128)(2,1)S(1)} custom-call(s32[4,16]{1,0:T(4,128)S(1)} %bitcast.9, s32[4,16]{1,0:T(4,128)S(1)} %bitcast.12, s32[16]{0:T(128)S(1)} %copy-done.2, bf16[2,64,64,128]{3,2,1,0:T(8,128)(2,1)S(1)} %get-tuple-element.52.l_ref, bf16[5,64,64,128]{3,2,1,0:T(8,128)(2,1)S(1)} %get-tuple-element.51.p_ref), custom_call_target="tpu_custom_call" | custom-call | tf_op jit(solution)/shard_map/triplets/pallas_call | solution.py:366
  35.9 0.2 collective-permute-start.13
  36.1 2.0 %triplets.3.mine_ref = bf16[64,4096]{1,0:T(8,128)(2,1)S(1)} custom-call(s32[4,16]{1,0:T(4,128)S(1)} %bitcast.10, s32[4,16]{1,0:T(4,128)S(1)} %bitcast.13, s32[16]{0:T(128)S(1)} %copy-done.2, bf16[2,64,64,128]{3,2,1,0:T(8,128)(2,1)S(1)} %get-tuple-element.52.l_ref, bf16[5,64,64,128]{3,2,1,0:T(8,128)(2,1)S(1)} %get-tuple-element.51.p_ref), custom_call_target="tpu_custom_call" | custom-call | tf_op jit(solution)/shard_map/triplets/pallas_call | solution.py:366
  38.1 0.4 %collective-permute-start.12 = (bf16[64,4096]{1,0:T(8,128)(2,1)S(1)}, bf16[64,4096]{1,0:T(8,128)(2,1)S(1)}, u32[]{:S(2)}, u32[]{:S(2)}) collective-permute-start(bf16[64,4096]{1,0:T(8,128)(2,1)S(1)} %triplets.3.mine_ref), channel_id=1, source_target_pairs={{0,1},{1,0},{2,3},{3,2},{4,5},{5,4},{6,7},{7,6},{8,9},{9,8},{10,11... | collective-permute-start | bytes 1572872 | tf_op jit(solution)/shard_map/ppermute | solution.py:526
  38.5 0.0 collective-permute-done.13.theirs_ref
  38.5 1.3 %finish.2.refs_0_ = bf16[64,4096]{1,0:T(8,128)(2,1)S(1)} custom-call(bf16[64,4096]{1,0:T(8,128)(2,1)S(1)} %triplets.2.mine_ref, bf16[64,4096]{1,0:T(8,128)(2,1)S(1)} %collective-permute-done.13.theirs_ref, bf16[2,64,4096]{2,1,0:T(8,128)(2,1)S(1)} %get-tuple-element.53.gate_ref, bf16[64,128]{1,0:T(8,128)(2,1)S(1)} %get-tuple-element.54.w_ref), custom_call_target="tpu_custom_call" | custom-call | tf_op jit(solution)/shard_map/finish/pallas_call | solution.py:423
  39.8 0.2 collective-permute-done.12.theirs_ref
  40.1 2.6 %finish.3 = bf16[2,64,4096]{2,1,0:T(8,128)(2,1)} custom-call(bf16[64,4096]{1,0:T(8,128)(2,1)S(1)} %triplets.3.mine_ref, bf16[64,4096]{1,0:T(8,128)(2,1)S(1)} %collective-permute-done.12.theirs_ref, bf16[2,64,4096]{2,1,0:T(8,128)(2,1)S(1)} %get-tuple-element.53.gate_ref, bf16[64,128]{1,0:T(8,128)(2,1)S(1)} %get-tuple-element.54.w_ref, ...), custom_call_target="tpu_custom_call" | custom-call | tf_op jit(solution)/shard_map/finish/pallas_call | solution.py:423
  (3 shorter events, 0.1 us)
Async XLA Ops:
  0.0 7.2 %collective-permute-start.4 = (bf16[2,64,4096]{2,1,0:T(8,128)(2,1)}, bf16[2,64,4096]{2,1,0:T(8,128)(2,1)S(1)}, u32[]{:S(2)}, u32[]{:S(2)}) collective-permute-start(bf16[2,64,4096]{2,1,0:T(8,128)(2,1)} %refs_1_.1), channel_id=1, source_target_pairs={{0,1},{1,0},{2,3},{3,2},{4,5},{5,4},{6,7},{7,6},{8,9},{9,8},{10,11... | collective-permute-start | bytes 3145736 | tf_op jit(solution)/shard_map/ppermute | solution.py:462
  2.5 11.9 %collective-permute-start.2 = (bf16[64,2048]{1,0:T(8,128)(2,1)S(1)}, bf16[64,2048]{1,0:T(8,128)(2,1)S(1)}, u32[]{:S(2)}, u32[]{:S(2)}) collective-permute-start(bf16[64,2048]{1,0:T(8,128)(2,1)S(1)} %get-tuple-element.32), channel_id=1, source_target_pairs={{0,4},{4,8},{8,12},{12,0},{1,5},{5,9},{9,13},{13,1},{2,6},{6,10},{... | collective-permute-start | bytes 786440 | tf_op jit(solution)/shard_map/ppermute | solution.py:466
  5.1 14.1 %collective-permute-start.3 = (bf16[64,2048]{1,0:T(8,128)(2,1)S(1)}, bf16[64,2048]{1,0:T(8,128)(2,1)S(1)}, u32[]{:S(2)}, u32[]{:S(2)}) collective-permute-start(bf16[64,2048]{1,0:T(8,128)(2,1)S(1)} %get-tuple-element.33), channel_id=1, source_target_pairs={{0,12},{4,0},{8,4},{12,8},{1,13},{5,1},{9,5},{13,9},{2,14},{6,2},{... | collective-permute-start | bytes 786440 | tf_op jit(solution)/shard_map/ppermute | solution.py:466
  7.2 18.4 %collective-permute-start.1 = (bf16[64,2048]{1,0:T(8,128)(2,1)S(1)}, bf16[64,2048]{1,0:T(8,128)(2,1)S(1)}, u32[]{:S(2)}, u32[]{:S(2)}) collective-permute-start(bf16[64,2048]{1,0:T(8,128)(2,1)S(1)} %get-tuple-element.31), channel_id=1, source_target_pairs={{0,4},{4,8},{8,12},{12,0},{1,5},{5,9},{9,13},{13,1},{2,6},{6,10},{... | collective-permute-start | bytes 786440 | tf_op jit(solution)/shard_map/ppermute | solution.py:466
  19.2 1.4 %collective-permute-start.7 = (bf16[64,1024]{1,0:T(8,128)(2,1)S(1)}, bf16[64,1024]{1,0:T(8,128)(2,1)S(1)}, u32[]{:S(2)}, u32[]{:S(2)}) collective-permute-start(bf16[64,1024]{1,0:T(8,128)(2,1)S(1)} %get-tuple-element.59), channel_id=1, source_target_pairs={{0,1},{1,0},{2,3},{3,2},{4,5},{5,4},{6,7},{7,6},{8,9},{9,8},{10,11... | collective-permute-start | bytes 393224 | tf_op jit(solution)/shard_map/ppermute | solution.py:489
  19.3 4.0 %collective-permute-start.5 = (bf16[64,1024]{1,0:T(8,128)(2,1)S(1)}, bf16[64,1024]{1,0:T(8,128)(2,1)S(1)}, u32[]{:S(2)}, u32[]{:S(2)}) collective-permute-start(bf16[64,1024]{1,0:T(8,128)(2,1)S(1)} %get-tuple-element.60), channel_id=1, source_target_pairs={{0,1},{1,0},{2,3},{3,2},{4,5},{5,4},{6,7},{7,6},{8,9},{9,8},{10,11... | collective-permute-start | bytes 393224 | tf_op jit(solution)/shard_map/ppermute | solution.py:489
  19.8 3.5 %collective-permute-start.8 = (bf16[64,1024]{1,0:T(8,128)(2,1)S(1)}, bf16[64,1024]{1,0:T(8,128)(2,1)S(1)}, u32[]{:S(2)}, u32[]{:S(2)}) collective-permute-start(bf16[64,1024]{1,0:T(8,128)(2,1)S(1)} %get-tuple-element.57), channel_id=1, source_target_pairs={{0,1},{1,0},{2,3},{3,2},{4,5},{5,4},{6,7},{7,6},{8,9},{9,8},{10,11... | collective-permute-start | bytes 393224 | tf_op jit(solution)/shard_map/ppermute | solution.py:489
  19.9 3.4 %collective-permute-start.6 = (bf16[64,1024]{1,0:T(8,128)(2,1)S(1)}, bf16[64,1024]{1,0:T(8,128)(2,1)S(1)}, u32[]{:S(2)}, u32[]{:S(2)}) collective-permute-start(bf16[64,1024]{1,0:T(8,128)(2,1)S(1)} %get-tuple-element.58), channel_id=1, source_target_pairs={{0,1},{1,0},{2,3},{3,2},{4,5},{5,4},{6,7},{7,6},{8,9},{9,8},{10,11... | collective-permute-start | bytes 393224 | tf_op jit(solution)/shard_map/ppermute | solution.py:489
  20.6 10.4 %collective-permute-start = (bf16[64,2048]{1,0:T(8,128)(2,1)S(1)}, bf16[64,2048]{1,0:T(8,128)(2,1)S(1)}, u32[]{:S(2)}, u32[]{:S(2)}) collective-permute-start(bf16[64,2048]{1,0:T(8,128)(2,1)S(1)} %get-tuple-element.30), channel_id=1, source_target_pairs={{0,12},{4,0},{8,4},{12,8},{1,13},{5,1},{9,5},{13,9},{2,14},{6,2},{... | collective-permute-start | bytes 786440 | tf_op jit(solution)/shard_map/ppermute | solution.py:466
  25.1 8.8 %copy-start = (s32[16,4]{0,1:T(4,128)S(1)}, s32[16,4]{0,1:T(4,128)}, u32[]{:S(2)}) copy-start(s32[16,4]{0,1:T(4,128)} %param.17) | copy-start | bytes 772
  25.1 8.8 %copy-start.1 = (s32[16,4]{0,1:T(4,128)S(1)}, s32[16,4]{0,1:T(4,128)}, u32[]{:S(2)}) copy-start(s32[16,4]{0,1:T(4,128)} %param.18) | copy-start | bytes 772
  25.1 8.8 %copy-start.2 = (s32[16]{0:T(128)S(1)}, s32[16]{0:T(128)}, u32[]{:S(2)}) copy-start(s32[16]{0:T(128)} %n_ref.5) | copy-start | bytes 196
  25.6 1.4 %collective-permute-start.10 = (bf16[64,1024]{1,0:T(8,128)(2,1)S(1)}, bf16[64,1024]{1,0:T(8,128)(2,1)S(1)}, u32[]{:S(2)}, u32[]{:S(2)}) collective-permute-start(bf16[64,1024]{1,0:T(8,128)(2,1)S(1)} %get-tuple-element.55), channel_id=1, source_target_pairs={{0,1},{1,0},{2,3},{3,2},{4,5},{5,4},{6,7},{7,6},{8,9},{9,8},{10,11... | collective-permute-start | bytes 393224 | tf_op jit(solution)/shard_map/ppermute | solution.py:503
  25.7 1.5 %collective-permute-start.9 = (bf16[64,1024]{1,0:T(8,128)(2,1)S(1)}, bf16[64,1024]{1,0:T(8,128)(2,1)S(1)}, u32[]{:S(2)}, u32[]{:S(2)}) collective-permute-start(bf16[64,1024]{1,0:T(8,128)(2,1)S(1)} %get-tuple-element.56), channel_id=1, source_target_pairs={{0,1},{1,0},{2,3},{3,2},{4,5},{5,4},{6,7},{7,6},{8,9},{9,8},{10,11... | collective-permute-start | bytes 393224 | tf_op jit(solution)/shard_map/ppermute | solution.py:503
  31.0 1.5 %collective-permute-start.11 = (bf16[64,2048]{1,0:T(8,128)(2,1)S(1)}, bf16[64,2048]{1,0:T(8,128)(2,1)S(1)}, u32[]{:S(2)}, u32[]{:S(2)}) collective-permute-start(bf16[64,2048]{1,0:T(8,128)(2,1)S(1)} %collective-permute-done.m_ref), channel_id=1, source_target_pairs={{0,1},{1,0},{2,3},{3,2},{4,5},{5,4},{6,7},{7,6},{8,9},{9,8},{10,11... | collective-permute-start | bytes 786440 | tf_op jit(solution)/shard_map/ppermute | solution.py:514
  35.9 2.6 %collective-permute-start.13 = (bf16[64,4096]{1,0:T(8,128)(2,1)S(1)}, bf16[64,4096]{1,0:T(8,128)(2,1)S(1)}, u32[]{:S(2)}, u32[]{:S(2)}) collective-permute-start(bf16[64,4096]{1,0:T(8,128)(2,1)S(1)} %triplets.2.mine_ref), channel_id=1, source_target_pairs={{0,1},{1,0},{2,3},{3,2},{4,5},{5,4},{6,7},{7,6},{8,9},{9,8},{10,11... | collective-permute-start | bytes 1572872 | tf_op jit(solution)/shard_map/ppermute | solution.py:526
  38.1 2.0 %collective-permute-start.12 = (bf16[64,4096]{1,0:T(8,128)(2,1)S(1)}, bf16[64,4096]{1,0:T(8,128)(2,1)S(1)}, u32[]{:S(2)}, u32[]{:S(2)}) collective-permute-start(bf16[64,4096]{1,0:T(8,128)(2,1)S(1)} %triplets.3.mine_ref), channel_id=1, source_target_pairs={{0,1},{1,0},{2,3},{3,2},{4,5},{5,4},{6,7},{7,6},{8,9},{9,8},{10,11... | collective-permute-start | bytes 1572872 | tf_op jit(solution)/shard_map/ppermute | solution.py:526

commit v10 on v9

--- a/solution.py
+++ b/solution.py
@@ -220,51 +220,32 @@
 
 
 def both_kernel(chunk, first_row, m0, m1, *refs):
-    theirs = refs[:4]
-    w_ref, gain_ref, _, _, l_ref, p_ref = refs[4:10]
-    held = refs[10:]
+    theirs = refs[:-10]
+    w_ref, gain_ref, _, _, l_ref, p_ref = refs[-10:-4]
+    held = refs[-4:]
     half = l_ref.shape[1]
     weight = w_ref[...]
+    wide = theirs[0].shape[1]
 
     def sides_at(n, start):
-        at = cells_at(n, chunk, start)
-        within = pl.ds(start, LANES)
-        return [
-            gated_sides(m[:, at], theirs[2 * n + x][:, within], weight, gain_ref[...], half)[0]
-            for x, m in enumerate((m0, m1))
-        ]
+        at = n * chunk + start
+        both = []
+        for x, m in enumerate((m0, m1)):
+            other = theirs[2 * (at // wide) + x][:, at % wide : at % wide + LANES]
+            both.append(
+                gated_sides(m[:, at : at + LANES], other, weight, gain_ref[...], half)[0]
+            )
+        return both
 
     two_chunks(sides_at, 0, chunk, held, l_ref, p_ref, 1, first_row, half)
 
 
-def early_kernel(chunk, m_ref, t0_ref, t1_ref, w_ref, gain_ref, l_ref, r_ref):
-    weight = w_ref[...]
-    half = m_ref.shape[0]
-    for n, t_ref in enumerate((t0_ref, t1_ref)):
-
-        @pl.loop(0, chunk, step=4 * LANES)
-        def _(base):
-            for start in range(0, 4 * LANES, LANES):
-                within = pl.ds(pl.multiple_of(base + start, LANES), LANES)
-                at = pl.ds(pl.multiple_of(n * chunk + base + start, LANES), LANES)
-                sides, _ = gated_sides(m_ref[:, at], t_ref[:, within], weight, gain_ref[...], half)
-                for out, groups in zip((l_ref, r_ref), sides):
-                    for row, group in enumerate(groups):
-                        out[8 * row : 8 * row + 8, at] = group
-
-
-def late_kernel(chunk, first_row, m_ref, t_ref, l0_ref, r0_ref, w_ref, gain_ref, *refs):
-    l_ref, p_ref = refs[2:4]
-    held = refs[4:]
-    half = l_ref.shape[1]
-    weight = w_ref[...]
-
-    def sides_at(n, start):
-        at = cells_at(n, chunk, start)
-        first = [[ref[row : row + 8, at] for row in range(0, half, 8)] for ref in (l0_ref, r0_ref)]
-        return first, gated_sides(m_ref[:, at], t_ref[:, at], weight, gain_ref[...], half)[0]
-
-    two_chunks(sides_at, 0, chunk, held, l_ref, p_ref, 1, first_row, half)
+def operand_shapes(half):
+    return [pltpu.VMEM((2, half, BLK, LANES), BF16), pltpu.VMEM((5, half, BLK, LANES), BF16)]
+
+
+def chunk_scratch(half, chunk):
+    return [pltpu.VMEM((chunk // BLK * (half + 8), LANES), F32)] * 4
 
 
 def call(kernel, name, operands, out_shape, scratch, aliased=0, hbm=0):
@@ -290,142 +271,128 @@
     )(*operands)
 
 
-def operand_shapes(half):
-    return [pltpu.VMEM((2, half, BLK, LANES), BF16), pltpu.VMEM((5, half, BLK, LANES), BF16)]
-
-
-def chunk_scratch(half, chunk):
-    return [pltpu.VMEM((chunk // BLK * (half + 8), LANES), F32)] * 4
-
-
-def triplet_kernel(s, slots, triplets, group, a_ref, b_ref, n_ref, l_ref, p_ref, out_ref, acc):
+def triplet_kernel(slots, triplets, group, first, a_ref, b_ref, n_ref, l_ref, p_ref, *refs):
+    outs, acc = blocks_of(refs[:-1]), refs[-1]
     me, behind, ahead = neighbour_tiles()
     low = lax.broadcasted_iota(jnp.int32, (BLK, LANES), 1) < BLK
-    block = me * slots + s
-    count = n_ref[block]
     picks = []
-    for pair_at in range(2):
-        for part in range(2):
-            chosen = jnp.int32(0)
-            used = jnp.int32(0)
-            for m in range(triplets):
-                left = a_ref[m, block]
-                if pair_at == 0:
-                    hit = left == me * slots + part
-                else:
-                    first = (behind, ahead)[part] * slots
-                    hit = jnp.logical_and(left >= first, left < first + slots)
-                hit = jnp.logical_and(hit, m < count)
-                place = b_ref[m, block] - me * slots
-                from_me = jnp.logical_and(place >= 0, place < slots)
-                right = b_ref[m, block] - behind * slots
-                from_behind = jnp.logical_and(right >= 0, right < slots)
-                place = jnp.where(from_me, place, jnp.where(from_behind, 2, 3))
-                chosen = jnp.where(hit, place, chosen)
-                used = jnp.where(hit, 1, used)
-            if part == 1:
-                chosen = chosen + 1 - 2 * (chosen & 1)
-            picks.append(jnp.where(used == 1, chosen, 4))
+    for s in range(slots):
+        block = me * slots + s
+        count = n_ref[block]
+        for pair_at in range(2):
+            for part in range(2):
+                chosen = jnp.int32(0)
+                used = jnp.int32(0)
+                for m in range(triplets):
+                    left = a_ref[m, block]
+                    if pair_at == 0:
+                        hit = left == me * slots + part
+                    else:
+                        base = (behind, ahead)[part] * slots
+                        hit = jnp.logical_and(left >= base, left < base + slots)
+                    hit = jnp.logical_and(hit, m < count)
+                    place = b_ref[m, block] - me * slots
+                    from_me = jnp.logical_and(place >= 0, place < slots)
+                    right = b_ref[m, block] - behind * slots
+                    from_behind = jnp.logical_and(right >= 0, right < slots)
+                    place = jnp.where(from_me, place, jnp.where(from_behind, 2, 3))
+                    chosen = jnp.where(hit, place, chosen)
+                    used = jnp.where(hit, 1, used)
+                if part == 1:
+                    chosen = chosen + 1 - 2 * (chosen & 1)
+                picks.append(jnp.where(used == 1, chosen, 4))
 
     take_low = lax.broadcasted_iota(jnp.int32, (group, LANES), 1) < BLK
-    half = l_ref.shape[1]
     pitch = acc.shape[0] // BLK
 
-    def update_of(c):
-        lhs = jnp.concatenate([l_ref[0, c], l_ref[1, c]], axis=1)
-        parts = [p_ref[pick, c] for pick in picks]
-        rhs = jnp.concatenate(
-            [jnp.where(low, parts[0], parts[1]), jnp.where(low, parts[2], parts[3])], axis=1
-        )
-        return lax.dot_general(lhs, rhs, (((1,), (1,)), ((), ())), preferred_element_type=F32)
-
-    @pl.loop(0, half // 2, step=group)
+    @pl.loop(0, outs[0].shape[0], step=group)
     def _(base):
         for at in range(group):
-            c = base + at
-            acc[pl.ds(at, BLK, stride=pitch), :] = jnp.concatenate(
-                [update_of(c), update_of(c + half // 2)], axis=1
+            c = first + base + at
+            lhs = jnp.concatenate([l_ref[0, c], l_ref[1, c]], axis=1)
+            parts = [p_ref[pick, c] for pick in picks]
+            tiles = [jnp.where(low, parts[k], parts[k + 1]) for k in range(0, len(parts), 2)]
+            rhs = jnp.concatenate(
+                [jnp.concatenate(tiles[k : k + 2], axis=1) for k in range(0, len(tiles), 2)], axis=0
+            )
+            acc[pl.ds(at, BLK, stride=pitch), :] = lax.dot_general(
+                lhs, rhs, (((1,), (1,)), ((), ())), preferred_element_type=F32
             )
         rows = pl.ds(pl.multiple_of(base, group), group)
-        upper = pl.ds(pl.multiple_of(base + half // 2, group), group)
         for t in range(BLK // 2):
             even = acc[2 * t * pitch : 2 * t * pitch + group, :]
             odd = acc[(2 * t + 1) * pitch : (2 * t + 1) * pitch + group, :]
             to = slice(t * LANES, (t + 1) * LANES)
-            out_ref[rows, to] = jnp.where(take_low, even, pltpu.roll(odd, BLK, 1)).astype(BF16)
-            out_ref[upper, to] = jnp.where(take_low, pltpu.roll(even, BLK, 1), odd).astype(BF16)
-
-
-def triplet_sum(s, lefts, rights, a_slots, b_slots, counts, slots, group):
-    half = lefts.shape[1]
+            outs[0][rows, to] = jnp.where(take_low, even, pltpu.roll(odd, BLK, 1)).astype(BF16)
+            outs[1][rows, to] = jnp.where(take_low, pltpu.roll(even, BLK, 1), odd).astype(BF16)
+
+
+def blocks_of(refs):
+    return [refs[0].at[0], refs[0].at[1]] if len(refs) == 1 else list(refs)
+
+
+def triplet_sum(first, out_shape, lefts, rights, a_slots, b_slots, counts, slots, group):
     smem = pl.BlockSpec(memory_space=pltpu.SMEM)
     vmem = pl.BlockSpec(memory_space=pltpu.VMEM)
     lefts, rights = (
         pltpu.with_memory_space_constraint(value, pltpu.VMEM) for value in (lefts, rights)
     )
     return pl.pallas_call(
-        functools.partial(triplet_kernel, s, slots, a_slots.shape[0], group),
+        functools.partial(triplet_kernel, slots, a_slots.shape[0], group, first),
         in_specs=[smem, smem, smem, vmem, vmem],
-        out_specs=vmem,
-        out_shape=pltpu.VMEM((half, BLK * BLK), BF16),
+        out_specs=[vmem] * len(out_shape),
+        out_shape=out_shape,
         scratch_shapes=[pltpu.VMEM((BLK * (group + 8), LANES), F32)],
         compiler_params=pltpu.CompilerParams(vmem_limit_bytes=VMEM_LIMIT),
         name="triplets",
     )(a_slots, b_slots, counts, lefts, rights)
 
 
-def finish_kernel(s, mine_ref, theirs_ref, gate_ref, w_ref, *refs):
+def finish_kernel(steps, *refs):
+    sides = [[blocks_of(refs[at : at + 1]), blocks_of(refs[at + 1 : at + 3])] for at in (0, 3)]
+    gate_ref, w_ref, out_ref, held, sems = refs[6:]
     weight = w_ref[...]
-    cells = mine_ref.shape[-1]
-    if s == 0:
-        held = refs[0]
-        steps = 4
-    else:
-        before_ref, out_ref, held, sems = refs
-        steps = sems.shape[0] - 1
-        before = pltpu.make_async_copy(before_ref, out_ref.at[0], sems.at[steps])
-        before.start()
+    slots, half, cells = gate_ref.shape
     size = cells // steps
 
-    def copy(n):
+    def copy(s, n):
         to = pl.ds(pl.multiple_of(n * size, size), size)
-        return pltpu.make_async_copy(held.at[:, to], out_ref.at[1, :, to], sems.at[n])
-
-    @pl.loop(0, steps)
-    def _(n):
-        for start in range(0, size, LANES):
-            to = pl.ds(pl.multiple_of(n * size + start, LANES), LANES)
-            normed = normed_of(mine_ref[:, to], theirs_ref[:, to])
-            projected = jnp.dot(weight, normed, preferred_element_type=F32)
-            held[:, to] = (gate_ref[s, :, to].astype(F32) * projected).astype(BF16)
-        if s > 0:
-            copy(n).start()
-
-    if s > 0:
+        return pltpu.make_async_copy(held.at[s, :, to], out_ref.at[s, :, to], sems.at[s, n])
+
+    for s in range(slots):
 
         @pl.loop(0, steps)
         def _(n):
-            copy(n).wait()
-
-        before.wait()
-
-
-def finish(s, mine, theirs, gate, weight, before=None):
+            for start in range(0, size, LANES):
+                to = pl.ds(pl.multiple_of(n * size + start, LANES), LANES)
+                mine, theirs = (
+                    jnp.concatenate([blocks[s][:, to] for blocks in side], axis=0) for side in sides
+                )
+                projected = jnp.dot(
+                    weight, normed_of(mine, theirs), preferred_element_type=F32
+                )
+                held[s, :, to] = (gate_ref[s, :, to].astype(F32) * projected).astype(BF16)
+            copy(s, n).start()
+
+    for s in range(slots):
+
+        @pl.loop(0, steps)
+        def _(n):
+            copy(s, n).wait()
+
+
+def finish(mine, theirs, gate, weight, steps):
     vmem = pl.BlockSpec(memory_space=pltpu.VMEM)
-    operands = [mine, theirs, gate, weight]
-    if s == 0:
-        out_shape, out_specs, scratch = pltpu.VMEM(mine.shape, BF16), vmem, []
-    else:
-        operands.append(before)
-        out_shape = jax.ShapeDtypeStruct(gate.shape, BF16)
-        out_specs = pl.BlockSpec(memory_space=pltpu.HBM)
-        scratch = [pltpu.VMEM(mine.shape, BF16), pltpu.SemaphoreType.DMA((9,))]
+    operands = [*mine, *theirs, gate, weight]
     return pl.pallas_call(
-        functools.partial(finish_kernel, s),
+        functools.partial(finish_kernel, steps),
         in_specs=[vmem] * len(operands),
-        out_specs=out_specs,
-        out_shape=out_shape,
-        scratch_shapes=scratch,
+        out_specs=pl.BlockSpec(memory_space=pltpu.HBM),
+        out_shape=jax.ShapeDtypeStruct(gate.shape, BF16),
+        scratch_shapes=[
+            pltpu.VMEM(gate.shape, BF16),
+            pltpu.SemaphoreType.DMA((gate.shape[0], steps)),
+        ],
         compiler_params=pltpu.CompilerParams(vmem_limit_bytes=VMEM_LIMIT),
         name="finish",
     )(*operands)
@@ -484,52 +451,35 @@
         + [pltpu.SemaphoreType.DMA((len(sources),))],
         hbm=len(sources),
     )
-    from_behind, from_ahead, lefts = lax.optimization_barrier((*arrived[0], lefts))
-    others = [
-        lax.ppermute(lax.slice_in_dim(value, at, at + chunk, axis=1), "chan", swap)
-        for at in (0, chunk)
-        for value in (from_behind, from_ahead)
-    ]
-    lefts, rights = call(
-        functools.partial(both_kernel, chunk, 0),
-        "project_first",
-        [from_behind, from_ahead, *others, weight, gain, lefts, rights],
-        operand_shapes(half),
-        chunk_scratch(half, chunk),
-        aliased=2,
-    )
-    from_behind, lefts = lax.optimization_barrier((arrived[1][0], lefts))
-    others = [
-        lax.ppermute(lax.slice_in_dim(from_behind, at, at + chunk, axis=1), "chan", swap)
-        for at in (0, chunk)
-    ]
-    early = call(
-        functools.partial(early_kernel, chunk),
-        "project_early",
-        [from_behind, *others, weight, gain],
-        [pltpu.VMEM((half, 2 * chunk), F32)] * 2,
-        [],
-    )
-    from_ahead, early = lax.optimization_barrier((arrived[1][1], early))
-    ahead_other = lax.ppermute(from_ahead, "chan", swap)
-    lefts, rights = call(
-        functools.partial(late_kernel, chunk, BLK // 2),
-        "project_late",
-        [from_ahead, ahead_other, *early, weight, gain, lefts, rights],
-        operand_shapes(half),
-        chunk_scratch(half, chunk),
-        aliased=2,
-    )
-    updates = []
-    for s in range(slots):
-        update = triplet_sum(s, lefts, rights, a_slots, b_slots, counts, slots, 16)
-        updates.append((update, lax.ppermute(update, "chan", swap)))
-        if s + 1 < slots:
-            update, lefts = lax.optimization_barrier((update, lefts))
-    out = None
-    for s, (mine, theirs) in enumerate(updates):
-        out = finish(s, mine, theirs, gate, last_weight, out)
-    return out
+    for (start, size), behind_ahead in zip(cuts, arrived):
+        *behind_ahead, lefts = lax.optimization_barrier((*behind_ahead, lefts))
+        wide = chunk if start == 0 else size
+        others = [
+            lax.ppermute(lax.slice_in_dim(value, at, at + wide, axis=1), "chan", swap)
+            for at in range(0, size, wide)
+            for value in behind_ahead
+        ]
+        lefts, rights = call(
+            functools.partial(both_kernel, chunk, start // BLK),
+            "project_fetched",
+            [*behind_ahead, *others, weight, gain, lefts, rights],
+            operand_shapes(half),
+            chunk_scratch(half, chunk),
+            aliased=2,
+        )
+    mine, theirs = [], []
+    wide = half // 2
+    for first, out_shape in (
+        (0, [pltpu.VMEM((slots, wide, cells), BF16)]),
+        (wide, [pltpu.VMEM((wide, cells), BF16)] * slots),
+    ):
+        update, *rest = triplet_sum(
+            first, out_shape, lefts, rights, a_slots, b_slots, counts, slots, 16
+        )
+        mine += [update, *rest]
+        theirs += [lax.ppermute(value, "chan", swap) for value in (update, *rest)]
+        update, lefts = lax.optimization_barrier((update, lefts))
+    return finish(mine, theirs, gate, last_weight, 4)
 
 
 def solution(mesh):

time: 42.9 us -> 43.7 us (1.019)
  Pallas kernels: 19.6 us -> 18.2 us
  waiting for transfers between devices: 12.7 us -> 14.1 us
  starting transfers between devices: 10.3 us -> 11.1 us
    ppermute x9, waiting for transfers between devices: 3.01 us -> 4.67 us  [the longest x6 3.27 us: per_device(): lax.ppermute(lax.slice_in_dim(value, at, at + wide, axis=1), 'chan', swap)]
    ppermute x2, waiting for transfers between devices: 2.19 us -> 1.06 us  [per_device(): lax.ppermute(chosen[2 * n], 'row', up)]
    ppermute x2, starting transfers between devices: 4.78 us -> 5.91 us  [per_device(): lax.ppermute(chosen[2 * n + 1], 'row', down)]
    ppermute x2, waiting for transfers between devices: 7.46 us -> 8.34 us  [per_device(): lax.ppermute(chosen[2 * n + 1], 'row', down)]
    pallas_call x4 -> x3, Pallas kernels: 9.68 us -> 8.89 us  [call(): pl.pallas_call(kernel, in_specs=specs, out_specs=[vmem] * len(out_shape),...]
    pallas_call x4 -> x3, Pallas kernels: 7.86 us -> 7.24 us  [the longest x2 3.94 us: triplet_sum(): pl.pallas_call(functools.partial(triplet_kernel, slots, a_slots.shape[0],...]
  transfers between devices with their start and end apart: 14 -> 14, of which waited for: 9 -> 10; matrix products, arithmetic and copies ran while one was open for 0% -> 0% of each run, Pallas kernels for 32% -> 26%
where the time goes in v10:
time: 43.7 us; the launch traced here: 43.5 us
  Pallas kernels  18.2 us (42%)
  waiting for transfers between devices  14.1 us (32%)
  starting transfers between devices  11.1 us (25%)
    pallas_call x3, Pallas kernels, call(): pl.pallas_call(kernel, in_specs=specs, out_specs=[vmem] * len(out_shape),...  8.89 us
    ppermute x2, waiting for transfers between devices, per_device(): lax.ppermute(chosen[2 * n + 1], 'row', down)  8.34 us
    ppermute x2, starting transfers between devices, per_device(): lax.ppermute(chosen[2 * n + 1], 'row', down)  5.91 us
    pallas_call x2, Pallas kernels, triplet_sum(): pl.pallas_call(functools.partial(triplet_kernel, slots, a_slots.shape[0],...  3.94 us
    pallas_call x1, Pallas kernels, finish(): pl.pallas_call(functools.partial(finish_kernel, steps), in_specs=[vmem] *...  3.3 us
    ppermute x6, waiting for transfers between devices, per_device(): lax.ppermute(lax.slice_in_dim(value, at, at + wide, axis=1), 'chan', swap)  3.27 us
    ppermute x2, starting transfers between devices, per_device(): lax.ppermute(chosen[2 * n], 'row', up)  2.63 us
    pallas_call x1, Pallas kernels, select_blocks(): pl.pallas_call(functools.partial(select_kernel, slots, a_slots.shape[0],...  2.02 us
  transfers between devices with their start and end apart: 14, of which 10 were waited for; matrix products, arithmetic and copies ran while one was open for 0% of the time, Pallas kernels for 26%

profile of v10, /device:TPU:0, one launch (start us, length us, event | category | flops | bytes accessed | tf_op | source)
XLA Modules:
  0.0 43.5 jit_solution(14043954899413146795)
XLA Ops:
  0.0 0.5 %collective-permute-start.4 = (bf16[2,64,4096]{2,1,0:T(8,128)(2,1)}, bf16[2,64,4096]{2,1,0:T(8,128)(2,1)S(1)}, u32[]{:S(2)}, u32[]{:S(2)}) collective-permute-start(bf16[2,64,4096]{2,1,0:T(8,128)(2,1)} %refs_1_.1), channel_id=1, source_target_pairs={{0,1},{1,0},{2,3},{3,2},{4,5},{5,4},{6,7},{7,6},{8,9},{9,8},{10,11... | collective-permute-start | bytes 3145736 | tf_op jit(solution)/shard_map/ppermute | solution.py:429
  0.5 2.0 %select_blocks.1 = (bf16[64,2048]{1,0:T(8,128)(2,1)S(1)}, bf16[64,2048]{1,0:T(8,128)(2,1)S(1)}, bf16[64,2048]{1,0:T(8,128)(2,1)S(1)}, bf16[64,2048]{1,0:T(8,128)(2,1)S(1)}) custom-call(s32[4,16]{1,0:T(4,128)} %bitcast.8, s32[4,16]{1,0:T(4,128)} %bitcast.11, s32[16]{0:T(128)} %n_ref.5, bf16[2,64,4096]{2,1,0:T(8,128)(2,1)} %refs_1_.1), custom_call_target="tpu_custom_call" | custom-call | tf_op jit(solution)/shard_map/select_blocks/pallas_call | solution.py:69
  2.5 2.6 %collective-permute-start.2 = (bf16[64,2048]{1,0:T(8,128)(2,1)S(1)}, bf16[64,2048]{1,0:T(8,128)(2,1)S(1)}, u32[]{:S(2)}, u32[]{:S(2)}) collective-permute-start(bf16[64,2048]{1,0:T(8,128)(2,1)S(1)} %get-tuple-element.30), channel_id=1, source_target_pairs={{0,4},{4,8},{8,12},{12,0},{1,5},{5,9},{9,13},{13,1},{2,6},{6,10},{... | collective-permute-start | bytes 786440 | tf_op jit(solution)/shard_map/ppermute | solution.py:433
  5.1 2.1 %collective-permute-start.3 = (bf16[64,2048]{1,0:T(8,128)(2,1)S(1)}, bf16[64,2048]{1,0:T(8,128)(2,1)S(1)}, u32[]{:S(2)}, u32[]{:S(2)}) collective-permute-start(bf16[64,2048]{1,0:T(8,128)(2,1)S(1)} %get-tuple-element.31), channel_id=1, source_target_pairs={{0,12},{4,0},{8,4},{12,8},{1,13},{5,1},{9,5},{13,9},{2,14},{6,2},{... | collective-permute-start | bytes 786440 | tf_op jit(solution)/shard_map/ppermute | solution.py:433
  7.2 0.0 collective-permute-start
  7.2 3.8 %collective-permute-start.1 = (bf16[64,2048]{1,0:T(8,128)(2,1)S(1)}, bf16[64,2048]{1,0:T(8,128)(2,1)S(1)}, u32[]{:S(2)}, u32[]{:S(2)}) collective-permute-start(bf16[64,2048]{1,0:T(8,128)(2,1)S(1)} %get-tuple-element.29), channel_id=1, source_target_pairs={{0,12},{4,0},{8,4},{12,8},{1,13},{5,1},{9,5},{13,9},{2,14},{6,2},{... | collective-permute-start | bytes 786440 | tf_op jit(solution)/shard_map/ppermute | solution.py:433
  11.0 0.0 collective-permute-done.4.refs_0_
  11.0 5.4 %project_own.1 = (bf16[2,64,64,128]{3,2,1,0:T(8,128)(2,1)S(1)}, bf16[5,64,64,128]{3,2,1,0:T(8,128)(2,1)S(1)}, bf16[2,64,4096]{2,1,0:T(8,128)(2,1)S(1)}, bf16[256...) custom-call(bf16[2,64,4096]{2,1,0:T(8,128)(2,1)S(1)} %collective-permute-done.4.refs_0_, ...), custom_call_target="tpu_custom_call" | custom-call | tf_op jit(solution)/shard_map/project_own/pallas_call | solution.py:262
  16.4 0.0 collective-permute-done.2.m0
  16.4 3.6 %collective-permute-done.3.m1 = bf16[64,2048]{1,0:T(8,128)(2,1)S(1)} collective-permute-done((bf16[64,2048]{1,0:T(8,128)(2,1)S(1)}, bf16[64,2048]{1,0:T(8,128)(2,1)S(1)}, u32[]{:S(2)}, u32[]{:S(2)}) %collective-permute-start.3) | collective-permute-done | bytes 262176 | tf_op jit(solution)/shard_map/ppermute | solution.py:433
  20.0 0.1 collective-permute-start.7
  20.1 0.5 %collective-permute-start.5 = (bf16[64,1024]{1,0:T(8,128)(2,1)S(1)}, bf16[64,1024]{1,0:T(8,128)(2,1)S(1)}, u32[]{:S(2)}, u32[]{:S(2)}) collective-permute-start(bf16[64,1024]{1,0:T(8,128)(2,1)S(1)} %get-tuple-element.54), channel_id=1, source_target_pairs={{0,1},{1,0},{2,3},{3,2},{4,5},{5,4},{6,7},{7,6},{8,9},{9,8},{10,11... | collective-permute-start | bytes 393224 | tf_op jit(solution)/shard_map/ppermute | solution.py:458
  20.6 0.1 collective-permute-start.8
  20.7 0.7 %collective-permute-done.7.refs_2_ = bf16[64,1024]{1,0:T(8,128)(2,1)S(1)} collective-permute-done((bf16[64,1024]{1,0:T(8,128)(2,1)S(1)}, bf16[64,1024]{1,0:T(8,128)(2,1)S(1)}, u32[]{:S(2)}, u32[]{:S(2)}) %collective-permute-start.7) | collective-permute-done | bytes 131104 | tf_op jit(solution)/shard_map/ppermute | solution.py:458
  21.4 0.1 collective-permute-start.6
  21.6 0.0 collective-permute-done.5.refs_0_
  21.6 0.4 collective-permute-done.8.refs_3_
  22.0 0.8 %collective-permute-done.6.refs_1_ = bf16[64,1024]{1,0:T(8,128)(2,1)S(1)} collective-permute-done((bf16[64,1024]{1,0:T(8,128)(2,1)S(1)}, bf16[64,1024]{1,0:T(8,128)(2,1)S(1)}, u32[]{:S(2)}, u32[]{:S(2)}) %collective-permute-start.6) | collective-permute-done | bytes 131104 | tf_op jit(solution)/shard_map/ppermute | solution.py:458
  22.8 1.8 %project_fetched.2 = (bf16[2,64,64,128]{3,2,1,0:T(8,128)(2,1)S(1)}, bf16[5,64,64,128]{3,2,1,0:T(8,128)(2,1)S(1)}) custom-call(bf16[64,2048]{1,0:T(8,128)(2,1)S(1)} %collective-permute-done.2.m0, bf16[64,2048]{1,0:T(8,128)(2,1)S(1)} %collective-permute-done.3.m1, ...), custom_call_target="tpu_custom_call", output_to_operand_aliasing={{0}: (8, {}), {1}: (9, {})} | custom-call | tf_op jit(solution)/shard_map/project_fetched/pallas_call | solution.py:262
  24.5 0.0 copy-start
  24.5 0.0 copy-start.1
  24.5 0.0 copy-start.2
  24.6 1.1 %collective-permute-done.m0 = bf16[64,2048]{1,0:T(8,128)(2,1)S(1)} collective-permute-done((bf16[64,2048]{1,0:T(8,128)(2,1)S(1)}, bf16[64,2048]{1,0:T(8,128)(2,1)S(1)}, u32[]{:S(2)}, u32[]{:S(2)}) %collective-permute-start) | collective-permute-done | bytes 262176 | tf_op jit(solution)/shard_map/ppermute | solution.py:433
  25.6 4.8 %collective-permute-done.1.m1 = bf16[64,2048]{1,0:T(8,128)(2,1)S(1)} collective-permute-done((bf16[64,2048]{1,0:T(8,128)(2,1)S(1)}, bf16[64,2048]{1,0:T(8,128)(2,1)S(1)}, u32[]{:S(2)}, u32[]{:S(2)}) %collective-permute-start.1) | collective-permute-done | bytes 262176 | tf_op jit(solution)/shard_map/ppermute | solution.py:433
  30.4 0.0 collective-permute-start.9
  30.4 0.5 %collective-permute-start.10 = (bf16[64,2048]{1,0:T(8,128)(2,1)S(1)}, bf16[64,2048]{1,0:T(8,128)(2,1)S(1)}, u32[]{:S(2)}, u32[]{:S(2)}) collective-permute-start(bf16[64,2048]{1,0:T(8,128)(2,1)S(1)} %collective-permute-done.1.m1), channel_id=1, source_target_pairs={{0,1},{1,0},{2,3},{3,2},{4,5},{5,4},{6,7},{7,6},{8,9},{9,8},{10,11... | collective-permute-start | bytes 786440 | tf_op jit(solution)/shard_map/ppermute | solution.py:458
  30.9 1.0 %collective-permute-done.9.refs_0_ = bf16[64,2048]{1,0:T(8,128)(2,1)S(1)} collective-permute-done((bf16[64,2048]{1,0:T(8,128)(2,1)S(1)}, bf16[64,2048]{1,0:T(8,128)(2,1)S(1)}, u32[]{:S(2)}, u32[]{:S(2)}) %collective-permute-start.9) | collective-permute-done | bytes 262176 | tf_op jit(solution)/shard_map/ppermute | solution.py:458
  31.9 0.4 collective-permute-done.10.refs_1_
  32.3 1.8 %project_fetched.3 = (bf16[2,64,64,128]{3,2,1,0:T(8,128)(2,1)S(1)}, bf16[5,64,64,128]{3,2,1,0:T(8,128)(2,1)S(1)}) custom-call(bf16[64,2048]{1,0:T(8,128)(2,1)S(1)} %collective-permute-done.m0, bf16[64,2048]{1,0:T(8,128)(2,1)S(1)} %collective-permute-done.1.m1, ...), custom_call_target="tpu_custom_call", output_to_operand_aliasing={{0}: (6, {}), {1}: (7, {})} | custom-call | tf_op jit(solution)/shard_map/project_fetched/pallas_call | solution.py:262
  34.1 0.0 copy-done
  34.1 0.0 copy-done.1
  34.1 0.0 copy-done.2
  34.1 2.0 %triplets.2.refs_0_ = bf16[2,32,4096]{2,1,0:T(8,128)(2,1)S(1)} custom-call(s32[4,16]{1,0:T(4,128)S(1)} %bitcast.9, s32[4,16]{1,0:T(4,128)S(1)} %bitcast.12, s32[16]{0:T(128)S(1)} %copy-done.2, bf16[2,64,64,128]{3,2,1,0:T(8,128)(2,1)S(1)} %get-tuple-element.46.l_ref, bf16[5,64,64,128]{3,2,1,0:T(8,128)(2,1)S(1)} %get-tuple-element.45.p_ref), custom_call_target="tpu_custom_call" | custom-call | tf_op jit(solution)/shard_map/triplets/pallas_call | solution.py:340
  36.1 0.2 collective-permute-start.11
  36.3 2.0 %triplets.3 = (bf16[32,4096]{1,0:T(8,128)(2,1)S(1)}, bf16[32,4096]{1,0:T(8,128)(2,1)S(1)}) custom-call(s32[4,16]{1,0:T(4,128)S(1)} %bitcast.10, s32[4,16]{1,0:T(4,128)S(1)} %bitcast.13, s32[16]{0:T(128)S(1)} %copy-done.2, bf16[2,64,64,128]{3,2,1,0:T(8,128)(2,1)S(1)} %get-tuple-element.46.l_ref, bf16[5,64,64,128]{3,2,1,0:T(8,128)(2,1)S(1)} %get-tuple-element.45.p_ref), custom_call_target="tpu_custom_call" | custom-call | tf_op jit(solution)/shard_map/triplets/pallas_call | solution.py:340
  38.3 0.4 %collective-permute-start.12 = (bf16[32,4096]{1,0:T(8,128)(2,1)S(1)}, bf16[32,4096]{1,0:T(8,128)(2,1)S(1)}, u32[]{:S(2)}, u32[]{:S(2)}) collective-permute-start(bf16[32,4096]{1,0:T(8,128)(2,1)S(1)} %get-tuple-element.47.refs_1_), channel_id=1, source_target_pairs={{0,1},{1,0},{2,3},{3,2},{4,5},{5,4},{6,7},{7,6},{8,9},{9,8},{10,11... | collective-permute-start | bytes 786440 | tf_op jit(solution)/shard_map/ppermute | solution.py:480
  38.7 0.1 collective-permute-start.13
  38.8 1.0 %collective-permute-done.12.refs_4_ = bf16[32,4096]{1,0:T(8,128)(2,1)S(1)} collective-permute-done((bf16[32,4096]{1,0:T(8,128)(2,1)S(1)}, bf16[32,4096]{1,0:T(8,128)(2,1)S(1)}, u32[]{:S(2)}, u32[]{:S(2)}) %collective-permute-start.12) | collective-permute-done | bytes 262176 | tf_op jit(solution)/shard_map/ppermute | solution.py:480
  39.9 0.4 collective-permute-done.13.refs_5_
  40.2 0.0 collective-permute-done.11.refs_3_
  40.2 3.3 %finish.1 = bf16[2,64,4096]{2,1,0:T(8,128)(2,1)} custom-call(bf16[2,32,4096]{2,1,0:T(8,128)(2,1)S(1)} %triplets.2.refs_0_, bf16[32,4096]{1,0:T(8,128)(2,1)S(1)} %get-tuple-element.47.refs_1_, bf16[32,4096]{1,0:T(8,128)(2,1)S(1)} %get-tuple-element.48.refs_2_, bf16[2,32,4096]{2,1,0:T(8,128)(2,1)S(1)} %collective-permute-done.11.refs_3_, ...), custom_call_target="tpu_custom_call" | custom-call | tf_op jit(solution)/shard_map/finish/pallas_call | solution.py:387
  (2 shorter events, 0.0 us)
Async XLA Ops:
  0.0 11.0 %collective-permute-start.4 = (bf16[2,64,4096]{2,1,0:T(8,128)(2,1)}, bf16[2,64,4096]{2,1,0:T(8,128)(2,1)S(1)}, u32[]{:S(2)}, u32[]{:S(2)}) collective-permute-start(bf16[2,64,4096]{2,1,0:T(8,128)(2,1)} %refs_1_.1), channel_id=1, source_target_pairs={{0,1},{1,0},{2,3},{3,2},{4,5},{5,4},{6,7},{7,6},{8,9},{9,8},{10,11... | collective-permute-start | bytes 3145736 | tf_op jit(solution)/shard_map/ppermute | solution.py:429
  2.5 13.9 %collective-permute-start.2 = (bf16[64,2048]{1,0:T(8,128)(2,1)S(1)}, bf16[64,2048]{1,0:T(8,128)(2,1)S(1)}, u32[]{:S(2)}, u32[]{:S(2)}) collective-permute-start(bf16[64,2048]{1,0:T(8,128)(2,1)S(1)} %get-tuple-element.30), channel_id=1, source_target_pairs={{0,4},{4,8},{8,12},{12,0},{1,5},{5,9},{9,13},{13,1},{2,6},{6,10},{... | collective-permute-start | bytes 786440 | tf_op jit(solution)/shard_map/ppermute | solution.py:433
  5.1 14.9 %collective-permute-start.3 = (bf16[64,2048]{1,0:T(8,128)(2,1)S(1)}, bf16[64,2048]{1,0:T(8,128)(2,1)S(1)}, u32[]{:S(2)}, u32[]{:S(2)}) collective-permute-start(bf16[64,2048]{1,0:T(8,128)(2,1)S(1)} %get-tuple-element.31), channel_id=1, source_target_pairs={{0,12},{4,0},{8,4},{12,8},{1,13},{5,1},{9,5},{13,9},{2,14},{6,2},{... | collective-permute-start | bytes 786440 | tf_op jit(solution)/shard_map/ppermute | solution.py:433
  7.2 18.4 %collective-permute-start = (bf16[64,2048]{1,0:T(8,128)(2,1)S(1)}, bf16[64,2048]{1,0:T(8,128)(2,1)S(1)}, u32[]{:S(2)}, u32[]{:S(2)}) collective-permute-start(bf16[64,2048]{1,0:T(8,128)(2,1)S(1)} %get-tuple-element.28), channel_id=1, source_target_pairs={{0,4},{4,8},{8,12},{12,0},{1,5},{5,9},{9,13},{13,1},{2,6},{6,10},{... | collective-permute-start | bytes 786440 | tf_op jit(solution)/shard_map/ppermute | solution.py:433
  7.2 23.2 %collective-permute-start.1 = (bf16[64,2048]{1,0:T(8,128)(2,1)S(1)}, bf16[64,2048]{1,0:T(8,128)(2,1)S(1)}, u32[]{:S(2)}, u32[]{:S(2)}) collective-permute-start(bf16[64,2048]{1,0:T(8,128)(2,1)S(1)} %get-tuple-element.29), channel_id=1, source_target_pairs={{0,12},{4,0},{8,4},{12,8},{1,13},{5,1},{9,5},{13,9},{2,14},{6,2},{... | collective-permute-start | bytes 786440 | tf_op jit(solution)/shard_map/ppermute | solution.py:433
  20.0 1.4 %collective-permute-start.7 = (bf16[64,1024]{1,0:T(8,128)(2,1)S(1)}, bf16[64,1024]{1,0:T(8,128)(2,1)S(1)}, u32[]{:S(2)}, u32[]{:S(2)}) collective-permute-start(bf16[64,1024]{1,0:T(8,128)(2,1)S(1)} %get-tuple-element.53), channel_id=1, source_target_pairs={{0,1},{1,0},{2,3},{3,2},{4,5},{5,4},{6,7},{7,6},{8,9},{9,8},{10,11... | collective-permute-start | bytes 393224 | tf_op jit(solution)/shard_map/ppermute | solution.py:458
  20.1 1.5 %collective-permute-start.5 = (bf16[64,1024]{1,0:T(8,128)(2,1)S(1)}, bf16[64,1024]{1,0:T(8,128)(2,1)S(1)}, u32[]{:S(2)}, u32[]{:S(2)}) collective-permute-start(bf16[64,1024]{1,0:T(8,128)(2,1)S(1)} %get-tuple-element.54), channel_id=1, source_target_pairs={{0,1},{1,0},{2,3},{3,2},{4,5},{5,4},{6,7},{7,6},{8,9},{9,8},{10,11... | collective-permute-start | bytes 393224 | tf_op jit(solution)/shard_map/ppermute | solution.py:458
  20.6 1.4 %collective-permute-start.8 = (bf16[64,1024]{1,0:T(8,128)(2,1)S(1)}, bf16[64,1024]{1,0:T(8,128)(2,1)S(1)}, u32[]{:S(2)}, u32[]{:S(2)}) collective-permute-start(bf16[64,1024]{1,0:T(8,128)(2,1)S(1)} %get-tuple-element.51), channel_id=1, source_target_pairs={{0,1},{1,0},{2,3},{3,2},{4,5},{5,4},{6,7},{7,6},{8,9},{9,8},{10,11... | collective-permute-start | bytes 393224 | tf_op jit(solution)/shard_map/ppermute | solution.py:458
  21.4 1.3 %collective-permute-start.6 = (bf16[64,1024]{1,0:T(8,128)(2,1)S(1)}, bf16[64,1024]{1,0:T(8,128)(2,1)S(1)}, u32[]{:S(2)}, u32[]{:S(2)}) collective-permute-start(bf16[64,1024]{1,0:T(8,128)(2,1)S(1)} %get-tuple-element.52), channel_id=1, source_target_pairs={{0,1},{1,0},{2,3},{3,2},{4,5},{5,4},{6,7},{7,6},{8,9},{9,8},{10,11... | collective-permute-start | bytes 393224 | tf_op jit(solution)/shard_map/ppermute | solution.py:458
  24.5 9.6 %copy-start = (s32[16,4]{0,1:T(4,128)S(1)}, s32[16,4]{0,1:T(4,128)}, u32[]{:S(2)}) copy-start(s32[16,4]{0,1:T(4,128)} %param.17) | copy-start | bytes 772
  24.5 9.6 %copy-start.1 = (s32[16,4]{0,1:T(4,128)S(1)}, s32[16,4]{0,1:T(4,128)}, u32[]{:S(2)}) copy-start(s32[16,4]{0,1:T(4,128)} %param.18) | copy-start | bytes 772
  24.5 9.6 %copy-start.2 = (s32[16]{0:T(128)S(1)}, s32[16]{0:T(128)}, u32[]{:S(2)}) copy-start(s32[16]{0:T(128)} %n_ref.5) | copy-start | bytes 196
  30.4 1.5 %collective-permute-start.9 = (bf16[64,2048]{1,0:T(8,128)(2,1)S(1)}, bf16[64,2048]{1,0:T(8,128)(2,1)S(1)}, u32[]{:S(2)}, u32[]{:S(2)}) collective-permute-start(bf16[64,2048]{1,0:T(8,128)(2,1)S(1)} %collective-permute-done.m0), channel_id=1, source_target_pairs={{0,1},{1,0},{2,3},{3,2},{4,5},{5,4},{6,7},{7,6},{8,9},{9,8},{10,11... | collective-permute-start | bytes 786440 | tf_op jit(solution)/shard_map/ppermute | solution.py:458
  30.4 1.9 %collective-permute-start.10 = (bf16[64,2048]{1,0:T(8,128)(2,1)S(1)}, bf16[64,2048]{1,0:T(8,128)(2,1)S(1)}, u32[]{:S(2)}, u32[]{:S(2)}) collective-permute-start(bf16[64,2048]{1,0:T(8,128)(2,1)S(1)} %collective-permute-done.1.m1), channel_id=1, source_target_pairs={{0,1},{1,0},{2,3},{3,2},{4,5},{5,4},{6,7},{7,6},{8,9},{9,8},{10,11... | collective-permute-start | bytes 786440 | tf_op jit(solution)/shard_map/ppermute | solution.py:458
  36.1 4.2 %collective-permute-start.11 = (bf16[2,32,4096]{2,1,0:T(8,128)(2,1)S(1)}, bf16[2,32,4096]{2,1,0:T(8,128)(2,1)S(1)}, u32[]{:S(2)}, u32[]{:S(2)}) collective-permute-start(bf16[2,32,4096]{2,1,0:T(8,128)(2,1)S(1)} %triplets.2.refs_0_), channel_id=1, source_target_pairs={{0,1},{1,0},{2,3},{3,2},{4,5},{5,4},{6,7},{7,6},{8,9},{9,8},{10,11... | collective-permute-start | bytes 1572872 | tf_op jit(solution)/shard_map/ppermute | solution.py:480
  38.3 1.6 %collective-permute-start.12 = (bf16[32,4096]{1,0:T(8,128)(2,1)S(1)}, bf16[32,4096]{1,0:T(8,128)(2,1)S(1)}, u32[]{:S(2)}, u32[]{:S(2)}) collective-permute-start(bf16[32,4096]{1,0:T(8,128)(2,1)S(1)} %get-tuple-element.47.refs_1_), channel_id=1, source_target_pairs={{0,1},{1,0},{2,3},{3,2},{4,5},{5,4},{6,7},{7,6},{8,9},{9,8},{10,11... | collective-permute-start | bytes 786440 | tf_op jit(solution)/shard_map/ppermute | solution.py:480
  38.7 1.5 %collective-permute-start.13 = (bf16[32,4096]{1,0:T(8,128)(2,1)S(1)}, bf16[32,4096]{1,0:T(8,128)(2,1)S(1)}, u32[]{:S(2)}, u32[]{:S(2)}) collective-permute-start(bf16[32,4096]{1,0:T(8,128)(2,1)S(1)} %get-tuple-element.48.refs_2_), channel_id=1, source_target_pairs={{0,1},{1,0},{2,3},{3,2},{4,5},{5,4},{6,7},{7,6},{8,9},{9,8},{10,11... | collective-permute-start | bytes 786440 | tf_op jit(solution)/shard_map/ppermute | solution.py:480

commit v11 on v9

--- a/solution.py
+++ b/solution.py
@@ -31,9 +31,19 @@
     return tile_of(row, col), tile_of(behind, col), tile_of(ahead, col)
 
 
-def select_kernel(slots, triplets, cuts, a_ref, b_ref, n_ref, pair_ref, *refs):
+def select_kernel(slots, triplets, cuts, a_hbm, b_hbm, n_hbm, pair_hbm, *refs):
+    pair_ref, *out_refs = refs[: 1 + 2 * len(cuts)]
+    a_ref, b_ref, n_ref, sems = refs[1 + 2 * len(cuts) :]
     me, behind, ahead = neighbour_tiles()
-    out_refs, sems = refs[:-1], refs[-1]
+    whole = pltpu.make_async_copy(pair_hbm, pair_ref, sems.at[0])
+    tables = [
+        pltpu.make_async_copy(source, target, sems.at[1 + at])
+        for at, (source, target) in enumerate(((a_hbm, a_ref), (b_hbm, b_ref), (n_hbm, n_ref)))
+    ]
+    for copy in (*tables, whole):
+        copy.start()
+    for copy in tables:
+        copy.wait()
     picks = []
     for target in (ahead, behind):
         pick = jnp.int32(0)
@@ -45,35 +55,32 @@
                     mine = jnp.logical_and(name >= 0, name < slots)
                     pick = jnp.where(jnp.logical_and(m < count, mine), name, pick)
         picks.append(pick)
-    copies = []
+    whole.wait()
     for at, (start, size) in enumerate(cuts):
         for which, pick in enumerate(picks):
-            out = 2 * at + which
-            copies.append(
-                pltpu.make_async_copy(
-                    pair_ref.at[pick, :, pl.ds(start, size)], out_refs[out], sems.at[out]
-                )
-            )
-            copies[-1].start()
-    for copy in copies:
-        copy.wait()
+            out_refs[2 * at + which][...] = pair_ref[pick, :, start : start + size]
 
 
 def select_blocks(pair, a_slots, b_slots, counts, cuts):
     slots, channels, cells = pair.shape
-    smem = pl.BlockSpec(memory_space=pltpu.SMEM)
+    hbm = pl.BlockSpec(memory_space=pltpu.HBM)
     vmem = pl.BlockSpec(memory_space=pltpu.VMEM)
-    out_shape = [
+    out_shape = [pltpu.VMEM(pair.shape, pair.dtype)] + [
         pltpu.VMEM((channels, size), pair.dtype) for _, size in cuts for _ in range(2)
+    ]
+    operands = [
+        pltpu.with_memory_space_constraint(value, pltpu.HBM)
+        for value in (a_slots, b_slots, counts, pair)
     ]
     return pl.pallas_call(
         functools.partial(select_kernel, slots, a_slots.shape[0], cuts),
         out_shape=out_shape,
-        in_specs=[smem, smem, smem, pl.BlockSpec(memory_space=pltpu.HBM)],
+        in_specs=[hbm] * 4,
         out_specs=[vmem] * len(out_shape),
-        scratch_shapes=[pltpu.SemaphoreType.DMA((len(out_shape),))],
+        scratch_shapes=[pltpu.SMEM(value.shape, value.dtype) for value in operands[:3]]
+        + [pltpu.SemaphoreType.DMA((4,))],
         name="select_blocks",
-    )(a_slots, b_slots, counts, pair)
+    )(*operands)
 
 
 def prepared(weight, gain=None):
@@ -120,7 +127,7 @@
     return sides, y[4 * half :]
 
 
-def pair_chunk(sides_at, chunk, held, half):
+def pair_chunk(sides_at, chunk, held):
     low = lax.broadcasted_iota(jnp.int32, (8, LANES), 1) < BLK
     pitch = held[0].shape[0] // (chunk // BLK)
     for start in range(0, chunk, LANES):
@@ -135,32 +142,30 @@
         yield
 
 
-def spread_chunk(chunk, held, l_ref, p_ref, pair_of, first_row, half):
-    rows = chunk // BLK
+def spread_chunk(rows, held, l_ref, pair_of, l_row, p_ref, p_row, before, turned_ref, half):
     pitch = held[0].shape[0] // rows
-    to = pl.ds(pl.multiple_of(first_row, 16), rows)
+    to = pl.ds(pl.multiple_of(l_row, 16), rows)
     for c in range(half):
         take = pl.ds(c, rows, stride=pitch)
         l_ref[pair_of, c, to, :] = held[0][take, :].astype(BF16)
-        right = held[1][take, :].astype(BF16)
-        p_ref[2 * pair_of, c, to, :] = right
-        p_ref[2 * pair_of + 1, c, to, :] = pltpu.roll(right, BLK, 1)
+        right = held[1][take, :]
+        if turned_ref is None:
+            p_ref[c, pl.ds(pl.multiple_of(p_row, 16), rows), :] = right.astype(BF16)
+        else:
+            whole = jnp.concatenate([ref[c, :size].astype(F32) for ref, size in before] + [right])
+            turned = jnp.transpose(whole).astype(BF16)
+            turned_ref[2 * pair_of, c] = turned[:BLK]
+            turned_ref[2 * pair_of + 1, c] = turned[BLK:]
         if c % 8 == 7:
             yield
 
 
-def two_chunks(sides_at, n, chunk, held, l_ref, p_ref, pair_of, first_row, half):
-    rows = chunk // BLK
+def two_chunks(sides_at, n, chunk, held, spread):
     steps = [
-        pair_chunk(functools.partial(sides_at, 2 * n + k), chunk, held[2 * k : 2 * k + 2], half)
+        pair_chunk(functools.partial(sides_at, n + k), chunk, held[2 * k : 2 * k + 2])
         for k in range(2)
     ]
-    spreads = [
-        spread_chunk(
-            chunk, held[2 * k : 2 * k + 2], l_ref, p_ref, pair_of, first_row + (2 * n + k) * rows, half
-        )
-        for k in range(2)
-    ]
+    spreads = [spread(n + k, held[2 * k : 2 * k + 2], k) for k in range(2)]
     for _ in steps[0]:
         pass
     for _ in zip(steps[1], spreads[0]):
@@ -176,11 +181,11 @@
 
 
 def own_kernel(chunk, *refs):
-    t_ref = refs[0]
-    sources = refs[1:8]
-    l_ref, p_ref, gate_ref, w_ref, v_ref, gain_ref = refs[8:14]
-    targets = refs[14:21]
-    held, sems = refs[21:25], refs[25]
+    m_ref, t_ref = refs[:2]
+    sources = refs[2:8]
+    l_ref, turned_ref, gate_ref, w_ref, v_ref, gain_ref = refs[8:14]
+    targets = refs[14:20]
+    p_ref, held, sems = refs[20], refs[21:25], refs[25]
     copies = [
         pltpu.make_async_copy(source, target, sems.at[at])
         for at, (source, target) in enumerate(zip(sources, targets))
@@ -191,11 +196,11 @@
 
     @pl.loop(0, half)
     def _(c):
-        p_ref[4, c] = jnp.zeros((BLK, LANES), BF16)
+        turned_ref[4, c] = jnp.zeros((BLK, BLK), BF16)
 
     for copy in copies:
         copy.wait()
-    m_ref, a_ref, b_ref, o_ref, u_ref, g_ref, h_ref = targets
+    a_ref, b_ref, o_ref, u_ref, g_ref, h_ref = targets
     rows = gated_rows(a_ref) + gated_rows(b_ref) + [0.5 * o_ref[...].astype(F32)]
     weight = prepared(jnp.concatenate(rows, axis=0))
     w_ref[...] = weight[: 4 * half]
@@ -204,6 +209,8 @@
     in_order = lax.axis_index("chan") == 0
     gain_ref[:half] = jnp.where(in_order, across[:half], across[half:])
     gain_ref[half:] = jnp.where(in_order, across[half:], across[:half])
+    chunks = m_ref.shape[-1] // chunk
+    rows = chunk // BLK
 
     def sides_at(n, start):
         at = cells_at(n, chunk, start)
@@ -214,57 +221,48 @@
             both.append(sides)
         return both
 
-    @pl.loop(0, m_ref.shape[-1] // chunk // 2)
+    def spread(last, n, held, k):
+        before, turned = ([(p_ref, (chunks - 1) * rows)], turned_ref) if last and k else (None, None)
+        return spread_chunk(rows, held, l_ref, 0, n * rows, p_ref, n * rows, before, turned, half)
+
+    @pl.loop(0, chunks - 2, step=2)
     def _(n):
-        two_chunks(sides_at, n, chunk, held, l_ref, p_ref, 0, 0, half)
-
-
-def both_kernel(chunk, first_row, m0, m1, *refs):
-    theirs = refs[:4]
-    w_ref, gain_ref, _, _, l_ref, p_ref = refs[4:10]
-    held = refs[10:]
+        two_chunks(sides_at, n, chunk, held, functools.partial(spread, False))
+
+    two_chunks(sides_at, chunks - 2, chunk, held, functools.partial(spread, True))
+
+
+def fetched_kernel(chunk, first_row, last, m0, m1, *refs):
+    if last:
+        *theirs, p0_ref, w_ref, gain_ref, _, _, l_ref, turned_ref, p_ref = refs[:-4]
+        before = [(p0_ref, p0_ref.shape[1]), (p_ref, p_ref.shape[1])]
+    else:
+        *theirs, w_ref, gain_ref, _, l_ref, p_ref = refs[:-4]
+    held = refs[-4:]
     half = l_ref.shape[1]
     weight = w_ref[...]
+    wide = theirs[0].shape[1]
+    rows = chunk // BLK
 
     def sides_at(n, start):
-        at = cells_at(n, chunk, start)
-        within = pl.ds(start, LANES)
-        return [
-            gated_sides(m[:, at], theirs[2 * n + x][:, within], weight, gain_ref[...], half)[0]
-            for x, m in enumerate((m0, m1))
-        ]
-
-    two_chunks(sides_at, 0, chunk, held, l_ref, p_ref, 1, first_row, half)
-
-
-def early_kernel(chunk, m_ref, t0_ref, t1_ref, w_ref, gain_ref, l_ref, r_ref):
-    weight = w_ref[...]
-    half = m_ref.shape[0]
-    for n, t_ref in enumerate((t0_ref, t1_ref)):
-
-        @pl.loop(0, chunk, step=4 * LANES)
-        def _(base):
-            for start in range(0, 4 * LANES, LANES):
-                within = pl.ds(pl.multiple_of(base + start, LANES), LANES)
-                at = pl.ds(pl.multiple_of(n * chunk + base + start, LANES), LANES)
-                sides, _ = gated_sides(m_ref[:, at], t_ref[:, within], weight, gain_ref[...], half)
-                for out, groups in zip((l_ref, r_ref), sides):
-                    for row, group in enumerate(groups):
-                        out[8 * row : 8 * row + 8, at] = group
-
-
-def late_kernel(chunk, first_row, m_ref, t_ref, l0_ref, r0_ref, w_ref, gain_ref, *refs):
-    l_ref, p_ref = refs[2:4]
-    held = refs[4:]
-    half = l_ref.shape[1]
-    weight = w_ref[...]
-
-    def sides_at(n, start):
-        at = cells_at(n, chunk, start)
-        first = [[ref[row : row + 8, at] for row in range(0, half, 8)] for ref in (l0_ref, r0_ref)]
-        return first, gated_sides(m_ref[:, at], t_ref[:, at], weight, gain_ref[...], half)[0]
-
-    two_chunks(sides_at, 0, chunk, held, l_ref, p_ref, 1, first_row, half)
+        at = n * chunk + start
+        both = []
+        for x, m in enumerate((m0, m1)):
+            other = theirs[2 * (at // wide) + x][:, at % wide : at % wide + LANES]
+            both.append(
+                gated_sides(m[:, at : at + LANES], other, weight, gain_ref[...], half)[0]
+            )
+        return both
+
+    def spread(n, held, k):
+        done = (before, turned_ref) if last and k else (None, None)
+        return spread_chunk(rows, held, l_ref, 1, first_row + n * rows, p_ref, n * rows, *done, half)
+
+    two_chunks(sides_at, 0, chunk, held, spread)
+
+
+def chunk_scratch(half, chunk):
+    return [pltpu.VMEM((chunk // BLK * (half + 8), LANES), F32)] * 4
 
 
 def call(kernel, name, operands, out_shape, scratch, aliased=0, hbm=0):
@@ -290,17 +288,8 @@
     )(*operands)
 
 
-def operand_shapes(half):
-    return [pltpu.VMEM((2, half, BLK, LANES), BF16), pltpu.VMEM((5, half, BLK, LANES), BF16)]
-
-
-def chunk_scratch(half, chunk):
-    return [pltpu.VMEM((chunk // BLK * (half + 8), LANES), F32)] * 4
-
-
-def triplet_kernel(s, slots, triplets, group, a_ref, b_ref, n_ref, l_ref, p_ref, out_ref, acc):
+def triplet_kernel(s, slots, triplets, group, a_ref, b_ref, n_ref, l_ref, turned_ref, out_ref, *accs):
     me, behind, ahead = neighbour_tiles()
-    low = lax.broadcasted_iota(jnp.int32, (BLK, LANES), 1) < BLK
     block = me * slots + s
     count = n_ref[block]
     picks = []
@@ -323,37 +312,29 @@
                 place = jnp.where(from_me, place, jnp.where(from_behind, 2, 3))
                 chosen = jnp.where(hit, place, chosen)
                 used = jnp.where(hit, 1, used)
-            if part == 1:
-                chosen = chosen + 1 - 2 * (chosen & 1)
             picks.append(jnp.where(used == 1, chosen, 4))
 
     take_low = lax.broadcasted_iota(jnp.int32, (group, LANES), 1) < BLK
     half = l_ref.shape[1]
-    pitch = acc.shape[0] // BLK
-
-    def update_of(c):
-        lhs = jnp.concatenate([l_ref[0, c], l_ref[1, c]], axis=1)
-        parts = [p_ref[pick, c] for pick in picks]
-        rhs = jnp.concatenate(
-            [jnp.where(low, parts[0], parts[1]), jnp.where(low, parts[2], parts[3])], axis=1
-        )
-        return lax.dot_general(lhs, rhs, (((1,), (1,)), ((), ())), preferred_element_type=F32)
-
-    @pl.loop(0, half // 2, step=group)
+    pitch = accs[0].shape[0] // BLK
+
+    @pl.loop(0, half, step=group * len(accs))
     def _(base):
-        for at in range(group):
-            c = base + at
-            acc[pl.ds(at, BLK, stride=pitch), :] = jnp.concatenate(
-                [update_of(c), update_of(c + half // 2)], axis=1
-            )
-        rows = pl.ds(pl.multiple_of(base, group), group)
-        upper = pl.ds(pl.multiple_of(base + half // 2, group), group)
-        for t in range(BLK // 2):
-            even = acc[2 * t * pitch : 2 * t * pitch + group, :]
-            odd = acc[(2 * t + 1) * pitch : (2 * t + 1) * pitch + group, :]
-            to = slice(t * LANES, (t + 1) * LANES)
-            out_ref[rows, to] = jnp.where(take_low, even, pltpu.roll(odd, BLK, 1)).astype(BF16)
-            out_ref[upper, to] = jnp.where(take_low, pltpu.roll(even, BLK, 1), odd).astype(BF16)
+        for which, acc in enumerate(accs):
+            for at in range(group):
+                c = base + which * group + at
+                lhs = jnp.concatenate([l_ref[0, c], l_ref[1, c]], axis=1)
+                rhs = jnp.concatenate([turned_ref[pick, c] for pick in picks], axis=0)
+                acc[pl.ds(at, BLK, stride=pitch), :BLK] = jnp.dot(
+                    lhs, rhs, preferred_element_type=F32
+                )
+            rows = pl.ds(pl.multiple_of(base + which * group, group), group)
+            for t in range(BLK // 2):
+                even = acc[2 * t * pitch : 2 * t * pitch + group, :]
+                odd = acc[(2 * t + 1) * pitch : (2 * t + 1) * pitch + group, :]
+                out_ref[rows, t * LANES : (t + 1) * LANES] = jnp.where(
+                    take_low, even, pltpu.roll(odd, BLK, 1)
+                ).astype(BF16)
 
 
 def triplet_sum(s, lefts, rights, a_slots, b_slots, counts, slots, group):
@@ -368,7 +349,7 @@
         in_specs=[smem, smem, smem, vmem, vmem],
         out_specs=vmem,
         out_shape=pltpu.VMEM((half, BLK * BLK), BF16),
-        scratch_shapes=[pltpu.VMEM((BLK * (group + 8), LANES), F32)],
+        scratch_shapes=[pltpu.VMEM((BLK * (group + 8), LANES), F32)] * 2,
         compiler_params=pltpu.CompilerParams(vmem_limit_bytes=VMEM_LIMIT),
         name="triplets",
     )(a_slots, b_slots, counts, lefts, rights)
@@ -419,7 +400,7 @@
         operands.append(before)
         out_shape = jax.ShapeDtypeStruct(gate.shape, BF16)
         out_specs = pl.BlockSpec(memory_space=pltpu.HBM)
-        scratch = [pltpu.VMEM(mine.shape, BF16), pltpu.SemaphoreType.DMA((9,))]
+        scratch = [pltpu.VMEM(mine.shape, BF16), pltpu.SemaphoreType.DMA((5,))]
     return pl.pallas_call(
         functools.partial(finish_kernel, s),
         in_specs=[vmem] * len(operands),
@@ -459,67 +440,61 @@
         ln_out_gain[None, :],
     ]
 
-    pair_other = lax.ppermute(pair, "chan", swap)
-    cuts = ((0, cells // 2), (cells // 2, cells // 2))
-    chosen = select_blocks(pair, a_slots, b_slots, counts, cuts)
+    chunk = cells // 4
+    cuts = ((0, 2 * chunk), (2 * chunk, 2 * chunk))
+    pair, *chosen = select_blocks(pair, a_slots, b_slots, counts, cuts)
     arrived = [
         (lax.ppermute(chosen[2 * n], "row", up), lax.ppermute(chosen[2 * n + 1], "row", down))
         for n in range(len(cuts))
     ]
-    chunk = cells // 4
-    sources = [pair, *weights]
+    pair_other = lax.ppermute(pair, "chan", swap)
+    left_shape = pltpu.VMEM((2, half, BLK, LANES), BF16)
+    right_shape = pltpu.VMEM((5, half, BLK, BLK), BF16)
     lefts, rights, gate, weight, last_weight, gain = call(
         functools.partial(own_kernel, chunk),
         "project_own",
-        [pair_other, *sources],
-        operand_shapes(half)
-        + [
+        [pair, pair_other, *weights],
+        [
+            left_shape,
+            right_shape,
             pltpu.VMEM((slots, half, cells), BF16),
             pltpu.VMEM((4 * half, 2 * half), BF16),
             pltpu.VMEM((half, 2 * half), BF16),
             pltpu.VMEM((2 * half, LANES), F32),
         ],
-        [pltpu.VMEM(value.shape, value.dtype) for value in sources]
+        [pltpu.VMEM(value.shape, value.dtype) for value in weights]
+        + [pltpu.VMEM((half, BLK, LANES), BF16)]
         + chunk_scratch(half, chunk)
-        + [pltpu.SemaphoreType.DMA((len(sources),))],
-        hbm=len(sources),
+        + [pltpu.SemaphoreType.DMA((len(weights),))],
+        hbm=len(weights),
     )
-    from_behind, from_ahead, lefts = lax.optimization_barrier((*arrived[0], lefts))
-    others = [
-        lax.ppermute(lax.slice_in_dim(value, at, at + chunk, axis=1), "chan", swap)
-        for at in (0, chunk)
-        for value in (from_behind, from_ahead)
-    ]
-    lefts, rights = call(
-        functools.partial(both_kernel, chunk, 0),
-        "project_first",
-        [from_behind, from_ahead, *others, weight, gain, lefts, rights],
-        operand_shapes(half),
-        chunk_scratch(half, chunk),
-        aliased=2,
-    )
-    from_behind, lefts = lax.optimization_barrier((arrived[1][0], lefts))
-    others = [
-        lax.ppermute(lax.slice_in_dim(from_behind, at, at + chunk, axis=1), "chan", swap)
-        for at in (0, chunk)
-    ]
-    early = call(
-        functools.partial(early_kernel, chunk),
-        "project_early",
-        [from_behind, *others, weight, gain],
-        [pltpu.VMEM((half, 2 * chunk), F32)] * 2,
-        [],
-    )
-    from_ahead, early = lax.optimization_barrier((arrived[1][1], early))
-    ahead_other = lax.ppermute(from_ahead, "chan", swap)
-    lefts, rights = call(
-        functools.partial(late_kernel, chunk, BLK // 2),
-        "project_late",
-        [from_ahead, ahead_other, *early, weight, gain, lefts, rights],
-        operand_shapes(half),
-        chunk_scratch(half, chunk),
-        aliased=2,
-    )
+    for (start, size), behind_ahead in zip(cuts, arrived):
+        *behind_ahead, lefts = lax.optimization_barrier((*behind_ahead, lefts))
+        wide = chunk if start == 0 else size
+        others = [
+            lax.ppermute(lax.slice_in_dim(value, at, at + wide, axis=1), "chan", swap)
+            for at in range(0, size, wide)
+            for value in behind_ahead
+        ]
+        paired = pltpu.VMEM((half, size // BLK, LANES), BF16)
+        if start == 0:
+            lefts, rights_first = call(
+                functools.partial(fetched_kernel, chunk, 0, False),
+                "project_first",
+                [*behind_ahead, *others, weight, gain, lefts],
+                [left_shape, paired],
+                chunk_scratch(half, chunk),
+                aliased=1,
+            )
+        else:
+            lefts, rights = call(
+                functools.partial(fetched_kernel, chunk, start // BLK, True),
+                "project_last",
+                [*behind_ahead, *others, rights_first, weight, gain, lefts, rights],
+                [left_shape, right_shape],
+                [pltpu.VMEM((half, chunk // BLK, LANES), BF16)] + chunk_scratch(half, chunk),
+                aliased=2,
+            )
     updates = []
     for s in range(slots):
         update = triplet_sum(s, lefts, rights, a_slots, b_slots, counts, slots, 16)

time: 42.9 us -> 41.9 us (0.977)
  Pallas kernels: 19.6 us -> 17.1 us
  starting transfers between devices: 10.3 us -> 11.1 us
  waiting for transfers between devices: 12.7 us -> 13.3 us
    ppermute x2, waiting for transfers between devices: 7.46 us -> 8.63 us  [per_device(): lax.ppermute(chosen[2 * n + 1], 'row', down)]
    ppermute x2, starting transfers between devices: 4.78 us -> 5.93 us  [per_device(): lax.ppermute(chosen[2 * n + 1], 'row', down)]
    ppermute x2, waiting for transfers between devices: 2.19 us -> 1.18 us  [per_device(): lax.ppermute(chosen[2 * n], 'row', up)]
    pallas_call x4 -> x3, Pallas kernels: 9.68 us -> 8.77 us  [call(): pl.pallas_call(kernel, in_specs=specs, out_specs=[vmem] * len(out_shape),...]
    pallas_call x1, Pallas kernels: 2.02 us -> 1.33 us  [select_blocks(): pl.pallas_call(functools.partial(select_kernel, slots, a_slots.shape[0],...]
    pallas_call x2, Pallas kernels: 3.92 us -> 3.27 us  [finish(): pl.pallas_call(functools.partial(finish_kernel, s), in_specs=[vmem] * len...]
    ppermute x7 -> x6, waiting for transfers between devices: 2.77 us -> 3.27 us  [per_device(): lax.ppermute(lax.slice_in_dim(value, at, at + wide, axis=1), 'chan', swap)]
    ppermute x7 -> x6, starting transfers between devices: 1.75 us -> 1.37 us  [per_device(): lax.ppermute(lax.slice_in_dim(value, at, at + wide, axis=1), 'chan', swap)]
  transfers between devices with their start and end apart: 14 -> 13, of which waited for: 9 -> 9; matrix products, arithmetic and copies ran while one was open for 0% -> 0% of each run, Pallas kernels for 32% -> 24%
where the time goes in v11:
time: 41.9 us; the launch traced here: 41.7 us
  Pallas kernels  17.1 us (41%)
  waiting for transfers between devices  13.3 us (32%)
  starting transfers between devices  11.1 us (26%)
    pallas_call x3, Pallas kernels, call(): pl.pallas_call(kernel, in_specs=specs, out_specs=[vmem] * len(out_shape),...  8.77 us
    ppermute x2, waiting for transfers between devices, per_device(): lax.ppermute(chosen[2 * n + 1], 'row', down)  8.63 us
    ppermute x2, starting transfers between devices, per_device(): lax.ppermute(chosen[2 * n + 1], 'row', down)  5.93 us
    pallas_call x2, Pallas kernels, triplet_sum(): pl.pallas_call(functools.partial(triplet_kernel, s, slots, a_slots.shape[...  3.77 us
    ppermute x6, waiting for transfers between devices, per_device(): lax.ppermute(lax.slice_in_dim(value, at, at + wide, axis=1), 'chan', swap)  3.27 us
    pallas_call x2, Pallas kernels, finish(): pl.pallas_call(functools.partial(finish_kernel, s), in_specs=[vmem] * len...  3.27 us
    ppermute x2, starting transfers between devices, per_device(): lax.ppermute(chosen[2 * n], 'row', up)  2.64 us
    ppermute x6, starting transfers between devices, per_device(): lax.ppermute(lax.slice_in_dim(value, at, at + wide, axis=1), 'chan', swap)  1.37 us
  transfers between devices with their start and end apart: 13, of which 9 were waited for; matrix products, arithmetic and copies ran while one was open for 0% of the time, Pallas kernels for 24%

profile of v11, /device:TPU:0, one launch (start us, length us, event | category | flops | bytes accessed | tf_op | source)
XLA Modules:
  0.0 41.7 jit_solution(1754451076685447616)
XLA Ops:
  0.0 1.3 %select_blocks.1 = (bf16[2,64,4096]{2,1,0:T(8,128)(2,1)S(1)}, bf16[64,2048]{1,0:T(8,128)(2,1)S(1)}, bf16[64,2048]{1,0:T(8,128)(2,1)S(1)}, bf16[64,2048]{1,0:T(8,128)(2,1)S(1)}, bf16[64,2048]{1,0:T(8,128)(2,1)S(1)}) custom-call(s32[4,16]{1,0:T(4,128)} %bitcast.8, s32[4,16]{1,0:T(4,128)} %bitcast.11, s32[16]{0:T(128)} %n_ref.3, bf16[2,64,4096]{2,1,0:T(8,128)(2,1)} %pair_hbm.1), custom_call_target="tpu_custom_call" | custom-call | tf_op jit(solution)/shard_map/select_blocks/pallas_call | solution.py:75
  1.3 0.5 %collective-permute-start.4 = (bf16[2,64,4096]{2,1,0:T(8,128)(2,1)S(1)}, bf16[2,64,4096]{2,1,0:T(8,128)(2,1)S(1)}, u32[]{:S(2)}, u32[]{:S(2)}) collective-permute-start(bf16[2,64,4096]{2,1,0:T(8,128)(2,1)S(1)} %get-tuple-element.31.refs_0_), channel_id=1, source_target_pairs={{0,1},{1,0},{2,3},{3,2},{4,5},{5,4},{6,7},{7,6},{8,9},{9,8},{10,11... | collective-permute-start | bytes 3145736 | tf_op jit(solution)/shard_map/ppermute | solution.py:450
  1.9 2.6 %collective-permute-start.2 = (bf16[64,2048]{1,0:T(8,128)(2,1)S(1)}, bf16[64,2048]{1,0:T(8,128)(2,1)S(1)}, u32[]{:S(2)}, u32[]{:S(2)}) collective-permute-start(bf16[64,2048]{1,0:T(8,128)(2,1)S(1)} %get-tuple-element.29), channel_id=1, source_target_pairs={{0,4},{4,8},{8,12},{12,0},{1,5},{5,9},{9,13},{13,1},{2,6},{6,10},{... | collective-permute-start | bytes 786440 | tf_op jit(solution)/shard_map/ppermute | solution.py:447
  4.5 2.1 %collective-permute-start.3 = (bf16[64,2048]{1,0:T(8,128)(2,1)S(1)}, bf16[64,2048]{1,0:T(8,128)(2,1)S(1)}, u32[]{:S(2)}, u32[]{:S(2)}) collective-permute-start(bf16[64,2048]{1,0:T(8,128)(2,1)S(1)} %get-tuple-element.30), channel_id=1, source_target_pairs={{0,12},{4,0},{8,4},{12,8},{1,13},{5,1},{9,5},{13,9},{2,14},{6,2},{... | collective-permute-start | bytes 786440 | tf_op jit(solution)/shard_map/ppermute | solution.py:447
  6.6 0.0 collective-permute-start
  6.6 3.8 %collective-permute-start.1 = (bf16[64,2048]{1,0:T(8,128)(2,1)S(1)}, bf16[64,2048]{1,0:T(8,128)(2,1)S(1)}, u32[]{:S(2)}, u32[]{:S(2)}) collective-permute-start(bf16[64,2048]{1,0:T(8,128)(2,1)S(1)} %get-tuple-element.28), channel_id=1, source_target_pairs={{0,12},{4,0},{8,4},{12,8},{1,13},{5,1},{9,5},{13,9},{2,14},{6,2},{... | collective-permute-start | bytes 786440 | tf_op jit(solution)/shard_map/ppermute | solution.py:447
  10.4 0.0 collective-permute-done.4.refs_1_
  10.4 5.0 %project_own.1 = (bf16[2,64,64,128]{3,2,1,0:T(8,128)(2,1)S(1)}, bf16[5,64,64,64]{3,2,1,0:T(8,128)(2,1)S(1)}, bf16[2,64,4096]{2,1,0:T(8,128)(2,1)S(1)}, bf16[256,...) custom-call(bf16[2,64,4096]{2,1,0:T(8,128)(2,1)S(1)} %get-tuple-element.31.refs_0_, ...), custom_call_target="tpu_custom_call" | custom-call | tf_op jit(solution)/shard_map/project_own/pallas_call | solution.py:279
  15.5 0.0 collective-permute-done.2.m0
  15.5 3.9 %collective-permute-done.3.m1 = bf16[64,2048]{1,0:T(8,128)(2,1)S(1)} collective-permute-done((bf16[64,2048]{1,0:T(8,128)(2,1)S(1)}, bf16[64,2048]{1,0:T(8,128)(2,1)S(1)}, u32[]{:S(2)}, u32[]{:S(2)}) %collective-permute-start.3) | collective-permute-done | bytes 262176 | tf_op jit(solution)/shard_map/ppermute | solution.py:447
  19.4 0.1 collective-permute-start.7
  19.5 0.5 %collective-permute-start.5 = (bf16[64,1024]{1,0:T(8,128)(2,1)S(1)}, bf16[64,1024]{1,0:T(8,128)(2,1)S(1)}, u32[]{:S(2)}, u32[]{:S(2)}) collective-permute-start(bf16[64,1024]{1,0:T(8,128)(2,1)S(1)} %get-tuple-element.52), channel_id=1, source_target_pairs={{0,1},{1,0},{2,3},{3,2},{4,5},{5,4},{6,7},{7,6},{8,9},{9,8},{10,11... | collective-permute-start | bytes 393224 | tf_op jit(solution)/shard_map/ppermute | solution.py:475
  20.0 0.1 collective-permute-start.8
  20.1 0.7 %collective-permute-done.7.refs_2_ = bf16[64,1024]{1,0:T(8,128)(2,1)S(1)} collective-permute-done((bf16[64,1024]{1,0:T(8,128)(2,1)S(1)}, bf16[64,1024]{1,0:T(8,128)(2,1)S(1)}, u32[]{:S(2)}, u32[]{:S(2)}) %collective-permute-start.7) | collective-permute-done | bytes 131104 | tf_op jit(solution)/shard_map/ppermute | solution.py:475
  20.8 0.1 collective-permute-start.6
  21.0 0.0 collective-permute-done.5.refs_0_
  21.0 0.4 collective-permute-done.8.refs_3_
  21.4 0.8 %collective-permute-done.6.refs_1_ = bf16[64,1024]{1,0:T(8,128)(2,1)S(1)} collective-permute-done((bf16[64,1024]{1,0:T(8,128)(2,1)S(1)}, bf16[64,1024]{1,0:T(8,128)(2,1)S(1)}, u32[]{:S(2)}, u32[]{:S(2)}) %collective-permute-start.6) | collective-permute-done | bytes 131104 | tf_op jit(solution)/shard_map/ppermute | solution.py:475
  22.2 1.7 %project_first.1 = (bf16[2,64,64,128]{3,2,1,0:T(8,128)(2,1)S(1)}, bf16[64,32,128]{2,1,0:T(8,128)(2,1)S(1)}) custom-call(bf16[64,2048]{1,0:T(8,128)(2,1)S(1)} %collective-permute-done.2.m0, bf16[64,2048]{1,0:T(8,128)(2,1)S(1)} %collective-permute-done.3.m1, bf16[64,1024]{1,0:T(8,128)(2,1)S(1)} %collective-permute-done.5.refs_0_, ...), custom_call_target="tpu_custom_call", output_to_operand_aliasing={{0}: (8, {})} | custom-call | tf_op jit(solution)/shard_map/project_first/pallas_call | solution.py:279
  23.8 1.2 %collective-permute-done.m0 = bf16[64,2048]{1,0:T(8,128)(2,1)S(1)} collective-permute-done((bf16[64,2048]{1,0:T(8,128)(2,1)S(1)}, bf16[64,2048]{1,0:T(8,128)(2,1)S(1)}, u32[]{:S(2)}, u32[]{:S(2)}) %collective-permute-start) | collective-permute-done | bytes 262176 | tf_op jit(solution)/shard_map/ppermute | solution.py:447
  25.0 4.7 %collective-permute-done.1.m1 = bf16[64,2048]{1,0:T(8,128)(2,1)S(1)} collective-permute-done((bf16[64,2048]{1,0:T(8,128)(2,1)S(1)}, bf16[64,2048]{1,0:T(8,128)(2,1)S(1)}, u32[]{:S(2)}, u32[]{:S(2)}) %collective-permute-start.1) | collective-permute-done | bytes 262176 | tf_op jit(solution)/shard_map/ppermute | solution.py:447
  29.7 0.0 collective-permute-start.9
  29.7 0.5 %collective-permute-start.10 = (bf16[64,2048]{1,0:T(8,128)(2,1)S(1)}, bf16[64,2048]{1,0:T(8,128)(2,1)S(1)}, u32[]{:S(2)}, u32[]{:S(2)}) collective-permute-start(bf16[64,2048]{1,0:T(8,128)(2,1)S(1)} %collective-permute-done.1.m1), channel_id=1, source_target_pairs={{0,1},{1,0},{2,3},{3,2},{4,5},{5,4},{6,7},{7,6},{8,9},{9,8},{10,11... | collective-permute-start | bytes 786440 | tf_op jit(solution)/shard_map/ppermute | solution.py:475
  30.2 1.0 %collective-permute-done.9.refs_0_ = bf16[64,2048]{1,0:T(8,128)(2,1)S(1)} collective-permute-done((bf16[64,2048]{1,0:T(8,128)(2,1)S(1)}, bf16[64,2048]{1,0:T(8,128)(2,1)S(1)}, u32[]{:S(2)}, u32[]{:S(2)}) %collective-permute-start.9) | collective-permute-done | bytes 262176 | tf_op jit(solution)/shard_map/ppermute | solution.py:475
  31.3 0.4 collective-permute-done.10.refs_1_
  31.6 0.0 copy-start
  31.6 0.0 copy-start.1
  31.6 0.0 copy-start.2
  31.6 2.1 %project_last.1 = (bf16[2,64,64,128]{3,2,1,0:T(8,128)(2,1)S(1)}, bf16[5,64,64,64]{3,2,1,0:T(8,128)(2,1)S(1)}) custom-call(bf16[64,2048]{1,0:T(8,128)(2,1)S(1)} %collective-permute-done.m0, bf16[64,2048]{1,0:T(8,128)(2,1)S(1)} %collective-permute-done.1.m1, ...), custom_call_target="tpu_custom_call", output_to_operand_aliasing={{0}: (7, {}), {1}: (8, {})} | custom-call | tf_op jit(solution)/shard_map/project_last/pallas_call | solution.py:279
  33.7 0.0 copy-done
  33.8 0.0 copy-done.1
  33.8 0.0 copy-done.2
  33.8 1.9 %triplets.2.mine_ref = bf16[64,4096]{1,0:T(8,128)(2,1)S(1)} custom-call(s32[4,16]{1,0:T(4,128)S(1)} %bitcast.9, s32[4,16]{1,0:T(4,128)S(1)} %bitcast.12, s32[16]{0:T(128)S(1)} %copy-done.2, bf16[2,64,64,128]{3,2,1,0:T(8,128)(2,1)S(1)} %get-tuple-element.46.l_ref, bf16[5,64,64,64]{3,2,1,0:T(8,128)(2,1)S(1)} %get-tuple-element.45.turned_ref), custom_call_target="tpu_custom_call" | custom-call | tf_op jit(solution)/shard_map/triplets/pallas_call | solution.py:347
  35.7 0.2 collective-permute-start.12
  35.9 1.9 %triplets.3.mine_ref = bf16[64,4096]{1,0:T(8,128)(2,1)S(1)} custom-call(s32[4,16]{1,0:T(4,128)S(1)} %bitcast.10, s32[4,16]{1,0:T(4,128)S(1)} %bitcast.13, s32[16]{0:T(128)S(1)} %copy-done.2, bf16[2,64,64,128]{3,2,1,0:T(8,128)(2,1)S(1)} %get-tuple-element.46.l_ref, bf16[5,64,64,64]{3,2,1,0:T(8,128)(2,1)S(1)} %get-tuple-element.45.turned_ref), custom_call_target="tpu_custom_call" | custom-call | tf_op jit(solution)/shard_map/triplets/pallas_call | solution.py:347
  37.8 0.4 %collective-permute-start.11 = (bf16[64,4096]{1,0:T(8,128)(2,1)S(1)}, bf16[64,4096]{1,0:T(8,128)(2,1)S(1)}, u32[]{:S(2)}, u32[]{:S(2)}) collective-permute-start(bf16[64,4096]{1,0:T(8,128)(2,1)S(1)} %triplets.3.mine_ref), channel_id=1, source_target_pairs={{0,1},{1,0},{2,3},{3,2},{4,5},{5,4},{6,7},{7,6},{8,9},{9,8},{10,11... | collective-permute-start | bytes 1572872 | tf_op jit(solution)/shard_map/ppermute | solution.py:501
  38.2 0.0 collective-permute-done.12.theirs_ref
  38.2 1.3 %finish.2.refs_0_ = bf16[64,4096]{1,0:T(8,128)(2,1)S(1)} custom-call(bf16[64,4096]{1,0:T(8,128)(2,1)S(1)} %triplets.2.mine_ref, bf16[64,4096]{1,0:T(8,128)(2,1)S(1)} %collective-permute-done.12.theirs_ref, bf16[2,64,4096]{2,1,0:T(8,128)(2,1)S(1)} %get-tuple-element.47.gate_ref, bf16[64,128]{1,0:T(8,128)(2,1)S(1)} %get-tuple-element.48.w_ref), custom_call_target="tpu_custom_call" | custom-call | tf_op jit(solution)/shard_map/finish/pallas_call | solution.py:404
  39.5 0.3 collective-permute-done.11.theirs_ref
  39.7 2.0 %finish.3 = bf16[2,64,4096]{2,1,0:T(8,128)(2,1)} custom-call(bf16[64,4096]{1,0:T(8,128)(2,1)S(1)} %triplets.3.mine_ref, bf16[64,4096]{1,0:T(8,128)(2,1)S(1)} %collective-permute-done.11.theirs_ref, bf16[2,64,4096]{2,1,0:T(8,128)(2,1)S(1)} %get-tuple-element.47.gate_ref, bf16[64,128]{1,0:T(8,128)(2,1)S(1)} %get-tuple-element.48.w_ref, ...), custom_call_target="tpu_custom_call" | custom-call | tf_op jit(solution)/shard_map/finish/pallas_call | solution.py:404
  (2 shorter events, 0.0 us)
Async XLA Ops:
  1.3 9.1 %collective-permute-start.4 = (bf16[2,64,4096]{2,1,0:T(8,128)(2,1)S(1)}, bf16[2,64,4096]{2,1,0:T(8,128)(2,1)S(1)}, u32[]{:S(2)}, u32[]{:S(2)}) collective-permute-start(bf16[2,64,4096]{2,1,0:T(8,128)(2,1)S(1)} %get-tuple-element.31.refs_0_), channel_id=1, source_target_pairs={{0,1},{1,0},{2,3},{3,2},{4,5},{5,4},{6,7},{7,6},{8,9},{9,8},{10,11... | collective-permute-start | bytes 3145736 | tf_op jit(solution)/shard_map/ppermute | solution.py:450
  1.9 13.6 %collective-permute-start.2 = (bf16[64,2048]{1,0:T(8,128)(2,1)S(1)}, bf16[64,2048]{1,0:T(8,128)(2,1)S(1)}, u32[]{:S(2)}, u32[]{:S(2)}) collective-permute-start(bf16[64,2048]{1,0:T(8,128)(2,1)S(1)} %get-tuple-element.29), channel_id=1, source_target_pairs={{0,4},{4,8},{8,12},{12,0},{1,5},{5,9},{9,13},{13,1},{2,6},{6,10},{... | collective-permute-start | bytes 786440 | tf_op jit(solution)/shard_map/ppermute | solution.py:447
  4.5 14.9 %collective-permute-start.3 = (bf16[64,2048]{1,0:T(8,128)(2,1)S(1)}, bf16[64,2048]{1,0:T(8,128)(2,1)S(1)}, u32[]{:S(2)}, u32[]{:S(2)}) collective-permute-start(bf16[64,2048]{1,0:T(8,128)(2,1)S(1)} %get-tuple-element.30), channel_id=1, source_target_pairs={{0,12},{4,0},{8,4},{12,8},{1,13},{5,1},{9,5},{13,9},{2,14},{6,2},{... | collective-permute-start | bytes 786440 | tf_op jit(solution)/shard_map/ppermute | solution.py:447
  6.6 18.4 %collective-permute-start = (bf16[64,2048]{1,0:T(8,128)(2,1)S(1)}, bf16[64,2048]{1,0:T(8,128)(2,1)S(1)}, u32[]{:S(2)}, u32[]{:S(2)}) collective-permute-start(bf16[64,2048]{1,0:T(8,128)(2,1)S(1)} %get-tuple-element.27), channel_id=1, source_target_pairs={{0,4},{4,8},{8,12},{12,0},{1,5},{5,9},{9,13},{13,1},{2,6},{6,10},{... | collective-permute-start | bytes 786440 | tf_op jit(solution)/shard_map/ppermute | solution.py:447
  6.6 23.1 %collective-permute-start.1 = (bf16[64,2048]{1,0:T(8,128)(2,1)S(1)}, bf16[64,2048]{1,0:T(8,128)(2,1)S(1)}, u32[]{:S(2)}, u32[]{:S(2)}) collective-permute-start(bf16[64,2048]{1,0:T(8,128)(2,1)S(1)} %get-tuple-element.28), channel_id=1, source_target_pairs={{0,12},{4,0},{8,4},{12,8},{1,13},{5,1},{9,5},{13,9},{2,14},{6,2},{... | collective-permute-start | bytes 786440 | tf_op jit(solution)/shard_map/ppermute | solution.py:447
  19.4 1.4 %collective-permute-start.7 = (bf16[64,1024]{1,0:T(8,128)(2,1)S(1)}, bf16[64,1024]{1,0:T(8,128)(2,1)S(1)}, u32[]{:S(2)}, u32[]{:S(2)}) collective-permute-start(bf16[64,1024]{1,0:T(8,128)(2,1)S(1)} %get-tuple-element.51), channel_id=1, source_target_pairs={{0,1},{1,0},{2,3},{3,2},{4,5},{5,4},{6,7},{7,6},{8,9},{9,8},{10,11... | collective-permute-start | bytes 393224 | tf_op jit(solution)/shard_map/ppermute | solution.py:475
  19.5 1.5 %collective-permute-start.5 = (bf16[64,1024]{1,0:T(8,128)(2,1)S(1)}, bf16[64,1024]{1,0:T(8,128)(2,1)S(1)}, u32[]{:S(2)}, u32[]{:S(2)}) collective-permute-start(bf16[64,1024]{1,0:T(8,128)(2,1)S(1)} %get-tuple-element.52), channel_id=1, source_target_pairs={{0,1},{1,0},{2,3},{3,2},{4,5},{5,4},{6,7},{7,6},{8,9},{9,8},{10,11... | collective-permute-start | bytes 393224 | tf_op jit(solution)/shard_map/ppermute | solution.py:475
  20.0 1.4 %collective-permute-start.8 = (bf16[64,1024]{1,0:T(8,128)(2,1)S(1)}, bf16[64,1024]{1,0:T(8,128)(2,1)S(1)}, u32[]{:S(2)}, u32[]{:S(2)}) collective-permute-start(bf16[64,1024]{1,0:T(8,128)(2,1)S(1)} %get-tuple-element.49), channel_id=1, source_target_pairs={{0,1},{1,0},{2,3},{3,2},{4,5},{5,4},{6,7},{7,6},{8,9},{9,8},{10,11... | collective-permute-start | bytes 393224 | tf_op jit(solution)/shard_map/ppermute | solution.py:475
  20.8 1.3 %collective-permute-start.6 = (bf16[64,1024]{1,0:T(8,128)(2,1)S(1)}, bf16[64,1024]{1,0:T(8,128)(2,1)S(1)}, u32[]{:S(2)}, u32[]{:S(2)}) collective-permute-start(bf16[64,1024]{1,0:T(8,128)(2,1)S(1)} %get-tuple-element.50), channel_id=1, source_target_pairs={{0,1},{1,0},{2,3},{3,2},{4,5},{5,4},{6,7},{7,6},{8,9},{9,8},{10,11... | collective-permute-start | bytes 393224 | tf_op jit(solution)/shard_map/ppermute | solution.py:475
  29.7 1.5 %collective-permute-start.9 = (bf16[64,2048]{1,0:T(8,128)(2,1)S(1)}, bf16[64,2048]{1,0:T(8,128)(2,1)S(1)}, u32[]{:S(2)}, u32[]{:S(2)}) collective-permute-start(bf16[64,2048]{1,0:T(8,128)(2,1)S(1)} %collective-permute-done.m0), channel_id=1, source_target_pairs={{0,1},{1,0},{2,3},{3,2},{4,5},{5,4},{6,7},{7,6},{8,9},{9,8},{10,11... | collective-permute-start | bytes 786440 | tf_op jit(solution)/shard_map/ppermute | solution.py:475
  29.7 1.9 %collective-permute-start.10 = (bf16[64,2048]{1,0:T(8,128)(2,1)S(1)}, bf16[64,2048]{1,0:T(8,128)(2,1)S(1)}, u32[]{:S(2)}, u32[]{:S(2)}) collective-permute-start(bf16[64,2048]{1,0:T(8,128)(2,1)S(1)} %collective-permute-done.1.m1), channel_id=1, source_target_pairs={{0,1},{1,0},{2,3},{3,2},{4,5},{5,4},{6,7},{7,6},{8,9},{9,8},{10,11... | collective-permute-start | bytes 786440 | tf_op jit(solution)/shard_map/ppermute | solution.py:475
  31.6 2.1 %copy-start = (s32[16,4]{0,1:T(4,128)S(1)}, s32[16,4]{0,1:T(4,128)}, u32[]{:S(2)}) copy-start(s32[16,4]{0,1:T(4,128)} %param.17) | copy-start | bytes 772
  31.6 2.1 %copy-start.1 = (s32[16,4]{0,1:T(4,128)S(1)}, s32[16,4]{0,1:T(4,128)}, u32[]{:S(2)}) copy-start(s32[16,4]{0,1:T(4,128)} %param.18) | copy-start | bytes 772
  31.6 2.1 %copy-start.2 = (s32[16]{0:T(128)S(1)}, s32[16]{0:T(128)}, u32[]{:S(2)}) copy-start(s32[16]{0:T(128)} %n_ref.3) | copy-start | bytes 196
  35.7 2.5 %collective-permute-start.12 = (bf16[64,4096]{1,0:T(8,128)(2,1)S(1)}, bf16[64,4096]{1,0:T(8,128)(2,1)S(1)}, u32[]{:S(2)}, u32[]{:S(2)}) collective-permute-start(bf16[64,4096]{1,0:T(8,128)(2,1)S(1)} %triplets.2.mine_ref), channel_id=1, source_target_pairs={{0,1},{1,0},{2,3},{3,2},{4,5},{5,4},{6,7},{7,6},{8,9},{9,8},{10,11... | collective-permute-start | bytes 1572872 | tf_op jit(solution)/shard_map/ppermute | solution.py:501
  37.8 2.0 %collective-permute-start.11 = (bf16[64,4096]{1,0:T(8,128)(2,1)S(1)}, bf16[64,4096]{1,0:T(8,128)(2,1)S(1)}, u32[]{:S(2)}, u32[]{:S(2)}) collective-permute-start(bf16[64,4096]{1,0:T(8,128)(2,1)S(1)} %triplets.3.mine_ref), channel_id=1, source_target_pairs={{0,1},{1,0},{2,3},{3,2},{4,5},{5,4},{6,7},{7,6},{8,9},{9,8},{10,11... | collective-permute-start | bytes 1572872 | tf_op jit(solution)/shard_map/ppermute | solution.py:501

commit v12 on v11

--- a/solution.py
+++ b/solution.py
@@ -31,9 +31,34 @@
     return tile_of(row, col), tile_of(behind, col), tile_of(ahead, col)
 
 
+def used_picks(s, slots, triplets, a_ref, b_ref, n_ref):
+    me, behind, ahead = neighbour_tiles()
+    block = me * slots + s
+    count = n_ref[block]
+    picks = []
+    for left_at in range(4):
+        pick = jnp.int32(4)
+        for m in range(triplets):
+            left = a_ref[m, block]
+            if left_at < 2:
+                hit = left == me * slots + left_at
+            else:
+                base = (behind, ahead)[left_at - 2] * slots
+                hit = jnp.logical_and(left >= base, left < base + slots)
+            hit = jnp.logical_and(hit, m < count)
+            place = b_ref[m, block] - me * slots
+            from_me = jnp.logical_and(place >= 0, place < slots)
+            right = b_ref[m, block] - behind * slots
+            from_behind = jnp.logical_and(right >= 0, right < slots)
+            place = jnp.where(from_me, place, jnp.where(from_behind, 2, 3))
+            pick = jnp.where(hit, place, pick)
+        picks.append(pick)
+    return picks
+
+
 def select_kernel(slots, triplets, cuts, a_hbm, b_hbm, n_hbm, pair_hbm, *refs):
-    pair_ref, *out_refs = refs[: 1 + 2 * len(cuts)]
-    a_ref, b_ref, n_ref, sems = refs[1 + 2 * len(cuts) :]
+    picks_ref, pair_ref, *out_refs = refs[: 2 + 3 * len(cuts)]
+    a_ref, b_ref, n_ref, sems = refs[2 + 3 * len(cuts) :]
     me, behind, ahead = neighbour_tiles()
     whole = pltpu.make_async_copy(pair_hbm, pair_ref, sems.at[0])
     tables = [
@@ -44,7 +69,7 @@
         copy.start()
     for copy in tables:
         copy.wait()
-    picks = []
+    chosen = []
     for target in (ahead, behind):
         pick = jnp.int32(0)
         for s in range(slots):
@@ -54,19 +79,23 @@
                     name = ids[m, target * slots + s] - me * slots
                     mine = jnp.logical_and(name >= 0, name < slots)
                     pick = jnp.where(jnp.logical_and(m < count, mine), name, pick)
-        picks.append(pick)
+        chosen.append(pick)
+    chosen.append(jnp.where(lax.axis_index("row") == 0, chosen[1], chosen[0]))
+    for s in range(slots):
+        for at, pick in enumerate(used_picks(s, slots, triplets, a_ref, b_ref, n_ref)):
+            picks_ref[4 * s + at] = pick
     whole.wait()
     for at, (start, size) in enumerate(cuts):
-        for which, pick in enumerate(picks):
-            out_refs[2 * at + which][...] = pair_ref[pick, :, start : start + size]
+        for which, pick in enumerate(chosen):
+            out_refs[3 * at + which][...] = pair_ref[pick, :, start : start + size]
 
 
 def select_blocks(pair, a_slots, b_slots, counts, cuts):
     slots, channels, cells = pair.shape
     hbm = pl.BlockSpec(memory_space=pltpu.HBM)
     vmem = pl.BlockSpec(memory_space=pltpu.VMEM)
-    out_shape = [pltpu.VMEM(pair.shape, pair.dtype)] + [
-        pltpu.VMEM((channels, size), pair.dtype) for _, size in cuts for _ in range(2)
+    out_shape = [pltpu.SMEM((4 * slots,), jnp.int32), pltpu.VMEM(pair.shape, pair.dtype)] + [
+        pltpu.VMEM((channels, size), pair.dtype) for _, size in cuts for _ in range(3)
     ]
     operands = [
         pltpu.with_memory_space_constraint(value, pltpu.HBM)
@@ -76,7 +105,7 @@
         functools.partial(select_kernel, slots, a_slots.shape[0], cuts),
         out_shape=out_shape,
         in_specs=[hbm] * 4,
-        out_specs=[vmem] * len(out_shape),
+        out_specs=[pl.BlockSpec(memory_space=pltpu.SMEM)] + [vmem] * (len(out_shape) - 1),
         scratch_shapes=[pltpu.SMEM(value.shape, value.dtype) for value in operands[:3]]
         + [pltpu.SemaphoreType.DMA((4,))],
         name="select_blocks",
@@ -288,32 +317,8 @@
     )(*operands)
 
 
-def triplet_kernel(s, slots, triplets, group, a_ref, b_ref, n_ref, l_ref, turned_ref, out_ref, *accs):
-    me, behind, ahead = neighbour_tiles()
-    block = me * slots + s
-    count = n_ref[block]
-    picks = []
-    for pair_at in range(2):
-        for part in range(2):
-            chosen = jnp.int32(0)
-            used = jnp.int32(0)
-            for m in range(triplets):
-                left = a_ref[m, block]
-                if pair_at == 0:
-                    hit = left == me * slots + part
-                else:
-                    first = (behind, ahead)[part] * slots
-                    hit = jnp.logical_and(left >= first, left < first + slots)
-                hit = jnp.logical_and(hit, m < count)
-                place = b_ref[m, block] - me * slots
-                from_me = jnp.logical_and(place >= 0, place < slots)
-                right = b_ref[m, block] - behind * slots
-                from_behind = jnp.logical_and(right >= 0, right < slots)
-                place = jnp.where(from_me, place, jnp.where(from_behind, 2, 3))
-                chosen = jnp.where(hit, place, chosen)
-                used = jnp.where(hit, 1, used)
-            picks.append(jnp.where(used == 1, chosen, 4))
-
+def triplet_kernel(s, group, picks_ref, l_ref, turned_ref, out_ref, *accs):
+    picks = [picks_ref[4 * s + at] for at in range(4)]
     take_low = lax.broadcasted_iota(jnp.int32, (group, LANES), 1) < BLK
     half = l_ref.shape[1]
     pitch = accs[0].shape[0] // BLK
@@ -337,22 +342,22 @@
                 ).astype(BF16)
 
 
-def triplet_sum(s, lefts, rights, a_slots, b_slots, counts, slots, group):
+def triplet_sum(s, picks, lefts, rights, group):
     half = lefts.shape[1]
-    smem = pl.BlockSpec(memory_space=pltpu.SMEM)
     vmem = pl.BlockSpec(memory_space=pltpu.VMEM)
+    picks = pltpu.with_memory_space_constraint(picks, pltpu.SMEM)
     lefts, rights = (
         pltpu.with_memory_space_constraint(value, pltpu.VMEM) for value in (lefts, rights)
     )
     return pl.pallas_call(
-        functools.partial(triplet_kernel, s, slots, a_slots.shape[0], group),
-        in_specs=[smem, smem, smem, vmem, vmem],
+        functools.partial(triplet_kernel, s, group),
+        in_specs=[pl.BlockSpec(memory_space=pltpu.SMEM), vmem, vmem],
         out_specs=vmem,
         out_shape=pltpu.VMEM((half, BLK * BLK), BF16),
         scratch_shapes=[pltpu.VMEM((BLK * (group + 8), LANES), F32)] * 2,
         compiler_params=pltpu.CompilerParams(vmem_limit_bytes=VMEM_LIMIT),
         name="triplets",
-    )(a_slots, b_slots, counts, lefts, rights)
+    )(picks, lefts, rights)
 
 
 def finish_kernel(s, mine_ref, theirs_ref, gate_ref, w_ref, *refs):
@@ -442,9 +447,14 @@
 
     chunk = cells // 4
     cuts = ((0, 2 * chunk), (2 * chunk, 2 * chunk))
-    pair, *chosen = select_blocks(pair, a_slots, b_slots, counts, cuts)
+    picks, pair, *chosen = select_blocks(pair, a_slots, b_slots, counts, cuts)
+    ends = [(0, rows - 1), (rows - 1, 0)]
+    row = lax.axis_index("row")
     arrived = [
-        (lax.ppermute(chosen[2 * n], "row", up), lax.ppermute(chosen[2 * n + 1], "row", down))
+        tuple(
+            lax.ppermute(chosen[3 * n + which], "row", pairs)
+            for which, pairs in ((2, ends), (0, up[:-1]), (1, down[1:]))
+        )
         for n in range(len(cuts))
     ]
     pair_other = lax.ppermute(pair, "chan", swap)
@@ -469,7 +479,11 @@
         hbm=len(weights),
     )
     for (start, size), behind_ahead in zip(cuts, arrived):
-        *behind_ahead, lefts = lax.optimization_barrier((*behind_ahead, lefts))
+        far, near_behind, near_ahead, lefts = lax.optimization_barrier((*behind_ahead, lefts))
+        behind_ahead = [
+            jnp.where(row == 0, far, near_behind),
+            jnp.where(row == rows - 1, far, near_ahead),
+        ]
         wide = chunk if start == 0 else size
         others = [
             lax.ppermute(lax.slice_in_dim(value, at, at + wide, axis=1), "chan", swap)
@@ -497,7 +511,7 @@
             )
     updates = []
     for s in range(slots):
-        update = triplet_sum(s, lefts, rights, a_slots, b_slots, counts, slots, 16)
+        update = triplet_sum(s, picks, lefts, rights, 16)
         updates.append((update, lax.ppermute(update, "chan", swap)))
         if s + 1 < slots:
             update, lefts = lax.optimization_barrier((update, lefts))

time: 41.9 us -> 45.7 us (1.091)
  starting transfers between devices: 11.1 us -> 20.2 us
  waiting for transfers between devices: 13.3 us -> 6.25 us
  other arithmetic: 0 us -> 2.08 us
  Pallas kernels: 17.1 us -> 15.9 us
  local copies, waits for them, and re-layouts: 0.05 us -> 0.73 us
    ppermute x4 -> x6, starting transfers between devices: 8.57 us -> 17.5 us  [per_device(): lax.ppermute(chosen[3 * n + which], 'row', pairs)]
    ppermute x4 -> x6, waiting for transfers between devices: 9.81 us -> 2.72 us  [per_device(): lax.ppermute(chosen[3 * n + which], 'row', pairs)]
    select_n x0 -> x2, other arithmetic: none -> 2.08 us  [per_device(): jnp.where(row == rows - 1, far, near_ahead)]
    pallas_call x2, Pallas kernels: 3.77 us -> 2.45 us  [triplet_sum(): pl.pallas_call(functools.partial(triplet_kernel, s, group), in_specs=[pl....]
    unnamed x6 -> x2, local copies, waits for them, and re-layouts: 0.01 us -> 0.7 us
  transfers between devices with their start and end apart: 13 -> 15, of which waited for: 9 -> 9; matrix products, arithmetic and copies ran while one was open for 0% -> 2% of each run, Pallas kernels for 24% -> 20%
where the time goes in v12:
time: 45.7 us; the launch traced here: 45.4 us
  starting transfers between devices  20.2 us (44%)
  Pallas kernels  15.9 us (35%)
  waiting for transfers between devices  6.25 us (14%)
  other arithmetic  2.08 us (5%)
  local copies, waits for them, and re-layouts  0.73 us (2%)
    ppermute x6, starting transfers between devices, per_device(): lax.ppermute(chosen[3 * n + which], 'row', pairs)  17.5 us
    pallas_call x3, Pallas kernels, call(): pl.pallas_call(kernel, in_specs=specs, out_specs=[vmem] * len(out_shape),...  8.78 us
    ppermute x6, waiting for transfers between devices, per_device(): lax.ppermute(lax.slice_in_dim(value, at, at + wide, axis=1), 'chan', swap)  3.27 us
    pallas_call x2, Pallas kernels, finish(): pl.pallas_call(functools.partial(finish_kernel, s), in_specs=[vmem] * len...  3.27 us
    ppermute x6, waiting for transfers between devices, per_device(): lax.ppermute(chosen[3 * n + which], 'row', pairs)  2.72 us
    pallas_call x2, Pallas kernels, triplet_sum(): pl.pallas_call(functools.partial(triplet_kernel, s, group), in_specs=[pl....  2.45 us
    select_n x2, other arithmetic, per_device(): jnp.where(row == rows - 1, far, near_ahead)  2.08 us
    ppermute x6, starting transfers between devices, per_device(): lax.ppermute(lax.slice_in_dim(value, at, at + wide, axis=1), 'chan', swap)  1.61 us
  transfers between devices with their start and end apart: 15, of which 9 were waited for; matrix products, arithmetic and copies ran while one was open for 2% of the time, Pallas kernels for 20%

profile of v12, /device:TPU:0, one launch (start us, length us, event | category | flops | bytes accessed | tf_op | source)
XLA Modules:
  0.0 45.4 jit_solution(3608790257088912921)
XLA Ops:
  0.0 1.4 %select_blocks.1 = (s32[8]{0:T(128)S(4)}, bf16[2,64,4096]{2,1,0:T(8,128)(2,1)S(1)}, bf16[64,2048]{1,0:T(8,128)(2,1)S(1)}, bf16[64,2048]{1,0:T(8,128)(2,1)S(1)}, ...) custom-call(s32[4,16]{1,0:T(4,128)} %bitcast.12, ...), custom_call_target="tpu_custom_call" | custom-call | tf_op jit(solution)/shard_map/select_blocks/pallas_call | solution.py:104
  1.4 0.0 copy-start
  1.4 0.7 %copy-done = bf16[64,2048]{1,0:T(8,128)(2,1)} copy-done((bf16[64,2048]{1,0:T(8,128)(2,1)}, bf16[64,2048]{1,0:T(8,128)(2,1)S(1)}, u32[]{:S(2)}) %copy-start) | copy-done | bytes 262168
  2.1 0.5 collective-permute-start.6
  2.5 6.5 %collective-permute-start.3 = (bf16[64,2048]{1,0:T(8,128)(2,1)}, bf16[64,2048]{1,0:T(8,128)(2,1)}, u32[]{:S(2)}, u32[]{:S(2)}) collective-permute-start(bf16[64,2048]{1,0:T(8,128)(2,1)} %copy-done), channel_id=1, source_target_pairs={{0,12},{12,0},{1,13},{13,1},{2,14},{14,2},{3,15},{15,3},{16,28},{2... | collective-permute-start | bytes 786440 | tf_op jit(solution)/shard_map/ppermute | solution.py:455
  9.0 2.0 %collective-permute-start.4 = (bf16[64,2048]{1,0:T(8,128)(2,1)S(1)}, bf16[64,2048]{1,0:T(8,128)(2,1)}, u32[]{:S(2)}, u32[]{:S(2)}) collective-permute-start(bf16[64,2048]{1,0:T(8,128)(2,1)S(1)} %get-tuple-element.37), channel_id=1, source_target_pairs={{0,4},{4,8},{8,12},{1,5},{5,9},{9,13},{2,6},{6,10},{10,14},{3,7},{... | collective-permute-start | bytes 786440 | tf_op jit(solution)/shard_map/ppermute | solution.py:455
  11.0 1.3 %collective-permute-start.5 = (bf16[64,2048]{1,0:T(8,128)(2,1)S(1)}, bf16[64,2048]{1,0:T(8,128)(2,1)}, u32[]{:S(2)}, u32[]{:S(2)}) collective-permute-start(bf16[64,2048]{1,0:T(8,128)(2,1)S(1)} %get-tuple-element.38), channel_id=1, source_target_pairs={{4,0},{8,4},{12,8},{5,1},{9,5},{13,9},{6,2},{10,6},{14,10},{7,3},{... | collective-permute-start | bytes 786440 | tf_op jit(solution)/shard_map/ppermute | solution.py:455
  12.3 5.2 %collective-permute-start = (bf16[64,2048]{1,0:T(8,128)(2,1)S(1)}, bf16[64,2048]{1,0:T(8,128)(2,1)}, u32[]{:S(2)}, u32[]{:S(2)}) collective-permute-start(bf16[64,2048]{1,0:T(8,128)(2,1)S(1)} %get-tuple-element.33), channel_id=1, source_target_pairs={{0,12},{12,0},{1,13},{13,1},{2,14},{14,2},{3,15},{15,3},{16,28},{2... | collective-permute-start | bytes 786440 | tf_op jit(solution)/shard_map/ppermute | solution.py:455
  17.5 0.0 collective-permute-done.6.refs_1_
  17.5 1.3 %collective-permute-start.1 = (bf16[64,2048]{1,0:T(8,128)(2,1)S(1)}, bf16[64,2048]{1,0:T(8,128)(2,1)S(1)}, u32[]{:S(2)}, u32[]{:S(2)}) collective-permute-start(bf16[64,2048]{1,0:T(8,128)(2,1)S(1)} %get-tuple-element.34), channel_id=1, source_target_pairs={{0,4},{4,8},{8,12},{1,5},{5,9},{9,13},{2,6},{6,10},{10,14},{3,7},{... | collective-permute-start | bytes 786440 | tf_op jit(solution)/shard_map/ppermute | solution.py:455
  18.8 5.0 %project_own.1 = (bf16[2,64,64,128]{3,2,1,0:T(8,128)(2,1)S(1)}, bf16[5,64,64,64]{3,2,1,0:T(8,128)(2,1)S(1)}, bf16[2,64,4096]{2,1,0:T(8,128)(2,1)S(1)}, bf16[256,...) custom-call(bf16[2,64,4096]{2,1,0:T(8,128)(2,1)S(1)} %get-tuple-element.39.refs_0_, ...), custom_call_target="tpu_custom_call" | custom-call | tf_op jit(solution)/shard_map/project_own/pallas_call | solution.py:308
  23.9 0.0 collective-permute-done.3
  23.9 1.3 %collective-permute-start.2 = (bf16[64,2048]{1,0:T(8,128)(2,1)S(1)}, bf16[64,2048]{1,0:T(8,128)(2,1)S(1)}, u32[]{:S(2)}, u32[]{:S(2)}) collective-permute-start(bf16[64,2048]{1,0:T(8,128)(2,1)S(1)} %get-tuple-element.35), channel_id=1, source_target_pairs={{4,0},{8,4},{12,8},{5,1},{9,5},{13,9},{6,2},{10,6},{14,10},{7,3},{... | collective-permute-start | bytes 786440 | tf_op jit(solution)/shard_map/ppermute | solution.py:455
  25.2 0.0 collective-permute-done.4
  25.2 0.0 collective-permute-done.5
  25.2 1.1 %broadcast_select_fusion.1 = (bf16[64,2048]{1,0:T(8,128)(2,1)S(1)}, bf16[64,2048]{1,0:T(8,128)(2,1)S(1)}) fusion(bf16[64,2048]{1,0:T(8,128)(2,1)} %collective-permute-done.3, bf16[64,2048]{1,0:T(8,128)(2,1)} %collective-permute-done.5, pred[]{:T(512)S(6)} %eq.9, bf16[64,2048]{1,0:T(8,128)(2,1)} %collective-permute-done.4, pred[]{:T(512)S(6)} %eq.8), kind=kLoop, calls=%fused_computation.1 | loop fusion | flops 262144 | bytes 1310722 | tf_op jit(solution)/shard_map/jit(_where)/select_n | solution.py:485
  26.3 0.1 collective-permute-start.10
  26.4 0.5 %collective-permute-start.8 = (bf16[64,1024]{1,0:T(8,128)(2,1)S(1)}, bf16[64,1024]{1,0:T(8,128)(2,1)S(1)}, u32[]{:S(2)}, u32[]{:S(2)}) collective-permute-start(bf16[64,1024]{1,0:T(8,128)(2,1)S(1)} %get-tuple-element.62), channel_id=1, source_target_pairs={{0,1},{1,0},{2,3},{3,2},{4,5},{5,4},{6,7},{7,6},{8,9},{9,8},{10,11... | collective-permute-start | bytes 393224 | tf_op jit(solution)/shard_map/ppermute | solution.py:489
  26.9 0.8 %collective-permute-done.10.refs_3_ = bf16[64,1024]{1,0:T(8,128)(2,1)S(1)} collective-permute-done((bf16[64,1024]{1,0:T(8,128)(2,1)S(1)}, bf16[64,1024]{1,0:T(8,128)(2,1)S(1)}, u32[]{:S(2)}, u32[]{:S(2)}) %collective-permute-start.10) | collective-permute-done | bytes 131104 | tf_op jit(solution)/shard_map/ppermute | solution.py:489
  27.7 0.1 collective-permute-start.9
  27.9 0.0 collective-permute-done.8.refs_1_
  27.9 0.3 collective-permute-start.7
  28.2 0.8 %collective-permute-done.9.refs_2_ = bf16[64,1024]{1,0:T(8,128)(2,1)S(1)} collective-permute-done((bf16[64,1024]{1,0:T(8,128)(2,1)S(1)}, bf16[64,1024]{1,0:T(8,128)(2,1)S(1)}, u32[]{:S(2)}, u32[]{:S(2)}) %collective-permute-start.9) | collective-permute-done | bytes 131104 | tf_op jit(solution)/shard_map/ppermute | solution.py:489
  29.1 0.2 collective-permute-done.7.refs_0_
  29.3 1.7 %project_first.1 = (bf16[2,64,64,128]{3,2,1,0:T(8,128)(2,1)S(1)}, bf16[64,32,128]{2,1,0:T(8,128)(2,1)S(1)}) custom-call(bf16[64,2048]{1,0:T(8,128)(2,1)S(1)} %get-tuple-element.66.m0, bf16[64,2048]{1,0:T(8,128)(2,1)S(1)} %get-tuple-element.65.m1, bf16[64,1024]{1,0:T(8,128)(2,1)S(1)} %collective-permute-done.7.refs_0_, ...), custom_call_target="tpu_custom_call", output_to_operand_aliasing={{0}: (8, {})} | custom-call | tf_op jit(solution)/shard_map/project_first/pallas_call | solution.py:308
  30.9 0.0 collective-permute-done
  30.9 1.5 %collective-permute-done.1 = bf16[64,2048]{1,0:T(8,128)(2,1)S(1)} collective-permute-done((bf16[64,2048]{1,0:T(8,128)(2,1)S(1)}, bf16[64,2048]{1,0:T(8,128)(2,1)S(1)}, u32[]{:S(2)}, u32[]{:S(2)}) %collective-permute-start.1) | collective-permute-done | bytes 262176 | tf_op jit(solution)/shard_map/ppermute | solution.py:455
  32.4 1.2 %collective-permute-done.2 = bf16[64,2048]{1,0:T(8,128)(2,1)S(1)} collective-permute-done((bf16[64,2048]{1,0:T(8,128)(2,1)S(1)}, bf16[64,2048]{1,0:T(8,128)(2,1)S(1)}, u32[]{:S(2)}, u32[]{:S(2)}) %collective-permute-start.2) | collective-permute-done | bytes 262176 | tf_op jit(solution)/shard_map/ppermute | solution.py:455
  33.7 1.0 %broadcast_select_fusion = (bf16[64,2048]{1,0:T(8,128)(2,1)S(1)}, bf16[64,2048]{1,0:T(8,128)(2,1)S(1)}) fusion(bf16[64,2048]{1,0:T(8,128)(2,1)} %collective-permute-done, bf16[64,2048]{1,0:T(8,128)(2,1)S(1)} %collective-permute-done.2, pred[]{:T(512)S(6)} %eq.9, bf16[64,2048]{1,0:T(8,128)(2,1)S(1)} %collective-permute-done.1, pred[]{:T(512)S(6)} %eq.8), kind=kLoop, calls=%fused_computation | loop fusion | flops 262144 | bytes 1310722 | tf_op jit(solution)/shard_map/jit(_where)/select_n | solution.py:485
  34.6 0.1 collective-permute-start.12
  34.7 0.5 %collective-permute-start.11 = (bf16[64,2048]{1,0:T(8,128)(2,1)S(1)}, bf16[64,2048]{1,0:T(8,128)(2,1)S(1)}, u32[]{:S(2)}, u32[]{:S(2)}) collective-permute-start(bf16[64,2048]{1,0:T(8,128)(2,1)S(1)} %get-tuple-element.60.m0), channel_id=1, source_target_pairs={{0,1},{1,0},{2,3},{3,2},{4,5},{5,4},{6,7},{7,6},{8,9},{9,8},{10,11... | collective-permute-start | bytes 786440 | tf_op jit(solution)/shard_map/ppermute | solution.py:489
  35.2 1.0 %collective-permute-done.12.refs_1_ = bf16[64,2048]{1,0:T(8,128)(2,1)S(1)} collective-permute-done((bf16[64,2048]{1,0:T(8,128)(2,1)S(1)}, bf16[64,2048]{1,0:T(8,128)(2,1)S(1)}, u32[]{:S(2)}, u32[]{:S(2)}) %collective-permute-start.12) | collective-permute-done | bytes 262176 | tf_op jit(solution)/shard_map/ppermute | solution.py:489
  36.2 0.4 collective-permute-done.11.refs_0_
  36.6 2.1 %project_last.1 = (bf16[2,64,64,128]{3,2,1,0:T(8,128)(2,1)S(1)}, bf16[5,64,64,64]{3,2,1,0:T(8,128)(2,1)S(1)}) custom-call(bf16[64,2048]{1,0:T(8,128)(2,1)S(1)} %get-tuple-element.60.m0, bf16[64,2048]{1,0:T(8,128)(2,1)S(1)} %get-tuple-element.59.m1, ...), custom_call_target="tpu_custom_call", output_to_operand_aliasing={{0}: (7, {}), {1}: (8, {})} | custom-call | tf_op jit(solution)/shard_map/project_last/pallas_call | solution.py:308
  38.7 1.2 %triplets.2.mine_ref = bf16[64,4096]{1,0:T(8,128)(2,1)S(1)} custom-call(s32[8]{0:T(128)S(4)} %get-tuple-element.32.picks_ref, bf16[2,64,64,128]{3,2,1,0:T(8,128)(2,1)S(1)} %get-tuple-element.56.l_ref, bf16[5,64,64,64]{3,2,1,0:T(8,128)(2,1)S(1)} %get-tuple-element.55.turned_ref), custom_call_target="tpu_custom_call" | custom-call | tf_op jit(solution)/shard_map/triplets/pallas_call | solution.py:352
  40.0 0.2 collective-permute-start.14
  40.2 1.2 %triplets.3.mine_ref = bf16[64,4096]{1,0:T(8,128)(2,1)S(1)} custom-call(s32[8]{0:T(128)S(4)} %get-tuple-element.32.picks_ref, bf16[2,64,64,128]{3,2,1,0:T(8,128)(2,1)S(1)} %get-tuple-element.56.l_ref, bf16[5,64,64,64]{3,2,1,0:T(8,128)(2,1)S(1)} %get-tuple-element.55.turned_ref), custom_call_target="tpu_custom_call" | custom-call | tf_op jit(solution)/shard_map/triplets/pallas_call | solution.py:352
  41.4 0.4 collective-permute-start.13
  41.8 0.1 collective-permute-done.14.theirs_ref
  41.9 1.3 %finish.2.refs_0_ = bf16[64,4096]{1,0:T(8,128)(2,1)S(1)} custom-call(bf16[64,4096]{1,0:T(8,128)(2,1)S(1)} %triplets.2.mine_ref, bf16[64,4096]{1,0:T(8,128)(2,1)S(1)} %collective-permute-done.14.theirs_ref, bf16[2,64,4096]{2,1,0:T(8,128)(2,1)S(1)} %get-tuple-element.57.gate_ref, bf16[64,128]{1,0:T(8,128)(2,1)S(1)} %get-tuple-element.58.w_ref), custom_call_target="tpu_custom_call" | custom-call | tf_op jit(solution)/shard_map/finish/pallas_call | solution.py:409
  43.2 0.1 collective-permute-done.13.theirs_ref
  43.4 2.0 %finish.3 = bf16[2,64,4096]{2,1,0:T(8,128)(2,1)} custom-call(bf16[64,4096]{1,0:T(8,128)(2,1)S(1)} %triplets.3.mine_ref, bf16[64,4096]{1,0:T(8,128)(2,1)S(1)} %collective-permute-done.13.theirs_ref, bf16[2,64,4096]{2,1,0:T(8,128)(2,1)S(1)} %get-tuple-element.57.gate_ref, bf16[64,128]{1,0:T(8,128)(2,1)S(1)} %get-tuple-element.58.w_ref, ...), custom_call_target="tpu_custom_call" | custom-call | tf_op jit(solution)/shard_map/finish/pallas_call | solution.py:409
  (2 shorter events, 0.0 us)
Async XLA Ops:
  1.4 0.7 %copy-start = (bf16[64,2048]{1,0:T(8,128)(2,1)}, bf16[64,2048]{1,0:T(8,128)(2,1)S(1)}, u32[]{:S(2)}) copy-start(bf16[64,2048]{1,0:T(8,128)(2,1)S(1)} %get-tuple-element.36) | copy-start | bytes 786436
  2.1 15.4 %collective-permute-start.6 = (bf16[2,64,4096]{2,1,0:T(8,128)(2,1)S(1)}, bf16[2,64,4096]{2,1,0:T(8,128)(2,1)S(1)}, u32[]{:S(2)}, u32[]{:S(2)}) collective-permute-start(bf16[2,64,4096]{2,1,0:T(8,128)(2,1)S(1)} %get-tuple-element.39.refs_0_), channel_id=1, source_target_pairs={{0,1},{1,0},{2,3},{3,2},{4,5},{5,4},{6,7},{7,6},{8,9},{9,8},{10,11... | collective-permute-start | bytes 3145736 | tf_op jit(solution)/shard_map/ppermute | solution.py:460
  2.5 21.3 %collective-permute-start.3 = (bf16[64,2048]{1,0:T(8,128)(2,1)}, bf16[64,2048]{1,0:T(8,128)(2,1)}, u32[]{:S(2)}, u32[]{:S(2)}) collective-permute-start(bf16[64,2048]{1,0:T(8,128)(2,1)} %copy-done), channel_id=1, source_target_pairs={{0,12},{12,0},{1,13},{13,1},{2,14},{14,2},{3,15},{15,3},{16,28},{2... | collective-permute-start | bytes 786440 | tf_op jit(solution)/shard_map/ppermute | solution.py:455
  9.0 16.1 %collective-permute-start.4 = (bf16[64,2048]{1,0:T(8,128)(2,1)S(1)}, bf16[64,2048]{1,0:T(8,128)(2,1)}, u32[]{:S(2)}, u32[]{:S(2)}) collective-permute-start(bf16[64,2048]{1,0:T(8,128)(2,1)S(1)} %get-tuple-element.37), channel_id=1, source_target_pairs={{0,4},{4,8},{8,12},{1,5},{5,9},{9,13},{2,6},{6,10},{10,14},{3,7},{... | collective-permute-start | bytes 786440 | tf_op jit(solution)/shard_map/ppermute | solution.py:455
  11.0 14.2 %collective-permute-start.5 = (bf16[64,2048]{1,0:T(8,128)(2,1)S(1)}, bf16[64,2048]{1,0:T(8,128)(2,1)}, u32[]{:S(2)}, u32[]{:S(2)}) collective-permute-start(bf16[64,2048]{1,0:T(8,128)(2,1)S(1)} %get-tuple-element.38), channel_id=1, source_target_pairs={{4,0},{8,4},{12,8},{5,1},{9,5},{13,9},{6,2},{10,6},{14,10},{7,3},{... | collective-permute-start | bytes 786440 | tf_op jit(solution)/shard_map/ppermute | solution.py:455
  12.3 18.6 %collective-permute-start = (bf16[64,2048]{1,0:T(8,128)(2,1)S(1)}, bf16[64,2048]{1,0:T(8,128)(2,1)}, u32[]{:S(2)}, u32[]{:S(2)}) collective-permute-start(bf16[64,2048]{1,0:T(8,128)(2,1)S(1)} %get-tuple-element.33), channel_id=1, source_target_pairs={{0,12},{12,0},{1,13},{13,1},{2,14},{14,2},{3,15},{15,3},{16,28},{2... | collective-permute-start | bytes 786440 | tf_op jit(solution)/shard_map/ppermute | solution.py:455
  17.5 14.9 %collective-permute-start.1 = (bf16[64,2048]{1,0:T(8,128)(2,1)S(1)}, bf16[64,2048]{1,0:T(8,128)(2,1)S(1)}, u32[]{:S(2)}, u32[]{:S(2)}) collective-permute-start(bf16[64,2048]{1,0:T(8,128)(2,1)S(1)} %get-tuple-element.34), channel_id=1, source_target_pairs={{0,4},{4,8},{8,12},{1,5},{5,9},{9,13},{2,6},{6,10},{10,14},{3,7},{... | collective-permute-start | bytes 786440 | tf_op jit(solution)/shard_map/ppermute | solution.py:455
  23.9 9.8 %collective-permute-start.2 = (bf16[64,2048]{1,0:T(8,128)(2,1)S(1)}, bf16[64,2048]{1,0:T(8,128)(2,1)S(1)}, u32[]{:S(2)}, u32[]{:S(2)}) collective-permute-start(bf16[64,2048]{1,0:T(8,128)(2,1)S(1)} %get-tuple-element.35), channel_id=1, source_target_pairs={{4,0},{8,4},{12,8},{5,1},{9,5},{13,9},{6,2},{10,6},{14,10},{7,3},{... | collective-permute-start | bytes 786440 | tf_op jit(solution)/shard_map/ppermute | solution.py:455
  26.3 1.4 %collective-permute-start.10 = (bf16[64,1024]{1,0:T(8,128)(2,1)S(1)}, bf16[64,1024]{1,0:T(8,128)(2,1)S(1)}, u32[]{:S(2)}, u32[]{:S(2)}) collective-permute-start(bf16[64,1024]{1,0:T(8,128)(2,1)S(1)} %get-tuple-element.61), channel_id=1, source_target_pairs={{0,1},{1,0},{2,3},{3,2},{4,5},{5,4},{6,7},{7,6},{8,9},{9,8},{10,11... | collective-permute-start | bytes 393224 | tf_op jit(solution)/shard_map/ppermute | solution.py:489
  26.4 1.5 %collective-permute-start.8 = (bf16[64,1024]{1,0:T(8,128)(2,1)S(1)}, bf16[64,1024]{1,0:T(8,128)(2,1)S(1)}, u32[]{:S(2)}, u32[]{:S(2)}) collective-permute-start(bf16[64,1024]{1,0:T(8,128)(2,1)S(1)} %get-tuple-element.62), channel_id=1, source_target_pairs={{0,1},{1,0},{2,3},{3,2},{4,5},{5,4},{6,7},{7,6},{8,9},{9,8},{10,11... | collective-permute-start | bytes 393224 | tf_op jit(solution)/shard_map/ppermute | solution.py:489
  27.7 1.3 %collective-permute-start.9 = (bf16[64,1024]{1,0:T(8,128)(2,1)S(1)}, bf16[64,1024]{1,0:T(8,128)(2,1)S(1)}, u32[]{:S(2)}, u32[]{:S(2)}) collective-permute-start(bf16[64,1024]{1,0:T(8,128)(2,1)S(1)} %get-tuple-element.63), channel_id=1, source_target_pairs={{0,1},{1,0},{2,3},{3,2},{4,5},{5,4},{6,7},{7,6},{8,9},{9,8},{10,11... | collective-permute-start | bytes 393224 | tf_op jit(solution)/shard_map/ppermute | solution.py:489
  27.9 1.3 %collective-permute-start.7 = (bf16[64,1024]{1,0:T(8,128)(2,1)S(1)}, bf16[64,1024]{1,0:T(8,128)(2,1)S(1)}, u32[]{:S(2)}, u32[]{:S(2)}) collective-permute-start(bf16[64,1024]{1,0:T(8,128)(2,1)S(1)} %get-tuple-element.64), channel_id=1, source_target_pairs={{0,1},{1,0},{2,3},{3,2},{4,5},{5,4},{6,7},{7,6},{8,9},{9,8},{10,11... | collective-permute-start | bytes 393224 | tf_op jit(solution)/shard_map/ppermute | solution.py:489
  34.6 1.6 %collective-permute-start.12 = (bf16[64,2048]{1,0:T(8,128)(2,1)S(1)}, bf16[64,2048]{1,0:T(8,128)(2,1)S(1)}, u32[]{:S(2)}, u32[]{:S(2)}) collective-permute-start(bf16[64,2048]{1,0:T(8,128)(2,1)S(1)} %get-tuple-element.59.m1), channel_id=1, source_target_pairs={{0,1},{1,0},{2,3},{3,2},{4,5},{5,4},{6,7},{7,6},{8,9},{9,8},{10,11... | collective-permute-start | bytes 786440 | tf_op jit(solution)/shard_map/ppermute | solution.py:489
  34.7 1.9 %collective-permute-start.11 = (bf16[64,2048]{1,0:T(8,128)(2,1)S(1)}, bf16[64,2048]{1,0:T(8,128)(2,1)S(1)}, u32[]{:S(2)}, u32[]{:S(2)}) collective-permute-start(bf16[64,2048]{1,0:T(8,128)(2,1)S(1)} %get-tuple-element.60.m0), channel_id=1, source_target_pairs={{0,1},{1,0},{2,3},{3,2},{4,5},{5,4},{6,7},{7,6},{8,9},{9,8},{10,11... | collective-permute-start | bytes 786440 | tf_op jit(solution)/shard_map/ppermute | solution.py:489
  40.0 2.0 %collective-permute-start.14 = (bf16[64,4096]{1,0:T(8,128)(2,1)S(1)}, bf16[64,4096]{1,0:T(8,128)(2,1)S(1)}, u32[]{:S(2)}, u32[]{:S(2)}) collective-permute-start(bf16[64,4096]{1,0:T(8,128)(2,1)S(1)} %triplets.2.mine_ref), channel_id=1, source_target_pairs={{0,1},{1,0},{2,3},{3,2},{4,5},{5,4},{6,7},{7,6},{8,9},{9,8},{10,11... | collective-permute-start | bytes 1572872 | tf_op jit(solution)/shard_map/ppermute | solution.py:515
  41.4 2.0 %collective-permute-start.13 = (bf16[64,4096]{1,0:T(8,128)(2,1)S(1)}, bf16[64,4096]{1,0:T(8,128)(2,1)S(1)}, u32[]{:S(2)}, u32[]{:S(2)}) collective-permute-start(bf16[64,4096]{1,0:T(8,128)(2,1)S(1)} %triplets.3.mine_ref), channel_id=1, source_target_pairs={{0,1},{1,0},{2,3},{3,2},{4,5},{5,4},{6,7},{7,6},{8,9},{9,8},{10,11... | collective-permute-start | bytes 1572872 | tf_op jit(solution)/shard_map/ppermute | solution.py:515

commit v13 on v12

--- a/solution.py
+++ b/solution.py
@@ -57,8 +57,8 @@
 
 
 def select_kernel(slots, triplets, cuts, a_hbm, b_hbm, n_hbm, pair_hbm, *refs):
-    picks_ref, pair_ref, *out_refs = refs[: 2 + 3 * len(cuts)]
-    a_ref, b_ref, n_ref, sems = refs[2 + 3 * len(cuts) :]
+    picks_ref, pair_ref, *out_refs = refs[: 2 + 2 * len(cuts)]
+    a_ref, b_ref, n_ref, sems = refs[2 + 2 * len(cuts) :]
     me, behind, ahead = neighbour_tiles()
     whole = pltpu.make_async_copy(pair_hbm, pair_ref, sems.at[0])
     tables = [
@@ -80,14 +80,13 @@
                     mine = jnp.logical_and(name >= 0, name < slots)
                     pick = jnp.where(jnp.logical_and(m < count, mine), name, pick)
         chosen.append(pick)
-    chosen.append(jnp.where(lax.axis_index("row") == 0, chosen[1], chosen[0]))
     for s in range(slots):
         for at, pick in enumerate(used_picks(s, slots, triplets, a_ref, b_ref, n_ref)):
             picks_ref[4 * s + at] = pick
     whole.wait()
     for at, (start, size) in enumerate(cuts):
         for which, pick in enumerate(chosen):
-            out_refs[3 * at + which][...] = pair_ref[pick, :, start : start + size]
+            out_refs[2 * at + which][...] = pair_ref[pick, :, start : start + size]
 
 
 def select_blocks(pair, a_slots, b_slots, counts, cuts):
@@ -95,7 +94,7 @@
     hbm = pl.BlockSpec(memory_space=pltpu.HBM)
     vmem = pl.BlockSpec(memory_space=pltpu.VMEM)
     out_shape = [pltpu.SMEM((4 * slots,), jnp.int32), pltpu.VMEM(pair.shape, pair.dtype)] + [
-        pltpu.VMEM((channels, size), pair.dtype) for _, size in cuts for _ in range(3)
+        pltpu.VMEM((channels, size), pair.dtype) for _, size in cuts for _ in range(2)
     ]
     operands = [
         pltpu.with_memory_space_constraint(value, pltpu.HBM)
@@ -189,7 +188,7 @@
             yield
 
 
-def two_chunks(sides_at, n, chunk, held, spread):
+def two_chunks(sides_at, n, chunk, held, spread, after=()):
     steps = [
         pair_chunk(functools.partial(sides_at, n + k), chunk, held[2 * k : 2 * k + 2])
         for k in range(2)
@@ -201,7 +200,10 @@
         pass
     for _ in spreads[0]:
         pass
-    for _ in spreads[1]:
+    for at, _ in enumerate(spreads[1]):
+        if at > 0:
+            next(iter(after), None)
+    for _ in after:
         pass
 
 
@@ -261,54 +263,105 @@
     two_chunks(sides_at, chunks - 2, chunk, held, functools.partial(spread, True))
 
 
-def fetched_kernel(chunk, first_row, last, m0, m1, *refs):
-    if last:
-        *theirs, p0_ref, w_ref, gain_ref, _, _, l_ref, turned_ref, p_ref = refs[:-4]
-        before = [(p0_ref, p0_ref.shape[1]), (p_ref, p_ref.shape[1])]
-    else:
-        *theirs, w_ref, gain_ref, _, l_ref, p_ref = refs[:-4]
-    held = refs[-4:]
-    half = l_ref.shape[1]
-    weight = w_ref[...]
+def fetched_sides(chunk, ours, theirs, weight, gain_ref, half):
     wide = theirs[0].shape[1]
-    rows = chunk // BLK
 
     def sides_at(n, start):
         at = n * chunk + start
         both = []
-        for x, m in enumerate((m0, m1)):
+        for x, m in enumerate(ours):
             other = theirs[2 * (at // wide) + x][:, at % wide : at % wide + LANES]
             both.append(
                 gated_sides(m[:, at : at + LANES], other, weight, gain_ref[...], half)[0]
             )
         return both
 
+    return sides_at
+
+
+def first_kernel(chunk, *refs):
+    *ours_theirs, w_ref, gain_ref, _, l_ref, p_ref = refs[:-4]
+    held = refs[-4:]
+    half = l_ref.shape[1]
+    rows = chunk // BLK
+    sides_at = fetched_sides(
+        chunk, ours_theirs[:2], ours_theirs[2:], w_ref[...], gain_ref, half
+    )
+
     def spread(n, held, k):
-        done = (before, turned_ref) if last and k else (None, None)
+        return spread_chunk(rows, held, l_ref, 1, n * rows, p_ref, n * rows, None, None, half)
+
+    two_chunks(sides_at, 0, chunk, held, spread)
+
+
+def last_kernel(chunk, first_row, group, picks_ref, *refs):
+    *ours_theirs, p0_ref, w_ref, gain_ref, _, _, l_ref, turned_ref, out_ref, p_ref = refs[:-6]
+    held, accs = refs[-6:-2], refs[-2:]
+    before = [(p0_ref, p0_ref.shape[1]), (p_ref, p_ref.shape[1])]
+    half = l_ref.shape[1]
+    rows = chunk // BLK
+    sides_at = fetched_sides(
+        chunk, ours_theirs[:2], ours_theirs[2:], w_ref[...], gain_ref, half
+    )
+
+    def spread(n, held, k):
+        done = (before, turned_ref) if k else (None, None)
         return spread_chunk(rows, held, l_ref, 1, first_row + n * rows, p_ref, n * rows, *done, half)
 
-    two_chunks(sides_at, 0, chunk, held, spread)
+    products = triplet_steps(0, group, picks_ref, l_ref, turned_ref, out_ref, accs)
+    two_chunks(sides_at, 0, chunk, held, spread, products)
+
+
+def triplet_steps(s, group, picks_ref, l_ref, turned_ref, out_ref, accs):
+    picks = [picks_ref[4 * s + at] for at in range(4)]
+    take_low = lax.broadcasted_iota(jnp.int32, (group, LANES), 1) < BLK
+    pitch = accs[0].shape[0] // BLK
+    for first in range(0, l_ref.shape[1], group):
+        acc = accs[first // group % len(accs)]
+        for at in range(group):
+            c = first + at
+            lhs = jnp.concatenate([l_ref[0, c], l_ref[1, c]], axis=1)
+            rhs = jnp.concatenate([turned_ref[pick, c] for pick in picks], axis=0)
+            acc[pl.ds(at, BLK, stride=pitch), :BLK] = jnp.dot(
+                lhs, rhs, preferred_element_type=F32
+            )
+            if at % 8 == 7 and at + 1 < group:
+                yield
+        for t in range(BLK // 2):
+            even = acc[2 * t * pitch : 2 * t * pitch + group, :]
+            odd = acc[(2 * t + 1) * pitch : (2 * t + 1) * pitch + group, :]
+            out_ref[first : first + group, t * LANES : (t + 1) * LANES] = jnp.where(
+                take_low, even, pltpu.roll(odd, BLK, 1)
+            ).astype(BF16)
+        yield
+
+
+def triplet_kernel(s, group, picks_ref, l_ref, turned_ref, out_ref, *accs):
+    for _ in triplet_steps(s, group, picks_ref, l_ref, turned_ref, out_ref, accs):
+        pass
+
+
+def acc_scratch(group):
+    return [pltpu.VMEM((BLK * (group + 8), LANES), F32)] * 2
 
 
 def chunk_scratch(half, chunk):
     return [pltpu.VMEM((chunk // BLK * (half + 8), LANES), F32)] * 4
 
 
-def call(kernel, name, operands, out_shape, scratch, aliased=0, hbm=0):
-    vmem = pl.BlockSpec(memory_space=pltpu.VMEM)
+def call(kernel, name, operands, out_shape, scratch, aliased=0, hbm=0, smem=0):
+    spaces = [pltpu.SMEM] * smem + [pltpu.VMEM] * (len(operands) - smem - hbm) + [pltpu.HBM] * hbm
     plain = len(operands) - aliased
-    operands = operands[:plain] + [
-        pltpu.with_memory_space_constraint(value, pltpu.VMEM) for value in operands[plain:]
-    ]
-    operands = operands[: len(operands) - hbm] + [
-        pltpu.with_memory_space_constraint(value, pltpu.HBM)
-        for value in operands[len(operands) - hbm :]
-    ]
-    specs = [vmem] * (len(operands) - hbm) + [pl.BlockSpec(memory_space=pltpu.HBM)] * hbm
+    operands = [
+        value
+        if space == pltpu.VMEM and at < plain
+        else pltpu.with_memory_space_constraint(value, space)
+        for at, (value, space) in enumerate(zip(operands, spaces))
+    ]
     return pl.pallas_call(
         kernel,
-        in_specs=specs,
-        out_specs=[vmem] * len(out_shape),
+        in_specs=[pl.BlockSpec(memory_space=space) for space in spaces],
+        out_specs=[pl.BlockSpec(memory_space=pltpu.VMEM)] * len(out_shape),
         out_shape=out_shape,
         scratch_shapes=scratch,
         input_output_aliases={plain + at: at for at in range(aliased)},
@@ -317,82 +370,35 @@
     )(*operands)
 
 
-def triplet_kernel(s, group, picks_ref, l_ref, turned_ref, out_ref, *accs):
-    picks = [picks_ref[4 * s + at] for at in range(4)]
-    take_low = lax.broadcasted_iota(jnp.int32, (group, LANES), 1) < BLK
-    half = l_ref.shape[1]
-    pitch = accs[0].shape[0] // BLK
-
-    @pl.loop(0, half, step=group * len(accs))
-    def _(base):
-        for which, acc in enumerate(accs):
-            for at in range(group):
-                c = base + which * group + at
-                lhs = jnp.concatenate([l_ref[0, c], l_ref[1, c]], axis=1)
-                rhs = jnp.concatenate([turned_ref[pick, c] for pick in picks], axis=0)
-                acc[pl.ds(at, BLK, stride=pitch), :BLK] = jnp.dot(
-                    lhs, rhs, preferred_element_type=F32
-                )
-            rows = pl.ds(pl.multiple_of(base + which * group, group), group)
-            for t in range(BLK // 2):
-                even = acc[2 * t * pitch : 2 * t * pitch + group, :]
-                odd = acc[(2 * t + 1) * pitch : (2 * t + 1) * pitch + group, :]
-                out_ref[rows, t * LANES : (t + 1) * LANES] = jnp.where(
-                    take_low, even, pltpu.roll(odd, BLK, 1)
-                ).astype(BF16)
-
-
-def triplet_sum(s, picks, lefts, rights, group):
-    half = lefts.shape[1]
-    vmem = pl.BlockSpec(memory_space=pltpu.VMEM)
-    picks = pltpu.with_memory_space_constraint(picks, pltpu.SMEM)
-    lefts, rights = (
-        pltpu.with_memory_space_constraint(value, pltpu.VMEM) for value in (lefts, rights)
-    )
-    return pl.pallas_call(
-        functools.partial(triplet_kernel, s, group),
-        in_specs=[pl.BlockSpec(memory_space=pltpu.SMEM), vmem, vmem],
-        out_specs=vmem,
-        out_shape=pltpu.VMEM((half, BLK * BLK), BF16),
-        scratch_shapes=[pltpu.VMEM((BLK * (group + 8), LANES), F32)] * 2,
-        compiler_params=pltpu.CompilerParams(vmem_limit_bytes=VMEM_LIMIT),
-        name="triplets",
-    )(picks, lefts, rights)
-
-
-def finish_kernel(s, mine_ref, theirs_ref, gate_ref, w_ref, *refs):
+def finish_kernel(s, run, pieces, mine_ref, theirs_ref, gate_ref, w_ref, *refs):
     weight = w_ref[...]
     cells = mine_ref.shape[-1]
     if s == 0:
         held = refs[0]
-        steps = 4
     else:
         before_ref, out_ref, held, sems = refs
-        steps = sems.shape[0] - 1
-        before = pltpu.make_async_copy(before_ref, out_ref.at[0], sems.at[steps])
+        before = pltpu.make_async_copy(before_ref, out_ref.at[0], sems.at[pieces])
         before.start()
-    size = cells // steps
+    size = cells // pieces
 
     def copy(n):
         to = pl.ds(pl.multiple_of(n * size, size), size)
         return pltpu.make_async_copy(held.at[:, to], out_ref.at[1, :, to], sems.at[n])
 
-    @pl.loop(0, steps)
+    @pl.loop(0, cells // run)
     def _(n):
-        for start in range(0, size, LANES):
-            to = pl.ds(pl.multiple_of(n * size + start, LANES), LANES)
+        for start in range(0, run, LANES):
+            to = cells_at(n, run, start)
             normed = normed_of(mine_ref[:, to], theirs_ref[:, to])
             projected = jnp.dot(weight, normed, preferred_element_type=F32)
             held[:, to] = (gate_ref[s, :, to].astype(F32) * projected).astype(BF16)
-        if s > 0:
-            copy(n).start()
+            done = start + LANES
+            if s > 0 and done % size == 0:
+                copy(n * (run // size) + done // size - 1).start()
 
     if s > 0:
-
-        @pl.loop(0, steps)
-        def _(n):
+        for n in range(pieces):
             copy(n).wait()
-
         before.wait()
 
 
@@ -407,7 +413,7 @@
         out_specs = pl.BlockSpec(memory_space=pltpu.HBM)
         scratch = [pltpu.VMEM(mine.shape, BF16), pltpu.SemaphoreType.DMA((5,))]
     return pl.pallas_call(
-        functools.partial(finish_kernel, s),
+        functools.partial(finish_kernel, s, mine.shape[1] // 2, 4),
         in_specs=[vmem] * len(operands),
         out_specs=out_specs,
         out_shape=out_shape,
@@ -448,13 +454,8 @@
     chunk = cells // 4
     cuts = ((0, 2 * chunk), (2 * chunk, 2 * chunk))
     picks, pair, *chosen = select_blocks(pair, a_slots, b_slots, counts, cuts)
-    ends = [(0, rows - 1), (rows - 1, 0)]
-    row = lax.axis_index("row")
     arrived = [
-        tuple(
-            lax.ppermute(chosen[3 * n + which], "row", pairs)
-            for which, pairs in ((2, ends), (0, up[:-1]), (1, down[1:]))
-        )
+        (lax.ppermute(chosen[2 * n], "row", up), lax.ppermute(chosen[2 * n + 1], "row", down))
         for n in range(len(cuts))
     ]
     pair_other = lax.ppermute(pair, "chan", swap)
@@ -479,11 +480,7 @@
         hbm=len(weights),
     )
     for (start, size), behind_ahead in zip(cuts, arrived):
-        far, near_behind, near_ahead, lefts = lax.optimization_barrier((*behind_ahead, lefts))
-        behind_ahead = [
-            jnp.where(row == 0, far, near_behind),
-            jnp.where(row == rows - 1, far, near_ahead),
-        ]
+        *behind_ahead, lefts = lax.optimization_barrier((*behind_ahead, lefts))
         wide = chunk if start == 0 else size
         others = [
             lax.ppermute(lax.slice_in_dim(value, at, at + wide, axis=1), "chan", swap)
@@ -493,7 +490,7 @@
         paired = pltpu.VMEM((half, size // BLK, LANES), BF16)
         if start == 0:
             lefts, rights_first = call(
-                functools.partial(fetched_kernel, chunk, 0, False),
+                functools.partial(first_kernel, chunk),
                 "project_first",
                 [*behind_ahead, *others, weight, gain, lefts],
                 [left_shape, paired],
@@ -501,20 +498,29 @@
                 aliased=1,
             )
         else:
-            lefts, rights = call(
-                functools.partial(fetched_kernel, chunk, start // BLK, True),
+            lefts, rights, update = call(
+                functools.partial(last_kernel, chunk, start // BLK, 16),
                 "project_last",
-                [*behind_ahead, *others, rights_first, weight, gain, lefts, rights],
-                [left_shape, right_shape],
-                [pltpu.VMEM((half, chunk // BLK, LANES), BF16)] + chunk_scratch(half, chunk),
+                [picks, *behind_ahead, *others, rights_first, weight, gain, lefts, rights],
+                [left_shape, right_shape, pltpu.VMEM((half, cells), BF16)],
+                [pltpu.VMEM((half, chunk // BLK, LANES), BF16)]
+                + chunk_scratch(half, chunk)
+                + acc_scratch(16),
                 aliased=2,
+                smem=1,
             )
-    updates = []
-    for s in range(slots):
-        update = triplet_sum(s, picks, lefts, rights, 16)
+    updates = [(update, lax.ppermute(update, "chan", swap))]
+    update, lefts = lax.optimization_barrier((update, lefts))
+    for s in range(1, slots):
+        (update,) = call(
+            functools.partial(triplet_kernel, s, 16),
+            "triplets",
+            [picks, lefts, rights],
+            [pltpu.VMEM((half, cells), BF16)],
+            acc_scratch(16),
+            smem=1,
+        )
         updates.append((update, lax.ppermute(update, "chan", swap)))
-        if s + 1 < slots:
-            update, lefts = lax.optimization_barrier((update, lefts))
     out = None
     for s, (mine, theirs) in enumerate(updates):
         out = finish(s, mine, theirs, gate, last_weight, out)

time: 45.7 us -> 39.6 us (0.87)
  starting transfers between devices: 20.2 us -> 11.1 us
  waiting for transfers between devices: 6.25 us -> 13.6 us
  other arithmetic: 2.08 us -> 0 us
  Pallas kernels: 15.9 us -> 14.6 us
  local copies, waits for them, and re-layouts: 0.73 us -> 0.04 us
    ppermute x6 -> x5, starting transfers between devices: 17.5 us -> 8.78 us  [the longest x2 5.93 us: per_device(): lax.ppermute(chosen[2 * n + 1], 'row', down)]
    ppermute x6 -> x5, waiting for transfers between devices: 2.72 us -> 10.1 us  [the longest x2 8.63 us: per_device(): lax.ppermute(chosen[2 * n + 1], 'row', down)]
    select_n x2 -> x0, other arithmetic: 2.08 us -> none  [per_device(): jnp.where(row == rows - 1, far, near_ahead)]
    pallas_call x7 -> x6, Pallas kernels: 14.5 us -> 13.3 us  [the longest x4 10.6 us: call(): pl.pallas_call(kernel, in_specs=[pl.BlockSpec(memory_space=space) for spa...]
    unnamed x2 -> x0, local copies, waits for them, and re-layouts: 0.7 us -> none
  transfers between devices with their start and end apart: 15 -> 13, of which waited for: 9 -> 10; matrix products, arithmetic and copies ran while one was open for 2% -> 0% of each run, Pallas kernels for 20% -> 22%
where the time goes in v13:
time: 39.6 us; the launch traced here: 39.4 us
  Pallas kernels  14.6 us (37%)
  waiting for transfers between devices  13.6 us (34%)
  starting transfers between devices  11.1 us (28%)
    pallas_call x4, Pallas kernels, call(): pl.pallas_call(kernel, in_specs=[pl.BlockSpec(memory_space=space) for spa...  10.6 us
    ppermute x2, waiting for transfers between devices, per_device(): lax.ppermute(chosen[2 * n + 1], 'row', down)  8.63 us
    ppermute x2, starting transfers between devices, per_device(): lax.ppermute(chosen[2 * n + 1], 'row', down)  5.93 us
    ppermute x6, waiting for transfers between devices, per_device(): lax.ppermute(lax.slice_in_dim(value, at, at + wide, axis=1), 'chan', swap)  3.27 us
    pallas_call x2, Pallas kernels, finish(): pl.pallas_call(functools.partial(finish_kernel, s, mine.shape[1] // 2, 4)...  2.65 us
    ppermute x2, starting transfers between devices, per_device(): lax.ppermute(chosen[2 * n], 'row', up)  2.64 us
    ppermute x6, starting transfers between devices, per_device(): lax.ppermute(lax.slice_in_dim(value, at, at + wide, axis=1), 'chan', swap)  1.37 us
    pallas_call x1, Pallas kernels, select_blocks(): pl.pallas_call(functools.partial(select_kernel, slots, a_slots.shape[0],...  1.33 us
  transfers between devices with their start and end apart: 13, of which 10 were waited for; matrix products, arithmetic and copies ran while one was open for 0% of the time, Pallas kernels for 22%

profile of v13, /device:TPU:0, one launch (start us, length us, event | category | flops | bytes accessed | tf_op | source)
XLA Modules:
  0.0 39.4 jit_solution(9431161894951525275)
XLA Ops:
  0.0 1.3 %select_blocks.1 = (s32[8]{0:T(128)S(4)}, bf16[2,64,4096]{2,1,0:T(8,128)(2,1)S(1)}, bf16[64,2048]{1,0:T(8,128)(2,1)S(1)}, bf16[64,2048]{1,0:T(8,128)(2,1)S(1)}, ...) custom-call(s32[4,16]{1,0:T(4,128)} %bitcast.12, s32[4,16]{1,0:T(4,128)} %bitcast.13, s32[16]{0:T(128)} %n_hbm.1, ...), custom_call_target="tpu_custom_call" | custom-call | tf_op jit(solution)/shard_map/select_blocks/pallas_call | solution.py:103
  1.3 0.5 %collective-permute-start.4 = (bf16[2,64,4096]{2,1,0:T(8,128)(2,1)S(1)}, bf16[2,64,4096]{2,1,0:T(8,128)(2,1)S(1)}, u32[]{:S(2)}, u32[]{:S(2)}) collective-permute-start(bf16[2,64,4096]{2,1,0:T(8,128)(2,1)S(1)} %get-tuple-element.34.refs_0_), channel_id=1, source_target_pairs={{0,1},{1,0},{2,3},{3,2},{4,5},{5,4},{6,7},{7,6},{8,9},{9,8},{10,11... | collective-permute-start | bytes 3145736 | tf_op jit(solution)/shard_map/ppermute | solution.py:461
  1.9 2.6 %collective-permute-start.2 = (bf16[64,2048]{1,0:T(8,128)(2,1)S(1)}, bf16[64,2048]{1,0:T(8,128)(2,1)S(1)}, u32[]{:S(2)}, u32[]{:S(2)}) collective-permute-start(bf16[64,2048]{1,0:T(8,128)(2,1)S(1)} %get-tuple-element.32), channel_id=1, source_target_pairs={{0,4},{4,8},{8,12},{12,0},{1,5},{5,9},{9,13},{13,1},{2,6},{6,10},{... | collective-permute-start | bytes 786440 | tf_op jit(solution)/shard_map/ppermute | solution.py:458
  4.5 2.1 %collective-permute-start.3 = (bf16[64,2048]{1,0:T(8,128)(2,1)S(1)}, bf16[64,2048]{1,0:T(8,128)(2,1)S(1)}, u32[]{:S(2)}, u32[]{:S(2)}) collective-permute-start(bf16[64,2048]{1,0:T(8,128)(2,1)S(1)} %get-tuple-element.33), channel_id=1, source_target_pairs={{0,12},{4,0},{8,4},{12,8},{1,13},{5,1},{9,5},{13,9},{2,14},{6,2},{... | collective-permute-start | bytes 786440 | tf_op jit(solution)/shard_map/ppermute | solution.py:458
  6.6 0.0 collective-permute-start
  6.6 3.8 %collective-permute-start.1 = (bf16[64,2048]{1,0:T(8,128)(2,1)S(1)}, bf16[64,2048]{1,0:T(8,128)(2,1)S(1)}, u32[]{:S(2)}, u32[]{:S(2)}) collective-permute-start(bf16[64,2048]{1,0:T(8,128)(2,1)S(1)} %get-tuple-element.31), channel_id=1, source_target_pairs={{0,12},{4,0},{8,4},{12,8},{1,13},{5,1},{9,5},{13,9},{2,14},{6,2},{... | collective-permute-start | bytes 786440 | tf_op jit(solution)/shard_map/ppermute | solution.py:458
  10.4 0.0 collective-permute-done.4.refs_1_
  10.4 5.0 %project_own.1 = (bf16[2,64,64,128]{3,2,1,0:T(8,128)(2,1)S(1)}, bf16[5,64,64,64]{3,2,1,0:T(8,128)(2,1)S(1)}, bf16[2,64,4096]{2,1,0:T(8,128)(2,1)S(1)}, bf16[256,...) custom-call(bf16[2,64,4096]{2,1,0:T(8,128)(2,1)S(1)} %get-tuple-element.34.refs_0_, ...), custom_call_target="tpu_custom_call" | custom-call | tf_op jit(solution)/shard_map/project_own/pallas_call | solution.py:361
  15.5 0.0 collective-permute-done.2.refs_0_
  15.5 3.9 %collective-permute-done.3.refs_1_ = bf16[64,2048]{1,0:T(8,128)(2,1)S(1)} collective-permute-done((bf16[64,2048]{1,0:T(8,128)(2,1)S(1)}, bf16[64,2048]{1,0:T(8,128)(2,1)S(1)}, u32[]{:S(2)}, u32[]{:S(2)}) %collective-permute-start.3) | collective-permute-done | bytes 262176 | tf_op jit(solution)/shard_map/ppermute | solution.py:458
  19.4 0.1 collective-permute-start.7
  19.5 0.5 %collective-permute-start.5 = (bf16[64,1024]{1,0:T(8,128)(2,1)S(1)}, bf16[64,1024]{1,0:T(8,128)(2,1)S(1)}, u32[]{:S(2)}, u32[]{:S(2)}) collective-permute-start(bf16[64,1024]{1,0:T(8,128)(2,1)S(1)} %get-tuple-element.56), channel_id=1, source_target_pairs={{0,1},{1,0},{2,3},{3,2},{4,5},{5,4},{6,7},{7,6},{8,9},{9,8},{10,11... | collective-permute-start | bytes 393224 | tf_op jit(solution)/shard_map/ppermute | solution.py:486
  20.0 0.1 collective-permute-start.8
  20.1 0.7 %collective-permute-done.7.refs_4_ = bf16[64,1024]{1,0:T(8,128)(2,1)S(1)} collective-permute-done((bf16[64,1024]{1,0:T(8,128)(2,1)S(1)}, bf16[64,1024]{1,0:T(8,128)(2,1)S(1)}, u32[]{:S(2)}, u32[]{:S(2)}) %collective-permute-start.7) | collective-permute-done | bytes 131104 | tf_op jit(solution)/shard_map/ppermute | solution.py:486
  20.8 0.1 collective-permute-start.6
  21.0 0.0 collective-permute-done.5.refs_2_
  21.0 0.4 %collective-permute-done.8.refs_5_ = bf16[64,1024]{1,0:T(8,128)(2,1)S(1)} collective-permute-done((bf16[64,1024]{1,0:T(8,128)(2,1)S(1)}, bf16[64,1024]{1,0:T(8,128)(2,1)S(1)}, u32[]{:S(2)}, u32[]{:S(2)}) %collective-permute-start.8) | collective-permute-done | bytes 131104 | tf_op jit(solution)/shard_map/ppermute | solution.py:486
  21.4 0.8 %collective-permute-done.6.refs_3_ = bf16[64,1024]{1,0:T(8,128)(2,1)S(1)} collective-permute-done((bf16[64,1024]{1,0:T(8,128)(2,1)S(1)}, bf16[64,1024]{1,0:T(8,128)(2,1)S(1)}, u32[]{:S(2)}, u32[]{:S(2)}) %collective-permute-start.6) | collective-permute-done | bytes 131104 | tf_op jit(solution)/shard_map/ppermute | solution.py:486
  22.2 1.7 %project_first.1 = (bf16[2,64,64,128]{3,2,1,0:T(8,128)(2,1)S(1)}, bf16[64,32,128]{2,1,0:T(8,128)(2,1)S(1)}) custom-call(bf16[64,2048]{1,0:T(8,128)(2,1)S(1)} %collective-permute-done.2.refs_0_, bf16[64,2048]{1,0:T(8,128)(2,1)S(1)} %collective-permute-done.3.refs_1_, ...), custom_call_target="tpu_custom_call", output_to_operand_aliasing={{0}: (8, {})} | custom-call | tf_op jit(solution)/shard_map/project_first/pallas_call | solution.py:361
  23.8 1.2 %collective-permute-done.refs_0_ = bf16[64,2048]{1,0:T(8,128)(2,1)S(1)} collective-permute-done((bf16[64,2048]{1,0:T(8,128)(2,1)S(1)}, bf16[64,2048]{1,0:T(8,128)(2,1)S(1)}, u32[]{:S(2)}, u32[]{:S(2)}) %collective-permute-start) | collective-permute-done | bytes 262176 | tf_op jit(solution)/shard_map/ppermute | solution.py:458
  25.0 4.7 %collective-permute-done.1.refs_1_ = bf16[64,2048]{1,0:T(8,128)(2,1)S(1)} collective-permute-done((bf16[64,2048]{1,0:T(8,128)(2,1)S(1)}, bf16[64,2048]{1,0:T(8,128)(2,1)S(1)}, u32[]{:S(2)}, u32[]{:S(2)}) %collective-permute-start.1) | collective-permute-done | bytes 262176 | tf_op jit(solution)/shard_map/ppermute | solution.py:458
  29.7 0.0 collective-permute-start.9
  29.7 0.5 %collective-permute-start.10 = (bf16[64,2048]{1,0:T(8,128)(2,1)S(1)}, bf16[64,2048]{1,0:T(8,128)(2,1)S(1)}, u32[]{:S(2)}, u32[]{:S(2)}) collective-permute-start(bf16[64,2048]{1,0:T(8,128)(2,1)S(1)} %collective-permute-done.1.refs_1_), channel_id=1, source_target_pairs={{0,1},{1,0},{2,3},{3,2},{4,5},{5,4},{6,7},{7,6},{8,9},{9,8},{10,11... | collective-permute-start | bytes 786440 | tf_op jit(solution)/shard_map/ppermute | solution.py:486
  30.2 1.0 %collective-permute-done.9.refs_2_ = bf16[64,2048]{1,0:T(8,128)(2,1)S(1)} collective-permute-done((bf16[64,2048]{1,0:T(8,128)(2,1)S(1)}, bf16[64,2048]{1,0:T(8,128)(2,1)S(1)}, u32[]{:S(2)}, u32[]{:S(2)}) %collective-permute-start.9) | collective-permute-done | bytes 262176 | tf_op jit(solution)/shard_map/ppermute | solution.py:486
  31.3 0.4 collective-permute-done.10.refs_3_
  31.6 2.9 %project_last.1 = (bf16[2,64,64,128]{3,2,1,0:T(8,128)(2,1)S(1)}, bf16[5,64,64,64]{3,2,1,0:T(8,128)(2,1)S(1)}, bf16[64,4096]{1,0:T(8,128)(2,1)S(1)}) custom-call(s32[8]{0:T(128)S(4)} %get-tuple-element.29.picks_ref, bf16[64,2048]{1,0:T(8,128)(2,1)S(1)} %collective-permute-done.refs_0_, ...), custom_call_target="tpu_custom_call", output_to_operand_aliasing={{0}: (8, {}), {1}: (9, {})} | custom-call | tf_op jit(solution)/shard_map/project_last/pallas_call | solution.py:361
  34.6 0.2 collective-permute-start.12
  34.8 1.0 %triplets.1.mine_ref = bf16[64,4096]{1,0:T(8,128)(2,1)S(1)} custom-call(s32[8]{0:T(128)S(4)} %get-tuple-element.29.picks_ref, bf16[2,64,64,128]{3,2,1,0:T(8,128)(2,1)S(1)} %get-tuple-element.49.l_ref, bf16[5,64,64,64]{3,2,1,0:T(8,128)(2,1)S(1)} %get-tuple-element.50.turned_ref), custom_call_target="tpu_custom_call" | custom-call | tf_op jit(solution)/shard_map/triplets/pallas_call | solution.py:361
  35.8 0.4 %collective-permute-start.11 = (bf16[64,4096]{1,0:T(8,128)(2,1)S(1)}, bf16[64,4096]{1,0:T(8,128)(2,1)S(1)}, u32[]{:S(2)}, u32[]{:S(2)}) collective-permute-start(bf16[64,4096]{1,0:T(8,128)(2,1)S(1)} %triplets.1.mine_ref), channel_id=1, source_target_pairs={{0,1},{1,0},{2,3},{3,2},{4,5},{5,4},{6,7},{7,6},{8,9},{9,8},{10,11... | collective-permute-start | bytes 1572872 | tf_op jit(solution)/shard_map/ppermute | solution.py:523
  36.2 0.3 collective-permute-done.12.theirs_ref
  36.5 1.0 %finish.2.refs_0_ = bf16[64,4096]{1,0:T(8,128)(2,1)S(1)} custom-call(bf16[64,4096]{1,0:T(8,128)(2,1)S(1)} %get-tuple-element.47.mine_ref, bf16[64,4096]{1,0:T(8,128)(2,1)S(1)} %collective-permute-done.12.theirs_ref, bf16[2,64,4096]{2,1,0:T(8,128)(2,1)S(1)} %get-tuple-element.51.gate_ref, bf16[64,128]{1,0:T(8,128)(2,1)S(1)} %get-tuple-element.52.w_ref), custom_call_target="tpu_custom_call" | custom-call | tf_op jit(solution)/shard_map/finish/pallas_call | solution.py:415
  37.5 0.3 collective-permute-done.11.theirs_ref
  37.8 1.7 %finish.3 = bf16[2,64,4096]{2,1,0:T(8,128)(2,1)} custom-call(bf16[64,4096]{1,0:T(8,128)(2,1)S(1)} %triplets.1.mine_ref, bf16[64,4096]{1,0:T(8,128)(2,1)S(1)} %collective-permute-done.11.theirs_ref, bf16[2,64,4096]{2,1,0:T(8,128)(2,1)S(1)} %get-tuple-element.51.gate_ref, bf16[64,128]{1,0:T(8,128)(2,1)S(1)} %get-tuple-element.52.w_ref, ...), custom_call_target="tpu_custom_call" | custom-call | tf_op jit(solution)/shard_map/finish/pallas_call | solution.py:415
  (2 shorter events, 0.0 us)
Async XLA Ops:
  1.3 9.1 %collective-permute-start.4 = (bf16[2,64,4096]{2,1,0:T(8,128)(2,1)S(1)}, bf16[2,64,4096]{2,1,0:T(8,128)(2,1)S(1)}, u32[]{:S(2)}, u32[]{:S(2)}) collective-permute-start(bf16[2,64,4096]{2,1,0:T(8,128)(2,1)S(1)} %get-tuple-element.34.refs_0_), channel_id=1, source_target_pairs={{0,1},{1,0},{2,3},{3,2},{4,5},{5,4},{6,7},{7,6},{8,9},{9,8},{10,11... | collective-permute-start | bytes 3145736 | tf_op jit(solution)/shard_map/ppermute | solution.py:461
  1.9 13.6 %collective-permute-start.2 = (bf16[64,2048]{1,0:T(8,128)(2,1)S(1)}, bf16[64,2048]{1,0:T(8,128)(2,1)S(1)}, u32[]{:S(2)}, u32[]{:S(2)}) collective-permute-start(bf16[64,2048]{1,0:T(8,128)(2,1)S(1)} %get-tuple-element.32), channel_id=1, source_target_pairs={{0,4},{4,8},{8,12},{12,0},{1,5},{5,9},{9,13},{13,1},{2,6},{6,10},{... | collective-permute-start | bytes 786440 | tf_op jit(solution)/shard_map/ppermute | solution.py:458
  4.5 14.9 %collective-permute-start.3 = (bf16[64,2048]{1,0:T(8,128)(2,1)S(1)}, bf16[64,2048]{1,0:T(8,128)(2,1)S(1)}, u32[]{:S(2)}, u32[]{:S(2)}) collective-permute-start(bf16[64,2048]{1,0:T(8,128)(2,1)S(1)} %get-tuple-element.33), channel_id=1, source_target_pairs={{0,12},{4,0},{8,4},{12,8},{1,13},{5,1},{9,5},{13,9},{2,14},{6,2},{... | collective-permute-start | bytes 786440 | tf_op jit(solution)/shard_map/ppermute | solution.py:458
  6.6 18.4 %collective-permute-start = (bf16[64,2048]{1,0:T(8,128)(2,1)S(1)}, bf16[64,2048]{1,0:T(8,128)(2,1)S(1)}, u32[]{:S(2)}, u32[]{:S(2)}) collective-permute-start(bf16[64,2048]{1,0:T(8,128)(2,1)S(1)} %get-tuple-element.30), channel_id=1, source_target_pairs={{0,4},{4,8},{8,12},{12,0},{1,5},{5,9},{9,13},{13,1},{2,6},{6,10},{... | collective-permute-start | bytes 786440 | tf_op jit(solution)/shard_map/ppermute | solution.py:458
  6.6 23.1 %collective-permute-start.1 = (bf16[64,2048]{1,0:T(8,128)(2,1)S(1)}, bf16[64,2048]{1,0:T(8,128)(2,1)S(1)}, u32[]{:S(2)}, u32[]{:S(2)}) collective-permute-start(bf16[64,2048]{1,0:T(8,128)(2,1)S(1)} %get-tuple-element.31), channel_id=1, source_target_pairs={{0,12},{4,0},{8,4},{12,8},{1,13},{5,1},{9,5},{13,9},{2,14},{6,2},{... | collective-permute-start | bytes 786440 | tf_op jit(solution)/shard_map/ppermute | solution.py:458
  19.4 1.4 %collective-permute-start.7 = (bf16[64,1024]{1,0:T(8,128)(2,1)S(1)}, bf16[64,1024]{1,0:T(8,128)(2,1)S(1)}, u32[]{:S(2)}, u32[]{:S(2)}) collective-permute-start(bf16[64,1024]{1,0:T(8,128)(2,1)S(1)} %get-tuple-element.55), channel_id=1, source_target_pairs={{0,1},{1,0},{2,3},{3,2},{4,5},{5,4},{6,7},{7,6},{8,9},{9,8},{10,11... | collective-permute-start | bytes 393224 | tf_op jit(solution)/shard_map/ppermute | solution.py:486
  19.5 1.5 %collective-permute-start.5 = (bf16[64,1024]{1,0:T(8,128)(2,1)S(1)}, bf16[64,1024]{1,0:T(8,128)(2,1)S(1)}, u32[]{:S(2)}, u32[]{:S(2)}) collective-permute-start(bf16[64,1024]{1,0:T(8,128)(2,1)S(1)} %get-tuple-element.56), channel_id=1, source_target_pairs={{0,1},{1,0},{2,3},{3,2},{4,5},{5,4},{6,7},{7,6},{8,9},{9,8},{10,11... | collective-permute-start | bytes 393224 | tf_op jit(solution)/shard_map/ppermute | solution.py:486
  20.0 1.4 %collective-permute-start.8 = (bf16[64,1024]{1,0:T(8,128)(2,1)S(1)}, bf16[64,1024]{1,0:T(8,128)(2,1)S(1)}, u32[]{:S(2)}, u32[]{:S(2)}) collective-permute-start(bf16[64,1024]{1,0:T(8,128)(2,1)S(1)} %get-tuple-element.53), channel_id=1, source_target_pairs={{0,1},{1,0},{2,3},{3,2},{4,5},{5,4},{6,7},{7,6},{8,9},{9,8},{10,11... | collective-permute-start | bytes 393224 | tf_op jit(solution)/shard_map/ppermute | solution.py:486
  20.8 1.3 %collective-permute-start.6 = (bf16[64,1024]{1,0:T(8,128)(2,1)S(1)}, bf16[64,1024]{1,0:T(8,128)(2,1)S(1)}, u32[]{:S(2)}, u32[]{:S(2)}) collective-permute-start(bf16[64,1024]{1,0:T(8,128)(2,1)S(1)} %get-tuple-element.54), channel_id=1, source_target_pairs={{0,1},{1,0},{2,3},{3,2},{4,5},{5,4},{6,7},{7,6},{8,9},{9,8},{10,11... | collective-permute-start | bytes 393224 | tf_op jit(solution)/shard_map/ppermute | solution.py:486
  29.7 1.5 %collective-permute-start.9 = (bf16[64,2048]{1,0:T(8,128)(2,1)S(1)}, bf16[64,2048]{1,0:T(8,128)(2,1)S(1)}, u32[]{:S(2)}, u32[]{:S(2)}) collective-permute-start(bf16[64,2048]{1,0:T(8,128)(2,1)S(1)} %collective-permute-done.refs_0_), channel_id=1, source_target_pairs={{0,1},{1,0},{2,3},{3,2},{4,5},{5,4},{6,7},{7,6},{8,9},{9,8},{10,11... | collective-permute-start | bytes 786440 | tf_op jit(solution)/shard_map/ppermute | solution.py:486
  29.7 1.9 %collective-permute-start.10 = (bf16[64,2048]{1,0:T(8,128)(2,1)S(1)}, bf16[64,2048]{1,0:T(8,128)(2,1)S(1)}, u32[]{:S(2)}, u32[]{:S(2)}) collective-permute-start(bf16[64,2048]{1,0:T(8,128)(2,1)S(1)} %collective-permute-done.1.refs_1_), channel_id=1, source_target_pairs={{0,1},{1,0},{2,3},{3,2},{4,5},{5,4},{6,7},{7,6},{8,9},{9,8},{10,11... | collective-permute-start | bytes 786440 | tf_op jit(solution)/shard_map/ppermute | solution.py:486
  34.6 2.0 %collective-permute-start.12 = (bf16[64,4096]{1,0:T(8,128)(2,1)S(1)}, bf16[64,4096]{1,0:T(8,128)(2,1)S(1)}, u32[]{:S(2)}, u32[]{:S(2)}) collective-permute-start(bf16[64,4096]{1,0:T(8,128)(2,1)S(1)} %get-tuple-element.47.mine_ref), channel_id=1, source_target_pairs={{0,1},{1,0},{2,3},{3,2},{4,5},{5,4},{6,7},{7,6},{8,9},{9,8},{10,11... | collective-permute-start | bytes 1572872 | tf_op jit(solution)/shard_map/ppermute | solution.py:512
  35.8 2.0 %collective-permute-start.11 = (bf16[64,4096]{1,0:T(8,128)(2,1)S(1)}, bf16[64,4096]{1,0:T(8,128)(2,1)S(1)}, u32[]{:S(2)}, u32[]{:S(2)}) collective-permute-start(bf16[64,4096]{1,0:T(8,128)(2,1)S(1)} %triplets.1.mine_ref), channel_id=1, source_target_pairs={{0,1},{1,0},{2,3},{3,2},{4,5},{5,4},{6,7},{7,6},{8,9},{9,8},{10,11... | collective-permute-start | bytes 1572872 | tf_op jit(solution)/shard_map/ppermute | solution.py:523

commit v14 on v13

--- a/solution.py
+++ b/solution.py
@@ -188,19 +188,15 @@
             yield
 
 
-def two_chunks(sides_at, n, chunk, held, spread, after=()):
-    steps = [
-        pair_chunk(functools.partial(sides_at, n + k), chunk, held[2 * k : 2 * k + 2])
-        for k in range(2)
-    ]
-    spreads = [spread(n + k, held[2 * k : 2 * k + 2], k) for k in range(2)]
-    for _ in steps[0]:
-        pass
-    for _ in zip(steps[1], spreads[0]):
-        pass
-    for _ in spreads[0]:
-        pass
-    for at, _ in enumerate(spreads[1]):
+def in_turn(sides_at, chunks, chunk, held, spread, after=(), pending=()):
+    for k, n in enumerate(chunks):
+        scratch = held[2 * (k % 2) : 2 * (k % 2) + 2]
+        for _ in pair_chunk(functools.partial(sides_at, n), chunk, scratch):
+            next(iter(pending), None)
+        for _ in pending:
+            pass
+        pending = spread(n, scratch, k + 1 == len(chunks))
+    for at, _ in enumerate(pending):
         if at > 0:
             next(iter(after), None)
     for _ in after:
@@ -258,58 +254,72 @@
 
     @pl.loop(0, chunks - 2, step=2)
     def _(n):
-        two_chunks(sides_at, n, chunk, held, functools.partial(spread, False))
-
-    two_chunks(sides_at, chunks - 2, chunk, held, functools.partial(spread, True))
+        in_turn(sides_at, (n, n + 1), chunk, held, functools.partial(spread, False))
+
+    in_turn(sides_at, (chunks - 2, chunks - 1), chunk, held, functools.partial(spread, True))
 
 
 def fetched_sides(chunk, ours, theirs, weight, gain_ref, half):
-    wide = theirs[0].shape[1]
-
     def sides_at(n, start):
         at = n * chunk + start
-        both = []
-        for x, m in enumerate(ours):
-            other = theirs[2 * (at // wide) + x][:, at % wide : at % wide + LANES]
-            both.append(
-                gated_sides(m[:, at : at + LANES], other, weight, gain_ref[...], half)[0]
-            )
-        return both
+        return [
+            gated_sides(
+                m[:, at : at + LANES], theirs[n][x, :, start : start + LANES], weight, gain_ref[...], half
+            )[0]
+            for x, m in enumerate(ours)
+        ]
 
     return sides_at
 
 
-def first_kernel(chunk, *refs):
-    *ours_theirs, w_ref, gain_ref, _, l_ref, p_ref = refs[:-4]
+def first_kernel(chunk, m0, m1, *refs):
+    *theirs, w_ref, gain_ref, _, l_ref, p_ref = refs[:-4]
     held = refs[-4:]
     half = l_ref.shape[1]
     rows = chunk // BLK
-    sides_at = fetched_sides(
-        chunk, ours_theirs[:2], ours_theirs[2:], w_ref[...], gain_ref, half
-    )
-
-    def spread(n, held, k):
+    weight = w_ref[...]
+
+    def sides_at(n, start):
+        at = n * chunk + start
+        return [
+            gated_sides(
+                m[:, at : at + LANES],
+                theirs[2 * n + x][:, start : start + LANES],
+                weight,
+                gain_ref[...],
+                half,
+            )[0]
+            for x, m in enumerate((m0, m1))
+        ]
+
+    def spread(n, held, last):
         return spread_chunk(rows, held, l_ref, 1, n * rows, p_ref, n * rows, None, None, half)
 
-    two_chunks(sides_at, 0, chunk, held, spread)
-
-
-def last_kernel(chunk, first_row, group, picks_ref, *refs):
-    *ours_theirs, p0_ref, w_ref, gain_ref, _, _, l_ref, turned_ref, out_ref, p_ref = refs[:-6]
-    held, accs = refs[-6:-2], refs[-2:]
-    before = [(p0_ref, p0_ref.shape[1]), (p_ref, p_ref.shape[1])]
+    in_turn(sides_at, range(2), chunk, held, spread)
+
+
+def half_kernel(chunk, m0, m1, t_ref, w_ref, gain_ref, *held):
+    half = m0.shape[0]
+    sides_at = fetched_sides(chunk, (m0, m1), (t_ref,), w_ref[...], gain_ref, half)
+    for _ in pair_chunk(functools.partial(sides_at, 0), chunk, held):
+        pass
+
+
+def last_kernel(chunk, first_row, group, picks_ref, m0, m1, t_ref, *refs):
+    earlier_ref, *done, w_ref, gain_ref, _, _, l_ref, turned_ref, out_ref, p_ref = refs[:-4]
+    held, accs = refs[-4:-2], refs[-2:]
     half = l_ref.shape[1]
     rows = chunk // BLK
-    sides_at = fetched_sides(
-        chunk, ours_theirs[:2], ours_theirs[2:], w_ref[...], gain_ref, half
-    )
-
-    def spread(n, held, k):
-        done = (before, turned_ref) if k else (None, None)
-        return spread_chunk(rows, held, l_ref, 1, first_row + n * rows, p_ref, n * rows, *done, half)
+    before = [(earlier_ref, earlier_ref.shape[1]), (p_ref, rows)]
+    sides_at = fetched_sides(chunk, (m0, m1), (None, t_ref), w_ref[...], gain_ref, half)
+
+    def spread(n, held, last):
+        row = first_row + n * rows
+        whole = (before, turned_ref) if last else (None, None)
+        return spread_chunk(rows, held, l_ref, 1, row, p_ref, n * rows, *whole, half)
 
     products = triplet_steps(0, group, picks_ref, l_ref, turned_ref, out_ref, accs)
-    two_chunks(sides_at, 0, chunk, held, spread, products)
+    in_turn(sides_at, (1,), chunk, held, spread, products, spread(0, done, False))
 
 
 def triplet_steps(s, group, picks_ref, l_ref, turned_ref, out_ref, accs):
@@ -481,30 +491,41 @@
     )
     for (start, size), behind_ahead in zip(cuts, arrived):
         *behind_ahead, lefts = lax.optimization_barrier((*behind_ahead, lefts))
-        wide = chunk if start == 0 else size
-        others = [
-            lax.ppermute(lax.slice_in_dim(value, at, at + wide, axis=1), "chan", swap)
-            for at in range(0, size, wide)
-            for value in behind_ahead
-        ]
-        paired = pltpu.VMEM((half, size // BLK, LANES), BF16)
         if start == 0:
-            lefts, rights_first = call(
+            others = [
+                lax.ppermute(lax.slice_in_dim(value, at, at + chunk, axis=1), "chan", swap)
+                for at in (0, chunk)
+                for value in behind_ahead
+            ]
+            lefts, earlier = call(
                 functools.partial(first_kernel, chunk),
                 "project_first",
                 [*behind_ahead, *others, weight, gain, lefts],
-                [left_shape, paired],
+                [left_shape, pltpu.VMEM((half, size // BLK, LANES), BF16)],
                 chunk_scratch(half, chunk),
                 aliased=1,
             )
         else:
+            others = [
+                lax.ppermute(
+                    jnp.stack([value[:, at : at + chunk] for value in behind_ahead]), "chan", swap
+                )
+                for at in (0, chunk)
+            ]
+            done = call(
+                functools.partial(half_kernel, chunk),
+                "project_half",
+                [*behind_ahead, others[0], weight, gain],
+                chunk_scratch(half, chunk)[:2],
+                [],
+            )
             lefts, rights, update = call(
                 functools.partial(last_kernel, chunk, start // BLK, 16),
                 "project_last",
-                [picks, *behind_ahead, *others, rights_first, weight, gain, lefts, rights],
+                [picks, *behind_ahead, others[1], earlier, *done, weight, gain, lefts, rights],
                 [left_shape, right_shape, pltpu.VMEM((half, cells), BF16)],
                 [pltpu.VMEM((half, chunk // BLK, LANES), BF16)]
-                + chunk_scratch(half, chunk)
+                + chunk_scratch(half, chunk)[:2]
                 + acc_scratch(16),
                 aliased=2,
                 smem=1,

time: 39.6 us -> 39.7 us (level)
  waiting for transfers between devices: 13.6 us -> 13.2 us
    ppermute x6, waiting for transfers between devices: 3.27 us -> 2.8 us  [the longest x4 1.87 us: per_device(): lax.ppermute(lax.slice_in_dim(value, at, at + chunk, axis=1), 'chan', swap)]
    pallas_call x4 -> x5, Pallas kernels: 10.6 us -> 10.9 us  [call(): pl.pallas_call(kernel, in_specs=[pl.BlockSpec(memory_space=space) for spa...]
  transfers between devices with their start and end apart: 13 -> 13, of which waited for: 10 -> 9; matrix products, arithmetic and copies ran while one was open for 0% -> 0% of each run, Pallas kernels for 22% -> 24%
where the time goes in v14:
time: 39.7 us; the launch traced here: 39.5 us
  Pallas kernels  14.8 us (37%)
  waiting for transfers between devices  13.2 us (33%)
  starting transfers between devices  11.2 us (28%)
    pallas_call x5, Pallas kernels, call(): pl.pallas_call(kernel, in_specs=[pl.BlockSpec(memory_space=space) for spa...  10.9 us
    ppermute x2, waiting for transfers between devices, per_device(): lax.ppermute(chosen[2 * n + 1], 'row', down)  8.64 us
    ppermute x2, starting transfers between devices, per_device(): lax.ppermute(chosen[2 * n + 1], 'row', down)  5.93 us
    pallas_call x2, Pallas kernels, finish(): pl.pallas_call(functools.partial(finish_kernel, s, mine.shape[1] // 2, 4)...  2.65 us
    ppermute x2, starting transfers between devices, per_device(): lax.ppermute(chosen[2 * n], 'row', up)  2.64 us
    ppermute x4, waiting for transfers between devices, per_device(): lax.ppermute(lax.slice_in_dim(value, at, at + chunk, axis=1), 'chan', swap)  1.87 us
    pallas_call x1, Pallas kernels, select_blocks(): pl.pallas_call(functools.partial(select_kernel, slots, a_slots.shape[0],...  1.33 us
    ppermute x2, waiting for transfers between devices, per_device(): lax.ppermute(chosen[2 * n], 'row', up)  1.17 us
  transfers between devices with their start and end apart: 13, of which 9 were waited for; matrix products, arithmetic and copies ran while one was open for 0% of the time, Pallas kernels for 24%

profile of v14, /device:TPU:0, one launch (start us, length us, event | category | flops | bytes accessed | tf_op | source)
XLA Modules:
  0.0 39.5 jit_solution(1415770677813753901)
XLA Ops:
  0.0 1.3 %select_blocks.1 = (s32[8]{0:T(128)S(4)}, bf16[2,64,4096]{2,1,0:T(8,128)(2,1)S(1)}, bf16[64,2048]{1,0:T(8,128)(2,1)S(1)}, bf16[64,2048]{1,0:T(8,128)(2,1)S(1)}, ...) custom-call(s32[4,16]{1,0:T(4,128)} %bitcast.20, s32[4,16]{1,0:T(4,128)} %bitcast.21, s32[16]{0:T(128)} %n_hbm.1, ...), custom_call_target="tpu_custom_call" | custom-call | tf_op jit(solution)/shard_map/select_blocks/pallas_call | solution.py:103
  1.3 0.5 %collective-permute-start.4 = (bf16[2,64,4096]{2,1,0:T(8,128)(2,1)S(1)}, bf16[2,64,4096]{2,1,0:T(8,128)(2,1)S(1)}, u32[]{:S(2)}, u32[]{:S(2)}) collective-permute-start(bf16[2,64,4096]{2,1,0:T(8,128)(2,1)S(1)} %get-tuple-element.36.refs_0_), channel_id=1, source_target_pairs={{0,1},{1,0},{2,3},{3,2},{4,5},{5,4},{6,7},{7,6},{8,9},{9,8},{10,11... | collective-permute-start | bytes 3145736 | tf_op jit(solution)/shard_map/ppermute | solution.py:471
  1.9 2.6 %collective-permute-start.2 = (bf16[64,2048]{1,0:T(8,128)(2,1)S(1)}, bf16[64,2048]{1,0:T(8,128)(2,1)S(1)}, u32[]{:S(2)}, u32[]{:S(2)}) collective-permute-start(bf16[64,2048]{1,0:T(8,128)(2,1)S(1)} %get-tuple-element.34), channel_id=1, source_target_pairs={{0,4},{4,8},{8,12},{12,0},{1,5},{5,9},{9,13},{13,1},{2,6},{6,10},{... | collective-permute-start | bytes 786440 | tf_op jit(solution)/shard_map/ppermute | solution.py:468
  4.5 2.1 %collective-permute-start.3 = (bf16[64,2048]{1,0:T(8,128)(2,1)S(1)}, bf16[64,2048]{1,0:T(8,128)(2,1)S(1)}, u32[]{:S(2)}, u32[]{:S(2)}) collective-permute-start(bf16[64,2048]{1,0:T(8,128)(2,1)S(1)} %get-tuple-element.35), channel_id=1, source_target_pairs={{0,12},{4,0},{8,4},{12,8},{1,13},{5,1},{9,5},{13,9},{2,14},{6,2},{... | collective-permute-start | bytes 786440 | tf_op jit(solution)/shard_map/ppermute | solution.py:468
  6.6 0.0 collective-permute-start
  6.6 3.8 %collective-permute-start.1 = (bf16[64,2048]{1,0:T(8,128)(2,1)S(1)}, bf16[64,2048]{1,0:T(8,128)(2,1)S(1)}, u32[]{:S(2)}, u32[]{:S(2)}) collective-permute-start(bf16[64,2048]{1,0:T(8,128)(2,1)S(1)} %get-tuple-element.33), channel_id=1, source_target_pairs={{0,12},{4,0},{8,4},{12,8},{1,13},{5,1},{9,5},{13,9},{2,14},{6,2},{... | collective-permute-start | bytes 786440 | tf_op jit(solution)/shard_map/ppermute | solution.py:468
  10.4 0.0 collective-permute-done.4.refs_1_
  10.4 5.0 %project_own.1 = (bf16[2,64,64,128]{3,2,1,0:T(8,128)(2,1)S(1)}, bf16[5,64,64,64]{3,2,1,0:T(8,128)(2,1)S(1)}, bf16[2,64,4096]{2,1,0:T(8,128)(2,1)S(1)}, bf16[256,...) custom-call(bf16[2,64,4096]{2,1,0:T(8,128)(2,1)S(1)} %get-tuple-element.36.refs_0_, ...), custom_call_target="tpu_custom_call" | custom-call | tf_op jit(solution)/shard_map/project_own/pallas_call | solution.py:371
  15.4 0.0 collective-permute-done.2.m0
  15.5 3.9 %collective-permute-done.3.m1 = bf16[64,2048]{1,0:T(8,128)(2,1)S(1)} collective-permute-done((bf16[64,2048]{1,0:T(8,128)(2,1)S(1)}, bf16[64,2048]{1,0:T(8,128)(2,1)S(1)}, u32[]{:S(2)}, u32[]{:S(2)}) %collective-permute-start.3) | collective-permute-done | bytes 262176 | tf_op jit(solution)/shard_map/ppermute | solution.py:468
  19.4 0.1 collective-permute-start.7
  19.5 0.5 %collective-permute-start.5 = (bf16[64,1024]{1,0:T(8,128)(2,1)S(1)}, bf16[64,1024]{1,0:T(8,128)(2,1)S(1)}, u32[]{:S(2)}, u32[]{:S(2)}) collective-permute-start(bf16[64,1024]{1,0:T(8,128)(2,1)S(1)} %get-tuple-element.64), channel_id=1, source_target_pairs={{0,1},{1,0},{2,3},{3,2},{4,5},{5,4},{6,7},{7,6},{8,9},{9,8},{10,11... | collective-permute-start | bytes 393224 | tf_op jit(solution)/shard_map/ppermute | solution.py:496
  20.0 0.1 collective-permute-start.8
  20.1 0.7 %collective-permute-done.7.refs_2_ = bf16[64,1024]{1,0:T(8,128)(2,1)S(1)} collective-permute-done((bf16[64,1024]{1,0:T(8,128)(2,1)S(1)}, bf16[64,1024]{1,0:T(8,128)(2,1)S(1)}, u32[]{:S(2)}, u32[]{:S(2)}) %collective-permute-start.7) | collective-permute-done | bytes 131104 | tf_op jit(solution)/shard_map/ppermute | solution.py:496
  20.8 0.1 collective-permute-start.6
  21.0 0.0 collective-permute-done.5.refs_0_
  21.0 0.4 %collective-permute-done.8.refs_3_ = bf16[64,1024]{1,0:T(8,128)(2,1)S(1)} collective-permute-done((bf16[64,1024]{1,0:T(8,128)(2,1)S(1)}, bf16[64,1024]{1,0:T(8,128)(2,1)S(1)}, u32[]{:S(2)}, u32[]{:S(2)}) %collective-permute-start.8) | collective-permute-done | bytes 131104 | tf_op jit(solution)/shard_map/ppermute | solution.py:496
  21.4 0.8 %collective-permute-done.6.refs_1_ = bf16[64,1024]{1,0:T(8,128)(2,1)S(1)} collective-permute-done((bf16[64,1024]{1,0:T(8,128)(2,1)S(1)}, bf16[64,1024]{1,0:T(8,128)(2,1)S(1)}, u32[]{:S(2)}, u32[]{:S(2)}) %collective-permute-start.6) | collective-permute-done | bytes 131104 | tf_op jit(solution)/shard_map/ppermute | solution.py:496
  22.2 1.7 %project_first.1 = (bf16[2,64,64,128]{3,2,1,0:T(8,128)(2,1)S(1)}, bf16[64,32,128]{2,1,0:T(8,128)(2,1)S(1)}) custom-call(bf16[64,2048]{1,0:T(8,128)(2,1)S(1)} %collective-permute-done.2.m0, bf16[64,2048]{1,0:T(8,128)(2,1)S(1)} %collective-permute-done.3.m1, bf16[64,1024]{1,0:T(8,128)(2,1)S(1)} %collective-permute-done.5.refs_0_, ...), custom_call_target="tpu_custom_call", output_to_operand_aliasing={{0}: (8, {})} | custom-call | tf_op jit(solution)/shard_map/project_first/pallas_call | solution.py:371
  23.8 1.2 %collective-permute-done.m0 = bf16[64,2048]{1,0:T(8,128)(2,1)S(1)} collective-permute-done((bf16[64,2048]{1,0:T(8,128)(2,1)S(1)}, bf16[64,2048]{1,0:T(8,128)(2,1)S(1)}, u32[]{:S(2)}, u32[]{:S(2)}) %collective-permute-start) | collective-permute-done | bytes 262176 | tf_op jit(solution)/shard_map/ppermute | solution.py:468
  25.0 4.7 %collective-permute-done.1.m1 = bf16[64,2048]{1,0:T(8,128)(2,1)S(1)} collective-permute-done((bf16[64,2048]{1,0:T(8,128)(2,1)S(1)}, bf16[64,2048]{1,0:T(8,128)(2,1)S(1)}, u32[]{:S(2)}, u32[]{:S(2)}) %collective-permute-start.1) | collective-permute-done | bytes 262176 | tf_op jit(solution)/shard_map/ppermute | solution.py:468
  29.8 0.1 collective-permute-start.10
  29.9 0.6 %collective-permute-start.9 = (bf16[2,64,1024]{2,1,0:T(8,128)(2,1)S(1)}, bf16[2,64,1024]{2,1,0:T(8,128)(2,1)S(1)}, u32[]{:S(2)}, u32[]{:S(2)}) collective-permute-start(bf16[2,64,1024]{2,1,0:T(8,128)(2,1)S(1)} %pad_maximum_fusion), channel_id=1, source_target_pairs={{0,1},{1,0},{2,3},{3,2},{4,5},{5,4},{6,7},{7,6},{8,9},{9,8},{10,11... | collective-permute-start | bytes 786440 | tf_op jit(solution)/shard_map/ppermute | solution.py:510
  30.5 0.9 %collective-permute-done.10.t_ref = bf16[2,64,1024]{2,1,0:T(8,128)(2,1)S(1)} collective-permute-done((bf16[2,64,1024]{2,1,0:T(8,128)(2,1)S(1)}, bf16[2,64,1024]{2,1,0:T(8,128)(2,1)S(1)}, u32[]{:S(2)}, u32[]{:S(2)}) %collective-permute-start.10) | collective-permute-done | bytes 262176 | tf_op jit(solution)/shard_map/ppermute | solution.py:510
  31.4 0.7 %project_half.1 = (f32[1152,128]{1,0:T(8,128)S(1)}, f32[1152,128]{1,0:T(8,128)S(1)}) custom-call(bf16[64,2048]{1,0:T(8,128)(2,1)S(1)} %collective-permute-done.m0, bf16[64,2048]{1,0:T(8,128)(2,1)S(1)} %collective-permute-done.1.m1, bf16[2,64,1024]{2,1,0:T(8,128)(2,1)S(1)} %collective-permute-done.10.t_ref, ...), custom_call_target="tpu_custom_call" | custom-call | tf_op jit(solution)/shard_map/project_half/pallas_call | solution.py:371
  32.1 0.0 collective-permute-done.9.t_ref
  32.1 2.5 %project_last.1 = (bf16[2,64,64,128]{3,2,1,0:T(8,128)(2,1)S(1)}, bf16[5,64,64,64]{3,2,1,0:T(8,128)(2,1)S(1)}, bf16[64,4096]{1,0:T(8,128)(2,1)S(1)}) custom-call(s32[8]{0:T(128)S(4)} %get-tuple-element.31.picks_ref, bf16[64,2048]{1,0:T(8,128)(2,1)S(1)} %collective-permute-done.m0, ...), custom_call_target="tpu_custom_call", output_to_operand_aliasing={{0}: (9, {}), {1}: (10, {})} | custom-call | tf_op jit(solution)/shard_map/project_last/pallas_call | solution.py:371
  34.6 0.2 collective-permute-start.12
  34.8 1.0 %triplets.1.mine_ref = bf16[64,4096]{1,0:T(8,128)(2,1)S(1)} custom-call(s32[8]{0:T(128)S(4)} %get-tuple-element.31.picks_ref, bf16[2,64,64,128]{3,2,1,0:T(8,128)(2,1)S(1)} %get-tuple-element.53.l_ref, bf16[5,64,64,64]{3,2,1,0:T(8,128)(2,1)S(1)} %get-tuple-element.54.turned_ref), custom_call_target="tpu_custom_call" | custom-call | tf_op jit(solution)/shard_map/triplets/pallas_call | solution.py:371
  35.8 0.4 %collective-permute-start.11 = (bf16[64,4096]{1,0:T(8,128)(2,1)S(1)}, bf16[64,4096]{1,0:T(8,128)(2,1)S(1)}, u32[]{:S(2)}, u32[]{:S(2)}) collective-permute-start(bf16[64,4096]{1,0:T(8,128)(2,1)S(1)} %triplets.1.mine_ref), channel_id=1, source_target_pairs={{0,1},{1,0},{2,3},{3,2},{4,5},{5,4},{6,7},{7,6},{8,9},{9,8},{10,11... | collective-permute-start | bytes 1572872 | tf_op jit(solution)/shard_map/ppermute | solution.py:544
  36.3 0.3 collective-permute-done.12.theirs_ref
  36.5 1.0 %finish.2.refs_0_ = bf16[64,4096]{1,0:T(8,128)(2,1)S(1)} custom-call(bf16[64,4096]{1,0:T(8,128)(2,1)S(1)} %get-tuple-element.51.mine_ref, bf16[64,4096]{1,0:T(8,128)(2,1)S(1)} %collective-permute-done.12.theirs_ref, bf16[2,64,4096]{2,1,0:T(8,128)(2,1)S(1)} %get-tuple-element.55.gate_ref, bf16[64,128]{1,0:T(8,128)(2,1)S(1)} %get-tuple-element.56.w_ref), custom_call_target="tpu_custom_call" | custom-call | tf_op jit(solution)/shard_map/finish/pallas_call | solution.py:425
  37.5 0.3 collective-permute-done.11.theirs_ref
  37.8 1.7 %finish.3 = bf16[2,64,4096]{2,1,0:T(8,128)(2,1)} custom-call(bf16[64,4096]{1,0:T(8,128)(2,1)S(1)} %triplets.1.mine_ref, bf16[64,4096]{1,0:T(8,128)(2,1)S(1)} %collective-permute-done.11.theirs_ref, bf16[2,64,4096]{2,1,0:T(8,128)(2,1)S(1)} %get-tuple-element.55.gate_ref, bf16[64,128]{1,0:T(8,128)(2,1)S(1)} %get-tuple-element.56.w_ref, ...), custom_call_target="tpu_custom_call" | custom-call | tf_op jit(solution)/shard_map/finish/pallas_call | solution.py:425
  (5 shorter events, 0.1 us)
Async XLA Ops:
  1.3 9.1 %collective-permute-start.4 = (bf16[2,64,4096]{2,1,0:T(8,128)(2,1)S(1)}, bf16[2,64,4096]{2,1,0:T(8,128)(2,1)S(1)}, u32[]{:S(2)}, u32[]{:S(2)}) collective-permute-start(bf16[2,64,4096]{2,1,0:T(8,128)(2,1)S(1)} %get-tuple-element.36.refs_0_), channel_id=1, source_target_pairs={{0,1},{1,0},{2,3},{3,2},{4,5},{5,4},{6,7},{7,6},{8,9},{9,8},{10,11... | collective-permute-start | bytes 3145736 | tf_op jit(solution)/shard_map/ppermute | solution.py:471
  1.9 13.6 %collective-permute-start.2 = (bf16[64,2048]{1,0:T(8,128)(2,1)S(1)}, bf16[64,2048]{1,0:T(8,128)(2,1)S(1)}, u32[]{:S(2)}, u32[]{:S(2)}) collective-permute-start(bf16[64,2048]{1,0:T(8,128)(2,1)S(1)} %get-tuple-element.34), channel_id=1, source_target_pairs={{0,4},{4,8},{8,12},{12,0},{1,5},{5,9},{9,13},{13,1},{2,6},{6,10},{... | collective-permute-start | bytes 786440 | tf_op jit(solution)/shard_map/ppermute | solution.py:468
  4.5 14.9 %collective-permute-start.3 = (bf16[64,2048]{1,0:T(8,128)(2,1)S(1)}, bf16[64,2048]{1,0:T(8,128)(2,1)S(1)}, u32[]{:S(2)}, u32[]{:S(2)}) collective-permute-start(bf16[64,2048]{1,0:T(8,128)(2,1)S(1)} %get-tuple-element.35), channel_id=1, source_target_pairs={{0,12},{4,0},{8,4},{12,8},{1,13},{5,1},{9,5},{13,9},{2,14},{6,2},{... | collective-permute-start | bytes 786440 | tf_op jit(solution)/shard_map/ppermute | solution.py:468
  6.6 18.4 %collective-permute-start = (bf16[64,2048]{1,0:T(8,128)(2,1)S(1)}, bf16[64,2048]{1,0:T(8,128)(2,1)S(1)}, u32[]{:S(2)}, u32[]{:S(2)}) collective-permute-start(bf16[64,2048]{1,0:T(8,128)(2,1)S(1)} %get-tuple-element.32), channel_id=1, source_target_pairs={{0,4},{4,8},{8,12},{12,0},{1,5},{5,9},{9,13},{13,1},{2,6},{6,10},{... | collective-permute-start | bytes 786440 | tf_op jit(solution)/shard_map/ppermute | solution.py:468
  6.6 23.1 %collective-permute-start.1 = (bf16[64,2048]{1,0:T(8,128)(2,1)S(1)}, bf16[64,2048]{1,0:T(8,128)(2,1)S(1)}, u32[]{:S(2)}, u32[]{:S(2)}) collective-permute-start(bf16[64,2048]{1,0:T(8,128)(2,1)S(1)} %get-tuple-element.33), channel_id=1, source_target_pairs={{0,12},{4,0},{8,4},{12,8},{1,13},{5,1},{9,5},{13,9},{2,14},{6,2},{... | collective-permute-start | bytes 786440 | tf_op jit(solution)/shard_map/ppermute | solution.py:468
  19.4 1.4 %collective-permute-start.7 = (bf16[64,1024]{1,0:T(8,128)(2,1)S(1)}, bf16[64,1024]{1,0:T(8,128)(2,1)S(1)}, u32[]{:S(2)}, u32[]{:S(2)}) collective-permute-start(bf16[64,1024]{1,0:T(8,128)(2,1)S(1)} %get-tuple-element.63), channel_id=1, source_target_pairs={{0,1},{1,0},{2,3},{3,2},{4,5},{5,4},{6,7},{7,6},{8,9},{9,8},{10,11... | collective-permute-start | bytes 393224 | tf_op jit(solution)/shard_map/ppermute | solution.py:496
  19.5 1.5 %collective-permute-start.5 = (bf16[64,1024]{1,0:T(8,128)(2,1)S(1)}, bf16[64,1024]{1,0:T(8,128)(2,1)S(1)}, u32[]{:S(2)}, u32[]{:S(2)}) collective-permute-start(bf16[64,1024]{1,0:T(8,128)(2,1)S(1)} %get-tuple-element.64), channel_id=1, source_target_pairs={{0,1},{1,0},{2,3},{3,2},{4,5},{5,4},{6,7},{7,6},{8,9},{9,8},{10,11... | collective-permute-start | bytes 393224 | tf_op jit(solution)/shard_map/ppermute | solution.py:496
  20.0 1.4 %collective-permute-start.8 = (bf16[64,1024]{1,0:T(8,128)(2,1)S(1)}, bf16[64,1024]{1,0:T(8,128)(2,1)S(1)}, u32[]{:S(2)}, u32[]{:S(2)}) collective-permute-start(bf16[64,1024]{1,0:T(8,128)(2,1)S(1)} %get-tuple-element.61), channel_id=1, source_target_pairs={{0,1},{1,0},{2,3},{3,2},{4,5},{5,4},{6,7},{7,6},{8,9},{9,8},{10,11... | collective-permute-start | bytes 393224 | tf_op jit(solution)/shard_map/ppermute | solution.py:496
  20.8 1.3 %collective-permute-start.6 = (bf16[64,1024]{1,0:T(8,128)(2,1)S(1)}, bf16[64,1024]{1,0:T(8,128)(2,1)S(1)}, u32[]{:S(2)}, u32[]{:S(2)}) collective-permute-start(bf16[64,1024]{1,0:T(8,128)(2,1)S(1)} %get-tuple-element.62), channel_id=1, source_target_pairs={{0,1},{1,0},{2,3},{3,2},{4,5},{5,4},{6,7},{7,6},{8,9},{9,8},{10,11... | collective-permute-start | bytes 393224 | tf_op jit(solution)/shard_map/ppermute | solution.py:496
  29.8 1.6 %collective-permute-start.10 = (bf16[2,64,1024]{2,1,0:T(8,128)(2,1)S(1)}, bf16[2,64,1024]{2,1,0:T(8,128)(2,1)S(1)}, u32[]{:S(2)}, u32[]{:S(2)}) collective-permute-start(bf16[2,64,1024]{2,1,0:T(8,128)(2,1)S(1)} %pad_maximum_fusion.1), channel_id=1, source_target_pairs={{0,1},{1,0},{2,3},{3,2},{4,5},{5,4},{6,7},{7,6},{8,9},{9,8},{10,11... | collective-permute-start | bytes 786440 | tf_op jit(solution)/shard_map/ppermute | solution.py:510
  29.9 2.2 %collective-permute-start.9 = (bf16[2,64,1024]{2,1,0:T(8,128)(2,1)S(1)}, bf16[2,64,1024]{2,1,0:T(8,128)(2,1)S(1)}, u32[]{:S(2)}, u32[]{:S(2)}) collective-permute-start(bf16[2,64,1024]{2,1,0:T(8,128)(2,1)S(1)} %pad_maximum_fusion), channel_id=1, source_target_pairs={{0,1},{1,0},{2,3},{3,2},{4,5},{5,4},{6,7},{7,6},{8,9},{9,8},{10,11... | collective-permute-start | bytes 786440 | tf_op jit(solution)/shard_map/ppermute | solution.py:510
  34.6 2.0 %collective-permute-start.12 = (bf16[64,4096]{1,0:T(8,128)(2,1)S(1)}, bf16[64,4096]{1,0:T(8,128)(2,1)S(1)}, u32[]{:S(2)}, u32[]{:S(2)}) collective-permute-start(bf16[64,4096]{1,0:T(8,128)(2,1)S(1)} %get-tuple-element.51.mine_ref), channel_id=1, source_target_pairs={{0,1},{1,0},{2,3},{3,2},{4,5},{5,4},{6,7},{7,6},{8,9},{9,8},{10,11... | collective-permute-start | bytes 1572872 | tf_op jit(solution)/shard_map/ppermute | solution.py:533
  35.8 2.0 %collective-permute-start.11 = (bf16[64,4096]{1,0:T(8,128)(2,1)S(1)}, bf16[64,4096]{1,0:T(8,128)(2,1)S(1)}, u32[]{:S(2)}, u32[]{:S(2)}) collective-permute-start(bf16[64,4096]{1,0:T(8,128)(2,1)S(1)} %triplets.1.mine_ref), channel_id=1, source_target_pairs={{0,1},{1,0},{2,3},{3,2},{4,5},{5,4},{6,7},{7,6},{8,9},{9,8},{10,11... | collective-permute-start | bytes 1572872 | tf_op jit(solution)/shard_map/ppermute | solution.py:544

commit v15 on v13

--- a/solution.py
+++ b/solution.py
@@ -57,8 +57,8 @@
 
 
 def select_kernel(slots, triplets, cuts, a_hbm, b_hbm, n_hbm, pair_hbm, *refs):
-    picks_ref, pair_ref, *out_refs = refs[: 2 + 2 * len(cuts)]
-    a_ref, b_ref, n_ref, sems = refs[2 + 2 * len(cuts) :]
+    pair_ref, *out_refs = refs[: 1 + 2 * len(cuts)]
+    a_ref, b_ref, n_ref, sems = refs[1 + 2 * len(cuts) :]
     me, behind, ahead = neighbour_tiles()
     whole = pltpu.make_async_copy(pair_hbm, pair_ref, sems.at[0])
     tables = [
@@ -80,9 +80,6 @@
                     mine = jnp.logical_and(name >= 0, name < slots)
                     pick = jnp.where(jnp.logical_and(m < count, mine), name, pick)
         chosen.append(pick)
-    for s in range(slots):
-        for at, pick in enumerate(used_picks(s, slots, triplets, a_ref, b_ref, n_ref)):
-            picks_ref[4 * s + at] = pick
     whole.wait()
     for at, (start, size) in enumerate(cuts):
         for which, pick in enumerate(chosen):
@@ -93,7 +90,7 @@
     slots, channels, cells = pair.shape
     hbm = pl.BlockSpec(memory_space=pltpu.HBM)
     vmem = pl.BlockSpec(memory_space=pltpu.VMEM)
-    out_shape = [pltpu.SMEM((4 * slots,), jnp.int32), pltpu.VMEM(pair.shape, pair.dtype)] + [
+    out_shape = [pltpu.VMEM(pair.shape, pair.dtype)] + [
         pltpu.VMEM((channels, size), pair.dtype) for _, size in cuts for _ in range(2)
     ]
     operands = [
@@ -104,7 +101,7 @@
         functools.partial(select_kernel, slots, a_slots.shape[0], cuts),
         out_shape=out_shape,
         in_specs=[hbm] * 4,
-        out_specs=[pl.BlockSpec(memory_space=pltpu.SMEM)] + [vmem] * (len(out_shape) - 1),
+        out_specs=[vmem] * len(out_shape),
         scratch_shapes=[pltpu.SMEM(value.shape, value.dtype) for value in operands[:3]]
         + [pltpu.SemaphoreType.DMA((4,))],
         name="select_blocks",
@@ -213,10 +210,10 @@
 
 def own_kernel(chunk, *refs):
     m_ref, t_ref = refs[:2]
-    sources = refs[2:8]
-    l_ref, turned_ref, gate_ref, w_ref, v_ref, gain_ref = refs[8:14]
-    targets = refs[14:20]
-    p_ref, held, sems = refs[20], refs[21:25], refs[25]
+    sources = refs[2:11]
+    picks_ref, l_ref, turned_ref, gate_ref, w_ref, v_ref, gain_ref = refs[11:18]
+    targets = refs[18:27]
+    p_ref, held, sems = refs[27], refs[28:32], refs[32]
     copies = [
         pltpu.make_async_copy(source, target, sems.at[at])
         for at, (source, target) in enumerate(zip(sources, targets))
@@ -231,7 +228,11 @@
 
     for copy in copies:
         copy.wait()
-    a_ref, b_ref, o_ref, u_ref, g_ref, h_ref = targets
+    a_ref, b_ref, o_ref, u_ref, g_ref, h_ref, *tables = targets
+    slots = m_ref.shape[0]
+    for s in range(slots):
+        for at, pick in enumerate(used_picks(s, slots, tables[0].shape[0], *tables)):
+            picks_ref[4 * s + at] = pick
     rows = gated_rows(a_ref) + gated_rows(b_ref) + [0.5 * o_ref[...].astype(F32)]
     weight = prepared(jnp.concatenate(rows, axis=0))
     w_ref[...] = weight[: 4 * half]
@@ -264,13 +265,14 @@
 
 
 def fetched_sides(chunk, ours, theirs, weight, gain_ref, half):
-    wide = theirs[0].shape[1]
-
     def sides_at(n, start):
         at = n * chunk + start
         both = []
         for x, m in enumerate(ours):
-            other = theirs[2 * (at // wide) + x][:, at % wide : at % wide + LANES]
+            if len(theirs) == 1:
+                other = theirs[0][x, :, at : at + LANES]
+            else:
+                other = theirs[2 * n + x][:, start : start + LANES]
             both.append(
                 gated_sides(m[:, at : at + LANES], other, weight, gain_ref[...], half)[0]
             )
@@ -361,7 +363,7 @@
     return pl.pallas_call(
         kernel,
         in_specs=[pl.BlockSpec(memory_space=space) for space in spaces],
-        out_specs=[pl.BlockSpec(memory_space=pltpu.VMEM)] * len(out_shape),
+        out_specs=[pl.BlockSpec(memory_space=value.memory_space) for value in out_shape],
         out_shape=out_shape,
         scratch_shapes=scratch,
         input_output_aliases={plain + at: at for at in range(aliased)},
@@ -453,7 +455,7 @@
 
     chunk = cells // 4
     cuts = ((0, 2 * chunk), (2 * chunk, 2 * chunk))
-    picks, pair, *chosen = select_blocks(pair, a_slots, b_slots, counts, cuts)
+    pair, *chosen = select_blocks(pair, a_slots, b_slots, counts, cuts)
     arrived = [
         (lax.ppermute(chosen[2 * n], "row", up), lax.ppermute(chosen[2 * n + 1], "row", down))
         for n in range(len(cuts))
@@ -461,11 +463,13 @@
     pair_other = lax.ppermute(pair, "chan", swap)
     left_shape = pltpu.VMEM((2, half, BLK, LANES), BF16)
     right_shape = pltpu.VMEM((5, half, BLK, BLK), BF16)
-    lefts, rights, gate, weight, last_weight, gain = call(
+    sources = [*weights, a_slots, b_slots, counts]
+    picks, lefts, rights, gate, weight, last_weight, gain = call(
         functools.partial(own_kernel, chunk),
         "project_own",
-        [pair, pair_other, *weights],
+        [pair, pair_other, *sources],
         [
+            pltpu.SMEM((4 * slots,), jnp.int32),
             left_shape,
             right_shape,
             pltpu.VMEM((slots, half, cells), BF16),
@@ -474,19 +478,22 @@
             pltpu.VMEM((2 * half, LANES), F32),
         ],
         [pltpu.VMEM(value.shape, value.dtype) for value in weights]
+        + [pltpu.SMEM(value.shape, value.dtype) for value in (a_slots, b_slots, counts)]
         + [pltpu.VMEM((half, BLK, LANES), BF16)]
         + chunk_scratch(half, chunk)
-        + [pltpu.SemaphoreType.DMA((len(weights),))],
-        hbm=len(weights),
+        + [pltpu.SemaphoreType.DMA((len(sources),))],
+        hbm=len(sources),
     )
     for (start, size), behind_ahead in zip(cuts, arrived):
         *behind_ahead, lefts = lax.optimization_barrier((*behind_ahead, lefts))
-        wide = chunk if start == 0 else size
-        others = [
-            lax.ppermute(lax.slice_in_dim(value, at, at + wide, axis=1), "chan", swap)
-            for at in range(0, size, wide)
-            for value in behind_ahead
-        ]
+        if start == 0:
+            others = [
+                lax.ppermute(lax.slice_in_dim(value, at, at + chunk, axis=1), "chan", swap)
+                for at in (0, chunk)
+                for value in behind_ahead
+            ]
+        else:
+            others = [lax.ppermute(jnp.stack(behind_ahead), "chan", swap)]
         paired = pltpu.VMEM((half, size // BLK, LANES), BF16)
         if start == 0:
             lefts, rights_first = call(

time: 39.6 us -> 39.8 us (level)
  starting transfers between devices: 11.1 us -> 10.7 us
  waiting for transfers between devices: 13.6 us -> 14 us
    ppermute x6 -> x5, waiting for transfers between devices: 3.27 us -> 3.77 us  [the longest x1 1.9 us: per_device(): others = [lax.ppermute(jnp.stack(behind_ahead), 'chan', swap)]]
    ppermute x6 -> x5, starting transfers between devices: 1.37 us -> 0.93 us  [the longest x4 0.86 us: per_device(): lax.ppermute(lax.slice_in_dim(value, at, at + chunk, axis=1), 'chan', swap)]
  transfers between devices with their start and end apart: 13 -> 12, of which waited for: 10 -> 9; matrix products, arithmetic and copies ran while one was open for 0% -> 0% of each run, Pallas kernels for 22% -> 22%
where the time goes in v15:
time: 39.8 us; the launch traced here: 39.6 us
  Pallas kernels  14.7 us (37%)
  waiting for transfers between devices  14 us (35%)
  starting transfers between devices  10.7 us (27%)
    pallas_call x4, Pallas kernels, call(): pl.pallas_call(kernel, in_specs=[pl.BlockSpec(memory_space=space) for spa...  10.7 us
    ppermute x2, waiting for transfers between devices, per_device(): lax.ppermute(chosen[2 * n + 1], 'row', down)  8.54 us
    ppermute x2, starting transfers between devices, per_device(): lax.ppermute(chosen[2 * n + 1], 'row', down)  5.93 us
    pallas_call x2, Pallas kernels, finish(): pl.pallas_call(functools.partial(finish_kernel, s, mine.shape[1] // 2, 4)...  2.65 us
    ppermute x2, starting transfers between devices, per_device(): lax.ppermute(chosen[2 * n], 'row', up)  2.64 us
    ppermute x1, waiting for transfers between devices, per_device(): others = [lax.ppermute(jnp.stack(behind_ahead), 'chan', swap)]  1.9 us
    ppermute x4, waiting for transfers between devices, per_device(): lax.ppermute(lax.slice_in_dim(value, at, at + chunk, axis=1), 'chan', swap)  1.87 us
    pallas_call x1, Pallas kernels, select_blocks(): pl.pallas_call(functools.partial(select_kernel, slots, a_slots.shape[0],...  1.33 us
  transfers between devices with their start and end apart: 12, of which 9 were waited for; matrix products, arithmetic and copies ran while one was open for 0% of the time, Pallas kernels for 22%

profile of v15, /device:TPU:0, one launch (start us, length us, event | category | flops | bytes accessed | tf_op | source)
XLA Modules:
  0.0 39.6 jit_solution(16200127005771808877)
XLA Ops:
  0.0 1.3 %select_blocks.1 = (bf16[2,64,4096]{2,1,0:T(8,128)(2,1)S(1)}, bf16[64,2048]{1,0:T(8,128)(2,1)S(1)}, bf16[64,2048]{1,0:T(8,128)(2,1)S(1)}, bf16[64,2048]{1,0:T(8,128)(2,1)S(1)}, bf16[64,2048]{1,0:T(8,128)(2,1)S(1)}) custom-call(s32[4,16]{1,0:T(4,128)} %bitcast.16, s32[4,16]{1,0:T(4,128)} %bitcast.18, s32[16]{0:T(128)} %refs_10_.1, bf16[2,64,4096]{2,1,0:T(8,128)(2,1)} %pair_hbm.1), custom_call_target="tpu_custom_call" | custom-call | tf_op jit(solution)/shard_map/select_blocks/pallas_call | solution.py:100
  1.3 0.5 %collective-permute-start = (bf16[2,64,4096]{2,1,0:T(8,128)(2,1)S(1)}, bf16[2,64,4096]{2,1,0:T(8,128)(2,1)S(1)}, u32[]{:S(2)}, u32[]{:S(2)}) collective-permute-start(bf16[2,64,4096]{2,1,0:T(8,128)(2,1)S(1)} %get-tuple-element.29.refs_0_), channel_id=1, source_target_pairs={{0,1},{1,0},{2,3},{3,2},{4,5},{5,4},{6,7},{7,6},{8,9},{9,8},{10,11... | collective-permute-start | bytes 3145736 | tf_op jit(solution)/shard_map/ppermute | solution.py:463
  1.9 2.6 %collective-permute-start.3 = (bf16[64,2048]{1,0:T(8,128)(2,1)S(1)}, bf16[64,2048]{1,0:T(8,128)(2,1)S(1)}, u32[]{:S(2)}, u32[]{:S(2)}) collective-permute-start(bf16[64,2048]{1,0:T(8,128)(2,1)S(1)} %get-tuple-element.33), channel_id=1, source_target_pairs={{0,4},{4,8},{8,12},{12,0},{1,5},{5,9},{9,13},{13,1},{2,6},{6,10},{... | collective-permute-start | bytes 786440 | tf_op jit(solution)/shard_map/ppermute | solution.py:460
  4.5 2.1 %collective-permute-start.4 = (bf16[64,2048]{1,0:T(8,128)(2,1)S(1)}, bf16[64,2048]{1,0:T(8,128)(2,1)S(1)}, u32[]{:S(2)}, u32[]{:S(2)}) collective-permute-start(bf16[64,2048]{1,0:T(8,128)(2,1)S(1)} %get-tuple-element.34), channel_id=1, source_target_pairs={{0,12},{4,0},{8,4},{12,8},{1,13},{5,1},{9,5},{13,9},{2,14},{6,2},{... | collective-permute-start | bytes 786440 | tf_op jit(solution)/shard_map/ppermute | solution.py:460
  6.6 0.0 collective-permute-start.1
  6.6 3.8 %collective-permute-start.2 = (bf16[64,2048]{1,0:T(8,128)(2,1)S(1)}, bf16[64,2048]{1,0:T(8,128)(2,1)S(1)}, u32[]{:S(2)}, u32[]{:S(2)}) collective-permute-start(bf16[64,2048]{1,0:T(8,128)(2,1)S(1)} %get-tuple-element.32), channel_id=1, source_target_pairs={{0,12},{4,0},{8,4},{12,8},{1,13},{5,1},{9,5},{13,9},{2,14},{6,2},{... | collective-permute-start | bytes 786440 | tf_op jit(solution)/shard_map/ppermute | solution.py:460
  10.4 0.0 collective-permute-done.refs_1_
  10.4 5.1 %project_own.1 = (s32[8]{0:T(128)S(4)}, bf16[2,64,64,128]{3,2,1,0:T(8,128)(2,1)S(1)}, bf16[5,64,64,64]{3,2,1,0:T(8,128)(2,1)S(1)}, bf16[2,64,4096]{2,1,0:T(8,128...) custom-call(bf16[2,64,4096]{2,1,0:T(8,128)(2,1)S(1)} %get-tuple-element.29.refs_0_, ...), custom_call_target="tpu_custom_call" | custom-call | tf_op jit(solution)/shard_map/project_own/pallas_call | solution.py:363
  15.5 0.0 collective-permute-done.3.refs_0_
  15.6 3.8 %collective-permute-done.4.refs_1_ = bf16[64,2048]{1,0:T(8,128)(2,1)S(1)} collective-permute-done((bf16[64,2048]{1,0:T(8,128)(2,1)S(1)}, bf16[64,2048]{1,0:T(8,128)(2,1)S(1)}, u32[]{:S(2)}, u32[]{:S(2)}) %collective-permute-start.4) | collective-permute-done | bytes 262176 | tf_op jit(solution)/shard_map/ppermute | solution.py:460
  19.4 0.1 collective-permute-start.7
  19.5 0.5 %collective-permute-start.5 = (bf16[64,1024]{1,0:T(8,128)(2,1)S(1)}, bf16[64,1024]{1,0:T(8,128)(2,1)S(1)}, u32[]{:S(2)}, u32[]{:S(2)}) collective-permute-start(bf16[64,1024]{1,0:T(8,128)(2,1)S(1)} %get-tuple-element.56), channel_id=1, source_target_pairs={{0,1},{1,0},{2,3},{3,2},{4,5},{5,4},{6,7},{7,6},{8,9},{9,8},{10,11... | collective-permute-start | bytes 393224 | tf_op jit(solution)/shard_map/ppermute | solution.py:491
  20.0 0.1 collective-permute-start.8
  20.1 0.7 %collective-permute-done.7.refs_4_ = bf16[64,1024]{1,0:T(8,128)(2,1)S(1)} collective-permute-done((bf16[64,1024]{1,0:T(8,128)(2,1)S(1)}, bf16[64,1024]{1,0:T(8,128)(2,1)S(1)}, u32[]{:S(2)}, u32[]{:S(2)}) %collective-permute-start.7) | collective-permute-done | bytes 131104 | tf_op jit(solution)/shard_map/ppermute | solution.py:491
  20.8 0.1 collective-permute-start.6
  21.0 0.0 collective-permute-done.5.refs_2_
  21.0 0.4 %collective-permute-done.8.refs_5_ = bf16[64,1024]{1,0:T(8,128)(2,1)S(1)} collective-permute-done((bf16[64,1024]{1,0:T(8,128)(2,1)S(1)}, bf16[64,1024]{1,0:T(8,128)(2,1)S(1)}, u32[]{:S(2)}, u32[]{:S(2)}) %collective-permute-start.8) | collective-permute-done | bytes 131104 | tf_op jit(solution)/shard_map/ppermute | solution.py:491
  21.4 0.8 %collective-permute-done.6.refs_3_ = bf16[64,1024]{1,0:T(8,128)(2,1)S(1)} collective-permute-done((bf16[64,1024]{1,0:T(8,128)(2,1)S(1)}, bf16[64,1024]{1,0:T(8,128)(2,1)S(1)}, u32[]{:S(2)}, u32[]{:S(2)}) %collective-permute-start.6) | collective-permute-done | bytes 131104 | tf_op jit(solution)/shard_map/ppermute | solution.py:491
  22.2 1.7 %project_first.1 = (bf16[2,64,64,128]{3,2,1,0:T(8,128)(2,1)S(1)}, bf16[64,32,128]{2,1,0:T(8,128)(2,1)S(1)}) custom-call(bf16[64,2048]{1,0:T(8,128)(2,1)S(1)} %collective-permute-done.3.refs_0_, bf16[64,2048]{1,0:T(8,128)(2,1)S(1)} %collective-permute-done.4.refs_1_, ...), custom_call_target="tpu_custom_call", output_to_operand_aliasing={{0}: (8, {})} | custom-call | tf_op jit(solution)/shard_map/project_first/pallas_call | solution.py:363
  23.8 1.2 %collective-permute-done.1.refs_0_ = bf16[64,2048]{1,0:T(8,128)(2,1)S(1)} collective-permute-done((bf16[64,2048]{1,0:T(8,128)(2,1)S(1)}, bf16[64,2048]{1,0:T(8,128)(2,1)S(1)}, u32[]{:S(2)}, u32[]{:S(2)}) %collective-permute-start.1) | collective-permute-done | bytes 262176 | tf_op jit(solution)/shard_map/ppermute | solution.py:460
  25.0 4.7 %collective-permute-done.2.refs_1_ = bf16[64,2048]{1,0:T(8,128)(2,1)S(1)} collective-permute-done((bf16[64,2048]{1,0:T(8,128)(2,1)S(1)}, bf16[64,2048]{1,0:T(8,128)(2,1)S(1)}, u32[]{:S(2)}, u32[]{:S(2)}) %collective-permute-start.2) | collective-permute-done | bytes 262176 | tf_op jit(solution)/shard_map/ppermute | solution.py:460
  29.7 0.1 pad_maximum_fusion
  29.8 0.1 collective-permute-start.9
  29.9 1.9 %collective-permute-done.9.refs_2_ = bf16[2,64,2048]{2,1,0:T(8,128)(2,1)S(1)} collective-permute-done((bf16[2,64,2048]{2,1,0:T(8,128)(2,1)S(1)}, bf16[2,64,2048]{2,1,0:T(8,128)(2,1)S(1)}, u32[]{:S(2)}, u32[]{:S(2)}) %collective-permute-start.9) | collective-permute-done | bytes 524320 | tf_op jit(solution)/shard_map/ppermute | solution.py:496
  31.8 2.9 %project_last.1 = (bf16[2,64,64,128]{3,2,1,0:T(8,128)(2,1)S(1)}, bf16[5,64,64,64]{3,2,1,0:T(8,128)(2,1)S(1)}, bf16[64,4096]{1,0:T(8,128)(2,1)S(1)}) custom-call(s32[8]{0:T(128)S(4)} %get-tuple-element.30.picks_ref, bf16[64,2048]{1,0:T(8,128)(2,1)S(1)} %collective-permute-done.1.refs_0_, ...), custom_call_target="tpu_custom_call", output_to_operand_aliasing={{0}: (7, {}), {1}: (8, {})} | custom-call | tf_op jit(solution)/shard_map/project_last/pallas_call | solution.py:363
  34.7 0.2 collective-permute-start.11
  34.9 1.0 %triplets.1.mine_ref = bf16[64,4096]{1,0:T(8,128)(2,1)S(1)} custom-call(s32[8]{0:T(128)S(4)} %get-tuple-element.30.picks_ref, bf16[2,64,64,128]{3,2,1,0:T(8,128)(2,1)S(1)} %get-tuple-element.49.l_ref, bf16[5,64,64,64]{3,2,1,0:T(8,128)(2,1)S(1)} %get-tuple-element.50.turned_ref), custom_call_target="tpu_custom_call" | custom-call | tf_op jit(solution)/shard_map/triplets/pallas_call | solution.py:363
  35.9 0.4 %collective-permute-start.10 = (bf16[64,4096]{1,0:T(8,128)(2,1)S(1)}, bf16[64,4096]{1,0:T(8,128)(2,1)S(1)}, u32[]{:S(2)}, u32[]{:S(2)}) collective-permute-start(bf16[64,4096]{1,0:T(8,128)(2,1)S(1)} %triplets.1.mine_ref), channel_id=1, source_target_pairs={{0,1},{1,0},{2,3},{3,2},{4,5},{5,4},{6,7},{7,6},{8,9},{9,8},{10,11... | collective-permute-start | bytes 1572872 | tf_op jit(solution)/shard_map/ppermute | solution.py:530
  36.4 0.3 collective-permute-done.11.theirs_ref
  36.6 1.0 %finish.2.refs_0_ = bf16[64,4096]{1,0:T(8,128)(2,1)S(1)} custom-call(bf16[64,4096]{1,0:T(8,128)(2,1)S(1)} %get-tuple-element.47.mine_ref, bf16[64,4096]{1,0:T(8,128)(2,1)S(1)} %collective-permute-done.11.theirs_ref, bf16[2,64,4096]{2,1,0:T(8,128)(2,1)S(1)} %get-tuple-element.51.gate_ref, bf16[64,128]{1,0:T(8,128)(2,1)S(1)} %get-tuple-element.52.w_ref), custom_call_target="tpu_custom_call" | custom-call | tf_op jit(solution)/shard_map/finish/pallas_call | solution.py:417
  37.6 0.3 collective-permute-done.10.theirs_ref
  37.9 1.7 %finish.3 = bf16[2,64,4096]{2,1,0:T(8,128)(2,1)} custom-call(bf16[64,4096]{1,0:T(8,128)(2,1)S(1)} %triplets.1.mine_ref, bf16[64,4096]{1,0:T(8,128)(2,1)S(1)} %collective-permute-done.10.theirs_ref, bf16[2,64,4096]{2,1,0:T(8,128)(2,1)S(1)} %get-tuple-element.51.gate_ref, bf16[64,128]{1,0:T(8,128)(2,1)S(1)} %get-tuple-element.52.w_ref, ...), custom_call_target="tpu_custom_call" | custom-call | tf_op jit(solution)/shard_map/finish/pallas_call | solution.py:417
  (2 shorter events, 0.0 us)
Async XLA Ops:
  1.3 9.1 %collective-permute-start = (bf16[2,64,4096]{2,1,0:T(8,128)(2,1)S(1)}, bf16[2,64,4096]{2,1,0:T(8,128)(2,1)S(1)}, u32[]{:S(2)}, u32[]{:S(2)}) collective-permute-start(bf16[2,64,4096]{2,1,0:T(8,128)(2,1)S(1)} %get-tuple-element.29.refs_0_), channel_id=1, source_target_pairs={{0,1},{1,0},{2,3},{3,2},{4,5},{5,4},{6,7},{7,6},{8,9},{9,8},{10,11... | collective-permute-start | bytes 3145736 | tf_op jit(solution)/shard_map/ppermute | solution.py:463
  1.9 13.7 %collective-permute-start.3 = (bf16[64,2048]{1,0:T(8,128)(2,1)S(1)}, bf16[64,2048]{1,0:T(8,128)(2,1)S(1)}, u32[]{:S(2)}, u32[]{:S(2)}) collective-permute-start(bf16[64,2048]{1,0:T(8,128)(2,1)S(1)} %get-tuple-element.33), channel_id=1, source_target_pairs={{0,4},{4,8},{8,12},{12,0},{1,5},{5,9},{9,13},{13,1},{2,6},{6,10},{... | collective-permute-start | bytes 786440 | tf_op jit(solution)/shard_map/ppermute | solution.py:460
  4.5 14.9 %collective-permute-start.4 = (bf16[64,2048]{1,0:T(8,128)(2,1)S(1)}, bf16[64,2048]{1,0:T(8,128)(2,1)S(1)}, u32[]{:S(2)}, u32[]{:S(2)}) collective-permute-start(bf16[64,2048]{1,0:T(8,128)(2,1)S(1)} %get-tuple-element.34), channel_id=1, source_target_pairs={{0,12},{4,0},{8,4},{12,8},{1,13},{5,1},{9,5},{13,9},{2,14},{6,2},{... | collective-permute-start | bytes 786440 | tf_op jit(solution)/shard_map/ppermute | solution.py:460
  6.6 18.4 %collective-permute-start.1 = (bf16[64,2048]{1,0:T(8,128)(2,1)S(1)}, bf16[64,2048]{1,0:T(8,128)(2,1)S(1)}, u32[]{:S(2)}, u32[]{:S(2)}) collective-permute-start(bf16[64,2048]{1,0:T(8,128)(2,1)S(1)} %get-tuple-element.31), channel_id=1, source_target_pairs={{0,4},{4,8},{8,12},{12,0},{1,5},{5,9},{9,13},{13,1},{2,6},{6,10},{... | collective-permute-start | bytes 786440 | tf_op jit(solution)/shard_map/ppermute | solution.py:460
  6.6 23.1 %collective-permute-start.2 = (bf16[64,2048]{1,0:T(8,128)(2,1)S(1)}, bf16[64,2048]{1,0:T(8,128)(2,1)S(1)}, u32[]{:S(2)}, u32[]{:S(2)}) collective-permute-start(bf16[64,2048]{1,0:T(8,128)(2,1)S(1)} %get-tuple-element.32), channel_id=1, source_target_pairs={{0,12},{4,0},{8,4},{12,8},{1,13},{5,1},{9,5},{13,9},{2,14},{6,2},{... | collective-permute-start | bytes 786440 | tf_op jit(solution)/shard_map/ppermute | solution.py:460
  19.4 1.4 %collective-permute-start.7 = (bf16[64,1024]{1,0:T(8,128)(2,1)S(1)}, bf16[64,1024]{1,0:T(8,128)(2,1)S(1)}, u32[]{:S(2)}, u32[]{:S(2)}) collective-permute-start(bf16[64,1024]{1,0:T(8,128)(2,1)S(1)} %get-tuple-element.55), channel_id=1, source_target_pairs={{0,1},{1,0},{2,3},{3,2},{4,5},{5,4},{6,7},{7,6},{8,9},{9,8},{10,11... | collective-permute-start | bytes 393224 | tf_op jit(solution)/shard_map/ppermute | solution.py:491
  19.5 1.5 %collective-permute-start.5 = (bf16[64,1024]{1,0:T(8,128)(2,1)S(1)}, bf16[64,1024]{1,0:T(8,128)(2,1)S(1)}, u32[]{:S(2)}, u32[]{:S(2)}) collective-permute-start(bf16[64,1024]{1,0:T(8,128)(2,1)S(1)} %get-tuple-element.56), channel_id=1, source_target_pairs={{0,1},{1,0},{2,3},{3,2},{4,5},{5,4},{6,7},{7,6},{8,9},{9,8},{10,11... | collective-permute-start | bytes 393224 | tf_op jit(solution)/shard_map/ppermute | solution.py:491
  20.0 1.4 %collective-permute-start.8 = (bf16[64,1024]{1,0:T(8,128)(2,1)S(1)}, bf16[64,1024]{1,0:T(8,128)(2,1)S(1)}, u32[]{:S(2)}, u32[]{:S(2)}) collective-permute-start(bf16[64,1024]{1,0:T(8,128)(2,1)S(1)} %get-tuple-element.53), channel_id=1, source_target_pairs={{0,1},{1,0},{2,3},{3,2},{4,5},{5,4},{6,7},{7,6},{8,9},{9,8},{10,11... | collective-permute-start | bytes 393224 | tf_op jit(solution)/shard_map/ppermute | solution.py:491
  20.8 1.3 %collective-permute-start.6 = (bf16[64,1024]{1,0:T(8,128)(2,1)S(1)}, bf16[64,1024]{1,0:T(8,128)(2,1)S(1)}, u32[]{:S(2)}, u32[]{:S(2)}) collective-permute-start(bf16[64,1024]{1,0:T(8,128)(2,1)S(1)} %get-tuple-element.54), channel_id=1, source_target_pairs={{0,1},{1,0},{2,3},{3,2},{4,5},{5,4},{6,7},{7,6},{8,9},{9,8},{10,11... | collective-permute-start | bytes 393224 | tf_op jit(solution)/shard_map/ppermute | solution.py:491
  29.8 2.0 %collective-permute-start.9 = (bf16[2,64,2048]{2,1,0:T(8,128)(2,1)S(1)}, bf16[2,64,2048]{2,1,0:T(8,128)(2,1)S(1)}, u32[]{:S(2)}, u32[]{:S(2)}) collective-permute-start(bf16[2,64,2048]{2,1,0:T(8,128)(2,1)S(1)} %pad_maximum_fusion), channel_id=1, source_target_pairs={{0,1},{1,0},{2,3},{3,2},{4,5},{5,4},{6,7},{7,6},{8,9},{9,8},{10,11... | collective-permute-start | bytes 1572872 | tf_op jit(solution)/shard_map/ppermute | solution.py:496
  34.7 2.0 %collective-permute-start.11 = (bf16[64,4096]{1,0:T(8,128)(2,1)S(1)}, bf16[64,4096]{1,0:T(8,128)(2,1)S(1)}, u32[]{:S(2)}, u32[]{:S(2)}) collective-permute-start(bf16[64,4096]{1,0:T(8,128)(2,1)S(1)} %get-tuple-element.47.mine_ref), channel_id=1, source_target_pairs={{0,1},{1,0},{2,3},{3,2},{4,5},{5,4},{6,7},{7,6},{8,9},{9,8},{10,11... | collective-permute-start | bytes 1572872 | tf_op jit(solution)/shard_map/ppermute | solution.py:519
  35.9 2.0 %collective-permute-start.10 = (bf16[64,4096]{1,0:T(8,128)(2,1)S(1)}, bf16[64,4096]{1,0:T(8,128)(2,1)S(1)}, u32[]{:S(2)}, u32[]{:S(2)}) collective-permute-start(bf16[64,4096]{1,0:T(8,128)(2,1)S(1)} %triplets.1.mine_ref), channel_id=1, source_target_pairs={{0,1},{1,0},{2,3},{3,2},{4,5},{5,4},{6,7},{7,6},{8,9},{9,8},{10,11... | collective-permute-start | bytes 1572872 | tf_op jit(solution)/shard_map/ppermute | solution.py:530

commit v16 on v13

--- a/solution.py
+++ b/solution.py
@@ -370,54 +370,67 @@
     )(*operands)
 
 
-def finish_kernel(s, run, pieces, mine_ref, theirs_ref, gate_ref, w_ref, *refs):
+def finish_kernel(s, pieces, mine_ref, theirs_ref, gate_ref, w_ref, *refs):
     weight = w_ref[...]
     cells = mine_ref.shape[-1]
+    size = cells // pieces
     if s == 0:
-        held = refs[0]
+        out_ref, rest_ref, held, sems = refs
+        written = pieces // 2
     else:
-        before_ref, out_ref, held, sems = refs
-        before = pltpu.make_async_copy(before_ref, out_ref.at[0], sems.at[pieces])
+        before_ref, _, out_ref, held, sems = refs
+        written = pieces
+        late = pl.ds(cells // 2, cells // 2)
+        before = pltpu.make_async_copy(before_ref, out_ref.at[0, :, late], sems.at[pieces])
         before.start()
-    size = cells // pieces
-
-    def copy(n):
-        to = pl.ds(pl.multiple_of(n * size, size), size)
-        return pltpu.make_async_copy(held.at[:, to], out_ref.at[1, :, to], sems.at[n])
-
-    @pl.loop(0, cells // run)
-    def _(n):
-        for start in range(0, run, LANES):
-            to = cells_at(n, run, start)
+    copies = []
+    for n in range(pieces):
+        for start in range(n * size, (n + 1) * size, LANES):
+            to = slice(start, start + LANES)
             normed = normed_of(mine_ref[:, to], theirs_ref[:, to])
             projected = jnp.dot(weight, normed, preferred_element_type=F32)
-            held[:, to] = (gate_ref[s, :, to].astype(F32) * projected).astype(BF16)
-            done = start + LANES
-            if s > 0 and done % size == 0:
-                copy(n * (run // size) + done // size - 1).start()
-
+            value = (gate_ref[s, :, to].astype(F32) * projected).astype(BF16)
+            if n < written:
+                held[:, to] = value
+            else:
+                rest_ref[:, start - written * size : start - written * size + LANES] = value
+        if n < written:
+            to = pl.ds(n * size, size)
+            copies.append(
+                pltpu.make_async_copy(held.at[:, to], out_ref.at[s, :, to], sems.at[n])
+            )
+            copies[-1].start()
+    for copy in copies:
+        copy.wait()
     if s > 0:
-        for n in range(pieces):
-            copy(n).wait()
         before.wait()
 
 
-def finish(s, mine, theirs, gate, weight, before=None):
+def finish(s, mine, theirs, gate, weight, before=()):
     vmem = pl.BlockSpec(memory_space=pltpu.VMEM)
-    operands = [mine, theirs, gate, weight]
+    hbm = pl.BlockSpec(memory_space=pltpu.HBM)
+    half, cells = mine.shape
+    pieces = 4
+    operands = [mine, theirs, gate, weight, *before]
+    in_specs = [vmem] * len(operands)
+    out_shape = [jax.ShapeDtypeStruct(gate.shape, BF16)]
+    out_specs = [hbm]
+    aliases = {}
     if s == 0:
-        out_shape, out_specs, scratch = pltpu.VMEM(mine.shape, BF16), vmem, []
+        out_shape.append(pltpu.VMEM((half, cells // 2), BF16))
+        out_specs.append(vmem)
+        wide = cells // 2
     else:
-        operands.append(before)
-        out_shape = jax.ShapeDtypeStruct(gate.shape, BF16)
-        out_specs = pl.BlockSpec(memory_space=pltpu.HBM)
-        scratch = [pltpu.VMEM(mine.shape, BF16), pltpu.SemaphoreType.DMA((5,))]
+        aliases = {len(operands) - 1: 0}
+        in_specs[-1] = hbm
+        wide = cells
     return pl.pallas_call(
-        functools.partial(finish_kernel, s, mine.shape[1] // 2, 4),
-        in_specs=[vmem] * len(operands),
+        functools.partial(finish_kernel, s, pieces),
+        in_specs=in_specs,
         out_specs=out_specs,
         out_shape=out_shape,
-        scratch_shapes=scratch,
+        scratch_shapes=[pltpu.VMEM((half, wide), BF16), pltpu.SemaphoreType.DMA((pieces + 1,))],
+        input_output_aliases=aliases,
         compiler_params=pltpu.CompilerParams(vmem_limit_bytes=VMEM_LIMIT),
         name="finish",
     )(*operands)
@@ -521,9 +534,8 @@
             smem=1,
         )
         updates.append((update, lax.ppermute(update, "chan", swap)))
-    out = None
-    for s, (mine, theirs) in enumerate(updates):
-        out = finish(s, mine, theirs, gate, last_weight, out)
+    out, rest = finish(0, *updates[0], gate, last_weight)
+    (out,) = finish(1, *updates[1], gate, last_weight, (rest, out))
     return out
 
 

time: 39.6 us -> 39.6 us (level)
  transfers between devices with their start and end apart: 13 -> 13, of which waited for: 10 -> 9; matrix products, arithmetic and copies ran while one was open for 0% -> 0% of each run, Pallas kernels for 22% -> 23%
where the time goes in v16:
time: 39.6 us; the launch traced here: 39.4 us
  Pallas kernels  14.8 us (37%)
  waiting for transfers between devices  13.4 us (34%)
  starting transfers between devices  11.1 us (28%)
    pallas_call x4, Pallas kernels, call(): pl.pallas_call(kernel, in_specs=[pl.BlockSpec(memory_space=space) for spa...  10.6 us
    ppermute x2, waiting for transfers between devices, per_device(): lax.ppermute(chosen[2 * n + 1], 'row', down)  8.63 us
    ppermute x2, starting transfers between devices, per_device(): lax.ppermute(chosen[2 * n + 1], 'row', down)  5.93 us
    ppermute x6, waiting for transfers between devices, per_device(): lax.ppermute(lax.slice_in_dim(value, at, at + wide, axis=1), 'chan', swap)  3.27 us
    pallas_call x2, Pallas kernels, finish(): pl.pallas_call(functools.partial(finish_kernel, s, pieces), in_specs=in_s...  2.85 us
    ppermute x2, starting transfers between devices, per_device(): lax.ppermute(chosen[2 * n], 'row', up)  2.64 us
    ppermute x6, starting transfers between devices, per_device(): lax.ppermute(lax.slice_in_dim(value, at, at + wide, axis=1), 'chan', swap)  1.37 us
    pallas_call x1, Pallas kernels, select_blocks(): pl.pallas_call(functools.partial(select_kernel, slots, a_slots.shape[0],...  1.33 us
  transfers between devices with their start and end apart: 13, of which 9 were waited for; matrix products, arithmetic and copies ran while one was open for 0% of the time, Pallas kernels for 23%

profile of v16, /device:TPU:0, one launch (start us, length us, event | category | flops | bytes accessed | tf_op | source)
XLA Modules:
  0.0 39.4 jit_solution(13173017585904138958)
XLA Ops:
  0.0 1.3 %select_blocks.1 = (s32[8]{0:T(128)S(4)}, bf16[2,64,4096]{2,1,0:T(8,128)(2,1)S(1)}, bf16[64,2048]{1,0:T(8,128)(2,1)S(1)}, bf16[64,2048]{1,0:T(8,128)(2,1)S(1)}, ...) custom-call(s32[4,16]{1,0:T(4,128)} %bitcast.12, s32[4,16]{1,0:T(4,128)} %bitcast.13, s32[16]{0:T(128)} %n_hbm.1, ...), custom_call_target="tpu_custom_call" | custom-call | tf_op jit(solution)/shard_map/select_blocks/pallas_call | solution.py:103
  1.3 0.5 %collective-permute-start.4 = (bf16[2,64,4096]{2,1,0:T(8,128)(2,1)S(1)}, bf16[2,64,4096]{2,1,0:T(8,128)(2,1)S(1)}, u32[]{:S(2)}, u32[]{:S(2)}) collective-permute-start(bf16[2,64,4096]{2,1,0:T(8,128)(2,1)S(1)} %get-tuple-element.36.refs_0_), channel_id=1, source_target_pairs={{0,1},{1,0},{2,3},{3,2},{4,5},{5,4},{6,7},{7,6},{8,9},{9,8},{10,11... | collective-permute-start | bytes 3145736 | tf_op jit(solution)/shard_map/ppermute | solution.py:474
  1.9 2.6 %collective-permute-start.2 = (bf16[64,2048]{1,0:T(8,128)(2,1)S(1)}, bf16[64,2048]{1,0:T(8,128)(2,1)S(1)}, u32[]{:S(2)}, u32[]{:S(2)}) collective-permute-start(bf16[64,2048]{1,0:T(8,128)(2,1)S(1)} %get-tuple-element.34), channel_id=1, source_target_pairs={{0,4},{4,8},{8,12},{12,0},{1,5},{5,9},{9,13},{13,1},{2,6},{6,10},{... | collective-permute-start | bytes 786440 | tf_op jit(solution)/shard_map/ppermute | solution.py:471
  4.5 2.1 %collective-permute-start.3 = (bf16[64,2048]{1,0:T(8,128)(2,1)S(1)}, bf16[64,2048]{1,0:T(8,128)(2,1)S(1)}, u32[]{:S(2)}, u32[]{:S(2)}) collective-permute-start(bf16[64,2048]{1,0:T(8,128)(2,1)S(1)} %get-tuple-element.35), channel_id=1, source_target_pairs={{0,12},{4,0},{8,4},{12,8},{1,13},{5,1},{9,5},{13,9},{2,14},{6,2},{... | collective-permute-start | bytes 786440 | tf_op jit(solution)/shard_map/ppermute | solution.py:471
  6.6 0.0 collective-permute-start
  6.6 3.8 %collective-permute-start.1 = (bf16[64,2048]{1,0:T(8,128)(2,1)S(1)}, bf16[64,2048]{1,0:T(8,128)(2,1)S(1)}, u32[]{:S(2)}, u32[]{:S(2)}) collective-permute-start(bf16[64,2048]{1,0:T(8,128)(2,1)S(1)} %get-tuple-element.33), channel_id=1, source_target_pairs={{0,12},{4,0},{8,4},{12,8},{1,13},{5,1},{9,5},{13,9},{2,14},{6,2},{... | collective-permute-start | bytes 786440 | tf_op jit(solution)/shard_map/ppermute | solution.py:471
  10.4 0.0 collective-permute-done.4.refs_1_
  10.4 5.0 %project_own.1 = (bf16[2,64,64,128]{3,2,1,0:T(8,128)(2,1)S(1)}, bf16[5,64,64,64]{3,2,1,0:T(8,128)(2,1)S(1)}, bf16[2,64,4096]{2,1,0:T(8,128)(2,1)S(1)}, bf16[256,...) custom-call(bf16[2,64,4096]{2,1,0:T(8,128)(2,1)S(1)} %get-tuple-element.36.refs_0_, ...), custom_call_target="tpu_custom_call" | custom-call | tf_op jit(solution)/shard_map/project_own/pallas_call | solution.py:361
  15.5 0.0 collective-permute-done.2.refs_0_
  15.5 3.9 %collective-permute-done.3.refs_1_ = bf16[64,2048]{1,0:T(8,128)(2,1)S(1)} collective-permute-done((bf16[64,2048]{1,0:T(8,128)(2,1)S(1)}, bf16[64,2048]{1,0:T(8,128)(2,1)S(1)}, u32[]{:S(2)}, u32[]{:S(2)}) %collective-permute-start.3) | collective-permute-done | bytes 262176 | tf_op jit(solution)/shard_map/ppermute | solution.py:471
  19.4 0.1 collective-permute-start.7
  19.5 0.5 %collective-permute-start.5 = (bf16[64,1024]{1,0:T(8,128)(2,1)S(1)}, bf16[64,1024]{1,0:T(8,128)(2,1)S(1)}, u32[]{:S(2)}, u32[]{:S(2)}) collective-permute-start(bf16[64,1024]{1,0:T(8,128)(2,1)S(1)} %get-tuple-element.60), channel_id=1, source_target_pairs={{0,1},{1,0},{2,3},{3,2},{4,5},{5,4},{6,7},{7,6},{8,9},{9,8},{10,11... | collective-permute-start | bytes 393224 | tf_op jit(solution)/shard_map/ppermute | solution.py:499
  20.0 0.1 collective-permute-start.8
  20.1 0.7 %collective-permute-done.7.refs_4_ = bf16[64,1024]{1,0:T(8,128)(2,1)S(1)} collective-permute-done((bf16[64,1024]{1,0:T(8,128)(2,1)S(1)}, bf16[64,1024]{1,0:T(8,128)(2,1)S(1)}, u32[]{:S(2)}, u32[]{:S(2)}) %collective-permute-start.7) | collective-permute-done | bytes 131104 | tf_op jit(solution)/shard_map/ppermute | solution.py:499
  20.8 0.1 collective-permute-start.6
  21.0 0.0 collective-permute-done.5.refs_2_
  21.0 0.4 %collective-permute-done.8.refs_5_ = bf16[64,1024]{1,0:T(8,128)(2,1)S(1)} collective-permute-done((bf16[64,1024]{1,0:T(8,128)(2,1)S(1)}, bf16[64,1024]{1,0:T(8,128)(2,1)S(1)}, u32[]{:S(2)}, u32[]{:S(2)}) %collective-permute-start.8) | collective-permute-done | bytes 131104 | tf_op jit(solution)/shard_map/ppermute | solution.py:499
  21.4 0.8 %collective-permute-done.6.refs_3_ = bf16[64,1024]{1,0:T(8,128)(2,1)S(1)} collective-permute-done((bf16[64,1024]{1,0:T(8,128)(2,1)S(1)}, bf16[64,1024]{1,0:T(8,128)(2,1)S(1)}, u32[]{:S(2)}, u32[]{:S(2)}) %collective-permute-start.6) | collective-permute-done | bytes 131104 | tf_op jit(solution)/shard_map/ppermute | solution.py:499
  22.2 1.7 %project_first.1 = (bf16[2,64,64,128]{3,2,1,0:T(8,128)(2,1)S(1)}, bf16[64,32,128]{2,1,0:T(8,128)(2,1)S(1)}) custom-call(bf16[64,2048]{1,0:T(8,128)(2,1)S(1)} %collective-permute-done.2.refs_0_, bf16[64,2048]{1,0:T(8,128)(2,1)S(1)} %collective-permute-done.3.refs_1_, ...), custom_call_target="tpu_custom_call", output_to_operand_aliasing={{0}: (8, {})} | custom-call | tf_op jit(solution)/shard_map/project_first/pallas_call | solution.py:361
  23.8 1.2 %collective-permute-done.refs_0_ = bf16[64,2048]{1,0:T(8,128)(2,1)S(1)} collective-permute-done((bf16[64,2048]{1,0:T(8,128)(2,1)S(1)}, bf16[64,2048]{1,0:T(8,128)(2,1)S(1)}, u32[]{:S(2)}, u32[]{:S(2)}) %collective-permute-start) | collective-permute-done | bytes 262176 | tf_op jit(solution)/shard_map/ppermute | solution.py:471
  25.0 4.7 %collective-permute-done.1.refs_1_ = bf16[64,2048]{1,0:T(8,128)(2,1)S(1)} collective-permute-done((bf16[64,2048]{1,0:T(8,128)(2,1)S(1)}, bf16[64,2048]{1,0:T(8,128)(2,1)S(1)}, u32[]{:S(2)}, u32[]{:S(2)}) %collective-permute-start.1) | collective-permute-done | bytes 262176 | tf_op jit(solution)/shard_map/ppermute | solution.py:471
  29.7 0.0 collective-permute-start.9
  29.7 0.5 %collective-permute-start.10 = (bf16[64,2048]{1,0:T(8,128)(2,1)S(1)}, bf16[64,2048]{1,0:T(8,128)(2,1)S(1)}, u32[]{:S(2)}, u32[]{:S(2)}) collective-permute-start(bf16[64,2048]{1,0:T(8,128)(2,1)S(1)} %collective-permute-done.1.refs_1_), channel_id=1, source_target_pairs={{0,1},{1,0},{2,3},{3,2},{4,5},{5,4},{6,7},{7,6},{8,9},{9,8},{10,11... | collective-permute-start | bytes 786440 | tf_op jit(solution)/shard_map/ppermute | solution.py:499
  30.2 1.0 %collective-permute-done.9.refs_2_ = bf16[64,2048]{1,0:T(8,128)(2,1)S(1)} collective-permute-done((bf16[64,2048]{1,0:T(8,128)(2,1)S(1)}, bf16[64,2048]{1,0:T(8,128)(2,1)S(1)}, u32[]{:S(2)}, u32[]{:S(2)}) %collective-permute-start.9) | collective-permute-done | bytes 262176 | tf_op jit(solution)/shard_map/ppermute | solution.py:499
  31.3 0.4 collective-permute-done.10.refs_3_
  31.6 2.9 %project_last.1 = (bf16[2,64,64,128]{3,2,1,0:T(8,128)(2,1)S(1)}, bf16[5,64,64,64]{3,2,1,0:T(8,128)(2,1)S(1)}, bf16[64,4096]{1,0:T(8,128)(2,1)S(1)}) custom-call(s32[8]{0:T(128)S(4)} %get-tuple-element.31.picks_ref, bf16[64,2048]{1,0:T(8,128)(2,1)S(1)} %collective-permute-done.refs_0_, ...), custom_call_target="tpu_custom_call", output_to_operand_aliasing={{0}: (8, {}), {1}: (9, {})} | custom-call | tf_op jit(solution)/shard_map/project_last/pallas_call | solution.py:361
  34.6 0.2 collective-permute-start.12
  34.8 1.0 %triplets.1.mine_ref = bf16[64,4096]{1,0:T(8,128)(2,1)S(1)} custom-call(s32[8]{0:T(128)S(4)} %get-tuple-element.31.picks_ref, bf16[2,64,64,128]{3,2,1,0:T(8,128)(2,1)S(1)} %get-tuple-element.51.l_ref, bf16[5,64,64,64]{3,2,1,0:T(8,128)(2,1)S(1)} %get-tuple-element.52.turned_ref), custom_call_target="tpu_custom_call" | custom-call | tf_op jit(solution)/shard_map/triplets/pallas_call | solution.py:361
  35.8 0.4 %collective-permute-start.11 = (bf16[64,4096]{1,0:T(8,128)(2,1)S(1)}, bf16[64,4096]{1,0:T(8,128)(2,1)S(1)}, u32[]{:S(2)}, u32[]{:S(2)}) collective-permute-start(bf16[64,4096]{1,0:T(8,128)(2,1)S(1)} %triplets.1.mine_ref), channel_id=1, source_target_pairs={{0,1},{1,0},{2,3},{3,2},{4,5},{5,4},{6,7},{7,6},{8,9},{9,8},{10,11... | collective-permute-start | bytes 1572872 | tf_op jit(solution)/shard_map/ppermute | solution.py:536
  36.2 0.3 collective-permute-done.12.theirs_ref
  36.5 1.3 %finish.2 = (bf16[2,64,4096]{2,1,0:T(8,128)(2,1)}, bf16[64,2048]{1,0:T(8,128)(2,1)S(1)}) custom-call(bf16[64,4096]{1,0:T(8,128)(2,1)S(1)} %get-tuple-element.49.mine_ref, bf16[64,4096]{1,0:T(8,128)(2,1)S(1)} %collective-permute-done.12.theirs_ref, bf16[2,64,4096]{2,1,0:T(8,128)(2,1)S(1)} %get-tuple-element.53.gate_ref, ...), custom_call_target="tpu_custom_call" | custom-call | tf_op jit(solution)/shard_map/finish/pallas_call | solution.py:427
  37.9 0.0 collective-permute-done.11.theirs_ref
  37.9 1.5 %finish.3 = bf16[2,64,4096]{2,1,0:T(8,128)(2,1)} custom-call(bf16[64,4096]{1,0:T(8,128)(2,1)S(1)} %triplets.1.mine_ref, bf16[64,4096]{1,0:T(8,128)(2,1)S(1)} %collective-permute-done.11.theirs_ref, bf16[2,64,4096]{2,1,0:T(8,128)(2,1)S(1)} %get-tuple-element.53.gate_ref, bf16[64,128]{1,0:T(8,128)(2,1)S(1)} %get-tuple-element.54.w_ref, ...), custom_call_target="tpu_custom_call", output_to_operand_aliasing={{}: (5, {})} | custom-call | tf_op jit(solution)/shard_map/finish/pallas_call | solution.py:427
  (2 shorter events, 0.0 us)
Async XLA Ops:
  1.3 9.1 %collective-permute-start.4 = (bf16[2,64,4096]{2,1,0:T(8,128)(2,1)S(1)}, bf16[2,64,4096]{2,1,0:T(8,128)(2,1)S(1)}, u32[]{:S(2)}, u32[]{:S(2)}) collective-permute-start(bf16[2,64,4096]{2,1,0:T(8,128)(2,1)S(1)} %get-tuple-element.36.refs_0_), channel_id=1, source_target_pairs={{0,1},{1,0},{2,3},{3,2},{4,5},{5,4},{6,7},{7,6},{8,9},{9,8},{10,11... | collective-permute-start | bytes 3145736 | tf_op jit(solution)/shard_map/ppermute | solution.py:474
  1.9 13.6 %collective-permute-start.2 = (bf16[64,2048]{1,0:T(8,128)(2,1)S(1)}, bf16[64,2048]{1,0:T(8,128)(2,1)S(1)}, u32[]{:S(2)}, u32[]{:S(2)}) collective-permute-start(bf16[64,2048]{1,0:T(8,128)(2,1)S(1)} %get-tuple-element.34), channel_id=1, source_target_pairs={{0,4},{4,8},{8,12},{12,0},{1,5},{5,9},{9,13},{13,1},{2,6},{6,10},{... | collective-permute-start | bytes 786440 | tf_op jit(solution)/shard_map/ppermute | solution.py:471
  4.5 14.9 %collective-permute-start.3 = (bf16[64,2048]{1,0:T(8,128)(2,1)S(1)}, bf16[64,2048]{1,0:T(8,128)(2,1)S(1)}, u32[]{:S(2)}, u32[]{:S(2)}) collective-permute-start(bf16[64,2048]{1,0:T(8,128)(2,1)S(1)} %get-tuple-element.35), channel_id=1, source_target_pairs={{0,12},{4,0},{8,4},{12,8},{1,13},{5,1},{9,5},{13,9},{2,14},{6,2},{... | collective-permute-start | bytes 786440 | tf_op jit(solution)/shard_map/ppermute | solution.py:471
  6.6 18.4 %collective-permute-start = (bf16[64,2048]{1,0:T(8,128)(2,1)S(1)}, bf16[64,2048]{1,0:T(8,128)(2,1)S(1)}, u32[]{:S(2)}, u32[]{:S(2)}) collective-permute-start(bf16[64,2048]{1,0:T(8,128)(2,1)S(1)} %get-tuple-element.32), channel_id=1, source_target_pairs={{0,4},{4,8},{8,12},{12,0},{1,5},{5,9},{9,13},{13,1},{2,6},{6,10},{... | collective-permute-start | bytes 786440 | tf_op jit(solution)/shard_map/ppermute | solution.py:471
  6.6 23.1 %collective-permute-start.1 = (bf16[64,2048]{1,0:T(8,128)(2,1)S(1)}, bf16[64,2048]{1,0:T(8,128)(2,1)S(1)}, u32[]{:S(2)}, u32[]{:S(2)}) collective-permute-start(bf16[64,2048]{1,0:T(8,128)(2,1)S(1)} %get-tuple-element.33), channel_id=1, source_target_pairs={{0,12},{4,0},{8,4},{12,8},{1,13},{5,1},{9,5},{13,9},{2,14},{6,2},{... | collective-permute-start | bytes 786440 | tf_op jit(solution)/shard_map/ppermute | solution.py:471
  19.4 1.4 %collective-permute-start.7 = (bf16[64,1024]{1,0:T(8,128)(2,1)S(1)}, bf16[64,1024]{1,0:T(8,128)(2,1)S(1)}, u32[]{:S(2)}, u32[]{:S(2)}) collective-permute-start(bf16[64,1024]{1,0:T(8,128)(2,1)S(1)} %get-tuple-element.59), channel_id=1, source_target_pairs={{0,1},{1,0},{2,3},{3,2},{4,5},{5,4},{6,7},{7,6},{8,9},{9,8},{10,11... | collective-permute-start | bytes 393224 | tf_op jit(solution)/shard_map/ppermute | solution.py:499
  19.5 1.5 %collective-permute-start.5 = (bf16[64,1024]{1,0:T(8,128)(2,1)S(1)}, bf16[64,1024]{1,0:T(8,128)(2,1)S(1)}, u32[]{:S(2)}, u32[]{:S(2)}) collective-permute-start(bf16[64,1024]{1,0:T(8,128)(2,1)S(1)} %get-tuple-element.60), channel_id=1, source_target_pairs={{0,1},{1,0},{2,3},{3,2},{4,5},{5,4},{6,7},{7,6},{8,9},{9,8},{10,11... | collective-permute-start | bytes 393224 | tf_op jit(solution)/shard_map/ppermute | solution.py:499
  20.0 1.4 %collective-permute-start.8 = (bf16[64,1024]{1,0:T(8,128)(2,1)S(1)}, bf16[64,1024]{1,0:T(8,128)(2,1)S(1)}, u32[]{:S(2)}, u32[]{:S(2)}) collective-permute-start(bf16[64,1024]{1,0:T(8,128)(2,1)S(1)} %get-tuple-element.57), channel_id=1, source_target_pairs={{0,1},{1,0},{2,3},{3,2},{4,5},{5,4},{6,7},{7,6},{8,9},{9,8},{10,11... | collective-permute-start | bytes 393224 | tf_op jit(solution)/shard_map/ppermute | solution.py:499
  20.8 1.3 %collective-permute-start.6 = (bf16[64,1024]{1,0:T(8,128)(2,1)S(1)}, bf16[64,1024]{1,0:T(8,128)(2,1)S(1)}, u32[]{:S(2)}, u32[]{:S(2)}) collective-permute-start(bf16[64,1024]{1,0:T(8,128)(2,1)S(1)} %get-tuple-element.58), channel_id=1, source_target_pairs={{0,1},{1,0},{2,3},{3,2},{4,5},{5,4},{6,7},{7,6},{8,9},{9,8},{10,11... | collective-permute-start | bytes 393224 | tf_op jit(solution)/shard_map/ppermute | solution.py:499
  29.7 1.5 %collective-permute-start.9 = (bf16[64,2048]{1,0:T(8,128)(2,1)S(1)}, bf16[64,2048]{1,0:T(8,128)(2,1)S(1)}, u32[]{:S(2)}, u32[]{:S(2)}) collective-permute-start(bf16[64,2048]{1,0:T(8,128)(2,1)S(1)} %collective-permute-done.refs_0_), channel_id=1, source_target_pairs={{0,1},{1,0},{2,3},{3,2},{4,5},{5,4},{6,7},{7,6},{8,9},{9,8},{10,11... | collective-permute-start | bytes 786440 | tf_op jit(solution)/shard_map/ppermute | solution.py:499
  29.7 1.9 %collective-permute-start.10 = (bf16[64,2048]{1,0:T(8,128)(2,1)S(1)}, bf16[64,2048]{1,0:T(8,128)(2,1)S(1)}, u32[]{:S(2)}, u32[]{:S(2)}) collective-permute-start(bf16[64,2048]{1,0:T(8,128)(2,1)S(1)} %collective-permute-done.1.refs_1_), channel_id=1, source_target_pairs={{0,1},{1,0},{2,3},{3,2},{4,5},{5,4},{6,7},{7,6},{8,9},{9,8},{10,11... | collective-permute-start | bytes 786440 | tf_op jit(solution)/shard_map/ppermute | solution.py:499
  34.6 2.0 %collective-permute-start.12 = (bf16[64,4096]{1,0:T(8,128)(2,1)S(1)}, bf16[64,4096]{1,0:T(8,128)(2,1)S(1)}, u32[]{:S(2)}, u32[]{:S(2)}) collective-permute-start(bf16[64,4096]{1,0:T(8,128)(2,1)S(1)} %get-tuple-element.49.mine_ref), channel_id=1, source_target_pairs={{0,1},{1,0},{2,3},{3,2},{4,5},{5,4},{6,7},{7,6},{8,9},{9,8},{10,11... | collective-permute-start | bytes 1572872 | tf_op jit(solution)/shard_map/ppermute | solution.py:525
  35.8 2.1 %collective-permute-start.11 = (bf16[64,4096]{1,0:T(8,128)(2,1)S(1)}, bf16[64,4096]{1,0:T(8,128)(2,1)S(1)}, u32[]{:S(2)}, u32[]{:S(2)}) collective-permute-start(bf16[64,4096]{1,0:T(8,128)(2,1)S(1)} %triplets.1.mine_ref), channel_id=1, source_target_pairs={{0,1},{1,0},{2,3},{3,2},{4,5},{5,4},{6,7},{7,6},{8,9},{9,8},{10,11... | collective-permute-start | bytes 1572872 | tf_op jit(solution)/shard_map/ppermute | solution.py:536

commit v17 on v13

--- a/solution.py
+++ b/solution.py
@@ -60,12 +60,18 @@
     picks_ref, pair_ref, *out_refs = refs[: 2 + 2 * len(cuts)]
     a_ref, b_ref, n_ref, sems = refs[2 + 2 * len(cuts) :]
     me, behind, ahead = neighbour_tiles()
-    whole = pltpu.make_async_copy(pair_hbm, pair_ref, sems.at[0])
     tables = [
-        pltpu.make_async_copy(source, target, sems.at[1 + at])
+        pltpu.make_async_copy(source, target, sems.at[at])
         for at, (source, target) in enumerate(((a_hbm, a_ref), (b_hbm, b_ref), (n_hbm, n_ref)))
     ]
-    for copy in (*tables, whole):
+    pieces = [(s, row) for s in range(slots) for row in range(0, pair_ref.shape[1], 16)]
+    fetches = [
+        pltpu.make_async_copy(
+            pair_hbm.at[s, pl.ds(row, 16)], pair_ref.at[s, pl.ds(row, 16)], sems.at[3 + at]
+        )
+        for at, (s, row) in enumerate(pieces)
+    ]
+    for copy in (*tables, *fetches):
         copy.start()
     for copy in tables:
         copy.wait()
@@ -83,7 +89,8 @@
     for s in range(slots):
         for at, pick in enumerate(used_picks(s, slots, triplets, a_ref, b_ref, n_ref)):
             picks_ref[4 * s + at] = pick
-    whole.wait()
+    for copy in fetches:
+        copy.wait()
     for at, (start, size) in enumerate(cuts):
         for which, pick in enumerate(chosen):
             out_refs[2 * at + which][...] = pair_ref[pick, :, start : start + size]
@@ -106,7 +113,7 @@
         in_specs=[hbm] * 4,
         out_specs=[pl.BlockSpec(memory_space=pltpu.SMEM)] + [vmem] * (len(out_shape) - 1),
         scratch_shapes=[pltpu.SMEM(value.shape, value.dtype) for value in operands[:3]]
-        + [pltpu.SemaphoreType.DMA((4,))],
+        + [pltpu.SemaphoreType.DMA((3 + slots * channels // 16,))],
         name="select_blocks",
     )(*operands)
 
@@ -377,8 +384,14 @@
         held = refs[0]
     else:
         before_ref, out_ref, held, sems = refs
-        before = pltpu.make_async_copy(before_ref, out_ref.at[0], sems.at[pieces])
-        before.start()
+        befores = [
+            pltpu.make_async_copy(
+                before_ref.at[pl.ds(row, 16)], out_ref.at[0, pl.ds(row, 16)], sems.at[pieces + row // 16]
+            )
+            for row in range(0, before_ref.shape[0], 16)
+        ]
+        for copy_before in befores:
+            copy_before.start()
     size = cells // pieces
 
     def copy(n):
@@ -399,7 +412,8 @@
     if s > 0:
         for n in range(pieces):
             copy(n).wait()
-        before.wait()
+        for copy_before in befores:
+            copy_before.wait()
 
 
 def finish(s, mine, theirs, gate, weight, before=None):
@@ -411,7 +425,7 @@
         operands.append(before)
         out_shape = jax.ShapeDtypeStruct(gate.shape, BF16)
         out_specs = pl.BlockSpec(memory_space=pltpu.HBM)
-        scratch = [pltpu.VMEM(mine.shape, BF16), pltpu.SemaphoreType.DMA((5,))]
+        scratch = [pltpu.VMEM(mine.shape, BF16), pltpu.SemaphoreType.DMA((4 + mine.shape[0] // 16,))]
     return pl.pallas_call(
         functools.partial(finish_kernel, s, mine.shape[1] // 2, 4),
         in_specs=[vmem] * len(operands),

time: 39.6 us -> 39.8 us (level)
  no operation moved by 1% of the time
where the time goes in v17:
time: 39.8 us; the launch traced here: 39.6 us
  Pallas kernels  14.7 us (37%)
  waiting for transfers between devices  13.6 us (34%)
  starting transfers between devices  11.1 us (28%)
    pallas_call x4, Pallas kernels, call(): pl.pallas_call(kernel, in_specs=[pl.BlockSpec(memory_space=space) for spa...  10.6 us
    ppermute x2, waiting for transfers between devices, per_device(): lax.ppermute(chosen[2 * n + 1], 'row', down)  8.64 us
    ppermute x2, starting transfers between devices, per_device(): lax.ppermute(chosen[2 * n + 1], 'row', down)  5.93 us
    ppermute x6, waiting for transfers between devices, per_device(): lax.ppermute(lax.slice_in_dim(value, at, at + wide, axis=1), 'chan', swap)  3.27 us
    pallas_call x2, Pallas kernels, finish(): pl.pallas_call(functools.partial(finish_kernel, s, mine.shape[1] // 2, 4)...  2.68 us
    ppermute x2, starting transfers between devices, per_device(): lax.ppermute(chosen[2 * n], 'row', up)  2.64 us
    pallas_call x1, Pallas kernels, select_blocks(): pl.pallas_call(functools.partial(select_kernel, slots, a_slots.shape[0],...  1.44 us
    ppermute x6, starting transfers between devices, per_device(): lax.ppermute(lax.slice_in_dim(value, at, at + wide, axis=1), 'chan', swap)  1.37 us
  transfers between devices with their start and end apart: 13, of which 10 were waited for; matrix products, arithmetic and copies ran while one was open for 0% of the time, Pallas kernels for 22%

profile of v17, /device:TPU:0, one launch (start us, length us, event | category | flops | bytes accessed | tf_op | source)
XLA Modules:
  0.0 39.6 jit_solution(332366434539480553)
XLA Ops:
  0.0 1.4 %select_blocks.1 = (s32[8]{0:T(128)S(4)}, bf16[2,64,4096]{2,1,0:T(8,128)(2,1)S(1)}, bf16[64,2048]{1,0:T(8,128)(2,1)S(1)}, bf16[64,2048]{1,0:T(8,128)(2,1)S(1)}, ...) custom-call(s32[4,16]{1,0:T(4,128)} %bitcast.12, s32[4,16]{1,0:T(4,128)} %bitcast.13, s32[16]{0:T(128)} %n_hbm.1, ...), custom_call_target="tpu_custom_call" | custom-call | tf_op jit(solution)/shard_map/select_blocks/pallas_call | solution.py:110
  1.5 0.5 %collective-permute-start.4 = (bf16[2,64,4096]{2,1,0:T(8,128)(2,1)S(1)}, bf16[2,64,4096]{2,1,0:T(8,128)(2,1)S(1)}, u32[]{:S(2)}, u32[]{:S(2)}) collective-permute-start(bf16[2,64,4096]{2,1,0:T(8,128)(2,1)S(1)} %get-tuple-element.34.refs_0_), channel_id=1, source_target_pairs={{0,1},{1,0},{2,3},{3,2},{4,5},{5,4},{6,7},{7,6},{8,9},{9,8},{10,11... | collective-permute-start | bytes 3145736 | tf_op jit(solution)/shard_map/ppermute | solution.py:475
  2.0 2.6 %collective-permute-start.2 = (bf16[64,2048]{1,0:T(8,128)(2,1)S(1)}, bf16[64,2048]{1,0:T(8,128)(2,1)S(1)}, u32[]{:S(2)}, u32[]{:S(2)}) collective-permute-start(bf16[64,2048]{1,0:T(8,128)(2,1)S(1)} %get-tuple-element.32), channel_id=1, source_target_pairs={{0,4},{4,8},{8,12},{12,0},{1,5},{5,9},{9,13},{13,1},{2,6},{6,10},{... | collective-permute-start | bytes 786440 | tf_op jit(solution)/shard_map/ppermute | solution.py:472
  4.6 2.1 %collective-permute-start.3 = (bf16[64,2048]{1,0:T(8,128)(2,1)S(1)}, bf16[64,2048]{1,0:T(8,128)(2,1)S(1)}, u32[]{:S(2)}, u32[]{:S(2)}) collective-permute-start(bf16[64,2048]{1,0:T(8,128)(2,1)S(1)} %get-tuple-element.33), channel_id=1, source_target_pairs={{0,12},{4,0},{8,4},{12,8},{1,13},{5,1},{9,5},{13,9},{2,14},{6,2},{... | collective-permute-start | bytes 786440 | tf_op jit(solution)/shard_map/ppermute | solution.py:472
  6.7 0.0 collective-permute-start
  6.7 3.8 %collective-permute-start.1 = (bf16[64,2048]{1,0:T(8,128)(2,1)S(1)}, bf16[64,2048]{1,0:T(8,128)(2,1)S(1)}, u32[]{:S(2)}, u32[]{:S(2)}) collective-permute-start(bf16[64,2048]{1,0:T(8,128)(2,1)S(1)} %get-tuple-element.31), channel_id=1, source_target_pairs={{0,12},{4,0},{8,4},{12,8},{1,13},{5,1},{9,5},{13,9},{2,14},{6,2},{... | collective-permute-start | bytes 786440 | tf_op jit(solution)/shard_map/ppermute | solution.py:472
  10.5 0.0 collective-permute-done.4.refs_1_
  10.5 5.0 %project_own.1 = (bf16[2,64,64,128]{3,2,1,0:T(8,128)(2,1)S(1)}, bf16[5,64,64,64]{3,2,1,0:T(8,128)(2,1)S(1)}, bf16[2,64,4096]{2,1,0:T(8,128)(2,1)S(1)}, bf16[256,...) custom-call(bf16[2,64,4096]{2,1,0:T(8,128)(2,1)S(1)} %get-tuple-element.34.refs_0_, ...), custom_call_target="tpu_custom_call" | custom-call | tf_op jit(solution)/shard_map/project_own/pallas_call | solution.py:368
  15.6 0.0 collective-permute-done.2.refs_0_
  15.6 3.9 %collective-permute-done.3.refs_1_ = bf16[64,2048]{1,0:T(8,128)(2,1)S(1)} collective-permute-done((bf16[64,2048]{1,0:T(8,128)(2,1)S(1)}, bf16[64,2048]{1,0:T(8,128)(2,1)S(1)}, u32[]{:S(2)}, u32[]{:S(2)}) %collective-permute-start.3) | collective-permute-done | bytes 262176 | tf_op jit(solution)/shard_map/ppermute | solution.py:472
  19.5 0.1 collective-permute-start.7
  19.6 0.5 %collective-permute-start.5 = (bf16[64,1024]{1,0:T(8,128)(2,1)S(1)}, bf16[64,1024]{1,0:T(8,128)(2,1)S(1)}, u32[]{:S(2)}, u32[]{:S(2)}) collective-permute-start(bf16[64,1024]{1,0:T(8,128)(2,1)S(1)} %get-tuple-element.56), channel_id=1, source_target_pairs={{0,1},{1,0},{2,3},{3,2},{4,5},{5,4},{6,7},{7,6},{8,9},{9,8},{10,11... | collective-permute-start | bytes 393224 | tf_op jit(solution)/shard_map/ppermute | solution.py:500
  20.1 0.1 collective-permute-start.8
  20.3 0.7 %collective-permute-done.7.refs_4_ = bf16[64,1024]{1,0:T(8,128)(2,1)S(1)} collective-permute-done((bf16[64,1024]{1,0:T(8,128)(2,1)S(1)}, bf16[64,1024]{1,0:T(8,128)(2,1)S(1)}, u32[]{:S(2)}, u32[]{:S(2)}) %collective-permute-start.7) | collective-permute-done | bytes 131104 | tf_op jit(solution)/shard_map/ppermute | solution.py:500
  20.9 0.1 collective-permute-start.6
  21.1 0.0 collective-permute-done.5.refs_2_
  21.1 0.4 %collective-permute-done.8.refs_5_ = bf16[64,1024]{1,0:T(8,128)(2,1)S(1)} collective-permute-done((bf16[64,1024]{1,0:T(8,128)(2,1)S(1)}, bf16[64,1024]{1,0:T(8,128)(2,1)S(1)}, u32[]{:S(2)}, u32[]{:S(2)}) %collective-permute-start.8) | collective-permute-done | bytes 131104 | tf_op jit(solution)/shard_map/ppermute | solution.py:500
  21.5 0.8 %collective-permute-done.6.refs_3_ = bf16[64,1024]{1,0:T(8,128)(2,1)S(1)} collective-permute-done((bf16[64,1024]{1,0:T(8,128)(2,1)S(1)}, bf16[64,1024]{1,0:T(8,128)(2,1)S(1)}, u32[]{:S(2)}, u32[]{:S(2)}) %collective-permute-start.6) | collective-permute-done | bytes 131104 | tf_op jit(solution)/shard_map/ppermute | solution.py:500
  22.3 1.7 %project_first.1 = (bf16[2,64,64,128]{3,2,1,0:T(8,128)(2,1)S(1)}, bf16[64,32,128]{2,1,0:T(8,128)(2,1)S(1)}) custom-call(bf16[64,2048]{1,0:T(8,128)(2,1)S(1)} %collective-permute-done.2.refs_0_, bf16[64,2048]{1,0:T(8,128)(2,1)S(1)} %collective-permute-done.3.refs_1_, ...), custom_call_target="tpu_custom_call", output_to_operand_aliasing={{0}: (8, {})} | custom-call | tf_op jit(solution)/shard_map/project_first/pallas_call | solution.py:368
  23.9 1.2 %collective-permute-done.refs_0_ = bf16[64,2048]{1,0:T(8,128)(2,1)S(1)} collective-permute-done((bf16[64,2048]{1,0:T(8,128)(2,1)S(1)}, bf16[64,2048]{1,0:T(8,128)(2,1)S(1)}, u32[]{:S(2)}, u32[]{:S(2)}) %collective-permute-start) | collective-permute-done | bytes 262176 | tf_op jit(solution)/shard_map/ppermute | solution.py:472
  25.1 4.7 %collective-permute-done.1.refs_1_ = bf16[64,2048]{1,0:T(8,128)(2,1)S(1)} collective-permute-done((bf16[64,2048]{1,0:T(8,128)(2,1)S(1)}, bf16[64,2048]{1,0:T(8,128)(2,1)S(1)}, u32[]{:S(2)}, u32[]{:S(2)}) %collective-permute-start.1) | collective-permute-done | bytes 262176 | tf_op jit(solution)/shard_map/ppermute | solution.py:472
  29.8 0.0 collective-permute-start.9
  29.8 0.5 %collective-permute-start.10 = (bf16[64,2048]{1,0:T(8,128)(2,1)S(1)}, bf16[64,2048]{1,0:T(8,128)(2,1)S(1)}, u32[]{:S(2)}, u32[]{:S(2)}) collective-permute-start(bf16[64,2048]{1,0:T(8,128)(2,1)S(1)} %collective-permute-done.1.refs_1_), channel_id=1, source_target_pairs={{0,1},{1,0},{2,3},{3,2},{4,5},{5,4},{6,7},{7,6},{8,9},{9,8},{10,11... | collective-permute-start | bytes 786440 | tf_op jit(solution)/shard_map/ppermute | solution.py:500
  30.3 1.0 %collective-permute-done.9.refs_2_ = bf16[64,2048]{1,0:T(8,128)(2,1)S(1)} collective-permute-done((bf16[64,2048]{1,0:T(8,128)(2,1)S(1)}, bf16[64,2048]{1,0:T(8,128)(2,1)S(1)}, u32[]{:S(2)}, u32[]{:S(2)}) %collective-permute-start.9) | collective-permute-done | bytes 262176 | tf_op jit(solution)/shard_map/ppermute | solution.py:500
  31.4 0.4 collective-permute-done.10.refs_3_
  31.7 2.9 %project_last.1 = (bf16[2,64,64,128]{3,2,1,0:T(8,128)(2,1)S(1)}, bf16[5,64,64,64]{3,2,1,0:T(8,128)(2,1)S(1)}, bf16[64,4096]{1,0:T(8,128)(2,1)S(1)}) custom-call(s32[8]{0:T(128)S(4)} %get-tuple-element.29.picks_ref, bf16[64,2048]{1,0:T(8,128)(2,1)S(1)} %collective-permute-done.refs_0_, ...), custom_call_target="tpu_custom_call", output_to_operand_aliasing={{0}: (8, {}), {1}: (9, {})} | custom-call | tf_op jit(solution)/shard_map/project_last/pallas_call | solution.py:368
  34.7 0.2 collective-permute-start.12
  34.9 1.0 %triplets.1.mine_ref = bf16[64,4096]{1,0:T(8,128)(2,1)S(1)} custom-call(s32[8]{0:T(128)S(4)} %get-tuple-element.29.picks_ref, bf16[2,64,64,128]{3,2,1,0:T(8,128)(2,1)S(1)} %get-tuple-element.49.l_ref, bf16[5,64,64,64]{3,2,1,0:T(8,128)(2,1)S(1)} %get-tuple-element.50.turned_ref), custom_call_target="tpu_custom_call" | custom-call | tf_op jit(solution)/shard_map/triplets/pallas_call | solution.py:368
  35.9 0.4 %collective-permute-start.11 = (bf16[64,4096]{1,0:T(8,128)(2,1)S(1)}, bf16[64,4096]{1,0:T(8,128)(2,1)S(1)}, u32[]{:S(2)}, u32[]{:S(2)}) collective-permute-start(bf16[64,4096]{1,0:T(8,128)(2,1)S(1)} %triplets.1.mine_ref), channel_id=1, source_target_pairs={{0,1},{1,0},{2,3},{3,2},{4,5},{5,4},{6,7},{7,6},{8,9},{9,8},{10,11... | collective-permute-start | bytes 1572872 | tf_op jit(solution)/shard_map/ppermute | solution.py:537
  36.4 0.3 collective-permute-done.12.theirs_ref
  36.6 1.0 %finish.2.refs_0_ = bf16[64,4096]{1,0:T(8,128)(2,1)S(1)} custom-call(bf16[64,4096]{1,0:T(8,128)(2,1)S(1)} %get-tuple-element.47.mine_ref, bf16[64,4096]{1,0:T(8,128)(2,1)S(1)} %collective-permute-done.12.theirs_ref, bf16[2,64,4096]{2,1,0:T(8,128)(2,1)S(1)} %get-tuple-element.51.gate_ref, bf16[64,128]{1,0:T(8,128)(2,1)S(1)} %get-tuple-element.52.w_ref), custom_call_target="tpu_custom_call" | custom-call | tf_op jit(solution)/shard_map/finish/pallas_call | solution.py:429
  37.6 0.3 collective-permute-done.11.theirs_ref
  37.9 1.7 %finish.3 = bf16[2,64,4096]{2,1,0:T(8,128)(2,1)} custom-call(bf16[64,4096]{1,0:T(8,128)(2,1)S(1)} %triplets.1.mine_ref, bf16[64,4096]{1,0:T(8,128)(2,1)S(1)} %collective-permute-done.11.theirs_ref, bf16[2,64,4096]{2,1,0:T(8,128)(2,1)S(1)} %get-tuple-element.51.gate_ref, bf16[64,128]{1,0:T(8,128)(2,1)S(1)} %get-tuple-element.52.w_ref, ...), custom_call_target="tpu_custom_call" | custom-call | tf_op jit(solution)/shard_map/finish/pallas_call | solution.py:429
  (2 shorter events, 0.0 us)
Async XLA Ops:
  1.5 9.1 %collective-permute-start.4 = (bf16[2,64,4096]{2,1,0:T(8,128)(2,1)S(1)}, bf16[2,64,4096]{2,1,0:T(8,128)(2,1)S(1)}, u32[]{:S(2)}, u32[]{:S(2)}) collective-permute-start(bf16[2,64,4096]{2,1,0:T(8,128)(2,1)S(1)} %get-tuple-element.34.refs_0_), channel_id=1, source_target_pairs={{0,1},{1,0},{2,3},{3,2},{4,5},{5,4},{6,7},{7,6},{8,9},{9,8},{10,11... | collective-permute-start | bytes 3145736 | tf_op jit(solution)/shard_map/ppermute | solution.py:475
  2.0 13.6 %collective-permute-start.2 = (bf16[64,2048]{1,0:T(8,128)(2,1)S(1)}, bf16[64,2048]{1,0:T(8,128)(2,1)S(1)}, u32[]{:S(2)}, u32[]{:S(2)}) collective-permute-start(bf16[64,2048]{1,0:T(8,128)(2,1)S(1)} %get-tuple-element.32), channel_id=1, source_target_pairs={{0,4},{4,8},{8,12},{12,0},{1,5},{5,9},{9,13},{13,1},{2,6},{6,10},{... | collective-permute-start | bytes 786440 | tf_op jit(solution)/shard_map/ppermute | solution.py:472
  4.6 14.9 %collective-permute-start.3 = (bf16[64,2048]{1,0:T(8,128)(2,1)S(1)}, bf16[64,2048]{1,0:T(8,128)(2,1)S(1)}, u32[]{:S(2)}, u32[]{:S(2)}) collective-permute-start(bf16[64,2048]{1,0:T(8,128)(2,1)S(1)} %get-tuple-element.33), channel_id=1, source_target_pairs={{0,12},{4,0},{8,4},{12,8},{1,13},{5,1},{9,5},{13,9},{2,14},{6,2},{... | collective-permute-start | bytes 786440 | tf_op jit(solution)/shard_map/ppermute | solution.py:472
  6.7 18.4 %collective-permute-start = (bf16[64,2048]{1,0:T(8,128)(2,1)S(1)}, bf16[64,2048]{1,0:T(8,128)(2,1)S(1)}, u32[]{:S(2)}, u32[]{:S(2)}) collective-permute-start(bf16[64,2048]{1,0:T(8,128)(2,1)S(1)} %get-tuple-element.30), channel_id=1, source_target_pairs={{0,4},{4,8},{8,12},{12,0},{1,5},{5,9},{9,13},{13,1},{2,6},{6,10},{... | collective-permute-start | bytes 786440 | tf_op jit(solution)/shard_map/ppermute | solution.py:472
  6.7 23.1 %collective-permute-start.1 = (bf16[64,2048]{1,0:T(8,128)(2,1)S(1)}, bf16[64,2048]{1,0:T(8,128)(2,1)S(1)}, u32[]{:S(2)}, u32[]{:S(2)}) collective-permute-start(bf16[64,2048]{1,0:T(8,128)(2,1)S(1)} %get-tuple-element.31), channel_id=1, source_target_pairs={{0,12},{4,0},{8,4},{12,8},{1,13},{5,1},{9,5},{13,9},{2,14},{6,2},{... | collective-permute-start | bytes 786440 | tf_op jit(solution)/shard_map/ppermute | solution.py:472
  19.5 1.4 %collective-permute-start.7 = (bf16[64,1024]{1,0:T(8,128)(2,1)S(1)}, bf16[64,1024]{1,0:T(8,128)(2,1)S(1)}, u32[]{:S(2)}, u32[]{:S(2)}) collective-permute-start(bf16[64,1024]{1,0:T(8,128)(2,1)S(1)} %get-tuple-element.55), channel_id=1, source_target_pairs={{0,1},{1,0},{2,3},{3,2},{4,5},{5,4},{6,7},{7,6},{8,9},{9,8},{10,11... | collective-permute-start | bytes 393224 | tf_op jit(solution)/shard_map/ppermute | solution.py:500
  19.6 1.5 %collective-permute-start.5 = (bf16[64,1024]{1,0:T(8,128)(2,1)S(1)}, bf16[64,1024]{1,0:T(8,128)(2,1)S(1)}, u32[]{:S(2)}, u32[]{:S(2)}) collective-permute-start(bf16[64,1024]{1,0:T(8,128)(2,1)S(1)} %get-tuple-element.56), channel_id=1, source_target_pairs={{0,1},{1,0},{2,3},{3,2},{4,5},{5,4},{6,7},{7,6},{8,9},{9,8},{10,11... | collective-permute-start | bytes 393224 | tf_op jit(solution)/shard_map/ppermute | solution.py:500
  20.1 1.4 %collective-permute-start.8 = (bf16[64,1024]{1,0:T(8,128)(2,1)S(1)}, bf16[64,1024]{1,0:T(8,128)(2,1)S(1)}, u32[]{:S(2)}, u32[]{:S(2)}) collective-permute-start(bf16[64,1024]{1,0:T(8,128)(2,1)S(1)} %get-tuple-element.53), channel_id=1, source_target_pairs={{0,1},{1,0},{2,3},{3,2},{4,5},{5,4},{6,7},{7,6},{8,9},{9,8},{10,11... | collective-permute-start | bytes 393224 | tf_op jit(solution)/shard_map/ppermute | solution.py:500
  20.9 1.3 %collective-permute-start.6 = (bf16[64,1024]{1,0:T(8,128)(2,1)S(1)}, bf16[64,1024]{1,0:T(8,128)(2,1)S(1)}, u32[]{:S(2)}, u32[]{:S(2)}) collective-permute-start(bf16[64,1024]{1,0:T(8,128)(2,1)S(1)} %get-tuple-element.54), channel_id=1, source_target_pairs={{0,1},{1,0},{2,3},{3,2},{4,5},{5,4},{6,7},{7,6},{8,9},{9,8},{10,11... | collective-permute-start | bytes 393224 | tf_op jit(solution)/shard_map/ppermute | solution.py:500
  29.8 1.5 %collective-permute-start.9 = (bf16[64,2048]{1,0:T(8,128)(2,1)S(1)}, bf16[64,2048]{1,0:T(8,128)(2,1)S(1)}, u32[]{:S(2)}, u32[]{:S(2)}) collective-permute-start(bf16[64,2048]{1,0:T(8,128)(2,1)S(1)} %collective-permute-done.refs_0_), channel_id=1, source_target_pairs={{0,1},{1,0},{2,3},{3,2},{4,5},{5,4},{6,7},{7,6},{8,9},{9,8},{10,11... | collective-permute-start | bytes 786440 | tf_op jit(solution)/shard_map/ppermute | solution.py:500
  29.8 1.9 %collective-permute-start.10 = (bf16[64,2048]{1,0:T(8,128)(2,1)S(1)}, bf16[64,2048]{1,0:T(8,128)(2,1)S(1)}, u32[]{:S(2)}, u32[]{:S(2)}) collective-permute-start(bf16[64,2048]{1,0:T(8,128)(2,1)S(1)} %collective-permute-done.1.refs_1_), channel_id=1, source_target_pairs={{0,1},{1,0},{2,3},{3,2},{4,5},{5,4},{6,7},{7,6},{8,9},{9,8},{10,11... | collective-permute-start | bytes 786440 | tf_op jit(solution)/shard_map/ppermute | solution.py:500
  34.7 2.0 %collective-permute-start.12 = (bf16[64,4096]{1,0:T(8,128)(2,1)S(1)}, bf16[64,4096]{1,0:T(8,128)(2,1)S(1)}, u32[]{:S(2)}, u32[]{:S(2)}) collective-permute-start(bf16[64,4096]{1,0:T(8,128)(2,1)S(1)} %get-tuple-element.47.mine_ref), channel_id=1, source_target_pairs={{0,1},{1,0},{2,3},{3,2},{4,5},{5,4},{6,7},{7,6},{8,9},{9,8},{10,11... | collective-permute-start | bytes 1572872 | tf_op jit(solution)/shard_map/ppermute | solution.py:526
  35.9 2.0 %collective-permute-start.11 = (bf16[64,4096]{1,0:T(8,128)(2,1)S(1)}, bf16[64,4096]{1,0:T(8,128)(2,1)S(1)}, u32[]{:S(2)}, u32[]{:S(2)}) collective-permute-start(bf16[64,4096]{1,0:T(8,128)(2,1)S(1)} %triplets.1.mine_ref), channel_id=1, source_target_pairs={{0,1},{1,0},{2,3},{3,2},{4,5},{5,4},{6,7},{7,6},{8,9},{9,8},{10,11... | collective-permute-start | bytes 1572872 | tf_op jit(solution)/shard_map/ppermute | solution.py:537

commit v18 on v13

--- a/solution.py
+++ b/solution.py
@@ -413,7 +413,7 @@
         out_specs = pl.BlockSpec(memory_space=pltpu.HBM)
         scratch = [pltpu.VMEM(mine.shape, BF16), pltpu.SemaphoreType.DMA((5,))]
     return pl.pallas_call(
-        functools.partial(finish_kernel, s, mine.shape[1] // 2, 4),
+        functools.partial(finish_kernel, s, mine.shape[1], 4),
         in_specs=[vmem] * len(operands),
         out_specs=out_specs,
         out_shape=out_shape,
@@ -454,10 +454,12 @@
     chunk = cells // 4
     cuts = ((0, 2 * chunk), (2 * chunk, 2 * chunk))
     picks, pair, *chosen = select_blocks(pair, a_slots, b_slots, counts, cuts)
-    arrived = [
-        (lax.ppermute(chosen[2 * n], "row", up), lax.ppermute(chosen[2 * n + 1], "row", down))
-        for n in range(len(cuts))
-    ]
+    arrived = []
+    for n in range(len(cuts)):
+        moved = {}
+        for which in (0, 1) if n == 0 else (1, 0):
+            moved[which] = lax.ppermute(chosen[2 * n + which], "row", (up, down)[which])
+        arrived.append((moved[0], moved[1]))
     pair_other = lax.ppermute(pair, "chan", swap)
     left_shape = pltpu.VMEM((2, half, BLK, LANES), BF16)
     right_shape = pltpu.VMEM((5, half, BLK, BLK), BF16)

time: 39.6 us -> 39.5 us (level)
  no operation moved by 1% of the time
where the time goes in v18:
time: 39.5 us; the launch traced here: 39.3 us
  Pallas kernels  14.3 us (36%)
  waiting for transfers between devices  13.8 us (35%)
  starting transfers between devices  11.1 us (28%)
    pallas_call x4, Pallas kernels, call(): pl.pallas_call(kernel, in_specs=[pl.BlockSpec(memory_space=space) for spa...  10.6 us
    ppermute x4, waiting for transfers between devices, per_device(): moved[which] = lax.ppermute(chosen[2 * n + which], 'row', (up, down)[which])  9.81 us
    ppermute x4, starting transfers between devices, per_device(): moved[which] = lax.ppermute(chosen[2 * n + which], 'row', (up, down)[which])  8.57 us
    ppermute x6, waiting for transfers between devices, per_device(): lax.ppermute(lax.slice_in_dim(value, at, at + wide, axis=1), 'chan', swap)  3.27 us
    pallas_call x2, Pallas kernels, finish(): pl.pallas_call(functools.partial(finish_kernel, s, mine.shape[1], 4), in_...  2.33 us
    ppermute x6, starting transfers between devices, per_device(): lax.ppermute(lax.slice_in_dim(value, at, at + wide, axis=1), 'chan', swap)  1.37 us
    pallas_call x1, Pallas kernels, select_blocks(): pl.pallas_call(functools.partial(select_kernel, slots, a_slots.shape[0],...  1.33 us
  transfers between devices with their start and end apart: 13, of which 10 were waited for; matrix products, arithmetic and copies ran while one was open for 0% of the time, Pallas kernels for 22%

profile of v18, /device:TPU:0, one launch (start us, length us, event | category | flops | bytes accessed | tf_op | source)
XLA Modules:
  0.0 39.3 jit_solution(15034473446281807729)
XLA Ops:
  0.0 1.3 %select_blocks.1 = (s32[8]{0:T(128)S(4)}, bf16[2,64,4096]{2,1,0:T(8,128)(2,1)S(1)}, bf16[64,2048]{1,0:T(8,128)(2,1)S(1)}, bf16[64,2048]{1,0:T(8,128)(2,1)S(1)}, ...) custom-call(s32[4,16]{1,0:T(4,128)} %bitcast.12, s32[4,16]{1,0:T(4,128)} %bitcast.13, s32[16]{0:T(128)} %n_hbm.1, ...), custom_call_target="tpu_custom_call" | custom-call | tf_op jit(solution)/shard_map/select_blocks/pallas_call | solution.py:103
  1.3 0.5 %collective-permute-start.4 = (bf16[2,64,4096]{2,1,0:T(8,128)(2,1)S(1)}, bf16[2,64,4096]{2,1,0:T(8,128)(2,1)S(1)}, u32[]{:S(2)}, u32[]{:S(2)}) collective-permute-start(bf16[2,64,4096]{2,1,0:T(8,128)(2,1)S(1)} %get-tuple-element.34.refs_0_), channel_id=1, source_target_pairs={{0,1},{1,0},{2,3},{3,2},{4,5},{5,4},{6,7},{7,6},{8,9},{9,8},{10,11... | collective-permute-start | bytes 3145736 | tf_op jit(solution)/shard_map/ppermute | solution.py:463
  1.9 2.6 %collective-permute-start.2 = (bf16[64,2048]{1,0:T(8,128)(2,1)S(1)}, bf16[64,2048]{1,0:T(8,128)(2,1)S(1)}, u32[]{:S(2)}, u32[]{:S(2)}) collective-permute-start(bf16[64,2048]{1,0:T(8,128)(2,1)S(1)} %get-tuple-element.32), channel_id=1, source_target_pairs={{0,4},{4,8},{8,12},{12,0},{1,5},{5,9},{9,13},{13,1},{2,6},{6,10},{... | collective-permute-start | bytes 786440 | tf_op jit(solution)/shard_map/ppermute | solution.py:461
  4.5 2.1 %collective-permute-start.3 = (bf16[64,2048]{1,0:T(8,128)(2,1)S(1)}, bf16[64,2048]{1,0:T(8,128)(2,1)S(1)}, u32[]{:S(2)}, u32[]{:S(2)}) collective-permute-start(bf16[64,2048]{1,0:T(8,128)(2,1)S(1)} %get-tuple-element.33), channel_id=1, source_target_pairs={{0,12},{4,0},{8,4},{12,8},{1,13},{5,1},{9,5},{13,9},{2,14},{6,2},{... | collective-permute-start | bytes 786440 | tf_op jit(solution)/shard_map/ppermute | solution.py:461
  6.6 0.0 collective-permute-start
  6.6 3.8 %collective-permute-start.1 = (bf16[64,2048]{1,0:T(8,128)(2,1)S(1)}, bf16[64,2048]{1,0:T(8,128)(2,1)S(1)}, u32[]{:S(2)}, u32[]{:S(2)}) collective-permute-start(bf16[64,2048]{1,0:T(8,128)(2,1)S(1)} %get-tuple-element.31), channel_id=1, source_target_pairs={{0,12},{4,0},{8,4},{12,8},{1,13},{5,1},{9,5},{13,9},{2,14},{6,2},{... | collective-permute-start | bytes 786440 | tf_op jit(solution)/shard_map/ppermute | solution.py:461
  10.4 0.0 collective-permute-done.4.refs_1_
  10.4 5.0 %project_own.1 = (bf16[2,64,64,128]{3,2,1,0:T(8,128)(2,1)S(1)}, bf16[5,64,64,64]{3,2,1,0:T(8,128)(2,1)S(1)}, bf16[2,64,4096]{2,1,0:T(8,128)(2,1)S(1)}, bf16[256,...) custom-call(bf16[2,64,4096]{2,1,0:T(8,128)(2,1)S(1)} %get-tuple-element.34.refs_0_, ...), custom_call_target="tpu_custom_call" | custom-call | tf_op jit(solution)/shard_map/project_own/pallas_call | solution.py:361
  15.5 0.0 collective-permute-done.2.refs_0_
  15.5 3.9 %collective-permute-done.3.refs_1_ = bf16[64,2048]{1,0:T(8,128)(2,1)S(1)} collective-permute-done((bf16[64,2048]{1,0:T(8,128)(2,1)S(1)}, bf16[64,2048]{1,0:T(8,128)(2,1)S(1)}, u32[]{:S(2)}, u32[]{:S(2)}) %collective-permute-start.3) | collective-permute-done | bytes 262176 | tf_op jit(solution)/shard_map/ppermute | solution.py:461
  19.4 0.1 collective-permute-start.7
  19.5 0.5 %collective-permute-start.5 = (bf16[64,1024]{1,0:T(8,128)(2,1)S(1)}, bf16[64,1024]{1,0:T(8,128)(2,1)S(1)}, u32[]{:S(2)}, u32[]{:S(2)}) collective-permute-start(bf16[64,1024]{1,0:T(8,128)(2,1)S(1)} %get-tuple-element.56), channel_id=1, source_target_pairs={{0,1},{1,0},{2,3},{3,2},{4,5},{5,4},{6,7},{7,6},{8,9},{9,8},{10,11... | collective-permute-start | bytes 393224 | tf_op jit(solution)/shard_map/ppermute | solution.py:488
  20.0 0.1 collective-permute-start.8
  20.1 0.7 %collective-permute-done.7.refs_4_ = bf16[64,1024]{1,0:T(8,128)(2,1)S(1)} collective-permute-done((bf16[64,1024]{1,0:T(8,128)(2,1)S(1)}, bf16[64,1024]{1,0:T(8,128)(2,1)S(1)}, u32[]{:S(2)}, u32[]{:S(2)}) %collective-permute-start.7) | collective-permute-done | bytes 131104 | tf_op jit(solution)/shard_map/ppermute | solution.py:488
  20.8 0.1 collective-permute-start.6
  21.0 0.0 collective-permute-done.5.refs_2_
  21.0 0.4 %collective-permute-done.8.refs_5_ = bf16[64,1024]{1,0:T(8,128)(2,1)S(1)} collective-permute-done((bf16[64,1024]{1,0:T(8,128)(2,1)S(1)}, bf16[64,1024]{1,0:T(8,128)(2,1)S(1)}, u32[]{:S(2)}, u32[]{:S(2)}) %collective-permute-start.8) | collective-permute-done | bytes 131104 | tf_op jit(solution)/shard_map/ppermute | solution.py:488
  21.4 0.8 %collective-permute-done.6.refs_3_ = bf16[64,1024]{1,0:T(8,128)(2,1)S(1)} collective-permute-done((bf16[64,1024]{1,0:T(8,128)(2,1)S(1)}, bf16[64,1024]{1,0:T(8,128)(2,1)S(1)}, u32[]{:S(2)}, u32[]{:S(2)}) %collective-permute-start.6) | collective-permute-done | bytes 131104 | tf_op jit(solution)/shard_map/ppermute | solution.py:488
  22.2 1.7 %project_first.1 = (bf16[2,64,64,128]{3,2,1,0:T(8,128)(2,1)S(1)}, bf16[64,32,128]{2,1,0:T(8,128)(2,1)S(1)}) custom-call(bf16[64,2048]{1,0:T(8,128)(2,1)S(1)} %collective-permute-done.2.refs_0_, bf16[64,2048]{1,0:T(8,128)(2,1)S(1)} %collective-permute-done.3.refs_1_, ...), custom_call_target="tpu_custom_call", output_to_operand_aliasing={{0}: (8, {})} | custom-call | tf_op jit(solution)/shard_map/project_first/pallas_call | solution.py:361
  23.8 1.2 %collective-permute-done.refs_0_ = bf16[64,2048]{1,0:T(8,128)(2,1)S(1)} collective-permute-done((bf16[64,2048]{1,0:T(8,128)(2,1)S(1)}, bf16[64,2048]{1,0:T(8,128)(2,1)S(1)}, u32[]{:S(2)}, u32[]{:S(2)}) %collective-permute-start) | collective-permute-done | bytes 262176 | tf_op jit(solution)/shard_map/ppermute | solution.py:461
  25.0 4.7 %collective-permute-done.1.refs_1_ = bf16[64,2048]{1,0:T(8,128)(2,1)S(1)} collective-permute-done((bf16[64,2048]{1,0:T(8,128)(2,1)S(1)}, bf16[64,2048]{1,0:T(8,128)(2,1)S(1)}, u32[]{:S(2)}, u32[]{:S(2)}) %collective-permute-start.1) | collective-permute-done | bytes 262176 | tf_op jit(solution)/shard_map/ppermute | solution.py:461
  29.7 0.0 collective-permute-start.9
  29.7 0.5 %collective-permute-start.10 = (bf16[64,2048]{1,0:T(8,128)(2,1)S(1)}, bf16[64,2048]{1,0:T(8,128)(2,1)S(1)}, u32[]{:S(2)}, u32[]{:S(2)}) collective-permute-start(bf16[64,2048]{1,0:T(8,128)(2,1)S(1)} %collective-permute-done.1.refs_1_), channel_id=1, source_target_pairs={{0,1},{1,0},{2,3},{3,2},{4,5},{5,4},{6,7},{7,6},{8,9},{9,8},{10,11... | collective-permute-start | bytes 786440 | tf_op jit(solution)/shard_map/ppermute | solution.py:488
  30.2 1.0 %collective-permute-done.9.refs_2_ = bf16[64,2048]{1,0:T(8,128)(2,1)S(1)} collective-permute-done((bf16[64,2048]{1,0:T(8,128)(2,1)S(1)}, bf16[64,2048]{1,0:T(8,128)(2,1)S(1)}, u32[]{:S(2)}, u32[]{:S(2)}) %collective-permute-start.9) | collective-permute-done | bytes 262176 | tf_op jit(solution)/shard_map/ppermute | solution.py:488
  31.3 0.4 collective-permute-done.10.refs_3_
  31.6 2.9 %project_last.1 = (bf16[2,64,64,128]{3,2,1,0:T(8,128)(2,1)S(1)}, bf16[5,64,64,64]{3,2,1,0:T(8,128)(2,1)S(1)}, bf16[64,4096]{1,0:T(8,128)(2,1)S(1)}) custom-call(s32[8]{0:T(128)S(4)} %get-tuple-element.29.picks_ref, bf16[64,2048]{1,0:T(8,128)(2,1)S(1)} %collective-permute-done.refs_0_, ...), custom_call_target="tpu_custom_call", output_to_operand_aliasing={{0}: (8, {}), {1}: (9, {})} | custom-call | tf_op jit(solution)/shard_map/project_last/pallas_call | solution.py:361
  34.6 0.2 collective-permute-start.12
  34.8 1.0 %triplets.1.mine_ref = bf16[64,4096]{1,0:T(8,128)(2,1)S(1)} custom-call(s32[8]{0:T(128)S(4)} %get-tuple-element.29.picks_ref, bf16[2,64,64,128]{3,2,1,0:T(8,128)(2,1)S(1)} %get-tuple-element.49.l_ref, bf16[5,64,64,64]{3,2,1,0:T(8,128)(2,1)S(1)} %get-tuple-element.50.turned_ref), custom_call_target="tpu_custom_call" | custom-call | tf_op jit(solution)/shard_map/triplets/pallas_call | solution.py:361
  35.8 0.4 %collective-permute-start.11 = (bf16[64,4096]{1,0:T(8,128)(2,1)S(1)}, bf16[64,4096]{1,0:T(8,128)(2,1)S(1)}, u32[]{:S(2)}, u32[]{:S(2)}) collective-permute-start(bf16[64,4096]{1,0:T(8,128)(2,1)S(1)} %triplets.1.mine_ref), channel_id=1, source_target_pairs={{0,1},{1,0},{2,3},{3,2},{4,5},{5,4},{6,7},{7,6},{8,9},{9,8},{10,11... | collective-permute-start | bytes 1572872 | tf_op jit(solution)/shard_map/ppermute | solution.py:525
  36.2 0.3 collective-permute-done.12.theirs_ref
  36.5 0.8 %finish.2.refs_0_ = bf16[64,4096]{1,0:T(8,128)(2,1)S(1)} custom-call(bf16[64,4096]{1,0:T(8,128)(2,1)S(1)} %get-tuple-element.47.mine_ref, bf16[64,4096]{1,0:T(8,128)(2,1)S(1)} %collective-permute-done.12.theirs_ref, bf16[2,64,4096]{2,1,0:T(8,128)(2,1)S(1)} %get-tuple-element.51.gate_ref, bf16[64,128]{1,0:T(8,128)(2,1)S(1)} %get-tuple-element.52.w_ref), custom_call_target="tpu_custom_call" | custom-call | tf_op jit(solution)/shard_map/finish/pallas_call | solution.py:415
  37.4 0.4 %collective-permute-done.11.theirs_ref = bf16[64,4096]{1,0:T(8,128)(2,1)S(1)} collective-permute-done((bf16[64,4096]{1,0:T(8,128)(2,1)S(1)}, bf16[64,4096]{1,0:T(8,128)(2,1)S(1)}, u32[]{:S(2)}, u32[]{:S(2)}) %collective-permute-start.11) | collective-permute-done | bytes 524320 | tf_op jit(solution)/shard_map/ppermute | solution.py:525
  37.8 1.5 %finish.3 = bf16[2,64,4096]{2,1,0:T(8,128)(2,1)} custom-call(bf16[64,4096]{1,0:T(8,128)(2,1)S(1)} %triplets.1.mine_ref, bf16[64,4096]{1,0:T(8,128)(2,1)S(1)} %collective-permute-done.11.theirs_ref, bf16[2,64,4096]{2,1,0:T(8,128)(2,1)S(1)} %get-tuple-element.51.gate_ref, bf16[64,128]{1,0:T(8,128)(2,1)S(1)} %get-tuple-element.52.w_ref, ...), custom_call_target="tpu_custom_call" | custom-call | tf_op jit(solution)/shard_map/finish/pallas_call | solution.py:415
  (2 shorter events, 0.0 us)
Async XLA Ops:
  1.3 9.1 %collective-permute-start.4 = (bf16[2,64,4096]{2,1,0:T(8,128)(2,1)S(1)}, bf16[2,64,4096]{2,1,0:T(8,128)(2,1)S(1)}, u32[]{:S(2)}, u32[]{:S(2)}) collective-permute-start(bf16[2,64,4096]{2,1,0:T(8,128)(2,1)S(1)} %get-tuple-element.34.refs_0_), channel_id=1, source_target_pairs={{0,1},{1,0},{2,3},{3,2},{4,5},{5,4},{6,7},{7,6},{8,9},{9,8},{10,11... | collective-permute-start | bytes 3145736 | tf_op jit(solution)/shard_map/ppermute | solution.py:463
  1.9 13.6 %collective-permute-start.2 = (bf16[64,2048]{1,0:T(8,128)(2,1)S(1)}, bf16[64,2048]{1,0:T(8,128)(2,1)S(1)}, u32[]{:S(2)}, u32[]{:S(2)}) collective-permute-start(bf16[64,2048]{1,0:T(8,128)(2,1)S(1)} %get-tuple-element.32), channel_id=1, source_target_pairs={{0,4},{4,8},{8,12},{12,0},{1,5},{5,9},{9,13},{13,1},{2,6},{6,10},{... | collective-permute-start | bytes 786440 | tf_op jit(solution)/shard_map/ppermute | solution.py:461
  4.5 14.9 %collective-permute-start.3 = (bf16[64,2048]{1,0:T(8,128)(2,1)S(1)}, bf16[64,2048]{1,0:T(8,128)(2,1)S(1)}, u32[]{:S(2)}, u32[]{:S(2)}) collective-permute-start(bf16[64,2048]{1,0:T(8,128)(2,1)S(1)} %get-tuple-element.33), channel_id=1, source_target_pairs={{0,12},{4,0},{8,4},{12,8},{1,13},{5,1},{9,5},{13,9},{2,14},{6,2},{... | collective-permute-start | bytes 786440 | tf_op jit(solution)/shard_map/ppermute | solution.py:461
  6.6 18.4 %collective-permute-start = (bf16[64,2048]{1,0:T(8,128)(2,1)S(1)}, bf16[64,2048]{1,0:T(8,128)(2,1)S(1)}, u32[]{:S(2)}, u32[]{:S(2)}) collective-permute-start(bf16[64,2048]{1,0:T(8,128)(2,1)S(1)} %get-tuple-element.30), channel_id=1, source_target_pairs={{0,4},{4,8},{8,12},{12,0},{1,5},{5,9},{9,13},{13,1},{2,6},{6,10},{... | collective-permute-start | bytes 786440 | tf_op jit(solution)/shard_map/ppermute | solution.py:461
  6.6 23.1 %collective-permute-start.1 = (bf16[64,2048]{1,0:T(8,128)(2,1)S(1)}, bf16[64,2048]{1,0:T(8,128)(2,1)S(1)}, u32[]{:S(2)}, u32[]{:S(2)}) collective-permute-start(bf16[64,2048]{1,0:T(8,128)(2,1)S(1)} %get-tuple-element.31), channel_id=1, source_target_pairs={{0,12},{4,0},{8,4},{12,8},{1,13},{5,1},{9,5},{13,9},{2,14},{6,2},{... | collective-permute-start | bytes 786440 | tf_op jit(solution)/shard_map/ppermute | solution.py:461
  19.4 1.4 %collective-permute-start.7 = (bf16[64,1024]{1,0:T(8,128)(2,1)S(1)}, bf16[64,1024]{1,0:T(8,128)(2,1)S(1)}, u32[]{:S(2)}, u32[]{:S(2)}) collective-permute-start(bf16[64,1024]{1,0:T(8,128)(2,1)S(1)} %get-tuple-element.55), channel_id=1, source_target_pairs={{0,1},{1,0},{2,3},{3,2},{4,5},{5,4},{6,7},{7,6},{8,9},{9,8},{10,11... | collective-permute-start | bytes 393224 | tf_op jit(solution)/shard_map/ppermute | solution.py:488
  19.5 1.5 %collective-permute-start.5 = (bf16[64,1024]{1,0:T(8,128)(2,1)S(1)}, bf16[64,1024]{1,0:T(8,128)(2,1)S(1)}, u32[]{:S(2)}, u32[]{:S(2)}) collective-permute-start(bf16[64,1024]{1,0:T(8,128)(2,1)S(1)} %get-tuple-element.56), channel_id=1, source_target_pairs={{0,1},{1,0},{2,3},{3,2},{4,5},{5,4},{6,7},{7,6},{8,9},{9,8},{10,11... | collective-permute-start | bytes 393224 | tf_op jit(solution)/shard_map/ppermute | solution.py:488
  20.0 1.4 %collective-permute-start.8 = (bf16[64,1024]{1,0:T(8,128)(2,1)S(1)}, bf16[64,1024]{1,0:T(8,128)(2,1)S(1)}, u32[]{:S(2)}, u32[]{:S(2)}) collective-permute-start(bf16[64,1024]{1,0:T(8,128)(2,1)S(1)} %get-tuple-element.53), channel_id=1, source_target_pairs={{0,1},{1,0},{2,3},{3,2},{4,5},{5,4},{6,7},{7,6},{8,9},{9,8},{10,11... | collective-permute-start | bytes 393224 | tf_op jit(solution)/shard_map/ppermute | solution.py:488
  20.8 1.3 %collective-permute-start.6 = (bf16[64,1024]{1,0:T(8,128)(2,1)S(1)}, bf16[64,1024]{1,0:T(8,128)(2,1)S(1)}, u32[]{:S(2)}, u32[]{:S(2)}) collective-permute-start(bf16[64,1024]{1,0:T(8,128)(2,1)S(1)} %get-tuple-element.54), channel_id=1, source_target_pairs={{0,1},{1,0},{2,3},{3,2},{4,5},{5,4},{6,7},{7,6},{8,9},{9,8},{10,11... | collective-permute-start | bytes 393224 | tf_op jit(solution)/shard_map/ppermute | solution.py:488
  29.7 1.5 %collective-permute-start.9 = (bf16[64,2048]{1,0:T(8,128)(2,1)S(1)}, bf16[64,2048]{1,0:T(8,128)(2,1)S(1)}, u32[]{:S(2)}, u32[]{:S(2)}) collective-permute-start(bf16[64,2048]{1,0:T(8,128)(2,1)S(1)} %collective-permute-done.refs_0_), channel_id=1, source_target_pairs={{0,1},{1,0},{2,3},{3,2},{4,5},{5,4},{6,7},{7,6},{8,9},{9,8},{10,11... | collective-permute-start | bytes 786440 | tf_op jit(solution)/shard_map/ppermute | solution.py:488
  29.7 1.9 %collective-permute-start.10 = (bf16[64,2048]{1,0:T(8,128)(2,1)S(1)}, bf16[64,2048]{1,0:T(8,128)(2,1)S(1)}, u32[]{:S(2)}, u32[]{:S(2)}) collective-permute-start(bf16[64,2048]{1,0:T(8,128)(2,1)S(1)} %collective-permute-done.1.refs_1_), channel_id=1, source_target_pairs={{0,1},{1,0},{2,3},{3,2},{4,5},{5,4},{6,7},{7,6},{8,9},{9,8},{10,11... | collective-permute-start | bytes 786440 | tf_op jit(solution)/shard_map/ppermute | solution.py:488
  34.6 2.0 %collective-permute-start.12 = (bf16[64,4096]{1,0:T(8,128)(2,1)S(1)}, bf16[64,4096]{1,0:T(8,128)(2,1)S(1)}, u32[]{:S(2)}, u32[]{:S(2)}) collective-permute-start(bf16[64,4096]{1,0:T(8,128)(2,1)S(1)} %get-tuple-element.47.mine_ref), channel_id=1, source_target_pairs={{0,1},{1,0},{2,3},{3,2},{4,5},{5,4},{6,7},{7,6},{8,9},{9,8},{10,11... | collective-permute-start | bytes 1572872 | tf_op jit(solution)/shard_map/ppermute | solution.py:514
  35.8 2.0 %collective-permute-start.11 = (bf16[64,4096]{1,0:T(8,128)(2,1)S(1)}, bf16[64,4096]{1,0:T(8,128)(2,1)S(1)}, u32[]{:S(2)}, u32[]{:S(2)}) collective-permute-start(bf16[64,4096]{1,0:T(8,128)(2,1)S(1)} %triplets.1.mine_ref), channel_id=1, source_target_pairs={{0,1},{1,0},{2,3},{3,2},{4,5},{5,4},{6,7},{7,6},{8,9},{9,8},{10,11... | collective-permute-start | bytes 1572872 | tf_op jit(solution)/shard_map/ppermute | solution.py:525

commit v19 on v18

--- a/solution.py
+++ b/solution.py
@@ -519,7 +519,7 @@
             "triplets",
             [picks, lefts, rights],
             [pltpu.VMEM((half, cells), BF16)],
-            acc_scratch(16),
+            acc_scratch(16) * 2,
             smem=1,
         )
         updates.append((update, lax.ppermute(update, "chan", swap)))

time: 39.5 us -> 39.5 us (level)
  no operation moved by 1% of the time
where the time goes in v19:
time: 39.5 us; the launch traced here: 39.3 us
  Pallas kernels  14.3 us (36%)
  waiting for transfers between devices  13.8 us (35%)
  starting transfers between devices  11.1 us (28%)
    pallas_call x4, Pallas kernels, call(): pl.pallas_call(kernel, in_specs=[pl.BlockSpec(memory_space=space) for spa...  10.6 us
    ppermute x4, waiting for transfers between devices, per_device(): moved[which] = lax.ppermute(chosen[2 * n + which], 'row', (up, down)[which])  9.81 us
    ppermute x4, starting transfers between devices, per_device(): moved[which] = lax.ppermute(chosen[2 * n + which], 'row', (up, down)[which])  8.57 us
    ppermute x6, waiting for transfers between devices, per_device(): lax.ppermute(lax.slice_in_dim(value, at, at + wide, axis=1), 'chan', swap)  3.27 us
    pallas_call x2, Pallas kernels, finish(): pl.pallas_call(functools.partial(finish_kernel, s, mine.shape[1], 4), in_...  2.33 us
    ppermute x6, starting transfers between devices, per_device(): lax.ppermute(lax.slice_in_dim(value, at, at + wide, axis=1), 'chan', swap)  1.37 us
    pallas_call x1, Pallas kernels, select_blocks(): pl.pallas_call(functools.partial(select_kernel, slots, a_slots.shape[0],...  1.33 us
  transfers between devices with their start and end apart: 13, of which 10 were waited for; matrix products, arithmetic and copies ran while one was open for 0% of the time, Pallas kernels for 22%

profile of v19, /device:TPU:0, one launch (start us, length us, event | category | flops | bytes accessed | tf_op | source)
XLA Modules:
  0.0 39.3 jit_solution(2502977453729208893)
XLA Ops:
  0.0 1.3 %select_blocks.1 = (s32[8]{0:T(128)S(4)}, bf16[2,64,4096]{2,1,0:T(8,128)(2,1)S(1)}, bf16[64,2048]{1,0:T(8,128)(2,1)S(1)}, bf16[64,2048]{1,0:T(8,128)(2,1)S(1)}, ...) custom-call(s32[4,16]{1,0:T(4,128)} %bitcast.12, s32[4,16]{1,0:T(4,128)} %bitcast.13, s32[16]{0:T(128)} %n_hbm.1, ...), custom_call_target="tpu_custom_call" | custom-call | tf_op jit(solution)/shard_map/select_blocks/pallas_call | solution.py:103
  1.3 0.5 %collective-permute-start.4 = (bf16[2,64,4096]{2,1,0:T(8,128)(2,1)S(1)}, bf16[2,64,4096]{2,1,0:T(8,128)(2,1)S(1)}, u32[]{:S(2)}, u32[]{:S(2)}) collective-permute-start(bf16[2,64,4096]{2,1,0:T(8,128)(2,1)S(1)} %get-tuple-element.34.refs_0_), channel_id=1, source_target_pairs={{0,1},{1,0},{2,3},{3,2},{4,5},{5,4},{6,7},{7,6},{8,9},{9,8},{10,11... | collective-permute-start | bytes 3145736 | tf_op jit(solution)/shard_map/ppermute | solution.py:463
  1.9 2.6 %collective-permute-start.2 = (bf16[64,2048]{1,0:T(8,128)(2,1)S(1)}, bf16[64,2048]{1,0:T(8,128)(2,1)S(1)}, u32[]{:S(2)}, u32[]{:S(2)}) collective-permute-start(bf16[64,2048]{1,0:T(8,128)(2,1)S(1)} %get-tuple-element.32), channel_id=1, source_target_pairs={{0,4},{4,8},{8,12},{12,0},{1,5},{5,9},{9,13},{13,1},{2,6},{6,10},{... | collective-permute-start | bytes 786440 | tf_op jit(solution)/shard_map/ppermute | solution.py:461
  4.5 2.1 %collective-permute-start.3 = (bf16[64,2048]{1,0:T(8,128)(2,1)S(1)}, bf16[64,2048]{1,0:T(8,128)(2,1)S(1)}, u32[]{:S(2)}, u32[]{:S(2)}) collective-permute-start(bf16[64,2048]{1,0:T(8,128)(2,1)S(1)} %get-tuple-element.33), channel_id=1, source_target_pairs={{0,12},{4,0},{8,4},{12,8},{1,13},{5,1},{9,5},{13,9},{2,14},{6,2},{... | collective-permute-start | bytes 786440 | tf_op jit(solution)/shard_map/ppermute | solution.py:461
  6.6 0.0 collective-permute-start
  6.6 3.8 %collective-permute-start.1 = (bf16[64,2048]{1,0:T(8,128)(2,1)S(1)}, bf16[64,2048]{1,0:T(8,128)(2,1)S(1)}, u32[]{:S(2)}, u32[]{:S(2)}) collective-permute-start(bf16[64,2048]{1,0:T(8,128)(2,1)S(1)} %get-tuple-element.31), channel_id=1, source_target_pairs={{0,12},{4,0},{8,4},{12,8},{1,13},{5,1},{9,5},{13,9},{2,14},{6,2},{... | collective-permute-start | bytes 786440 | tf_op jit(solution)/shard_map/ppermute | solution.py:461
  10.4 0.0 collective-permute-done.4.refs_1_
  10.4 5.0 %project_own.1 = (bf16[2,64,64,128]{3,2,1,0:T(8,128)(2,1)S(1)}, bf16[5,64,64,64]{3,2,1,0:T(8,128)(2,1)S(1)}, bf16[2,64,4096]{2,1,0:T(8,128)(2,1)S(1)}, bf16[256,...) custom-call(bf16[2,64,4096]{2,1,0:T(8,128)(2,1)S(1)} %get-tuple-element.34.refs_0_, ...), custom_call_target="tpu_custom_call" | custom-call | tf_op jit(solution)/shard_map/project_own/pallas_call | solution.py:361
  15.5 0.0 collective-permute-done.2.refs_0_
  15.5 3.9 %collective-permute-done.3.refs_1_ = bf16[64,2048]{1,0:T(8,128)(2,1)S(1)} collective-permute-done((bf16[64,2048]{1,0:T(8,128)(2,1)S(1)}, bf16[64,2048]{1,0:T(8,128)(2,1)S(1)}, u32[]{:S(2)}, u32[]{:S(2)}) %collective-permute-start.3) | collective-permute-done | bytes 262176 | tf_op jit(solution)/shard_map/ppermute | solution.py:461
  19.4 0.1 collective-permute-start.7
  19.5 0.5 %collective-permute-start.5 = (bf16[64,1024]{1,0:T(8,128)(2,1)S(1)}, bf16[64,1024]{1,0:T(8,128)(2,1)S(1)}, u32[]{:S(2)}, u32[]{:S(2)}) collective-permute-start(bf16[64,1024]{1,0:T(8,128)(2,1)S(1)} %get-tuple-element.56), channel_id=1, source_target_pairs={{0,1},{1,0},{2,3},{3,2},{4,5},{5,4},{6,7},{7,6},{8,9},{9,8},{10,11... | collective-permute-start | bytes 393224 | tf_op jit(solution)/shard_map/ppermute | solution.py:488
  20.0 0.1 collective-permute-start.8
  20.1 0.7 %collective-permute-done.7.refs_4_ = bf16[64,1024]{1,0:T(8,128)(2,1)S(1)} collective-permute-done((bf16[64,1024]{1,0:T(8,128)(2,1)S(1)}, bf16[64,1024]{1,0:T(8,128)(2,1)S(1)}, u32[]{:S(2)}, u32[]{:S(2)}) %collective-permute-start.7) | collective-permute-done | bytes 131104 | tf_op jit(solution)/shard_map/ppermute | solution.py:488
  20.8 0.1 collective-permute-start.6
  21.0 0.0 collective-permute-done.5.refs_2_
  21.0 0.4 %collective-permute-done.8.refs_5_ = bf16[64,1024]{1,0:T(8,128)(2,1)S(1)} collective-permute-done((bf16[64,1024]{1,0:T(8,128)(2,1)S(1)}, bf16[64,1024]{1,0:T(8,128)(2,1)S(1)}, u32[]{:S(2)}, u32[]{:S(2)}) %collective-permute-start.8) | collective-permute-done | bytes 131104 | tf_op jit(solution)/shard_map/ppermute | solution.py:488
  21.4 0.8 %collective-permute-done.6.refs_3_ = bf16[64,1024]{1,0:T(8,128)(2,1)S(1)} collective-permute-done((bf16[64,1024]{1,0:T(8,128)(2,1)S(1)}, bf16[64,1024]{1,0:T(8,128)(2,1)S(1)}, u32[]{:S(2)}, u32[]{:S(2)}) %collective-permute-start.6) | collective-permute-done | bytes 131104 | tf_op jit(solution)/shard_map/ppermute | solution.py:488
  22.2 1.7 %project_first.1 = (bf16[2,64,64,128]{3,2,1,0:T(8,128)(2,1)S(1)}, bf16[64,32,128]{2,1,0:T(8,128)(2,1)S(1)}) custom-call(bf16[64,2048]{1,0:T(8,128)(2,1)S(1)} %collective-permute-done.2.refs_0_, bf16[64,2048]{1,0:T(8,128)(2,1)S(1)} %collective-permute-done.3.refs_1_, ...), custom_call_target="tpu_custom_call", output_to_operand_aliasing={{0}: (8, {})} | custom-call | tf_op jit(solution)/shard_map/project_first/pallas_call | solution.py:361
  23.8 1.2 %collective-permute-done.refs_0_ = bf16[64,2048]{1,0:T(8,128)(2,1)S(1)} collective-permute-done((bf16[64,2048]{1,0:T(8,128)(2,1)S(1)}, bf16[64,2048]{1,0:T(8,128)(2,1)S(1)}, u32[]{:S(2)}, u32[]{:S(2)}) %collective-permute-start) | collective-permute-done | bytes 262176 | tf_op jit(solution)/shard_map/ppermute | solution.py:461
  25.0 4.7 %collective-permute-done.1.refs_1_ = bf16[64,2048]{1,0:T(8,128)(2,1)S(1)} collective-permute-done((bf16[64,2048]{1,0:T(8,128)(2,1)S(1)}, bf16[64,2048]{1,0:T(8,128)(2,1)S(1)}, u32[]{:S(2)}, u32[]{:S(2)}) %collective-permute-start.1) | collective-permute-done | bytes 262176 | tf_op jit(solution)/shard_map/ppermute | solution.py:461
  29.7 0.0 collective-permute-start.9
  29.7 0.5 %collective-permute-start.10 = (bf16[64,2048]{1,0:T(8,128)(2,1)S(1)}, bf16[64,2048]{1,0:T(8,128)(2,1)S(1)}, u32[]{:S(2)}, u32[]{:S(2)}) collective-permute-start(bf16[64,2048]{1,0:T(8,128)(2,1)S(1)} %collective-permute-done.1.refs_1_), channel_id=1, source_target_pairs={{0,1},{1,0},{2,3},{3,2},{4,5},{5,4},{6,7},{7,6},{8,9},{9,8},{10,11... | collective-permute-start | bytes 786440 | tf_op jit(solution)/shard_map/ppermute | solution.py:488
  30.2 1.0 %collective-permute-done.9.refs_2_ = bf16[64,2048]{1,0:T(8,128)(2,1)S(1)} collective-permute-done((bf16[64,2048]{1,0:T(8,128)(2,1)S(1)}, bf16[64,2048]{1,0:T(8,128)(2,1)S(1)}, u32[]{:S(2)}, u32[]{:S(2)}) %collective-permute-start.9) | collective-permute-done | bytes 262176 | tf_op jit(solution)/shard_map/ppermute | solution.py:488
  31.3 0.4 collective-permute-done.10.refs_3_
  31.6 2.9 %project_last.1 = (bf16[2,64,64,128]{3,2,1,0:T(8,128)(2,1)S(1)}, bf16[5,64,64,64]{3,2,1,0:T(8,128)(2,1)S(1)}, bf16[64,4096]{1,0:T(8,128)(2,1)S(1)}) custom-call(s32[8]{0:T(128)S(4)} %get-tuple-element.29.picks_ref, bf16[64,2048]{1,0:T(8,128)(2,1)S(1)} %collective-permute-done.refs_0_, ...), custom_call_target="tpu_custom_call", output_to_operand_aliasing={{0}: (8, {}), {1}: (9, {})} | custom-call | tf_op jit(solution)/shard_map/project_last/pallas_call | solution.py:361
  34.6 0.2 collective-permute-start.12
  34.8 1.0 %triplets.1.mine_ref = bf16[64,4096]{1,0:T(8,128)(2,1)S(1)} custom-call(s32[8]{0:T(128)S(4)} %get-tuple-element.29.picks_ref, bf16[2,64,64,128]{3,2,1,0:T(8,128)(2,1)S(1)} %get-tuple-element.49.l_ref, bf16[5,64,64,64]{3,2,1,0:T(8,128)(2,1)S(1)} %get-tuple-element.50.turned_ref), custom_call_target="tpu_custom_call" | custom-call | tf_op jit(solution)/shard_map/triplets/pallas_call | solution.py:361
  35.8 0.4 %collective-permute-start.11 = (bf16[64,4096]{1,0:T(8,128)(2,1)S(1)}, bf16[64,4096]{1,0:T(8,128)(2,1)S(1)}, u32[]{:S(2)}, u32[]{:S(2)}) collective-permute-start(bf16[64,4096]{1,0:T(8,128)(2,1)S(1)} %triplets.1.mine_ref), channel_id=1, source_target_pairs={{0,1},{1,0},{2,3},{3,2},{4,5},{5,4},{6,7},{7,6},{8,9},{9,8},{10,11... | collective-permute-start | bytes 1572872 | tf_op jit(solution)/shard_map/ppermute | solution.py:525
  36.2 0.3 collective-permute-done.12.theirs_ref
  36.5 0.8 %finish.2.refs_0_ = bf16[64,4096]{1,0:T(8,128)(2,1)S(1)} custom-call(bf16[64,4096]{1,0:T(8,128)(2,1)S(1)} %get-tuple-element.47.mine_ref, bf16[64,4096]{1,0:T(8,128)(2,1)S(1)} %collective-permute-done.12.theirs_ref, bf16[2,64,4096]{2,1,0:T(8,128)(2,1)S(1)} %get-tuple-element.51.gate_ref, bf16[64,128]{1,0:T(8,128)(2,1)S(1)} %get-tuple-element.52.w_ref), custom_call_target="tpu_custom_call" | custom-call | tf_op jit(solution)/shard_map/finish/pallas_call | solution.py:415
  37.4 0.4 %collective-permute-done.11.theirs_ref = bf16[64,4096]{1,0:T(8,128)(2,1)S(1)} collective-permute-done((bf16[64,4096]{1,0:T(8,128)(2,1)S(1)}, bf16[64,4096]{1,0:T(8,128)(2,1)S(1)}, u32[]{:S(2)}, u32[]{:S(2)}) %collective-permute-start.11) | collective-permute-done | bytes 524320 | tf_op jit(solution)/shard_map/ppermute | solution.py:525
  37.8 1.5 %finish.3 = bf16[2,64,4096]{2,1,0:T(8,128)(2,1)} custom-call(bf16[64,4096]{1,0:T(8,128)(2,1)S(1)} %triplets.1.mine_ref, bf16[64,4096]{1,0:T(8,128)(2,1)S(1)} %collective-permute-done.11.theirs_ref, bf16[2,64,4096]{2,1,0:T(8,128)(2,1)S(1)} %get-tuple-element.51.gate_ref, bf16[64,128]{1,0:T(8,128)(2,1)S(1)} %get-tuple-element.52.w_ref, ...), custom_call_target="tpu_custom_call" | custom-call | tf_op jit(solution)/shard_map/finish/pallas_call | solution.py:415
  (2 shorter events, 0.0 us)
Async XLA Ops:
  1.3 9.1 %collective-permute-start.4 = (bf16[2,64,4096]{2,1,0:T(8,128)(2,1)S(1)}, bf16[2,64,4096]{2,1,0:T(8,128)(2,1)S(1)}, u32[]{:S(2)}, u32[]{:S(2)}) collective-permute-start(bf16[2,64,4096]{2,1,0:T(8,128)(2,1)S(1)} %get-tuple-element.34.refs_0_), channel_id=1, source_target_pairs={{0,1},{1,0},{2,3},{3,2},{4,5},{5,4},{6,7},{7,6},{8,9},{9,8},{10,11... | collective-permute-start | bytes 3145736 | tf_op jit(solution)/shard_map/ppermute | solution.py:463
  1.9 13.6 %collective-permute-start.2 = (bf16[64,2048]{1,0:T(8,128)(2,1)S(1)}, bf16[64,2048]{1,0:T(8,128)(2,1)S(1)}, u32[]{:S(2)}, u32[]{:S(2)}) collective-permute-start(bf16[64,2048]{1,0:T(8,128)(2,1)S(1)} %get-tuple-element.32), channel_id=1, source_target_pairs={{0,4},{4,8},{8,12},{12,0},{1,5},{5,9},{9,13},{13,1},{2,6},{6,10},{... | collective-permute-start | bytes 786440 | tf_op jit(solution)/shard_map/ppermute | solution.py:461
  4.5 14.9 %collective-permute-start.3 = (bf16[64,2048]{1,0:T(8,128)(2,1)S(1)}, bf16[64,2048]{1,0:T(8,128)(2,1)S(1)}, u32[]{:S(2)}, u32[]{:S(2)}) collective-permute-start(bf16[64,2048]{1,0:T(8,128)(2,1)S(1)} %get-tuple-element.33), channel_id=1, source_target_pairs={{0,12},{4,0},{8,4},{12,8},{1,13},{5,1},{9,5},{13,9},{2,14},{6,2},{... | collective-permute-start | bytes 786440 | tf_op jit(solution)/shard_map/ppermute | solution.py:461
  6.6 18.4 %collective-permute-start = (bf16[64,2048]{1,0:T(8,128)(2,1)S(1)}, bf16[64,2048]{1,0:T(8,128)(2,1)S(1)}, u32[]{:S(2)}, u32[]{:S(2)}) collective-permute-start(bf16[64,2048]{1,0:T(8,128)(2,1)S(1)} %get-tuple-element.30), channel_id=1, source_target_pairs={{0,4},{4,8},{8,12},{12,0},{1,5},{5,9},{9,13},{13,1},{2,6},{6,10},{... | collective-permute-start | bytes 786440 | tf_op jit(solution)/shard_map/ppermute | solution.py:461
  6.6 23.1 %collective-permute-start.1 = (bf16[64,2048]{1,0:T(8,128)(2,1)S(1)}, bf16[64,2048]{1,0:T(8,128)(2,1)S(1)}, u32[]{:S(2)}, u32[]{:S(2)}) collective-permute-start(bf16[64,2048]{1,0:T(8,128)(2,1)S(1)} %get-tuple-element.31), channel_id=1, source_target_pairs={{0,12},{4,0},{8,4},{12,8},{1,13},{5,1},{9,5},{13,9},{2,14},{6,2},{... | collective-permute-start | bytes 786440 | tf_op jit(solution)/shard_map/ppermute | solution.py:461
  19.4 1.4 %collective-permute-start.7 = (bf16[64,1024]{1,0:T(8,128)(2,1)S(1)}, bf16[64,1024]{1,0:T(8,128)(2,1)S(1)}, u32[]{:S(2)}, u32[]{:S(2)}) collective-permute-start(bf16[64,1024]{1,0:T(8,128)(2,1)S(1)} %get-tuple-element.55), channel_id=1, source_target_pairs={{0,1},{1,0},{2,3},{3,2},{4,5},{5,4},{6,7},{7,6},{8,9},{9,8},{10,11... | collective-permute-start | bytes 393224 | tf_op jit(solution)/shard_map/ppermute | solution.py:488
  19.5 1.5 %collective-permute-start.5 = (bf16[64,1024]{1,0:T(8,128)(2,1)S(1)}, bf16[64,1024]{1,0:T(8,128)(2,1)S(1)}, u32[]{:S(2)}, u32[]{:S(2)}) collective-permute-start(bf16[64,1024]{1,0:T(8,128)(2,1)S(1)} %get-tuple-element.56), channel_id=1, source_target_pairs={{0,1},{1,0},{2,3},{3,2},{4,5},{5,4},{6,7},{7,6},{8,9},{9,8},{10,11... | collective-permute-start | bytes 393224 | tf_op jit(solution)/shard_map/ppermute | solution.py:488
  20.0 1.4 %collective-permute-start.8 = (bf16[64,1024]{1,0:T(8,128)(2,1)S(1)}, bf16[64,1024]{1,0:T(8,128)(2,1)S(1)}, u32[]{:S(2)}, u32[]{:S(2)}) collective-permute-start(bf16[64,1024]{1,0:T(8,128)(2,1)S(1)} %get-tuple-element.53), channel_id=1, source_target_pairs={{0,1},{1,0},{2,3},{3,2},{4,5},{5,4},{6,7},{7,6},{8,9},{9,8},{10,11... | collective-permute-start | bytes 393224 | tf_op jit(solution)/shard_map/ppermute | solution.py:488
  20.8 1.3 %collective-permute-start.6 = (bf16[64,1024]{1,0:T(8,128)(2,1)S(1)}, bf16[64,1024]{1,0:T(8,128)(2,1)S(1)}, u32[]{:S(2)}, u32[]{:S(2)}) collective-permute-start(bf16[64,1024]{1,0:T(8,128)(2,1)S(1)} %get-tuple-element.54), channel_id=1, source_target_pairs={{0,1},{1,0},{2,3},{3,2},{4,5},{5,4},{6,7},{7,6},{8,9},{9,8},{10,11... | collective-permute-start | bytes 393224 | tf_op jit(solution)/shard_map/ppermute | solution.py:488
  29.7 1.5 %collective-permute-start.9 = (bf16[64,2048]{1,0:T(8,128)(2,1)S(1)}, bf16[64,2048]{1,0:T(8,128)(2,1)S(1)}, u32[]{:S(2)}, u32[]{:S(2)}) collective-permute-start(bf16[64,2048]{1,0:T(8,128)(2,1)S(1)} %collective-permute-done.refs_0_), channel_id=1, source_target_pairs={{0,1},{1,0},{2,3},{3,2},{4,5},{5,4},{6,7},{7,6},{8,9},{9,8},{10,11... | collective-permute-start | bytes 786440 | tf_op jit(solution)/shard_map/ppermute | solution.py:488
  29.7 1.9 %collective-permute-start.10 = (bf16[64,2048]{1,0:T(8,128)(2,1)S(1)}, bf16[64,2048]{1,0:T(8,128)(2,1)S(1)}, u32[]{:S(2)}, u32[]{:S(2)}) collective-permute-start(bf16[64,2048]{1,0:T(8,128)(2,1)S(1)} %collective-permute-done.1.refs_1_), channel_id=1, source_target_pairs={{0,1},{1,0},{2,3},{3,2},{4,5},{5,4},{6,7},{7,6},{8,9},{9,8},{10,11... | collective-permute-start | bytes 786440 | tf_op jit(solution)/shard_map/ppermute | solution.py:488
  34.6 2.0 %collective-permute-start.12 = (bf16[64,4096]{1,0:T(8,128)(2,1)S(1)}, bf16[64,4096]{1,0:T(8,128)(2,1)S(1)}, u32[]{:S(2)}, u32[]{:S(2)}) collective-permute-start(bf16[64,4096]{1,0:T(8,128)(2,1)S(1)} %get-tuple-element.47.mine_ref), channel_id=1, source_target_pairs={{0,1},{1,0},{2,3},{3,2},{4,5},{5,4},{6,7},{7,6},{8,9},{9,8},{10,11... | collective-permute-start | bytes 1572872 | tf_op jit(solution)/shard_map/ppermute | solution.py:514
  35.8 2.0 %collective-permute-start.11 = (bf16[64,4096]{1,0:T(8,128)(2,1)S(1)}, bf16[64,4096]{1,0:T(8,128)(2,1)S(1)}, u32[]{:S(2)}, u32[]{:S(2)}) collective-permute-start(bf16[64,4096]{1,0:T(8,128)(2,1)S(1)} %triplets.1.mine_ref), channel_id=1, source_target_pairs={{0,1},{1,0},{2,3},{3,2},{4,5},{5,4},{6,7},{7,6},{8,9},{9,8},{10,11... | collective-permute-start | bytes 1572872 | tf_op jit(solution)/shard_map/ppermute | solution.py:525
